TPU v7x, 32 devices: a whole 2x2x4 slice. The times are simulated.
32 devices in a mesh: groups: 2 (over y), fsdp: 16 (over z, x, core).
Axes of the slice: x: 2, y: 2, z: 4, core: 2. Of those that a mesh axis runs over, the one named last changes fastest.
Arguments:
- inputs: bfloat16 [2048, 5120], P(('groups', 'fsdp')), parts along dimension 0, may hold values from -6 to 6
- out_grad: bfloat16 [2048, 5120], P(('groups', 'fsdp')), parts along dimension 0, may hold values from -6 to 6
- example_ids: int32 [2048], P(('groups', 'fsdp')), parts along dimension 0, may hold values from 0 to 1, never falling along the last dimension, each value on 1 to 768 neighbouring positions
- gate_weight: bfloat16 [5120, 13824], P(None, 'fsdp'), may hold values from -0.078125 to 0.078125
- up_weight: bfloat16 [5120, 13824], P(None, 'fsdp'), may hold values from -0.078125 to 0.078125
- down_weight: bfloat16 [13824, 5120], P('fsdp'), may hold values from -0.0546875 to 0.0546875
- unit_buckets: int32 [3, 13824], P(None, 'fsdp'), may hold values from 0 to 255
- unit_signs: int32 [3, 13824], P(None, 'fsdp'), may hold values from 0 to 1
- feature_buckets: int32 [5120], replicated, may hold values from 0 to 255
- feature_signs: int32 [5120], replicated, may hold values from 0 to 1
Outputs:
- sketch: float32 [4, 256, 256], P('groups', 'fsdp'), parts along dimension 0
There are 2 independent parts, one for each index of `groups`. A program takes and returns all parts, laid end to end along the dimension named above; an argument that names none is the same for every part. Nothing has to cross between parts.
Inputs may be any that keep to these rules, and one draw needn't show every extreme that they name: `example_ids`: ids never fall along the tokens; every example has 1 to min(1024, 768) tokens in one run.
All inputs are finite; a program needn't handle non-finite values.
Results may differ from a plain program's by a relative error of at most 0.0046.
Values may be sent and summed in bfloat16 or wider, within the bound.
No kernel may reach another device: no remote copies, remote signals or barrier semaphores. Data moves between devices by JAX's collectives and lax.ppermute only.
A program may use at most 128 MiB of HBM per device.

v0:
```python
import functools

import jax
import jax.numpy as jnp
from jax import lax
from jax.experimental import pallas as pl
from jax.experimental.pallas import tpu as pltpu
from jax.sharding import PartitionSpec as P

D = 5120
FF = 13824
EX = 2
SEQ = 512
K1 = 256
K2 = 256
CORES = 2
OUTER = 4
DEPTH = 1024
LANES = 128
VMEM_LIMIT = 56 << 20


def sign_tables(buckets, sign_bits, buckets_count):
    matches = buckets[..., None, :] == jnp.arange(buckets_count, dtype=jnp.int32)[:, None]
    signed = (2 * sign_bits - 1).astype(jnp.bfloat16)[..., None, :]
    return jnp.where(matches, signed, jnp.zeros_like(signed))


class Layout:
    def __init__(self, count):
        self.outer = OUTER if count % (OUTER * CORES) == 0 else 1
        self.inner = count // (self.outer * CORES)
        self.count = count

    def index(self, outer, inner, core):
        return ((outer % self.outer) * self.inner + inner % self.inner) * CORES + core

    def pairs(self, step):
        places = [
            (o, i, c)
            for o in range(self.outer)
            for i in range(self.inner)
            for c in range(CORES)
        ]
        return [(self.index(o, i, c), self.index(*step(o, i, c))) for o, i, c in places]

    def outer_ring(self):
        return self.pairs(lambda o, i, c: (o + 1 - 2 * c, i, c))

    def inner_ring(self):
        return self.pairs(lambda o, i, c: (o, i + 1 - 2 * c, c))

    def outer_shift(self, by):
        return self.pairs(lambda o, i, c: (o + by, i, c))

    def inner_shift(self, by):
        return self.pairs(lambda o, i, c: (o, i + by, c))

    def core_swap(self):
        return self.pairs(lambda o, i, c: (o, i, 1 - c))


def rows_of(refs):
    return jnp.concatenate([ref[...] for ref in refs], axis=0) if len(refs) > 1 else refs[0][...]


def dot(left, right):
    return jnp.dot(left, right, preferred_element_type=jnp.float32)


def dot_rows(left, right):
    return lax.dot_general(
        left, right, (((1,), (1,)), ((), ())), preferred_element_type=jnp.float32
    )


def chunk_kernel(pieces, *refs):
    ins, outs, ids = (refs[i * pieces : (i + 1) * pieces] for i in range(3))
    gate_w, up_w, down_w, feature_w, tables, before, total = refs[3 * pieces : 3 * pieces + 7]
    gate_acc, up_acc, hidden_acc, in_acc, out_acc = accs = refs[3 * pieces + 7 :]
    step = pl.program_id(0)

    @pl.when(step == 0)
    def _():
        for acc in accs:
            acc[...] = jnp.zeros_like(acc)

    rows_in, rows_out = rows_of(ins), rows_of(outs)
    gate_acc[...] += dot_rows(gate_w[...], rows_in)
    up_acc[...] += dot_rows(up_w[...], rows_in)
    in_acc[...] += dot_rows(rows_in, feature_w[...])
    hidden_acc[...] += dot_rows(down_w[...], rows_out)
    out_acc[...] += dot_rows(rows_out, feature_w[...])

    @pl.when(step == pl.num_programs(0) - 1)
    def _():
        gate, up, hidden_grad = gate_acc[...], up_acc[...], hidden_acc[...]
        sigmoid = jax.nn.sigmoid(gate)
        activated = gate * sigmoid
        hidden = activated * up
        gate_grad = hidden_grad * up * sigmoid * (1.0 + gate * (1.0 - sigmoid))
        up_grad = hidden_grad * activated
        bf16 = jnp.bfloat16
        down_part = dot(tables[2], hidden.astype(bf16)).astype(bf16)
        input_part = (
            dot(tables[0], gate_grad.astype(bf16)) + dot(tables[1], up_grad.astype(bf16))
        ).astype(bf16)
        example = rows_of(ids).astype(jnp.float32)
        example = jnp.concatenate([example] * (K2 // LANES), axis=1)

        def by_example(features):
            rounded = features.astype(bf16).astype(jnp.float32)
            return jnp.concatenate(
                [jnp.where(example == e, rounded, 0.0) for e in range(EX)], axis=1
            ).astype(bf16)

        total[...] = (
            before[...]
            + dot(down_part, by_example(out_acc[...]))
            + dot(input_part, by_example(in_acc[...]))
        )


def chunk(pieces, gate_rows, up_rows, down_rows, feature_table, tables, before):
    own = pieces[0].shape[0]
    units, model = gate_rows.shape
    rows = own * len(pieces)
    depth = min(DEPTH, model)
    steps = model // depth
    whole = lambda shape: pl.BlockSpec(shape, lambda k: (0,) * len(shape))
    weight = pl.BlockSpec((units, depth), lambda k: (0, k))
    f32 = jnp.float32
    return pl.pallas_call(
        functools.partial(chunk_kernel, len(pieces)),
        grid=(steps,),
        in_specs=[pl.BlockSpec((own, depth), lambda k: (0, k))] * len(pieces)
        + [pl.BlockSpec((own, depth), lambda k: (0, steps + k))] * len(pieces)
        + [pl.BlockSpec((own, LANES), lambda k: (0, 2 * model // LANES))] * len(pieces)
        + [weight, weight, weight, pl.BlockSpec((K2, depth), lambda k: (0, k))]
        + [whole(tables.shape), whole(before.shape)],
        out_specs=whole(before.shape),
        out_shape=jax.ShapeDtypeStruct(before.shape, f32),
        scratch_shapes=[pltpu.VMEM((units, rows), f32)] * 3 + [pltpu.VMEM((rows, K2), f32)] * 2,
        compiler_params=pltpu.CompilerParams(vmem_limit_bytes=VMEM_LIMIT),
        cost_estimate=pl.CostEstimate(
            flops=2 * rows * model * (3 * units + 2 * K2),
            bytes_accessed=2 * model * (3 * units + K2 + 2 * rows),
            transcendentals=rows * units,
        ),
        name="chunk",
    )(*pieces, *pieces, *pieces, gate_rows, up_rows, down_rows, feature_table, tables, before)


def on_device(
    layout,
    inputs,
    out_grad,
    example_ids,
    gate_weight,
    up_weight,
    down_weight,
    unit_buckets,
    unit_signs,
    feature_buckets,
    feature_signs,
):
    def move(value, pairs):
        return lax.ppermute(value, "fsdp", pairs)

    me = lax.axis_index("fsdp")
    core = me % CORES
    inner = (me // CORES) % layout.inner
    outer = me // (CORES * layout.inner)
    rows = inputs.shape[0]

    unit_tables = sign_tables(unit_buckets, unit_signs, K1)
    feature_table = sign_tables(feature_buckets, feature_signs, K2)

    example = jnp.broadcast_to(example_ids[:, None], (rows, LANES)).astype(jnp.bfloat16)
    own = jnp.concatenate([inputs, out_grad, example], axis=1)

    if layout.inner == 2:
        held = {(0, 0): own}
        for o in range(layout.outer):
            if o:
                held[o, 0] = move(held[o - 1, 0], layout.outer_ring())
            held[o, 1] = move(held[o, 0], layout.inner_ring())
        swapped = {at: move(piece, layout.core_swap()) for at, piece in held.items()}
        chunks = {}
        for at in sorted(held, key=lambda at: (sum(at), at[1])):
            chunks.setdefault(sum(at), []).extend([held[at], swapped[at]])
        chunks = [chunks[when] for when in sorted(chunks)]
    else:
        chunks = [[lax.all_gather(own, "fsdp", axis=0, tiled=True)]]

    total = jnp.zeros((K1, EX * K2), jnp.float32)
    for pieces in chunks:
        total = chunk(
            pieces,
            gate_weight.T,
            up_weight.T,
            down_weight,
            feature_table,
            unit_tables,
            total,
        )

    part = total.reshape(layout.outer, layout.inner, CORES, -1, EX * K2)
    take = lambda v, at, axis: lax.dynamic_index_in_dim(v, at, axis, keepdims=False)
    part = take(part, core, 2) + move(take(part, 1 - core, 2), layout.core_swap())
    part = take(part, inner, 1) + sum(
        move(take(part, (inner + by) % layout.inner, 1), layout.inner_shift(by))
        for by in range(1, layout.inner)
    )
    part = take(part, outer, 0) + sum(
        move(take(part, (outer + by) % layout.outer, 0), layout.outer_shift(by))
        for by in range(1, layout.outer)
    )
    factor = (3.0 * SEQ * FF * D / (K1 * K2)) ** (-0.5)
    return (factor * part).reshape(-1, EX, K2).transpose(1, 0, 2)


def solution(mesh):
    layout = Layout(mesh.shape["fsdp"])
    in_specs = (
        P(("groups", "fsdp"), None),
        P(("groups", "fsdp"), None),
        P(("groups", "fsdp")),
        P(None, "fsdp"),
        P(None, "fsdp"),
        P("fsdp", None),
        P(None, "fsdp"),
        P(None, "fsdp"),
        P(),
        P(),
    )
    out_specs = P("groups", "fsdp", None)
    return jax.shard_map(
        lambda *args: on_device(layout, *args),
        mesh=mesh,
        in_specs=in_specs,
        out_specs=out_specs,
        check_vma=False,
    )
```

profile of v0, /device:TPU:0, one launch (start us, length us, event | category | flops | bytes accessed | tf_op | source)
XLA Modules:
  0.0 212.1 jit_solution(11943579301119751938)
XLA Ops:
  0.0 0.7 convert_element_type.10
  0.7 0.1 broadcast_in_dim.48
  0.7 1.4 pad_maximum_fusion.refs_0_.refs_2_.refs_4_
  2.1 0.0 copy-start
  2.2 3.1 %collective-permute-start = (bf16[64,10368]{1,0:T(8,128)(2,1)S(1)}, bf16[64,10368]{1,0:T(8,128)(2,1)}, u32[]{:S(2)}, u32[]{:S(2)}) collective-permute-start(bf16[64,10368]{1,0:T(8,128)(2,1)S(1)} %pad_maximum_fusion.refs_0_.refs_2_.refs_4_), channel_id=1, source_target_pairs={{0,4},{1,13},{2,6},{3,15},{4,8},{5,1},{6,10},{7,3},{8,12},{9,5},{1... | collective-permute-start | bytes 3981320 | tf_op jit(solution)/shard_map/ppermute | solution.py:168
  5.2 1.5 collective-permute-start.12
  6.7 29.9 %collective-permute-done.refs_0_.refs_4_.refs_8_ = bf16[64,10368]{1,0:T(8,128)(2,1)} collective-permute-done((bf16[64,10368]{1,0:T(8,128)(2,1)S(1)}, bf16[64,10368]{1,0:T(8,128)(2,1)}, u32[]{:S(2)}, u32[]{:S(2)}) %collective-permute-start) | collective-permute-done | bytes 1327136 | tf_op jit(solution)/shard_map/ppermute | solution.py:168
  36.7 0.0 collective-permute-start.1
  36.7 2.1 %collective-permute-start.14 = (bf16[64,10368]{1,0:T(8,128)(2,1)S(1)}, bf16[64,10368]{1,0:T(8,128)(2,1)S(1)}, u32[]{:S(2)}, u32[]{:S(2)}) collective-permute-start(bf16[64,10368]{1,0:T(8,128)(2,1)S(1)} %pad_maximum_fusion.refs_0_.refs_2_.refs_4_), channel_id=1, source_target_pairs={{0,1},{1,0},{2,3},{3,2},{4,5},{5,4},{6,7},{7,6},{8,9},{9,8},{10,11... | collective-permute-start | bytes 3981320 | tf_op jit(solution)/shard_map/ppermute | solution.py:168
  38.8 0.0 copy-done.8
  38.8 0.0 copy-start.10
  38.8 0.0 copy-start.9
  38.8 0.1 collective-permute-start.11
  38.9 1.6 collective-permute-start.9
  40.5 0.0 collective-permute-done.12.refs_2_.refs_6_.refs_10_
  40.5 0.2 collective-permute-start.13
  40.6 28.0 %collective-permute-done.1.refs_0_.refs_4_.refs_8_ = bf16[64,10368]{1,0:T(8,128)(2,1)S(1)} collective-permute-done((bf16[64,10368]{1,0:T(8,128)(2,1)}, bf16[64,10368]{1,0:T(8,128)(2,1)S(1)}, u32[]{:S(2)}, u32[]{:S(2)}) %collective-permute-start.1) | collective-permute-done | bytes 1327136 | tf_op jit(solution)/shard_map/ppermute | solution.py:168
  68.6 0.1 collective-permute-start.2
  68.8 0.0 collective-permute-done.14.refs_1_.refs_3_.refs_5_
  68.8 1.2 copy-done.2
  70.0 1.5 collective-permute-start.6
  71.4 2.2 %fusion.refs_9_.refs_15_ = bf16[256,5120]{1,0:T(8,128)(2,1)} fusion(s32[5120]{0:T(1024)S(1)} %copy-done.7, bf16[5120]{0:T(1024)(128)(2,1)S(1)} %add_convert_fusion), kind=kLoop, calls=%fused_computation.1 | loop fusion | flops 2621440 | bytes 2652160 | tf_op jit(solution)/shard_map/jit(_where)/select_n | solution.py:26
  73.7 0.0 copy-done.10
  73.7 0.0 collective-permute-done.11.refs_1_.refs_5_.refs_9_
  73.7 1.3 collective-permute-start.8
  75.0 0.0 collective-permute-done.9.refs_2_.refs_6_.refs_10_
  75.0 0.1 collective-permute-start.10
  75.1 25.0 %collective-permute-done.2.refs_0_.refs_4_.refs_8_ = bf16[64,10368]{1,0:T(8,128)(2,1)} collective-permute-done((bf16[64,10368]{1,0:T(8,128)(2,1)S(1)}, bf16[64,10368]{1,0:T(8,128)(2,1)}, u32[]{:S(2)}, u32[]{:S(2)}) %collective-permute-start.2) | collective-permute-done | bytes 1327136 | tf_op jit(solution)/shard_map/ppermute | solution.py:168
  100.0 1.5 collective-permute-start.3
  101.5 1.5 fusion.1.refs_10_.refs_16_
  103.1 0.9 broadcast_in_dim.53.refs_11_
  103.9 16.6 %chunk.5.refs_17_ = f32[256,512]{1,0:T(8,128)} custom-call(bf16[64,10368]{1,0:T(8,128)(2,1)} %copy-done, bf16[64,10368]{1,0:T(8,128)(2,1)} %copy-done.2, bf16[64,10368]{1,0:T(8,128)(2,1)} %copy-done, bf16[64,10368]{1,0:T(8,128)(2,1)} %copy-done.2, bf16[64,10368]{1,0:T(8,128)(2,1)} %copy-done, bf16[64,10368]{1,0:T(8,128)(2,1)} %copy-done.2, ...), custom_call_target="tpu_custom_call" | custom-call | flops 4068474880 | bytes 31784960 | tf_op jit(solution)/shard_map/chunk/pallas_call | solution.py:133
  120.5 0.0 collective-permute-done.13.refs_3_.refs_7_.refs_11_
  120.5 0.1 collective-permute-start.5
  120.6 0.0 collective-permute-done.6.refs_2_.refs_6_.refs_10_
  120.6 0.5 collective-permute-start.7
  121.1 17.4 %chunk.6.refs_17_ = f32[256,512]{1,0:T(8,128)} custom-call(bf16[64,10368]{1,0:T(8,128)(2,1)} %collective-permute-done.refs_0_.refs_4_.refs_8_, bf16[64,10368]{1,0:T(8,128)(2,1)} %collective-permute-done.11.refs_1_.refs_5_.refs_9_, bf16[64,10368]{1,0:T(8,128)(2,1)} %collective-permute-done.12.refs_2_.refs_6_.refs_10_, ...), custom_call_target="tpu_custom_call" | custom-call | flops 8136949760 | bytes 34406400 | tf_op jit(solution)/shard_map/chunk/pallas_call | solution.py:133
  138.5 0.0 collective-permute-done.3.refs_0_.refs_2_.refs_4_
  138.5 0.0 copy-start.3
  138.5 0.2 collective-permute-start.4
  138.7 0.0 collective-permute-done.8.refs_1_.refs_5_.refs_9_
  138.7 0.0 collective-permute-done.10.refs_3_.refs_7_.refs_11_
  138.7 1.2 copy-done.4
  139.9 1.1 copy-done.5
  141.0 17.4 %chunk.7.refs_17_ = f32[256,512]{1,0:T(8,128)} custom-call(bf16[64,10368]{1,0:T(8,128)(2,1)} %copy-done.1, bf16[64,10368]{1,0:T(8,128)(2,1)} %copy-done.4, bf16[64,10368]{1,0:T(8,128)(2,1)} %collective-permute-done.9.refs_2_.refs_6_.refs_10_, bf16[64,10368]{1,0:T(8,128)(2,1)} %copy-done.5, bf16[64,10368]{1,0:T(8,128)(2,1)} %copy-done.1, ...), custom_call_target="tpu_custom_call" | custom-call | flops 8136949760 | bytes 34406400 | tf_op jit(solution)/shard_map/chunk/pallas_call | solution.py:133
  158.5 0.0 collective-permute-done.5.refs_1_.refs_5_.refs_9_
  158.5 0.0 collective-permute-done.7.refs_3_.refs_7_.refs_11_
  158.5 1.1 copy-done.6
  159.6 17.4 %chunk.8.refs_11_ = f32[256,512]{1,0:T(8,128)} custom-call(bf16[64,10368]{1,0:T(8,128)(2,1)} %collective-permute-done.2.refs_0_.refs_4_.refs_8_, bf16[64,10368]{1,0:T(8,128)(2,1)} %copy-done.6, bf16[64,10368]{1,0:T(8,128)(2,1)} %collective-permute-done.6.refs_2_.refs_6_.refs_10_, bf16[64,10368]{1,0:T(8,128)(2,1)} %collective-permute-done.7.refs_3_.refs_7_.refs_11_, ...), custom_call_target="tpu_custom_call" | custom-call | flops 8136949760 | bytes 34406400 | tf_op jit(solution)/shard_map/chunk/pallas_call | solution.py:133
  177.0 0.0 collective-permute-done.4.refs_1_.refs_3_.refs_5_
  177.1 16.8 %chunk.9 = f32[256,512]{1,0:T(8,128)} custom-call(bf16[64,10368]{1,0:T(8,128)(2,1)} %copy-done.3, bf16[64,10368]{1,0:T(8,128)(2,1)} %collective-permute-done.4.refs_1_.refs_3_.refs_5_, bf16[64,10368]{1,0:T(8,128)(2,1)} %copy-done.3, bf16[64,10368]{1,0:T(8,128)(2,1)} %collective-permute-done.4.refs_1_.refs_3_.refs_5_, bf16[64,10368]{1,0:T(8,128)(2,1)} %copy-done.3, ...), custom_call_target="tpu_custom_call" | custom-call | flops 4068474880 | bytes 31784960 | tf_op jit(solution)/shard_map/chunk/pallas_call | solution.py:133
  193.9 1.0 dynamic-slice_bitcast_fusion
  194.9 0.3 collective-permute-start.15
  195.2 1.3 collective-permute-done.15
  196.5 1.0 bitcast_add_fusion
  197.5 0.6 collective-permute-start.16
  198.1 5.1 %collective-permute-done.16 = f32[4,16,512]{2,1,0:T(8,128)S(1)} collective-permute-done((f32[4,16,512]{2,1,0:T(8,128)S(1)}, f32[4,16,512]{2,1,0:T(8,128)S(1)}, u32[]{:S(2)}, u32[]{:S(2)}) %collective-permute-start.16) | collective-permute-done | bytes 131104 | tf_op jit(solution)/shard_map/ppermute | solution.py:168
  203.2 0.7 collective-permute-start.17
  203.9 3.6 %collective-permute-start.18 = (f32[16,512]{1,0:T(8,128)S(1)}, f32[16,512]{1,0:T(8,128)S(1)}, u32[]{:S(2)}, u32[]{:S(2)}) collective-permute-start(f32[16,512]{1,0:T(8,128)S(1)} %get-tuple-element.5), channel_id=1, source_target_pairs={{0,8},{1,9},{2,10},{3,11},{4,12},{5,13},{6,14},{7,15},{8,0},{9,1},... | collective-permute-start | bytes 98312 | tf_op jit(solution)/shard_map/ppermute | solution.py:168
  207.5 1.3 collective-permute-start.19
  208.9 0.5 collective-permute-done.17
  209.4 0.6 collective-permute-done.18
  210.0 1.4 collective-permute-done.19
  211.5 0.6 copy.11
  (19 shorter events, 0.1 us)
Async XLA Ops:
  0.7 38.0 %copy-start.8 = (s32[5120]{0:T(1024)S(1)}, s32[5120]{0:T(1024)}, u32[]{:S(2)}) copy-start(s32[5120]{0:T(1024)} %param.19) | copy-start | bytes 61444
  0.7 70.7 %copy-start.7 = (s32[5120]{0:T(1024)S(1)}, s32[5120]{0:T(1024)}, u32[]{:S(2)}) copy-start(s32[5120]{0:T(1024)} %param.18) | copy-start | bytes 61444
  2.1 71.5 %copy-start = (bf16[64,10368]{1,0:T(8,128)(2,1)}, bf16[64,10368]{1,0:T(8,128)(2,1)S(1)}, u32[]{:S(2)}) copy-start(bf16[64,10368]{1,0:T(8,128)(2,1)S(1)} %pad_maximum_fusion.refs_0_.refs_2_.refs_4_) | copy-start | bytes 3981316
  2.2 34.5 %collective-permute-start = (bf16[64,10368]{1,0:T(8,128)(2,1)S(1)}, bf16[64,10368]{1,0:T(8,128)(2,1)}, u32[]{:S(2)}, u32[]{:S(2)}) collective-permute-start(bf16[64,10368]{1,0:T(8,128)(2,1)S(1)} %pad_maximum_fusion.refs_0_.refs_2_.refs_4_), channel_id=1, source_target_pairs={{0,4},{1,13},{2,6},{3,15},{4,8},{5,1},{6,10},{7,3},{8,12},{9,5},{1... | collective-permute-start | bytes 3981320 | tf_op jit(solution)/shard_map/ppermute | solution.py:168
  5.2 35.2 %collective-permute-start.12 = (bf16[64,10368]{1,0:T(8,128)(2,1)S(1)}, bf16[64,10368]{1,0:T(8,128)(2,1)}, u32[]{:S(2)}, u32[]{:S(2)}) collective-permute-start(bf16[64,10368]{1,0:T(8,128)(2,1)S(1)} %pad_maximum_fusion.refs_0_.refs_2_.refs_4_), channel_id=1, source_target_pairs={{0,2},{1,3},{2,0},{3,1},{4,6},{5,7},{6,4},{7,5},{8,10},{9,11},{10,... | collective-permute-start | bytes 3981320 | tf_op jit(solution)/shard_map/ppermute | solution.py:168
  36.7 32.0 %collective-permute-start.1 = (bf16[64,10368]{1,0:T(8,128)(2,1)}, bf16[64,10368]{1,0:T(8,128)(2,1)S(1)}, u32[]{:S(2)}, u32[]{:S(2)}) collective-permute-start(bf16[64,10368]{1,0:T(8,128)(2,1)} %collective-permute-done.refs_0_.refs_4_.refs_8_), channel_id=1, source_target_pairs={{0,4},{1,13},{2,6},{3,15},{4,8},{5,1},{6,10},{7,3},{8,12},{9,5},{1... | collective-permute-start | bytes 3981320 | tf_op jit(solution)/shard_map/ppermute | solution.py:168
  36.7 32.1 %collective-permute-start.14 = (bf16[64,10368]{1,0:T(8,128)(2,1)S(1)}, bf16[64,10368]{1,0:T(8,128)(2,1)S(1)}, u32[]{:S(2)}, u32[]{:S(2)}) collective-permute-start(bf16[64,10368]{1,0:T(8,128)(2,1)S(1)} %pad_maximum_fusion.refs_0_.refs_2_.refs_4_), channel_id=1, source_target_pairs={{0,1},{1,0},{2,3},{3,2},{4,5},{5,4},{6,7},{7,6},{8,9},{9,8},{10,11... | collective-permute-start | bytes 3981320 | tf_op jit(solution)/shard_map/ppermute | solution.py:168
  38.8 34.9 %copy-start.10 = (s32[3,864]{1,0:T(4,128)S(1)}, s32[3,864]{1,0:T(4,128)}, u32[]{:S(2)}) copy-start(s32[3,864]{1,0:T(4,128)} %param.17) | copy-start | bytes 31108
  38.8 62.7 %copy-start.9 = (s32[3,864]{1,0:T(4,128)S(1)}, s32[3,864]{1,0:T(4,128)}, u32[]{:S(2)}) copy-start(s32[3,864]{1,0:T(4,128)} %param.16) | copy-start | bytes 31108
  38.8 34.9 %collective-permute-start.11 = (bf16[64,10368]{1,0:T(8,128)(2,1)}, bf16[64,10368]{1,0:T(8,128)(2,1)}, u32[]{:S(2)}, u32[]{:S(2)}) collective-permute-start(bf16[64,10368]{1,0:T(8,128)(2,1)} %collective-permute-done.refs_0_.refs_4_.refs_8_), channel_id=1, source_target_pairs={{0,1},{1,0},{2,3},{3,2},{4,5},{5,4},{6,7},{7,6},{8,9},{9,8},{10,11... | collective-permute-start | bytes 3981320 | tf_op jit(solution)/shard_map/ppermute | solution.py:168
  38.9 36.1 %collective-permute-start.9 = (bf16[64,10368]{1,0:T(8,128)(2,1)}, bf16[64,10368]{1,0:T(8,128)(2,1)}, u32[]{:S(2)}, u32[]{:S(2)}) collective-permute-start(bf16[64,10368]{1,0:T(8,128)(2,1)} %collective-permute-done.refs_0_.refs_4_.refs_8_), channel_id=1, source_target_pairs={{0,2},{1,3},{2,0},{3,1},{4,6},{5,7},{6,4},{7,5},{8,10},{9,11},{10,... | collective-permute-start | bytes 3981320 | tf_op jit(solution)/shard_map/ppermute | solution.py:168
  40.5 80.1 %collective-permute-start.13 = (bf16[64,10368]{1,0:T(8,128)(2,1)}, bf16[64,10368]{1,0:T(8,128)(2,1)}, u32[]{:S(2)}, u32[]{:S(2)}) collective-permute-start(bf16[64,10368]{1,0:T(8,128)(2,1)} %collective-permute-done.12.refs_2_.refs_6_.refs_10_), channel_id=1, source_target_pairs={{0,1},{1,0},{2,3},{3,2},{4,5},{5,4},{6,7},{7,6},{8,9},{9,8},{10,11... | collective-permute-start | bytes 3981320 | tf_op jit(solution)/shard_map/ppermute | solution.py:168
  68.6 5.1 %copy-start.1 = (bf16[64,10368]{1,0:T(8,128)(2,1)}, bf16[64,10368]{1,0:T(8,128)(2,1)S(1)}, u32[]{:S(2)}) copy-start(bf16[64,10368]{1,0:T(8,128)(2,1)S(1)} %collective-permute-done.1.refs_0_.refs_4_.refs_8_) | copy-start | bytes 3981316
  68.6 31.4 %collective-permute-start.2 = (bf16[64,10368]{1,0:T(8,128)(2,1)S(1)}, bf16[64,10368]{1,0:T(8,128)(2,1)}, u32[]{:S(2)}, u32[]{:S(2)}) collective-permute-start(bf16[64,10368]{1,0:T(8,128)(2,1)S(1)} %collective-permute-done.1.refs_0_.refs_4_.refs_8_), channel_id=1, source_target_pairs={{0,4},{1,13},{2,6},{3,15},{4,8},{5,1},{6,10},{7,3},{8,12},{9,5},{1... | collective-permute-start | bytes 3981320 | tf_op jit(solution)/shard_map/ppermute | solution.py:168
  68.8 1.2 copy-start.2
  70.0 50.7 %collective-permute-start.6 = (bf16[64,10368]{1,0:T(8,128)(2,1)S(1)}, bf16[64,10368]{1,0:T(8,128)(2,1)}, u32[]{:S(2)}, u32[]{:S(2)}) collective-permute-start(bf16[64,10368]{1,0:T(8,128)(2,1)S(1)} %collective-permute-done.1.refs_0_.refs_4_.refs_8_), channel_id=1, source_target_pairs={{0,2},{1,3},{2,0},{3,1},{4,6},{5,7},{6,4},{7,5},{8,10},{9,11},{10,... | collective-permute-start | bytes 3981320 | tf_op jit(solution)/shard_map/ppermute | solution.py:168
  73.7 65.0 %collective-permute-start.8 = (bf16[64,10368]{1,0:T(8,128)(2,1)S(1)}, bf16[64,10368]{1,0:T(8,128)(2,1)S(1)}, u32[]{:S(2)}, u32[]{:S(2)}) collective-permute-start(bf16[64,10368]{1,0:T(8,128)(2,1)S(1)} %collective-permute-done.1.refs_0_.refs_4_.refs_8_), channel_id=1, source_target_pairs={{0,1},{1,0},{2,3},{3,2},{4,5},{5,4},{6,7},{7,6},{8,9},{9,8},{10,11... | collective-permute-start | bytes 3981320 | tf_op jit(solution)/shard_map/ppermute | solution.py:168
  75.0 63.7 %collective-permute-start.10 = (bf16[64,10368]{1,0:T(8,128)(2,1)}, bf16[64,10368]{1,0:T(8,128)(2,1)S(1)}, u32[]{:S(2)}, u32[]{:S(2)}) collective-permute-start(bf16[64,10368]{1,0:T(8,128)(2,1)} %collective-permute-done.9.refs_2_.refs_6_.refs_10_), channel_id=1, source_target_pairs={{0,1},{1,0},{2,3},{3,2},{4,5},{5,4},{6,7},{7,6},{8,9},{9,8},{10,11... | collective-permute-start | bytes 3981320 | tf_op jit(solution)/shard_map/ppermute | solution.py:168
  100.0 38.5 %collective-permute-start.3 = (bf16[64,10368]{1,0:T(8,128)(2,1)}, bf16[64,10368]{1,0:T(8,128)(2,1)S(1)}, u32[]{:S(2)}, u32[]{:S(2)}) collective-permute-start(bf16[64,10368]{1,0:T(8,128)(2,1)} %collective-permute-done.2.refs_0_.refs_4_.refs_8_), channel_id=1, source_target_pairs={{0,2},{1,3},{2,0},{3,1},{4,6},{5,7},{6,4},{7,5},{8,10},{9,11},{10,... | collective-permute-start | bytes 3981320 | tf_op jit(solution)/shard_map/ppermute | solution.py:168
  120.5 38.0 %collective-permute-start.5 = (bf16[64,10368]{1,0:T(8,128)(2,1)}, bf16[64,10368]{1,0:T(8,128)(2,1)S(1)}, u32[]{:S(2)}, u32[]{:S(2)}) collective-permute-start(bf16[64,10368]{1,0:T(8,128)(2,1)} %collective-permute-done.2.refs_0_.refs_4_.refs_8_), channel_id=1, source_target_pairs={{0,1},{1,0},{2,3},{3,2},{4,5},{5,4},{6,7},{7,6},{8,9},{9,8},{10,11... | collective-permute-start | bytes 3981320 | tf_op jit(solution)/shard_map/ppermute | solution.py:168
  120.6 37.9 %collective-permute-start.7 = (bf16[64,10368]{1,0:T(8,128)(2,1)}, bf16[64,10368]{1,0:T(8,128)(2,1)}, u32[]{:S(2)}, u32[]{:S(2)}) collective-permute-start(bf16[64,10368]{1,0:T(8,128)(2,1)} %collective-permute-done.6.refs_2_.refs_6_.refs_10_), channel_id=1, source_target_pairs={{0,1},{1,0},{2,3},{3,2},{4,5},{5,4},{6,7},{7,6},{8,9},{9,8},{10,11... | collective-permute-start | bytes 3981320 | tf_op jit(solution)/shard_map/ppermute | solution.py:168
  138.5 19.9 %copy-start.3 = (bf16[64,10368]{1,0:T(8,128)(2,1)}, bf16[64,10368]{1,0:T(8,128)(2,1)S(1)}, u32[]{:S(2)}) copy-start(bf16[64,10368]{1,0:T(8,128)(2,1)S(1)} %collective-permute-done.3.refs_0_.refs_2_.refs_4_) | copy-start | bytes 3981316
  138.5 38.5 %collective-permute-start.4 = (bf16[64,10368]{1,0:T(8,128)(2,1)S(1)}, bf16[64,10368]{1,0:T(8,128)(2,1)}, u32[]{:S(2)}, u32[]{:S(2)}) collective-permute-start(bf16[64,10368]{1,0:T(8,128)(2,1)S(1)} %collective-permute-done.3.refs_0_.refs_2_.refs_4_), channel_id=1, source_target_pairs={{0,1},{1,0},{2,3},{3,2},{4,5},{5,4},{6,7},{7,6},{8,9},{9,8},{10,11... | collective-permute-start | bytes 3981320 | tf_op jit(solution)/shard_map/ppermute | solution.py:168
  138.7 1.2 copy-start.4
  139.9 1.1 copy-start.5
  158.5 1.1 copy-start.6
  194.9 1.6 collective-permute-start.15
  197.5 5.7 %collective-permute-start.16 = (f32[4,16,512]{2,1,0:T(8,128)S(1)}, f32[4,16,512]{2,1,0:T(8,128)S(1)}, u32[]{:S(2)}, u32[]{:S(2)}) collective-permute-start(f32[4,16,512]{2,1,0:T(8,128)S(1)} %dynamic-slice_bitcast_fusion.1), channel_id=1, source_target_pairs={{0,2},{1,3},{2,0},{3,1},{4,6},{5,7},{6,4},{7,5},{8,10},{9,11},{10,... | collective-permute-start | bytes 393224 | tf_op jit(solution)/shard_map/ppermute | solution.py:168
  203.2 6.1 %collective-permute-start.17 = (f32[16,512]{1,0:T(8,128)S(1)}, f32[16,512]{1,0:T(8,128)S(1)}, u32[]{:S(2)}, u32[]{:S(2)}) collective-permute-start(f32[16,512]{1,0:T(8,128)S(1)} %get-tuple-element.7), channel_id=1, source_target_pairs={{0,4},{1,5},{2,6},{3,7},{4,8},{5,9},{6,10},{7,11},{8,12},{9,13},{1... | collective-permute-start | bytes 98312 | tf_op jit(solution)/shard_map/ppermute | solution.py:168
  203.9 6.1 %collective-permute-start.18 = (f32[16,512]{1,0:T(8,128)S(1)}, f32[16,512]{1,0:T(8,128)S(1)}, u32[]{:S(2)}, u32[]{:S(2)}) collective-permute-start(f32[16,512]{1,0:T(8,128)S(1)} %get-tuple-element.5), channel_id=1, source_target_pairs={{0,8},{1,9},{2,10},{3,11},{4,12},{5,13},{6,14},{7,15},{8,0},{9,1},... | collective-permute-start | bytes 98312 | tf_op jit(solution)/shard_map/ppermute | solution.py:168
  207.5 3.9 %collective-permute-start.19 = (f32[16,512]{1,0:T(8,128)S(1)}, f32[16,512]{1,0:T(8,128)S(1)}, u32[]{:S(2)}, u32[]{:S(2)}) collective-permute-start(f32[16,512]{1,0:T(8,128)S(1)} %get-tuple-element.6), channel_id=1, source_target_pairs={{0,12},{1,13},{2,14},{3,15},{4,0},{5,1},{6,2},{7,3},{8,4},{9,5},{1... | collective-permute-start | bytes 98312 | tf_op jit(solution)/shard_map/ppermute | solution.py:168
where the time goes:
time: 212 us
  waiting for transfers between devices  91.9 us (43%)
  Pallas kernels  85.7 us (40%)
  starting transfers between devices  20.2 us (10%)
  local copies, waits for them, and re-layouts  7.22 us (3%)
  other arithmetic  6.85 us (3%)
    ppermute x20, waiting for transfers between devices, move(): return lax.ppermute(value, 'fsdp', pairs)  91.9 us
    pallas_call x5, Pallas kernels, chunk(): pl.pallas_call(functools.partial(chunk_kernel, len(pieces)), grid=(steps,...  85.7 us
    ppermute x20, starting transfers between devices, move(): return lax.ppermute(value, 'fsdp', pairs)  20.2 us
    unnamed x22, local copies, waits for them, and re-layouts  4.62 us
  transfers between devices with their start and end apart: 20, of which 8 were waited for; matrix products, arithmetic and copies ran while one was open for 2% of the time, Pallas kernels for 32%

commit v1 on v0

--- a/solution.py
+++ b/solution.py
@@ -179,31 +179,27 @@
     example = jnp.broadcast_to(example_ids[:, None], (rows, LANES)).astype(jnp.bfloat16)
     own = jnp.concatenate([inputs, out_grad, example], axis=1)
 
+    total = jnp.zeros((K1, EX * K2), jnp.float32)
+    add = lambda pieces, total: chunk(
+        pieces, gate_weight.T, up_weight.T, down_weight, feature_table, unit_tables, total
+    )
     if layout.inner == 2:
-        held = {(0, 0): own}
-        for o in range(layout.outer):
-            if o:
-                held[o, 0] = move(held[o - 1, 0], layout.outer_ring())
-            held[o, 1] = move(held[o, 0], layout.inner_ring())
-        swapped = {at: move(piece, layout.core_swap()) for at, piece in held.items()}
-        chunks = {}
-        for at in sorted(held, key=lambda at: (sum(at), at[1])):
-            chunks.setdefault(sum(at), []).extend([held[at], swapped[at]])
-        chunks = [chunks[when] for when in sorted(chunks)]
+        swap = lambda piece: move(piece, layout.core_swap())
+        here, across = own, None
+        for step in range(layout.outer):
+            ahead = move(here, layout.outer_ring()) if step < layout.outer - 1 else None
+            next_across = move(here, layout.inner_ring())
+            pieces = [here, swap(here)]
+            if across is not None:
+                pieces += [across, swap(across)]
+            total = add(pieces, total)
+            if ahead is not None:
+                here, across, total = lax.optimization_barrier((ahead, next_across, total))
+            else:
+                across, total = lax.optimization_barrier((next_across, total))
+        total = add([across, swap(across)], total)
     else:
-        chunks = [[lax.all_gather(own, "fsdp", axis=0, tiled=True)]]
-
-    total = jnp.zeros((K1, EX * K2), jnp.float32)
-    for pieces in chunks:
-        total = chunk(
-            pieces,
-            gate_weight.T,
-            up_weight.T,
-            down_weight,
-            feature_table,
-            unit_tables,
-            total,
-        )
+        total = add([lax.all_gather(own, "fsdp", axis=0, tiled=True)], total)
 
     part = total.reshape(layout.outer, layout.inner, CORES, -1, EX * K2)
     take = lambda v, at, axis: lax.dynamic_index_in_dim(v, at, axis, keepdims=False)

time: 212 us -> 172 us (0.81)
  waiting for transfers between devices: 91.9 us -> 54.3 us
  starting transfers between devices: 20.2 us -> 17.6 us
    ppermute x20, waiting for transfers between devices: 91.9 us -> 54.3 us  [move(): return lax.ppermute(value, 'fsdp', pairs)]
    ppermute x20, starting transfers between devices: 20.2 us -> 17.6 us  [move(): return lax.ppermute(value, 'fsdp', pairs)]
    unnamed x22 -> x40, local copies, waits for them, and re-layouts: 4.62 us -> 4.83 us
  transfers between devices with their start and end apart: 20 -> 20, of which waited for: 8 -> 15; matrix products, arithmetic and copies ran while one was open for 2% -> 3% of each run, Pallas kernels for 32% -> 40%
where the time goes in v1:
time: 172 us
  Pallas kernels  85.3 us (50%)
  waiting for transfers between devices  54.3 us (32%)
  starting transfers between devices  17.6 us (10%)
  local copies, waits for them, and re-layouts  7.49 us (4%)
  other arithmetic  6.82 us (4%)
    pallas_call x5, Pallas kernels, chunk(): pl.pallas_call(functools.partial(chunk_kernel, len(pieces)), grid=(steps,...  85.3 us
    ppermute x20, waiting for transfers between devices, move(): return lax.ppermute(value, 'fsdp', pairs)  54.3 us
    ppermute x20, starting transfers between devices, move(): return lax.ppermute(value, 'fsdp', pairs)  17.6 us
    unnamed x40, local copies, waits for them, and re-layouts  4.83 us
    select_n x2, other arithmetic, sign_tables(): return jnp.where(matches, signed, jnp.zeros_like(signed))  3.73 us
  transfers between devices with their start and end apart: 20, of which 15 were waited for; matrix products, arithmetic and copies ran while one was open for 3% of the time, Pallas kernels for 40%

profile of v1, /device:TPU:0, one launch (start us, length us, event | category | flops | bytes accessed | tf_op | source)
XLA Modules:
  0.0 171.7 jit_solution(3787006651303916311)
XLA Ops:
  0.0 0.7 convert_element_type.10
  0.7 0.1 broadcast_in_dim.48
  0.7 1.4 pad_maximum_fusion.refs_0_.refs_2_.refs_4_
  2.2 0.0 copy-start.17
  2.2 0.0 copy-start.16
  2.2 0.5 collective-permute-start.2
  2.7 2.6 %collective-permute-start = (bf16[64,10368]{1,0:T(8,128)(2,1)S(1)}, bf16[64,10368]{1,0:T(8,128)(2,1)S(1)}, u32[]{:S(2)}, u32[]{:S(2)}) collective-permute-start(bf16[64,10368]{1,0:T(8,128)(2,1)S(1)} %pad_maximum_fusion.refs_0_.refs_2_.refs_4_), channel_id=1, source_target_pairs={{0,4},{1,13},{2,6},{3,15},{4,8},{5,1},{6,10},{7,3},{8,12},{9,5},{1... | collective-permute-start | bytes 3981320 | tf_op jit(solution)/shard_map/ppermute | solution.py:168
  5.3 1.5 collective-permute-start.1
  6.9 1.5 fusion.1.refs_10_.refs_16_
  8.4 0.0 copy-done.17
  8.4 2.2 %fusion.refs_9_.refs_15_ = bf16[256,5120]{1,0:T(8,128)(2,1)} fusion(s32[5120]{0:T(1024)S(1)} %copy-done.16, bf16[5120]{0:T(1024)(128)(2,1)S(1)} %add_convert_fusion), kind=kLoop, calls=%fused_computation.1 | loop fusion | flops 2621440 | bytes 2652160 | tf_op jit(solution)/shard_map/jit(_where)/select_n | solution.py:26
  10.6 0.0 copy-done
  10.6 0.0 collective-permute-done.2.refs_1_.refs_3_.refs_5_
  10.6 0.9 broadcast_in_dim.53.refs_11_
  11.6 0.3 copy-done.11
  11.9 16.6 %chunk.5.refs_17_ = f32[256,512]{1,0:T(8,128)} custom-call(bf16[64,10368]{1,0:T(8,128)(2,1)} %copy-done, bf16[64,10368]{1,0:T(8,128)(2,1)} %copy-done.11, bf16[64,10368]{1,0:T(8,128)(2,1)} %copy-done, bf16[64,10368]{1,0:T(8,128)(2,1)} %copy-done.11, bf16[64,10368]{1,0:T(8,128)(2,1)} %copy-done, bf16[64,10368]{1,0:T(8,128)(2,1)} %copy-done.11, ...), custom_call_target="tpu_custom_call" | custom-call | flops 4068474880 | bytes 31784960 | tf_op jit(solution)/shard_map/chunk/pallas_call | solution.py:133
  28.4 8.8 %collective-permute-done.refs_0_.refs_4_.refs_8_ = bf16[64,10368]{1,0:T(8,128)(2,1)S(1)} collective-permute-done((bf16[64,10368]{1,0:T(8,128)(2,1)S(1)}, bf16[64,10368]{1,0:T(8,128)(2,1)S(1)}, u32[]{:S(2)}, u32[]{:S(2)}) %collective-permute-start) | collective-permute-done | bytes 1327136 | tf_op jit(solution)/shard_map/ppermute | solution.py:168
  37.3 0.0 collective-permute-done.1.refs_2_.refs_6_.refs_10_
  37.3 0.1 collective-permute-start.5
  37.4 0.5 collective-permute-start.6
  37.8 0.0 collective-permute-start.3
  37.8 1.5 collective-permute-start.4
  39.3 1.1 collective-permute-done.5.refs_1_.refs_5_.refs_9_
  40.4 1.9 %collective-permute-done.6.refs_3_.refs_7_.refs_11_ = bf16[64,10368]{1,0:T(8,128)(2,1)S(1)} collective-permute-done((bf16[64,10368]{1,0:T(8,128)(2,1)S(1)}, bf16[64,10368]{1,0:T(8,128)(2,1)S(1)}, u32[]{:S(2)}, u32[]{:S(2)}) %collective-permute-start.6) | collective-permute-done | bytes 1327136 | tf_op jit(solution)/shard_map/ppermute | solution.py:168
  42.3 0.0 copy-done.9
  42.3 1.1 copy-done.12
  43.4 17.4 %chunk.6.refs_17_ = f32[256,512]{1,0:T(8,128)} custom-call(bf16[64,10368]{1,0:T(8,128)(2,1)} %copy-done.2, bf16[64,10368]{1,0:T(8,128)(2,1)} %copy-done.9, bf16[64,10368]{1,0:T(8,128)(2,1)} %copy-done.5, bf16[64,10368]{1,0:T(8,128)(2,1)} %copy-done.12, bf16[64,10368]{1,0:T(8,128)(2,1)} %copy-done.2, bf16[64,10368]{1,0:T(8,128)(2,1)} %copy-done.9, ...), custom_call_target="tpu_custom_call" | custom-call | flops 8136949760 | bytes 34406400 | tf_op jit(solution)/shard_map/chunk/pallas_call | solution.py:133
  60.8 8.6 %collective-permute-done.3.refs_0_.refs_4_.refs_8_ = bf16[64,10368]{1,0:T(8,128)(2,1)S(1)} collective-permute-done((bf16[64,10368]{1,0:T(8,128)(2,1)S(1)}, bf16[64,10368]{1,0:T(8,128)(2,1)S(1)}, u32[]{:S(2)}, u32[]{:S(2)}) %collective-permute-start.3) | collective-permute-done | bytes 1327136 | tf_op jit(solution)/shard_map/ppermute | solution.py:168
  69.5 0.0 collective-permute-done.4.refs_2_.refs_6_.refs_10_
  69.5 0.2 collective-permute-start.10
  69.7 0.4 collective-permute-start.9
  70.1 1.2 collective-permute-start.7
  71.2 1.5 collective-permute-start.8
  72.7 0.0 collective-permute-done.10.refs_3_.refs_7_.refs_11_
  72.7 1.8 %collective-permute-done.9.refs_1_.refs_5_.refs_9_ = bf16[64,10368]{1,0:T(8,128)(2,1)S(1)} collective-permute-done((bf16[64,10368]{1,0:T(8,128)(2,1)S(1)}, bf16[64,10368]{1,0:T(8,128)(2,1)S(1)}, u32[]{:S(2)}, u32[]{:S(2)}) %collective-permute-start.9) | collective-permute-done | bytes 1327136 | tf_op jit(solution)/shard_map/ppermute | solution.py:168
  74.5 1.1 copy-done.13
  75.6 17.4 %chunk.7.refs_17_ = f32[256,512]{1,0:T(8,128)} custom-call(bf16[64,10368]{1,0:T(8,128)(2,1)} %copy-done.3, bf16[64,10368]{1,0:T(8,128)(2,1)} %copy-done.13, bf16[64,10368]{1,0:T(8,128)(2,1)} %copy-done.6, bf16[64,10368]{1,0:T(8,128)(2,1)} %copy-done.10, bf16[64,10368]{1,0:T(8,128)(2,1)} %copy-done.3, bf16[64,10368]{1,0:T(8,128)(2,1)} %copy-done.13, ...), custom_call_target="tpu_custom_call" | custom-call | flops 8136949760 | bytes 34406400 | tf_op jit(solution)/shard_map/chunk/pallas_call | solution.py:133
  93.1 9.0 %collective-permute-done.7.refs_0_.refs_4_.refs_8_ = bf16[64,10368]{1,0:T(8,128)(2,1)S(1)} collective-permute-done((bf16[64,10368]{1,0:T(8,128)(2,1)S(1)}, bf16[64,10368]{1,0:T(8,128)(2,1)S(1)}, u32[]{:S(2)}, u32[]{:S(2)}) %collective-permute-start.7) | collective-permute-done | bytes 1327136 | tf_op jit(solution)/shard_map/ppermute | solution.py:168
  102.1 1.0 collective-permute-done.8.refs_2_.refs_6_.refs_10_
  103.1 0.1 collective-permute-start.12
  103.2 0.4 collective-permute-start.13
  103.6 1.5 collective-permute-start.11
  105.1 1.1 collective-permute-done.12.refs_1_.refs_5_.refs_9_
  106.1 1.9 %collective-permute-done.13.refs_3_.refs_7_.refs_11_ = bf16[64,10368]{1,0:T(8,128)(2,1)S(1)} collective-permute-done((bf16[64,10368]{1,0:T(8,128)(2,1)S(1)}, bf16[64,10368]{1,0:T(8,128)(2,1)S(1)}, u32[]{:S(2)}, u32[]{:S(2)}) %collective-permute-start.13) | collective-permute-done | bytes 1327136 | tf_op jit(solution)/shard_map/ppermute | solution.py:168
  108.1 1.1 copy-done.15
  109.2 17.4 %chunk.8.refs_11_ = f32[256,512]{1,0:T(8,128)} custom-call(bf16[64,10368]{1,0:T(8,128)(2,1)} %copy-done.4, bf16[64,10368]{1,0:T(8,128)(2,1)} %copy-done.14, bf16[64,10368]{1,0:T(8,128)(2,1)} %copy-done.8, bf16[64,10368]{1,0:T(8,128)(2,1)} %copy-done.15, bf16[64,10368]{1,0:T(8,128)(2,1)} %copy-done.4, bf16[64,10368]{1,0:T(8,128)(2,1)} %copy-done.14, ...), custom_call_target="tpu_custom_call" | custom-call | flops 8136949760 | bytes 34406400 | tf_op jit(solution)/shard_map/chunk/pallas_call | solution.py:133
  126.6 8.2 %collective-permute-done.11.refs_0_.refs_2_.refs_4_ = bf16[64,10368]{1,0:T(8,128)(2,1)S(1)} collective-permute-done((bf16[64,10368]{1,0:T(8,128)(2,1)S(1)}, bf16[64,10368]{1,0:T(8,128)(2,1)S(1)}, u32[]{:S(2)}, u32[]{:S(2)}) %collective-permute-start.11) | collective-permute-done | bytes 1327136 | tf_op jit(solution)/shard_map/ppermute | solution.py:168
  134.7 0.0 collective-permute-start.14
  134.7 3.1 %collective-permute-done.14.refs_1_.refs_3_.refs_5_ = bf16[64,10368]{1,0:T(8,128)(2,1)S(1)} collective-permute-done((bf16[64,10368]{1,0:T(8,128)(2,1)S(1)}, bf16[64,10368]{1,0:T(8,128)(2,1)S(1)}, u32[]{:S(2)}, u32[]{:S(2)}) %collective-permute-start.14) | collective-permute-done | bytes 1327136 | tf_op jit(solution)/shard_map/ppermute | solution.py:168
  137.8 1.1 copy-done.7
  138.9 16.5 %chunk.9 = f32[256,512]{1,0:T(8,128)} custom-call(bf16[64,10368]{1,0:T(8,128)(2,1)} %copy-done.1, bf16[64,10368]{1,0:T(8,128)(2,1)} %copy-done.7, bf16[64,10368]{1,0:T(8,128)(2,1)} %copy-done.1, bf16[64,10368]{1,0:T(8,128)(2,1)} %copy-done.7, bf16[64,10368]{1,0:T(8,128)(2,1)} %copy-done.1, bf16[64,10368]{1,0:T(8,128)(2,1)} %copy-done.7, ...), custom_call_target="tpu_custom_call" | custom-call | flops 4068474880 | bytes 31784960 | tf_op jit(solution)/shard_map/chunk/pallas_call | solution.py:133
  155.4 1.0 dynamic-slice_bitcast_fusion
  156.4 0.2 collective-permute-start.15
  156.6 1.4 collective-permute-done.15
  158.0 1.0 bitcast_add_fusion
  159.0 1.6 collective-permute-start.16
  160.6 4.1 %collective-permute-done.16 = f32[4,16,512]{2,1,0:T(8,128)S(1)} collective-permute-done((f32[4,16,512]{2,1,0:T(8,128)S(1)}, f32[4,16,512]{2,1,0:T(8,128)S(1)}, u32[]{:S(2)}, u32[]{:S(2)}) %collective-permute-start.16) | collective-permute-done | bytes 131104 | tf_op jit(solution)/shard_map/ppermute | solution.py:168
  164.7 0.1 collective-permute-start.17
  164.8 2.3 %collective-permute-start.18 = (f32[16,512]{1,0:T(8,128)S(1)}, f32[16,512]{1,0:T(8,128)S(1)}, u32[]{:S(2)}, u32[]{:S(2)}) collective-permute-start(f32[16,512]{1,0:T(8,128)S(1)} %get-tuple-element.27), channel_id=1, source_target_pairs={{0,8},{1,9},{2,10},{3,11},{4,12},{5,13},{6,14},{7,15},{8,0},{9,1},... | collective-permute-start | bytes 98312 | tf_op jit(solution)/shard_map/ppermute | solution.py:168
  167.0 1.5 collective-permute-start.19
  168.6 2.0 %collective-permute-done.17 = f32[16,512]{1,0:T(8,128)S(1)} collective-permute-done((f32[16,512]{1,0:T(8,128)S(1)}, f32[16,512]{1,0:T(8,128)S(1)}, u32[]{:S(2)}, u32[]{:S(2)}) %collective-permute-start.17) | collective-permute-done | bytes 32800 | tf_op jit(solution)/shard_map/ppermute | solution.py:168
  170.6 0.0 collective-permute-done.18
  170.6 0.5 collective-permute-done.19
  171.1 0.6 copy.11
  (37 shorter events, 0.2 us)
Async XLA Ops:
  0.7 6.1 %copy-start.19 = (s32[3,864]{1,0:T(4,128)S(1)}, s32[3,864]{1,0:T(4,128)}, u32[]{:S(2)}) copy-start(s32[3,864]{1,0:T(4,128)} %param.17) | copy-start | bytes 31108
  0.7 6.1 %copy-start.18 = (s32[3,864]{1,0:T(4,128)S(1)}, s32[3,864]{1,0:T(4,128)}, u32[]{:S(2)}) copy-start(s32[3,864]{1,0:T(4,128)} %param.16) | copy-start | bytes 31108
  2.1 8.5 %copy-start = (bf16[64,10368]{1,0:T(8,128)(2,1)}, bf16[64,10368]{1,0:T(8,128)(2,1)S(1)}, u32[]{:S(2)}) copy-start(bf16[64,10368]{1,0:T(8,128)(2,1)S(1)} %pad_maximum_fusion.refs_0_.refs_2_.refs_4_) | copy-start | bytes 3981316
  2.2 6.2 %copy-start.17 = (s32[5120]{0:T(1024)S(1)}, s32[5120]{0:T(1024)}, u32[]{:S(2)}) copy-start(s32[5120]{0:T(1024)} %param.19) | copy-start | bytes 61444
  2.2 6.2 %copy-start.16 = (s32[5120]{0:T(1024)S(1)}, s32[5120]{0:T(1024)}, u32[]{:S(2)}) copy-start(s32[5120]{0:T(1024)} %param.18) | copy-start | bytes 61444
  2.2 8.4 %collective-permute-start.2 = (bf16[64,10368]{1,0:T(8,128)(2,1)S(1)}, bf16[64,10368]{1,0:T(8,128)(2,1)S(1)}, u32[]{:S(2)}, u32[]{:S(2)}) collective-permute-start(bf16[64,10368]{1,0:T(8,128)(2,1)S(1)} %pad_maximum_fusion.refs_0_.refs_2_.refs_4_), channel_id=1, source_target_pairs={{0,1},{1,0},{2,3},{3,2},{4,5},{5,4},{6,7},{7,6},{8,9},{9,8},{10,11... | collective-permute-start | bytes 3981320 | tf_op jit(solution)/shard_map/ppermute | solution.py:168
  2.7 34.6 %collective-permute-start = (bf16[64,10368]{1,0:T(8,128)(2,1)S(1)}, bf16[64,10368]{1,0:T(8,128)(2,1)S(1)}, u32[]{:S(2)}, u32[]{:S(2)}) collective-permute-start(bf16[64,10368]{1,0:T(8,128)(2,1)S(1)} %pad_maximum_fusion.refs_0_.refs_2_.refs_4_), channel_id=1, source_target_pairs={{0,4},{1,13},{2,6},{3,15},{4,8},{5,1},{6,10},{7,3},{8,12},{9,5},{1... | collective-permute-start | bytes 3981320 | tf_op jit(solution)/shard_map/ppermute | solution.py:168
  5.3 31.9 %collective-permute-start.1 = (bf16[64,10368]{1,0:T(8,128)(2,1)S(1)}, bf16[64,10368]{1,0:T(8,128)(2,1)S(1)}, u32[]{:S(2)}, u32[]{:S(2)}) collective-permute-start(bf16[64,10368]{1,0:T(8,128)(2,1)S(1)} %pad_maximum_fusion.refs_0_.refs_2_.refs_4_), channel_id=1, source_target_pairs={{0,2},{1,3},{2,0},{3,1},{4,6},{5,7},{6,4},{7,5},{8,10},{9,11},{10,... | collective-permute-start | bytes 3981320 | tf_op jit(solution)/shard_map/ppermute | solution.py:168
  10.6 1.3 copy-start.11
  37.3 5.0 %copy-start.2 = (bf16[64,10368]{1,0:T(8,128)(2,1)}, bf16[64,10368]{1,0:T(8,128)(2,1)S(1)}, u32[]{:S(2)}) copy-start(bf16[64,10368]{1,0:T(8,128)(2,1)S(1)} %collective-permute-done.refs_0_.refs_4_.refs_8_) | copy-start | bytes 3981316
  37.3 5.0 %copy-start.5 = (bf16[64,10368]{1,0:T(8,128)(2,1)}, bf16[64,10368]{1,0:T(8,128)(2,1)S(1)}, u32[]{:S(2)}) copy-start(bf16[64,10368]{1,0:T(8,128)(2,1)S(1)} %collective-permute-done.1.refs_2_.refs_6_.refs_10_) | copy-start | bytes 3981316
  37.3 3.1 %collective-permute-start.5 = (bf16[64,10368]{1,0:T(8,128)(2,1)S(1)}, bf16[64,10368]{1,0:T(8,128)(2,1)S(1)}, u32[]{:S(2)}, u32[]{:S(2)}) collective-permute-start(bf16[64,10368]{1,0:T(8,128)(2,1)S(1)} %collective-permute-done.refs_0_.refs_4_.refs_8_), channel_id=1, source_target_pairs={{0,1},{1,0},{2,3},{3,2},{4,5},{5,4},{6,7},{7,6},{8,9},{9,8},{10,11... | collective-permute-start | bytes 3981320 | tf_op jit(solution)/shard_map/ppermute | solution.py:168
  37.4 4.9 %collective-permute-start.6 = (bf16[64,10368]{1,0:T(8,128)(2,1)S(1)}, bf16[64,10368]{1,0:T(8,128)(2,1)S(1)}, u32[]{:S(2)}, u32[]{:S(2)}) collective-permute-start(bf16[64,10368]{1,0:T(8,128)(2,1)S(1)} %collective-permute-done.1.refs_2_.refs_6_.refs_10_), channel_id=1, source_target_pairs={{0,1},{1,0},{2,3},{3,2},{4,5},{5,4},{6,7},{7,6},{8,9},{9,8},{10,11... | collective-permute-start | bytes 3981320 | tf_op jit(solution)/shard_map/ppermute | solution.py:168
  37.8 31.6 %collective-permute-start.3 = (bf16[64,10368]{1,0:T(8,128)(2,1)S(1)}, bf16[64,10368]{1,0:T(8,128)(2,1)S(1)}, u32[]{:S(2)}, u32[]{:S(2)}) collective-permute-start(bf16[64,10368]{1,0:T(8,128)(2,1)S(1)} %collective-permute-done.refs_0_.refs_4_.refs_8_), channel_id=1, source_target_pairs={{0,4},{1,13},{2,6},{3,15},{4,8},{5,1},{6,10},{7,3},{8,12},{9,5},{1... | collective-permute-start | bytes 3981320 | tf_op jit(solution)/shard_map/ppermute | solution.py:168
  37.8 31.6 %collective-permute-start.4 = (bf16[64,10368]{1,0:T(8,128)(2,1)S(1)}, bf16[64,10368]{1,0:T(8,128)(2,1)S(1)}, u32[]{:S(2)}, u32[]{:S(2)}) collective-permute-start(bf16[64,10368]{1,0:T(8,128)(2,1)S(1)} %collective-permute-done.refs_0_.refs_4_.refs_8_), channel_id=1, source_target_pairs={{0,2},{1,3},{2,0},{3,1},{4,6},{5,7},{6,4},{7,5},{8,10},{9,11},{10,... | collective-permute-start | bytes 3981320 | tf_op jit(solution)/shard_map/ppermute | solution.py:168
  40.4 1.9 %copy-start.9 = (bf16[64,10368]{1,0:T(8,128)(2,1)}, bf16[64,10368]{1,0:T(8,128)(2,1)S(1)}, u32[]{:S(2)}) copy-start(bf16[64,10368]{1,0:T(8,128)(2,1)S(1)} %collective-permute-done.5.refs_1_.refs_5_.refs_9_) | copy-start | bytes 3981316
  42.3 1.1 copy-start.12
  69.5 5.0 %copy-start.3 = (bf16[64,10368]{1,0:T(8,128)(2,1)}, bf16[64,10368]{1,0:T(8,128)(2,1)S(1)}, u32[]{:S(2)}) copy-start(bf16[64,10368]{1,0:T(8,128)(2,1)S(1)} %collective-permute-done.3.refs_0_.refs_4_.refs_8_) | copy-start | bytes 3981316
  69.5 5.0 %copy-start.6 = (bf16[64,10368]{1,0:T(8,128)(2,1)}, bf16[64,10368]{1,0:T(8,128)(2,1)S(1)}, u32[]{:S(2)}) copy-start(bf16[64,10368]{1,0:T(8,128)(2,1)S(1)} %collective-permute-done.4.refs_2_.refs_6_.refs_10_) | copy-start | bytes 3981316
  69.5 3.2 %collective-permute-start.10 = (bf16[64,10368]{1,0:T(8,128)(2,1)S(1)}, bf16[64,10368]{1,0:T(8,128)(2,1)S(1)}, u32[]{:S(2)}, u32[]{:S(2)}) collective-permute-start(bf16[64,10368]{1,0:T(8,128)(2,1)S(1)} %collective-permute-done.4.refs_2_.refs_6_.refs_10_), channel_id=1, source_target_pairs={{0,1},{1,0},{2,3},{3,2},{4,5},{5,4},{6,7},{7,6},{8,9},{9,8},{10,11... | collective-permute-start | bytes 3981320 | tf_op jit(solution)/shard_map/ppermute | solution.py:168
  69.7 4.8 %collective-permute-start.9 = (bf16[64,10368]{1,0:T(8,128)(2,1)S(1)}, bf16[64,10368]{1,0:T(8,128)(2,1)S(1)}, u32[]{:S(2)}, u32[]{:S(2)}) collective-permute-start(bf16[64,10368]{1,0:T(8,128)(2,1)S(1)} %collective-permute-done.3.refs_0_.refs_4_.refs_8_), channel_id=1, source_target_pairs={{0,1},{1,0},{2,3},{3,2},{4,5},{5,4},{6,7},{7,6},{8,9},{9,8},{10,11... | collective-permute-start | bytes 3981320 | tf_op jit(solution)/shard_map/ppermute | solution.py:168
  70.1 32.0 %collective-permute-start.7 = (bf16[64,10368]{1,0:T(8,128)(2,1)S(1)}, bf16[64,10368]{1,0:T(8,128)(2,1)S(1)}, u32[]{:S(2)}, u32[]{:S(2)}) collective-permute-start(bf16[64,10368]{1,0:T(8,128)(2,1)S(1)} %collective-permute-done.3.refs_0_.refs_4_.refs_8_), channel_id=1, source_target_pairs={{0,4},{1,13},{2,6},{3,15},{4,8},{5,1},{6,10},{7,3},{8,12},{9,5},{1... | collective-permute-start | bytes 3981320 | tf_op jit(solution)/shard_map/ppermute | solution.py:168
  71.2 31.9 %collective-permute-start.8 = (bf16[64,10368]{1,0:T(8,128)(2,1)S(1)}, bf16[64,10368]{1,0:T(8,128)(2,1)S(1)}, u32[]{:S(2)}, u32[]{:S(2)}) collective-permute-start(bf16[64,10368]{1,0:T(8,128)(2,1)S(1)} %collective-permute-done.3.refs_0_.refs_4_.refs_8_), channel_id=1, source_target_pairs={{0,2},{1,3},{2,0},{3,1},{4,6},{5,7},{6,4},{7,5},{8,10},{9,11},{10,... | collective-permute-start | bytes 3981320 | tf_op jit(solution)/shard_map/ppermute | solution.py:168
  72.7 1.8 %copy-start.10 = (bf16[64,10368]{1,0:T(8,128)(2,1)}, bf16[64,10368]{1,0:T(8,128)(2,1)S(1)}, u32[]{:S(2)}) copy-start(bf16[64,10368]{1,0:T(8,128)(2,1)S(1)} %collective-permute-done.10.refs_3_.refs_7_.refs_11_) | copy-start | bytes 3981316
  74.5 1.1 copy-start.13
  102.1 6.0 %copy-start.4 = (bf16[64,10368]{1,0:T(8,128)(2,1)}, bf16[64,10368]{1,0:T(8,128)(2,1)S(1)}, u32[]{:S(2)}) copy-start(bf16[64,10368]{1,0:T(8,128)(2,1)S(1)} %collective-permute-done.7.refs_0_.refs_4_.refs_8_) | copy-start | bytes 3981316
  103.1 5.0 %copy-start.8 = (bf16[64,10368]{1,0:T(8,128)(2,1)}, bf16[64,10368]{1,0:T(8,128)(2,1)S(1)}, u32[]{:S(2)}) copy-start(bf16[64,10368]{1,0:T(8,128)(2,1)S(1)} %collective-permute-done.8.refs_2_.refs_6_.refs_10_) | copy-start | bytes 3981316
  103.1 3.1 %collective-permute-start.12 = (bf16[64,10368]{1,0:T(8,128)(2,1)S(1)}, bf16[64,10368]{1,0:T(8,128)(2,1)S(1)}, u32[]{:S(2)}, u32[]{:S(2)}) collective-permute-start(bf16[64,10368]{1,0:T(8,128)(2,1)S(1)} %collective-permute-done.7.refs_0_.refs_4_.refs_8_), channel_id=1, source_target_pairs={{0,1},{1,0},{2,3},{3,2},{4,5},{5,4},{6,7},{7,6},{8,9},{9,8},{10,11... | collective-permute-start | bytes 3981320 | tf_op jit(solution)/shard_map/ppermute | solution.py:168
  103.2 4.8 %collective-permute-start.13 = (bf16[64,10368]{1,0:T(8,128)(2,1)S(1)}, bf16[64,10368]{1,0:T(8,128)(2,1)S(1)}, u32[]{:S(2)}, u32[]{:S(2)}) collective-permute-start(bf16[64,10368]{1,0:T(8,128)(2,1)S(1)} %collective-permute-done.8.refs_2_.refs_6_.refs_10_), channel_id=1, source_target_pairs={{0,1},{1,0},{2,3},{3,2},{4,5},{5,4},{6,7},{7,6},{8,9},{9,8},{10,11... | collective-permute-start | bytes 3981320 | tf_op jit(solution)/shard_map/ppermute | solution.py:168
  103.6 31.1 %collective-permute-start.11 = (bf16[64,10368]{1,0:T(8,128)(2,1)S(1)}, bf16[64,10368]{1,0:T(8,128)(2,1)S(1)}, u32[]{:S(2)}, u32[]{:S(2)}) collective-permute-start(bf16[64,10368]{1,0:T(8,128)(2,1)S(1)} %collective-permute-done.7.refs_0_.refs_4_.refs_8_), channel_id=1, source_target_pairs={{0,2},{1,3},{2,0},{3,1},{4,6},{5,7},{6,4},{7,5},{8,10},{9,11},{10,... | collective-permute-start | bytes 3981320 | tf_op jit(solution)/shard_map/ppermute | solution.py:168
  106.1 1.9 %copy-start.14 = (bf16[64,10368]{1,0:T(8,128)(2,1)}, bf16[64,10368]{1,0:T(8,128)(2,1)S(1)}, u32[]{:S(2)}) copy-start(bf16[64,10368]{1,0:T(8,128)(2,1)S(1)} %collective-permute-done.12.refs_1_.refs_5_.refs_9_) | copy-start | bytes 3981316
  108.0 1.1 copy-start.15
  134.7 3.1 %copy-start.1 = (bf16[64,10368]{1,0:T(8,128)(2,1)}, bf16[64,10368]{1,0:T(8,128)(2,1)S(1)}, u32[]{:S(2)}) copy-start(bf16[64,10368]{1,0:T(8,128)(2,1)S(1)} %collective-permute-done.11.refs_0_.refs_2_.refs_4_) | copy-start | bytes 3981316
  134.7 3.1 %collective-permute-start.14 = (bf16[64,10368]{1,0:T(8,128)(2,1)S(1)}, bf16[64,10368]{1,0:T(8,128)(2,1)S(1)}, u32[]{:S(2)}, u32[]{:S(2)}) collective-permute-start(bf16[64,10368]{1,0:T(8,128)(2,1)S(1)} %collective-permute-done.11.refs_0_.refs_2_.refs_4_), channel_id=1, source_target_pairs={{0,1},{1,0},{2,3},{3,2},{4,5},{5,4},{6,7},{7,6},{8,9},{9,8},{10,11... | collective-permute-start | bytes 3981320 | tf_op jit(solution)/shard_map/ppermute | solution.py:168
  137.8 1.1 copy-start.7
  156.4 1.6 collective-permute-start.15
  159.0 5.6 %collective-permute-start.16 = (f32[4,16,512]{2,1,0:T(8,128)S(1)}, f32[4,16,512]{2,1,0:T(8,128)S(1)}, u32[]{:S(2)}, u32[]{:S(2)}) collective-permute-start(f32[4,16,512]{2,1,0:T(8,128)S(1)} %dynamic-slice_bitcast_fusion.1), channel_id=1, source_target_pairs={{0,2},{1,3},{2,0},{3,1},{4,6},{5,7},{6,4},{7,5},{8,10},{9,11},{10,... | collective-permute-start | bytes 393224 | tf_op jit(solution)/shard_map/ppermute | solution.py:168
  164.7 5.9 %collective-permute-start.17 = (f32[16,512]{1,0:T(8,128)S(1)}, f32[16,512]{1,0:T(8,128)S(1)}, u32[]{:S(2)}, u32[]{:S(2)}) collective-permute-start(f32[16,512]{1,0:T(8,128)S(1)} %get-tuple-element.29), channel_id=1, source_target_pairs={{0,4},{1,5},{2,6},{3,7},{4,8},{5,9},{6,10},{7,11},{8,12},{9,13},{1... | collective-permute-start | bytes 98312 | tf_op jit(solution)/shard_map/ppermute | solution.py:168
  164.8 5.8 %collective-permute-start.18 = (f32[16,512]{1,0:T(8,128)S(1)}, f32[16,512]{1,0:T(8,128)S(1)}, u32[]{:S(2)}, u32[]{:S(2)}) collective-permute-start(f32[16,512]{1,0:T(8,128)S(1)} %get-tuple-element.27), channel_id=1, source_target_pairs={{0,8},{1,9},{2,10},{3,11},{4,12},{5,13},{6,14},{7,15},{8,0},{9,1},... | collective-permute-start | bytes 98312 | tf_op jit(solution)/shard_map/ppermute | solution.py:168
  167.0 4.0 %collective-permute-start.19 = (f32[16,512]{1,0:T(8,128)S(1)}, f32[16,512]{1,0:T(8,128)S(1)}, u32[]{:S(2)}, u32[]{:S(2)}) collective-permute-start(f32[16,512]{1,0:T(8,128)S(1)} %get-tuple-element.28), channel_id=1, source_target_pairs={{0,12},{1,13},{2,14},{3,15},{4,0},{5,1},{6,2},{7,3},{8,4},{9,5},{1... | collective-permute-start | bytes 98312 | tf_op jit(solution)/shard_map/ppermute | solution.py:168

commit v2 on v1

v2 whole, which is shorter than its diff:
```python
import jax
import jax.numpy as jnp
from jax import lax
from jax.experimental import pallas as pl
from jax.experimental.pallas import tpu as pltpu
from jax.sharding import PartitionSpec as P

D = 5120
FF = 13824
EX = 2
SEQ = 512
K1 = 256
K2 = 256
CORES = 2
OUTER = 4
DEPTH = 1024
LANES = 128
VMEM_LIMIT = 56 << 20


def sign_tables(buckets, sign_bits, buckets_count):
    matches = buckets[..., None, :] == jnp.arange(buckets_count, dtype=jnp.int32)[:, None]
    signed = (2 * sign_bits - 1).astype(jnp.bfloat16)[..., None, :]
    return jnp.where(matches, signed, jnp.zeros_like(signed))


class Layout:
    def __init__(self, count):
        self.outer = OUTER if count % (OUTER * CORES) == 0 else 1
        self.inner = count // (self.outer * CORES)
        self.count = count

    def index(self, outer, inner, core):
        return ((outer % self.outer) * self.inner + inner % self.inner) * CORES + core

    def pairs(self, step):
        places = [
            (o, i, c)
            for o in range(self.outer)
            for i in range(self.inner)
            for c in range(CORES)
        ]
        return [(self.index(o, i, c), self.index(*step(o, i, c))) for o, i, c in places]

    def outer_ring(self):
        return self.pairs(lambda o, i, c: (o + 1 - 2 * c, i, c))

    def inner_ring(self):
        return self.pairs(lambda o, i, c: (o, i + 1 - 2 * c, c))

    def outer_shift(self, by):
        return self.pairs(lambda o, i, c: (o + by, i, c))

    def inner_shift(self, by):
        return self.pairs(lambda o, i, c: (o, i + by, c))

    def core_swap(self):
        return self.pairs(lambda o, i, c: (o, i, 1 - c))


def dot(left, right):
    return jnp.dot(left, right, preferred_element_type=jnp.float32)


def dot_rows(left, right):
    return lax.dot_general(
        left, right, (((1,), (1,)), ((), ())), preferred_element_type=jnp.float32
    )


def chunk_kernel(own, offsets, refs, scratch):
    ins, outs, gate_w, up_w, down_w, feature_w, tables_in, before_in, total = refs
    in_w, out_w, in_x, out_x, in_acc, out_acc, tables, before, ids, sems, late_sems = scratch
    units, model = gate_w.shape
    pieces = len(ins)
    depth = in_w.shape[-1]
    steps = model // depth
    places = [pl.ds(p * own, own) for p in range(pieces)]

    def copies(step, slot, side):
        here = pl.ds(pl.multiple_of(step * depth, depth), depth)
        if side == 0:
            weights, buffer, xs, x_buffer = (gate_w, up_w, feature_w), in_w, ins, in_x
        else:
            weights, buffer, xs, x_buffer = (down_w, feature_w), out_w, outs, out_x
        at = 0
        found = []
        for weight in weights:
            height = weight.shape[0]
            found.append((weight.at[:, here], buffer.at[slot, pl.ds(at, height)]))
            at += height
        for x, offset, place in zip(xs, offsets[side], places):
            there = pl.ds(pl.multiple_of(offset + step * depth, LANES), depth)
            found.append((x.at[:, there], x_buffer.at[slot, place]))
        return [
            pltpu.make_async_copy(source, target, sems.at[slot, side, i])
            for i, (source, target) in enumerate(found)
        ]

    def start(step, slot):
        for side in range(2):
            for copy in copies(step, slot, side):
                copy.start()

    start(0, 0)
    late = [(tables_in, tables), (before_in, before)] + [
        (x.at[:, pl.ds(offset + model, LANES)], ids.at[place])
        for x, offset, place in zip(outs, offsets[1], places)
    ]
    late = [
        pltpu.make_async_copy(source, target, late_sems.at[i])
        for i, (source, target) in enumerate(late)
    ]
    for copy in late:
        copy.start()
    in_acc[...] = jnp.zeros_like(in_acc)
    out_acc[...] = jnp.zeros_like(out_acc)

    def body(step, _):
        slot = step % 2

        @pl.when(step < steps - 1)
        def _():
            start(step + 1, 1 - slot)

        for side, (weight, x, acc) in enumerate(((in_w, in_x, in_acc), (out_w, out_x, out_acc))):
            for copy in copies(step, slot, side):
                copy.wait()
            acc[...] += dot_rows(weight[slot], x[slot])
        return 0

    lax.fori_loop(0, steps, body, 0)
    for copy in late:
        copy.wait()

    bf16 = jnp.bfloat16
    gate, up, hidden_grad = in_acc[:units], in_acc[units : 2 * units], out_acc[:units]
    sigmoid = jax.nn.sigmoid(gate)
    activated = gate * sigmoid
    hidden = activated * up
    gate_grad = hidden_grad * up * sigmoid * (1.0 + gate * (1.0 - sigmoid))
    up_grad = hidden_grad * activated
    down_part = dot(tables[2], hidden.astype(bf16)).astype(bf16)
    input_part = (
        dot(tables[0], gate_grad.astype(bf16)) + dot(tables[1], up_grad.astype(bf16))
    ).astype(bf16)
    example = ids[...].astype(jnp.float32).T[:1, :]

    def by_example(features):
        return jnp.concatenate(
            [jnp.where(example == e, features, 0.0) for e in range(EX)], axis=0
        ).astype(bf16)

    total[...] = (
        before[...]
        + dot_rows(down_part, by_example(out_acc[units:]))
        + dot_rows(input_part, by_example(in_acc[2 * units :]))
    )


def chunk(pieces, gate_rows, up_rows, down_rows, feature_table, tables, before):
    own = pieces[0][0].shape[0]
    units, model = gate_rows.shape
    short = -units % 16
    if short:
        gate_rows, up_rows, down_rows = (
            jnp.pad(weight, ((0, short), (0, 0))) for weight in (gate_rows, up_rows, down_rows)
        )
        tables = jnp.pad(tables, ((0, 0), (0, 0), (0, short)))
        units += short
    rows = own * len(pieces)
    depth = min(DEPTH, model)
    ins, in_at, outs, out_at = zip(*pieces)
    f32, bf16 = jnp.float32, jnp.bfloat16
    in_height, out_height = 2 * units + K2, units + K2

    def kernel(*refs):
        count = len(pieces)
        named = (refs[:count], refs[count : 2 * count], *refs[2 * count : 2 * count + 7])
        chunk_kernel(own, (in_at, out_at), named, refs[2 * count + 7 :])

    return pl.pallas_call(
        kernel,
        in_specs=[pl.BlockSpec(memory_space=pl.ANY)] * (2 * len(pieces) + 6),
        out_specs=pl.BlockSpec(memory_space=pltpu.VMEM),
        out_shape=jax.ShapeDtypeStruct(before.shape, f32),
        scratch_shapes=[
            pltpu.VMEM((2, in_height, depth), bf16),
            pltpu.VMEM((2, out_height, depth), bf16),
            pltpu.VMEM((2, rows, depth), bf16),
            pltpu.VMEM((2, rows, depth), bf16),
            pltpu.VMEM((in_height, rows), f32),
            pltpu.VMEM((out_height, rows), f32),
            pltpu.VMEM(tables.shape, bf16),
            pltpu.VMEM(before.shape, f32),
            pltpu.VMEM((rows, LANES), bf16),
            pltpu.SemaphoreType.DMA((2, 2, 3 + len(pieces))),
            pltpu.SemaphoreType.DMA((2 + len(pieces),)),
        ],
        compiler_params=pltpu.CompilerParams(vmem_limit_bytes=VMEM_LIMIT),
        cost_estimate=pl.CostEstimate(
            flops=2 * rows * model * (3 * units + 2 * K2),
            bytes_accessed=2 * model * (3 * units + K2 + 2 * rows),
            transcendentals=rows * units,
        ),
        name="chunk",
    )(*ins, *outs, gate_rows, up_rows, down_rows, feature_table, tables, before)


def on_device(
    layout,
    inputs,
    out_grad,
    example_ids,
    gate_weight,
    up_weight,
    down_weight,
    unit_buckets,
    unit_signs,
    feature_buckets,
    feature_signs,
):
    def move(value, pairs):
        return lax.ppermute(value, "fsdp", pairs)

    me = lax.axis_index("fsdp")
    core = me % CORES
    inner = (me // CORES) % layout.inner
    outer = me // (CORES * layout.inner)
    rows = inputs.shape[0]

    unit_tables = sign_tables(unit_buckets, unit_signs, K1)
    feature_table = sign_tables(feature_buckets, feature_signs, K2)

    example = jnp.broadcast_to(example_ids[:, None], (rows, LANES)).astype(jnp.bfloat16)
    own = jnp.concatenate([inputs, out_grad, example], axis=1)

    total = jnp.zeros((K1, EX * K2), jnp.float32)
    add = lambda pieces, total: chunk(
        pieces, gate_weight.T, up_weight.T, down_weight, feature_table, unit_tables, total
    )
    width = inputs.shape[1]
    both = lambda piece: (piece, 0, piece, width)
    swap = lambda piece: move(piece, layout.core_swap())
    if layout.inner == 2:
        here, across = own, None
        for step in range(layout.outer):
            if step < layout.outer - 1:
                coming = [
                    move(here, layout.outer_ring()),
                    move(here, layout.inner_ring()),
                ]
            else:
                coming = [
                    move(here[:, :width], layout.inner_ring()),
                    move(across[:, width:], layout.outer_ring()),
                ]
            pieces = [both(here), both(swap(here))]
            if across is not None:
                pieces += [both(across), both(swap(across))]
            total = add(pieces, total)
            here, across, total = lax.optimization_barrier((*coming, total))
        pieces = [(here, 0, across, 0), (swap(here), 0, swap(across), 0)]
        total = add(pieces, total)
    else:
        total = add([both(lax.all_gather(own, "fsdp", axis=0, tiled=True))], total)

    part = total.reshape(layout.outer, layout.inner, CORES, -1, EX * K2)
    take = lambda v, at, axis: lax.dynamic_index_in_dim(v, at, axis, keepdims=False)
    part = take(part, core, 2) + move(take(part, 1 - core, 2), layout.core_swap())
    part = take(part, inner, 1) + sum(
        move(take(part, (inner + by) % layout.inner, 1), layout.inner_shift(by))
        for by in range(1, layout.inner)
    )
    part = take(part, outer, 0) + sum(
        move(take(part, (outer + by) % layout.outer, 0), layout.outer_shift(by))
        for by in range(1, layout.outer)
    )
    factor = (3.0 * SEQ * FF * D / (K1 * K2)) ** (-0.5)
    return (factor * part).reshape(-1, EX, K2).transpose(1, 0, 2)


def solution(mesh):
    layout = Layout(mesh.shape["fsdp"])
    in_specs = (
        P(("groups", "fsdp"), None),
        P(("groups", "fsdp"), None),
        P(("groups", "fsdp")),
        P(None, "fsdp"),
        P(None, "fsdp"),
        P("fsdp", None),
        P(None, "fsdp"),
        P(None, "fsdp"),
        P(),
        P(),
    )
    out_specs = P("groups", "fsdp", None)
    return jax.shard_map(
        lambda *args: on_device(layout, *args),
        mesh=mesh,
        in_specs=in_specs,
        out_specs=out_specs,
        check_vma=False,
    )
```

time: 172 us -> 167 us (0.971)
  waiting for transfers between devices: 54.3 us -> 40.6 us
  Pallas kernels: 85.3 us -> 92.3 us
    ppermute x20 -> x22, waiting for transfers between devices: 54.3 us -> 40.6 us  [move(): return lax.ppermute(value, 'fsdp', pairs)]
    pallas_call x5, Pallas kernels: 85.3 us -> 92.3 us  [chunk(): pl.pallas_call(kernel, in_specs=[pl.BlockSpec(memory_space=pl.ANY)] * (2...]
    ppermute x20 -> x22, starting transfers between devices: 17.6 us -> 18.3 us  [move(): return lax.ppermute(value, 'fsdp', pairs)]
    unnamed x40 -> x44, local copies, waits for them, and re-layouts: 4.83 us -> 5.48 us
  transfers between devices with their start and end apart: 20 -> 22, of which waited for: 15 -> 14; matrix products, arithmetic and copies ran while one was open for 3% -> 3% of each run, Pallas kernels for 40% -> 46%
where the time goes in v2:
time: 167 us; the launch traced here: 166 us
  Pallas kernels  92.3 us (55%)
  waiting for transfers between devices  40.6 us (24%)
  starting transfers between devices  18.3 us (11%)
  local copies, waits for them, and re-layouts  8.24 us (5%)
  other arithmetic  6.81 us (4%)
    pallas_call x5, Pallas kernels, chunk(): pl.pallas_call(kernel, in_specs=[pl.BlockSpec(memory_space=pl.ANY)] * (2...  92.3 us
    ppermute x22, waiting for transfers between devices, move(): return lax.ppermute(value, 'fsdp', pairs)  40.6 us
    ppermute x22, starting transfers between devices, move(): return lax.ppermute(value, 'fsdp', pairs)  18.3 us
    unnamed x44, local copies, waits for them, and re-layouts  5.48 us
    select_n x2, other arithmetic, sign_tables(): return jnp.where(matches, signed, jnp.zeros_like(signed))  3.72 us
  transfers between devices with their start and end apart: 22, of which 14 were waited for; matrix products, arithmetic and copies ran while one was open for 3% of the time, Pallas kernels for 46%

profile of v2, /device:TPU:0, one launch (start us, length us, event | category | flops | bytes accessed | tf_op | source)
XLA Modules:
  0.0 166.5 jit_solution(15402332091016678435)
XLA Ops:
  0.0 0.7 convert_element_type.10
  0.7 0.1 broadcast_in_dim.48
  0.8 1.4 pad_maximum_fusion.refs_0_.refs_2_
  2.2 0.0 copy-start.18
  2.2 0.5 collective-permute-start.2
  2.7 2.6 %collective-permute-start = (bf16[64,10368]{1,0:T(8,128)(2,1)S(1)}, bf16[64,10368]{1,0:T(8,128)(2,1)S(1)}, u32[]{:S(2)}, u32[]{:S(2)}) collective-permute-start(bf16[64,10368]{1,0:T(8,128)(2,1)S(1)} %pad_maximum_fusion.refs_0_.refs_2_), channel_id=1, source_target_pairs={{0,4},{1,13},{2,6},{3,15},{4,8},{5,1},{6,10},{7,3},{8,12},{9,5},{1... | collective-permute-start | bytes 3981320 | tf_op jit(solution)/shard_map/ppermute | solution.py:224
  5.3 1.5 collective-permute-start.1
  6.8 1.5 fusion.1.refs_8_.refs_12_
  8.4 2.2 %fusion.refs_7_.refs_11_ = bf16[256,5120]{1,0:T(8,128)(2,1)} fusion(s32[5120]{0:T(1024)S(1)} %copy-done.18, bf16[5120]{0:T(1024)(128)(2,1)S(1)} %add_convert_fusion), kind=kLoop, calls=%fused_computation.1 | loop fusion | flops 2621440 | bytes 2652160 | tf_op jit(solution)/shard_map/jit(_where)/select_n | solution.py:24
  10.6 0.0 collective-permute-done.2.refs_1_.refs_3_
  10.6 0.9 broadcast_in_dim.53.refs_9_
  11.5 0.3 copy-done.13
  11.8 15.2 %chunk.5.refs_13_ = f32[256,512]{1,0:T(8,128)} custom-call(bf16[64,10368]{1,0:T(8,128)(2,1)} %copy-done, bf16[64,10368]{1,0:T(8,128)(2,1)} %copy-done.13, bf16[64,10368]{1,0:T(8,128)(2,1)} %copy-done, bf16[64,10368]{1,0:T(8,128)(2,1)} %copy-done.13, bf16[864,5120]{1,0:T(8,128)(2,1)} %bitcast.22, bf16[864,5120]{1,0:T(8,128)(2,1)} %bitcast.27, ...), custom_call_target="tpu_custom_call" | custom-call | flops 4068474880 | bytes 31784960 | tf_op jit(solution)/shard_map/chunk/pallas_call | solution.py:182
  27.0 10.2 %collective-permute-done.refs_0_.refs_4_ = bf16[64,10368]{1,0:T(8,128)(2,1)S(1)} collective-permute-done((bf16[64,10368]{1,0:T(8,128)(2,1)S(1)}, bf16[64,10368]{1,0:T(8,128)(2,1)S(1)}, u32[]{:S(2)}, u32[]{:S(2)}) %collective-permute-start) | collective-permute-done | bytes 1327136 | tf_op jit(solution)/shard_map/ppermute | solution.py:224
  37.3 0.0 collective-permute-done.1.refs_2_.refs_6_
  37.3 0.1 collective-permute-start.5
  37.4 0.5 collective-permute-start.6
  37.8 0.0 collective-permute-start.3
  37.8 1.5 collective-permute-start.4
  39.3 1.1 collective-permute-done.5.refs_1_.refs_5_
  40.4 1.9 %collective-permute-done.6.refs_3_.refs_7_ = bf16[64,10368]{1,0:T(8,128)(2,1)S(1)} collective-permute-done((bf16[64,10368]{1,0:T(8,128)(2,1)S(1)}, bf16[64,10368]{1,0:T(8,128)(2,1)S(1)}, u32[]{:S(2)}, u32[]{:S(2)}) %collective-permute-start.6) | collective-permute-done | bytes 1327136 | tf_op jit(solution)/shard_map/ppermute | solution.py:224
  42.3 1.1 copy-done.11
  43.4 20.6 %chunk.6.refs_13_ = f32[256,512]{1,0:T(8,128)} custom-call(bf16[64,10368]{1,0:T(8,128)(2,1)} %copy-done.3, bf16[64,10368]{1,0:T(8,128)(2,1)} %copy-done.8, bf16[64,10368]{1,0:T(8,128)(2,1)} %copy-done.5, bf16[64,10368]{1,0:T(8,128)(2,1)} %copy-done.11, bf16[64,10368]{1,0:T(8,128)(2,1)} %copy-done.3, bf16[64,10368]{1,0:T(8,128)(2,1)} %copy-done.8, ...), custom_call_target="tpu_custom_call" | custom-call | flops 8136949760 | bytes 34406400 | tf_op jit(solution)/shard_map/chunk/pallas_call | solution.py:182
  64.1 5.4 %collective-permute-done.3.refs_0_.refs_4_ = bf16[64,10368]{1,0:T(8,128)(2,1)S(1)} collective-permute-done((bf16[64,10368]{1,0:T(8,128)(2,1)S(1)}, bf16[64,10368]{1,0:T(8,128)(2,1)S(1)}, u32[]{:S(2)}, u32[]{:S(2)}) %collective-permute-start.3) | collective-permute-done | bytes 1327136 | tf_op jit(solution)/shard_map/ppermute | solution.py:224
  69.5 0.0 collective-permute-done.4.refs_2_.refs_6_
  69.5 0.2 collective-permute-start.10
  69.7 0.4 collective-permute-start.9
  70.1 1.2 collective-permute-start.7
  71.2 1.5 collective-permute-start.8
  72.7 0.0 collective-permute-done.10.refs_3_.refs_7_
  72.7 1.8 %collective-permute-done.9.refs_1_.refs_5_ = bf16[64,10368]{1,0:T(8,128)(2,1)S(1)} collective-permute-done((bf16[64,10368]{1,0:T(8,128)(2,1)S(1)}, bf16[64,10368]{1,0:T(8,128)(2,1)S(1)}, u32[]{:S(2)}, u32[]{:S(2)}) %collective-permute-start.9) | collective-permute-done | bytes 1327136 | tf_op jit(solution)/shard_map/ppermute | solution.py:224
  74.5 1.1 copy-done.12
  75.6 20.7 %chunk.7.refs_13_ = f32[256,512]{1,0:T(8,128)} custom-call(bf16[64,10368]{1,0:T(8,128)(2,1)} %copy-done.4, bf16[64,10368]{1,0:T(8,128)(2,1)} %copy-done.12, bf16[64,10368]{1,0:T(8,128)(2,1)} %copy-done.6, bf16[64,10368]{1,0:T(8,128)(2,1)} %copy-done.9, bf16[64,10368]{1,0:T(8,128)(2,1)} %copy-done.4, bf16[64,10368]{1,0:T(8,128)(2,1)} %copy-done.12, ...), custom_call_target="tpu_custom_call" | custom-call | flops 8136949760 | bytes 34406400 | tf_op jit(solution)/shard_map/chunk/pallas_call | solution.py:182
  96.3 5.8 %collective-permute-done.7.refs_0_.refs_4_ = bf16[64,10368]{1,0:T(8,128)(2,1)S(1)} collective-permute-done((bf16[64,10368]{1,0:T(8,128)(2,1)S(1)}, bf16[64,10368]{1,0:T(8,128)(2,1)S(1)}, u32[]{:S(2)}, u32[]{:S(2)}) %collective-permute-start.7) | collective-permute-done | bytes 1327136 | tf_op jit(solution)/shard_map/ppermute | solution.py:224
  102.1 1.0 collective-permute-done.8.refs_2_.refs_6_
  103.1 0.1 collective-permute-start.13
  103.2 0.4 collective-permute-start.14
  103.7 0.1 collective-permute-start.12
  103.8 1.6 collective-permute-start.11
  105.3 0.8 collective-permute-done.13.refs_1_.refs_5_
  106.1 1.9 %collective-permute-done.14.refs_3_.refs_7_ = bf16[64,10368]{1,0:T(8,128)(2,1)S(1)} collective-permute-done((bf16[64,10368]{1,0:T(8,128)(2,1)S(1)}, bf16[64,10368]{1,0:T(8,128)(2,1)S(1)}, u32[]{:S(2)}, u32[]{:S(2)}) %collective-permute-start.14) | collective-permute-done | bytes 1327136 | tf_op jit(solution)/shard_map/ppermute | solution.py:224
  108.1 1.1 copy-done.10
  109.2 20.6 %chunk.8.refs_9_ = f32[256,512]{1,0:T(8,128)} custom-call(bf16[64,10368]{1,0:T(8,128)(2,1)} %copy-done.2, bf16[64,10368]{1,0:T(8,128)(2,1)} %copy-done.7, bf16[64,10368]{1,0:T(8,128)(2,1)} %copy-done.1, bf16[64,10368]{1,0:T(8,128)(2,1)} %copy-done.10, bf16[64,10368]{1,0:T(8,128)(2,1)} %copy-done.2, bf16[64,10368]{1,0:T(8,128)(2,1)} %copy-done.7, ...), custom_call_target="tpu_custom_call" | custom-call | flops 8136949760 | bytes 34406400 | tf_op jit(solution)/shard_map/chunk/pallas_call | solution.py:182
  129.8 0.0 collective-permute-done.11.refs_0_
  129.8 0.0 collective-permute-done.12.refs_2_
  129.9 0.2 collective-permute-start.16
  130.1 0.4 collective-permute-start.15
  130.4 2.5 %collective-permute-done.15.refs_1_ = bf16[64,5120]{1,0:T(8,128)(2,1)S(1)} collective-permute-done((bf16[64,5120]{1,0:T(8,128)(2,1)S(1)}, bf16[64,5120]{1,0:T(8,128)(2,1)S(1)}, u32[]{:S(2)}, u32[]{:S(2)}) %collective-permute-start.15) | collective-permute-done | bytes 655392 | tf_op jit(solution)/shard_map/ppermute | solution.py:224
  133.0 0.8 copy-done.17
  133.9 0.9 copy-done.15
  134.7 15.2 %chunk.9 = f32[256,512]{1,0:T(8,128)} custom-call(bf16[64,5120]{1,0:T(8,128)(2,1)} %copy-done.16, bf16[64,5120]{1,0:T(8,128)(2,1)} %copy-done.17, bf16[64,5248]{1,0:T(8,128)(2,1)} %copy-done.14, bf16[64,5248]{1,0:T(8,128)(2,1)} %copy-done.15, bf16[864,5120]{1,0:T(8,128)(2,1)} %bitcast.26, bf16[864,5120]{1,0:T(8,128)(2,1)} %bitcast.31, ...), custom_call_target="tpu_custom_call" | custom-call | flops 4068474880 | bytes 31784960 | tf_op jit(solution)/shard_map/chunk/pallas_call | solution.py:182
  149.9 1.0 dynamic-slice_bitcast_fusion
  150.9 0.2 collective-permute-start.17
  151.1 1.4 collective-permute-done.17
  152.5 1.0 bitcast_add_fusion
  153.5 1.6 collective-permute-start.18
  155.1 4.0 %collective-permute-done.18 = f32[4,16,512]{2,1,0:T(8,128)S(1)} collective-permute-done((f32[4,16,512]{2,1,0:T(8,128)S(1)}, f32[4,16,512]{2,1,0:T(8,128)S(1)}, u32[]{:S(2)}, u32[]{:S(2)}) %collective-permute-start.18) | collective-permute-done | bytes 131104 | tf_op jit(solution)/shard_map/ppermute | solution.py:224
  159.2 0.1 collective-permute-start.19
  159.2 2.7 %collective-permute-start.20 = (f32[16,512]{1,0:T(8,128)S(1)}, f32[16,512]{1,0:T(8,128)S(1)}, u32[]{:S(2)}, u32[]{:S(2)}) collective-permute-start(f32[16,512]{1,0:T(8,128)S(1)} %get-tuple-element.29), channel_id=1, source_target_pairs={{0,8},{1,9},{2,10},{3,11},{4,12},{5,13},{6,14},{7,15},{8,0},{9,1},... | collective-permute-start | bytes 98312 | tf_op jit(solution)/shard_map/ppermute | solution.py:224
  161.9 1.1 collective-permute-start.21
  163.1 2.0 %collective-permute-done.19 = f32[16,512]{1,0:T(8,128)S(1)} collective-permute-done((f32[16,512]{1,0:T(8,128)S(1)}, f32[16,512]{1,0:T(8,128)S(1)}, u32[]{:S(2)}, u32[]{:S(2)}) %collective-permute-start.19) | collective-permute-done | bytes 32800 | tf_op jit(solution)/shard_map/ppermute | solution.py:224
  165.0 0.0 collective-permute-done.20
  165.0 0.8 collective-permute-done.21
  165.9 0.6 copy.11
  (47 shorter events, 0.3 us)
Async XLA Ops:
  0.0 6.8 %copy-start.21 = (s32[3,864]{1,0:T(4,128)S(1)}, s32[3,864]{1,0:T(4,128)}, u32[]{:S(2)}) copy-start(s32[3,864]{1,0:T(4,128)} %param.17) | copy-start | bytes 31108
  0.0 6.8 %copy-start.20 = (s32[3,864]{1,0:T(4,128)S(1)}, s32[3,864]{1,0:T(4,128)}, u32[]{:S(2)}) copy-start(s32[3,864]{1,0:T(4,128)} %param.16) | copy-start | bytes 31108
  0.8 7.6 %copy-start.19 = (s32[5120]{0:T(1024)S(1)}, s32[5120]{0:T(1024)}, u32[]{:S(2)}) copy-start(s32[5120]{0:T(1024)} %param.19) | copy-start | bytes 61444
  2.2 8.4 %copy-start = (bf16[64,10368]{1,0:T(8,128)(2,1)}, bf16[64,10368]{1,0:T(8,128)(2,1)S(1)}, u32[]{:S(2)}) copy-start(bf16[64,10368]{1,0:T(8,128)(2,1)S(1)} %pad_maximum_fusion.refs_0_.refs_2_) | copy-start | bytes 3981316
  2.2 6.2 %copy-start.18 = (s32[5120]{0:T(1024)S(1)}, s32[5120]{0:T(1024)}, u32[]{:S(2)}) copy-start(s32[5120]{0:T(1024)} %param.18) | copy-start | bytes 61444
  2.2 8.4 %collective-permute-start.2 = (bf16[64,10368]{1,0:T(8,128)(2,1)S(1)}, bf16[64,10368]{1,0:T(8,128)(2,1)S(1)}, u32[]{:S(2)}, u32[]{:S(2)}) collective-permute-start(bf16[64,10368]{1,0:T(8,128)(2,1)S(1)} %pad_maximum_fusion.refs_0_.refs_2_), channel_id=1, source_target_pairs={{0,1},{1,0},{2,3},{3,2},{4,5},{5,4},{6,7},{7,6},{8,9},{9,8},{10,11... | collective-permute-start | bytes 3981320 | tf_op jit(solution)/shard_map/ppermute | solution.py:224
  2.7 34.6 %collective-permute-start = (bf16[64,10368]{1,0:T(8,128)(2,1)S(1)}, bf16[64,10368]{1,0:T(8,128)(2,1)S(1)}, u32[]{:S(2)}, u32[]{:S(2)}) collective-permute-start(bf16[64,10368]{1,0:T(8,128)(2,1)S(1)} %pad_maximum_fusion.refs_0_.refs_2_), channel_id=1, source_target_pairs={{0,4},{1,13},{2,6},{3,15},{4,8},{5,1},{6,10},{7,3},{8,12},{9,5},{1... | collective-permute-start | bytes 3981320 | tf_op jit(solution)/shard_map/ppermute | solution.py:224
  5.3 31.9 %collective-permute-start.1 = (bf16[64,10368]{1,0:T(8,128)(2,1)S(1)}, bf16[64,10368]{1,0:T(8,128)(2,1)S(1)}, u32[]{:S(2)}, u32[]{:S(2)}) collective-permute-start(bf16[64,10368]{1,0:T(8,128)(2,1)S(1)} %pad_maximum_fusion.refs_0_.refs_2_), channel_id=1, source_target_pairs={{0,2},{1,3},{2,0},{3,1},{4,6},{5,7},{6,4},{7,5},{8,10},{9,11},{10,... | collective-permute-start | bytes 3981320 | tf_op jit(solution)/shard_map/ppermute | solution.py:224
  10.6 1.3 copy-start.13
  37.3 5.0 %copy-start.3 = (bf16[64,10368]{1,0:T(8,128)(2,1)}, bf16[64,10368]{1,0:T(8,128)(2,1)S(1)}, u32[]{:S(2)}) copy-start(bf16[64,10368]{1,0:T(8,128)(2,1)S(1)} %collective-permute-done.refs_0_.refs_4_) | copy-start | bytes 3981316
  37.3 5.0 %copy-start.5 = (bf16[64,10368]{1,0:T(8,128)(2,1)}, bf16[64,10368]{1,0:T(8,128)(2,1)S(1)}, u32[]{:S(2)}) copy-start(bf16[64,10368]{1,0:T(8,128)(2,1)S(1)} %collective-permute-done.1.refs_2_.refs_6_) | copy-start | bytes 3981316
  37.3 3.1 %collective-permute-start.5 = (bf16[64,10368]{1,0:T(8,128)(2,1)S(1)}, bf16[64,10368]{1,0:T(8,128)(2,1)S(1)}, u32[]{:S(2)}, u32[]{:S(2)}) collective-permute-start(bf16[64,10368]{1,0:T(8,128)(2,1)S(1)} %collective-permute-done.refs_0_.refs_4_), channel_id=1, source_target_pairs={{0,1},{1,0},{2,3},{3,2},{4,5},{5,4},{6,7},{7,6},{8,9},{9,8},{10,11... | collective-permute-start | bytes 3981320 | tf_op jit(solution)/shard_map/ppermute | solution.py:224
  37.4 4.9 %collective-permute-start.6 = (bf16[64,10368]{1,0:T(8,128)(2,1)S(1)}, bf16[64,10368]{1,0:T(8,128)(2,1)S(1)}, u32[]{:S(2)}, u32[]{:S(2)}) collective-permute-start(bf16[64,10368]{1,0:T(8,128)(2,1)S(1)} %collective-permute-done.1.refs_2_.refs_6_), channel_id=1, source_target_pairs={{0,1},{1,0},{2,3},{3,2},{4,5},{5,4},{6,7},{7,6},{8,9},{9,8},{10,11... | collective-permute-start | bytes 3981320 | tf_op jit(solution)/shard_map/ppermute | solution.py:224
  37.8 31.6 %collective-permute-start.3 = (bf16[64,10368]{1,0:T(8,128)(2,1)S(1)}, bf16[64,10368]{1,0:T(8,128)(2,1)S(1)}, u32[]{:S(2)}, u32[]{:S(2)}) collective-permute-start(bf16[64,10368]{1,0:T(8,128)(2,1)S(1)} %collective-permute-done.refs_0_.refs_4_), channel_id=1, source_target_pairs={{0,4},{1,13},{2,6},{3,15},{4,8},{5,1},{6,10},{7,3},{8,12},{9,5},{1... | collective-permute-start | bytes 3981320 | tf_op jit(solution)/shard_map/ppermute | solution.py:224
  37.8 31.6 %collective-permute-start.4 = (bf16[64,10368]{1,0:T(8,128)(2,1)S(1)}, bf16[64,10368]{1,0:T(8,128)(2,1)S(1)}, u32[]{:S(2)}, u32[]{:S(2)}) collective-permute-start(bf16[64,10368]{1,0:T(8,128)(2,1)S(1)} %collective-permute-done.refs_0_.refs_4_), channel_id=1, source_target_pairs={{0,2},{1,3},{2,0},{3,1},{4,6},{5,7},{6,4},{7,5},{8,10},{9,11},{10,... | collective-permute-start | bytes 3981320 | tf_op jit(solution)/shard_map/ppermute | solution.py:224
  40.4 1.9 %copy-start.8 = (bf16[64,10368]{1,0:T(8,128)(2,1)}, bf16[64,10368]{1,0:T(8,128)(2,1)S(1)}, u32[]{:S(2)}) copy-start(bf16[64,10368]{1,0:T(8,128)(2,1)S(1)} %collective-permute-done.5.refs_1_.refs_5_) | copy-start | bytes 3981316
  42.3 1.2 copy-start.11
  69.5 5.0 %copy-start.4 = (bf16[64,10368]{1,0:T(8,128)(2,1)}, bf16[64,10368]{1,0:T(8,128)(2,1)S(1)}, u32[]{:S(2)}) copy-start(bf16[64,10368]{1,0:T(8,128)(2,1)S(1)} %collective-permute-done.3.refs_0_.refs_4_) | copy-start | bytes 3981316
  69.5 5.0 %copy-start.6 = (bf16[64,10368]{1,0:T(8,128)(2,1)}, bf16[64,10368]{1,0:T(8,128)(2,1)S(1)}, u32[]{:S(2)}) copy-start(bf16[64,10368]{1,0:T(8,128)(2,1)S(1)} %collective-permute-done.4.refs_2_.refs_6_) | copy-start | bytes 3981316
  69.5 3.2 %collective-permute-start.10 = (bf16[64,10368]{1,0:T(8,128)(2,1)S(1)}, bf16[64,10368]{1,0:T(8,128)(2,1)S(1)}, u32[]{:S(2)}, u32[]{:S(2)}) collective-permute-start(bf16[64,10368]{1,0:T(8,128)(2,1)S(1)} %collective-permute-done.4.refs_2_.refs_6_), channel_id=1, source_target_pairs={{0,1},{1,0},{2,3},{3,2},{4,5},{5,4},{6,7},{7,6},{8,9},{9,8},{10,11... | collective-permute-start | bytes 3981320 | tf_op jit(solution)/shard_map/ppermute | solution.py:224
  69.7 4.8 %collective-permute-start.9 = (bf16[64,10368]{1,0:T(8,128)(2,1)S(1)}, bf16[64,10368]{1,0:T(8,128)(2,1)S(1)}, u32[]{:S(2)}, u32[]{:S(2)}) collective-permute-start(bf16[64,10368]{1,0:T(8,128)(2,1)S(1)} %collective-permute-done.3.refs_0_.refs_4_), channel_id=1, source_target_pairs={{0,1},{1,0},{2,3},{3,2},{4,5},{5,4},{6,7},{7,6},{8,9},{9,8},{10,11... | collective-permute-start | bytes 3981320 | tf_op jit(solution)/shard_map/ppermute | solution.py:224
  70.1 32.0 %collective-permute-start.7 = (bf16[64,10368]{1,0:T(8,128)(2,1)S(1)}, bf16[64,10368]{1,0:T(8,128)(2,1)S(1)}, u32[]{:S(2)}, u32[]{:S(2)}) collective-permute-start(bf16[64,10368]{1,0:T(8,128)(2,1)S(1)} %collective-permute-done.3.refs_0_.refs_4_), channel_id=1, source_target_pairs={{0,4},{1,13},{2,6},{3,15},{4,8},{5,1},{6,10},{7,3},{8,12},{9,5},{1... | collective-permute-start | bytes 3981320 | tf_op jit(solution)/shard_map/ppermute | solution.py:224
  71.2 31.9 %collective-permute-start.8 = (bf16[64,10368]{1,0:T(8,128)(2,1)S(1)}, bf16[64,10368]{1,0:T(8,128)(2,1)S(1)}, u32[]{:S(2)}, u32[]{:S(2)}) collective-permute-start(bf16[64,10368]{1,0:T(8,128)(2,1)S(1)} %collective-permute-done.3.refs_0_.refs_4_), channel_id=1, source_target_pairs={{0,2},{1,3},{2,0},{3,1},{4,6},{5,7},{6,4},{7,5},{8,10},{9,11},{10,... | collective-permute-start | bytes 3981320 | tf_op jit(solution)/shard_map/ppermute | solution.py:224
  72.7 1.8 %copy-start.9 = (bf16[64,10368]{1,0:T(8,128)(2,1)}, bf16[64,10368]{1,0:T(8,128)(2,1)S(1)}, u32[]{:S(2)}) copy-start(bf16[64,10368]{1,0:T(8,128)(2,1)S(1)} %collective-permute-done.10.refs_3_.refs_7_) | copy-start | bytes 3981316
  74.5 1.1 copy-start.12
  102.1 6.0 %copy-start.2 = (bf16[64,10368]{1,0:T(8,128)(2,1)}, bf16[64,10368]{1,0:T(8,128)(2,1)S(1)}, u32[]{:S(2)}) copy-start(bf16[64,10368]{1,0:T(8,128)(2,1)S(1)} %collective-permute-done.7.refs_0_.refs_4_) | copy-start | bytes 3981316
  103.1 5.0 %copy-start.1 = (bf16[64,10368]{1,0:T(8,128)(2,1)}, bf16[64,10368]{1,0:T(8,128)(2,1)S(1)}, u32[]{:S(2)}) copy-start(bf16[64,10368]{1,0:T(8,128)(2,1)S(1)} %collective-permute-done.8.refs_2_.refs_6_) | copy-start | bytes 3981316
  103.1 3.1 %collective-permute-start.13 = (bf16[64,10368]{1,0:T(8,128)(2,1)S(1)}, bf16[64,10368]{1,0:T(8,128)(2,1)S(1)}, u32[]{:S(2)}, u32[]{:S(2)}) collective-permute-start(bf16[64,10368]{1,0:T(8,128)(2,1)S(1)} %collective-permute-done.7.refs_0_.refs_4_), channel_id=1, source_target_pairs={{0,1},{1,0},{2,3},{3,2},{4,5},{5,4},{6,7},{7,6},{8,9},{9,8},{10,11... | collective-permute-start | bytes 3981320 | tf_op jit(solution)/shard_map/ppermute | solution.py:224
  103.2 4.8 %collective-permute-start.14 = (bf16[64,10368]{1,0:T(8,128)(2,1)S(1)}, bf16[64,10368]{1,0:T(8,128)(2,1)S(1)}, u32[]{:S(2)}, u32[]{:S(2)}) collective-permute-start(bf16[64,10368]{1,0:T(8,128)(2,1)S(1)} %collective-permute-done.8.refs_2_.refs_6_), channel_id=1, source_target_pairs={{0,1},{1,0},{2,3},{3,2},{4,5},{5,4},{6,7},{7,6},{8,9},{9,8},{10,11... | collective-permute-start | bytes 3981320 | tf_op jit(solution)/shard_map/ppermute | solution.py:224
  103.7 26.2 %collective-permute-start.12 = (bf16[64,5248]{1,0:T(8,128)(2,1)S(1)}, bf16[64,5248]{1,0:T(8,128)(2,1)S(1)}, u32[]{:S(2)}, u32[]{:S(2)}) collective-permute-start(bf16[64,5248]{1,0:T(8,128)(2,1)S(1)} %slice.7), channel_id=1, source_target_pairs={{0,4},{1,13},{2,6},{3,15},{4,8},{5,1},{6,10},{7,3},{8,12},{9,5},{1... | collective-permute-start | bytes 2015240 | tf_op jit(solution)/shard_map/ppermute | solution.py:224
  103.8 26.1 %collective-permute-start.11 = (bf16[64,5120]{1,0:T(8,128)(2,1)S(1)}, bf16[64,5120]{1,0:T(8,128)(2,1)S(1)}, u32[]{:S(2)}, u32[]{:S(2)}) collective-permute-start(bf16[64,5120]{1,0:T(8,128)(2,1)S(1)} %slice.6), channel_id=1, source_target_pairs={{0,2},{1,3},{2,0},{3,1},{4,6},{5,7},{6,4},{7,5},{8,10},{9,11},{10,... | collective-permute-start | bytes 1966088 | tf_op jit(solution)/shard_map/ppermute | solution.py:224
  106.1 1.9 %copy-start.7 = (bf16[64,10368]{1,0:T(8,128)(2,1)}, bf16[64,10368]{1,0:T(8,128)(2,1)S(1)}, u32[]{:S(2)}) copy-start(bf16[64,10368]{1,0:T(8,128)(2,1)S(1)} %collective-permute-done.13.refs_1_.refs_5_) | copy-start | bytes 3981316
  108.0 1.2 copy-start.10
  129.8 3.2 %copy-start.16 = (bf16[64,5120]{1,0:T(8,128)(2,1)}, bf16[64,5120]{1,0:T(8,128)(2,1)S(1)}, u32[]{:S(2)}) copy-start(bf16[64,5120]{1,0:T(8,128)(2,1)S(1)} %collective-permute-done.11.refs_0_) | copy-start | bytes 1966084
  129.9 3.1 %copy-start.14 = (bf16[64,5248]{1,0:T(8,128)(2,1)}, bf16[64,5248]{1,0:T(8,128)(2,1)S(1)}, u32[]{:S(2)}) copy-start(bf16[64,5248]{1,0:T(8,128)(2,1)S(1)} %collective-permute-done.12.refs_2_) | copy-start | bytes 2015236
  129.9 3.1 %collective-permute-start.16 = (bf16[64,5248]{1,0:T(8,128)(2,1)S(1)}, bf16[64,5248]{1,0:T(8,128)(2,1)S(1)}, u32[]{:S(2)}, u32[]{:S(2)}) collective-permute-start(bf16[64,5248]{1,0:T(8,128)(2,1)S(1)} %collective-permute-done.12.refs_2_), channel_id=1, source_target_pairs={{0,1},{1,0},{2,3},{3,2},{4,5},{5,4},{6,7},{7,6},{8,9},{9,8},{10,11... | collective-permute-start | bytes 2015240 | tf_op jit(solution)/shard_map/ppermute | solution.py:224
  130.1 2.9 %collective-permute-start.15 = (bf16[64,5120]{1,0:T(8,128)(2,1)S(1)}, bf16[64,5120]{1,0:T(8,128)(2,1)S(1)}, u32[]{:S(2)}, u32[]{:S(2)}) collective-permute-start(bf16[64,5120]{1,0:T(8,128)(2,1)S(1)} %collective-permute-done.11.refs_0_), channel_id=1, source_target_pairs={{0,1},{1,0},{2,3},{3,2},{4,5},{5,4},{6,7},{7,6},{8,9},{9,8},{10,11... | collective-permute-start | bytes 1966088 | tf_op jit(solution)/shard_map/ppermute | solution.py:224
  133.0 0.9 copy-start.17
  133.9 0.9 copy-start.15
  150.9 1.6 collective-permute-start.17
  153.5 5.6 %collective-permute-start.18 = (f32[4,16,512]{2,1,0:T(8,128)S(1)}, f32[4,16,512]{2,1,0:T(8,128)S(1)}, u32[]{:S(2)}, u32[]{:S(2)}) collective-permute-start(f32[4,16,512]{2,1,0:T(8,128)S(1)} %dynamic-slice_bitcast_fusion.1), channel_id=1, source_target_pairs={{0,2},{1,3},{2,0},{3,1},{4,6},{5,7},{6,4},{7,5},{8,10},{9,11},{10,... | collective-permute-start | bytes 393224 | tf_op jit(solution)/shard_map/ppermute | solution.py:224
  159.2 5.9 %collective-permute-start.19 = (f32[16,512]{1,0:T(8,128)S(1)}, f32[16,512]{1,0:T(8,128)S(1)}, u32[]{:S(2)}, u32[]{:S(2)}) collective-permute-start(f32[16,512]{1,0:T(8,128)S(1)} %get-tuple-element.31), channel_id=1, source_target_pairs={{0,4},{1,5},{2,6},{3,7},{4,8},{5,9},{6,10},{7,11},{8,12},{9,13},{1... | collective-permute-start | bytes 98312 | tf_op jit(solution)/shard_map/ppermute | solution.py:224
  159.2 5.8 %collective-permute-start.20 = (f32[16,512]{1,0:T(8,128)S(1)}, f32[16,512]{1,0:T(8,128)S(1)}, u32[]{:S(2)}, u32[]{:S(2)}) collective-permute-start(f32[16,512]{1,0:T(8,128)S(1)} %get-tuple-element.29), channel_id=1, source_target_pairs={{0,8},{1,9},{2,10},{3,11},{4,12},{5,13},{6,14},{7,15},{8,0},{9,1},... | collective-permute-start | bytes 98312 | tf_op jit(solution)/shard_map/ppermute | solution.py:224
  161.9 3.9 %collective-permute-start.21 = (f32[16,512]{1,0:T(8,128)S(1)}, f32[16,512]{1,0:T(8,128)S(1)}, u32[]{:S(2)}, u32[]{:S(2)}) collective-permute-start(f32[16,512]{1,0:T(8,128)S(1)} %get-tuple-element.30), channel_id=1, source_target_pairs={{0,12},{1,13},{2,14},{3,15},{4,0},{5,1},{6,2},{7,3},{8,4},{9,5},{1... | collective-permute-start | bytes 98312 | tf_op jit(solution)/shard_map/ppermute | solution.py:224

commit v3 on v2

--- a/solution.py
+++ b/solution.py
@@ -15,7 +15,7 @@
 OUTER = 4
 DEPTH = 1024
 LANES = 128
-VMEM_LIMIT = 56 << 20
+VMEM_LIMIT = 16 << 20
 
 
 def sign_tables(buckets, sign_bits, buckets_count):
@@ -68,135 +68,79 @@
     )
 
 
-def chunk_kernel(own, offsets, refs, scratch):
-    ins, outs, gate_w, up_w, down_w, feature_w, tables_in, before_in, total = refs
-    in_w, out_w, in_x, out_x, in_acc, out_acc, tables, before, ids, sems, late_sems = scratch
-    units, model = gate_w.shape
-    pieces = len(ins)
-    depth = in_w.shape[-1]
-    steps = model // depth
-    places = [pl.ds(p * own, own) for p in range(pieces)]
-
-    def copies(step, slot, side):
-        here = pl.ds(pl.multiple_of(step * depth, depth), depth)
-        if side == 0:
-            weights, buffer, xs, x_buffer = (gate_w, up_w, feature_w), in_w, ins, in_x
-        else:
-            weights, buffer, xs, x_buffer = (down_w, feature_w), out_w, outs, out_x
-        at = 0
-        found = []
-        for weight in weights:
-            height = weight.shape[0]
-            found.append((weight.at[:, here], buffer.at[slot, pl.ds(at, height)]))
-            at += height
-        for x, offset, place in zip(xs, offsets[side], places):
-            there = pl.ds(pl.multiple_of(offset + step * depth, LANES), depth)
-            found.append((x.at[:, there], x_buffer.at[slot, place]))
-        return [
-            pltpu.make_async_copy(source, target, sems.at[slot, side, i])
-            for i, (source, target) in enumerate(found)
+def chunk_kernel(offsets, refs, scratch):
+    ins, outs, gate_w, up_w, down_w, feature_w, tables, before, total = refs
+    gate_acc, up_acc, hidden_acc, in_acc, out_acc = scratch
+    model = gate_w.shape[1]
+    depth = min(DEPTH, model)
+    for acc in scratch:
+        acc[...] = jnp.zeros_like(acc)
+
+    def rows_of(xs, side, first, count):
+        parts = [
+            x[:, pl.ds(pl.multiple_of(offset + first, LANES), count)]
+            for x, offset in zip(xs, offsets[side])
         ]
-
-    def start(step, slot):
-        for side in range(2):
-            for copy in copies(step, slot, side):
-                copy.start()
-
-    start(0, 0)
-    late = [(tables_in, tables), (before_in, before)] + [
-        (x.at[:, pl.ds(offset + model, LANES)], ids.at[place])
-        for x, offset, place in zip(outs, offsets[1], places)
-    ]
-    late = [
-        pltpu.make_async_copy(source, target, late_sems.at[i])
-        for i, (source, target) in enumerate(late)
-    ]
-    for copy in late:
-        copy.start()
-    in_acc[...] = jnp.zeros_like(in_acc)
-    out_acc[...] = jnp.zeros_like(out_acc)
+        return jnp.concatenate(parts, axis=0) if len(parts) > 1 else parts[0]
 
     def body(step, _):
-        slot = step % 2
-
-        @pl.when(step < steps - 1)
-        def _():
-            start(step + 1, 1 - slot)
-
-        for side, (weight, x, acc) in enumerate(((in_w, in_x, in_acc), (out_w, out_x, out_acc))):
-            for copy in copies(step, slot, side):
-                copy.wait()
-            acc[...] += dot_rows(weight[slot], x[slot])
+        first = pl.multiple_of(step * depth, depth)
+        here = pl.ds(first, depth)
+        rows_in, rows_out = (rows_of(xs, side, first, depth) for side, xs in enumerate((ins, outs)))
+        gate_acc[...] += dot_rows(rows_in, gate_w[:, here])
+        up_acc[...] += dot_rows(rows_in, up_w[:, here])
+        in_acc[...] += dot_rows(rows_in, feature_w[:, here])
+        hidden_acc[...] += dot_rows(rows_out, down_w[:, here])
+        out_acc[...] += dot_rows(rows_out, feature_w[:, here])
         return 0
 
-    lax.fori_loop(0, steps, body, 0)
-    for copy in late:
-        copy.wait()
+    lax.fori_loop(0, model // depth, body, 0)
 
     bf16 = jnp.bfloat16
-    gate, up, hidden_grad = in_acc[:units], in_acc[units : 2 * units], out_acc[:units]
+    gate, up, hidden_grad = gate_acc[...], up_acc[...], hidden_acc[...]
     sigmoid = jax.nn.sigmoid(gate)
     activated = gate * sigmoid
     hidden = activated * up
     gate_grad = hidden_grad * up * sigmoid * (1.0 + gate * (1.0 - sigmoid))
     up_grad = hidden_grad * activated
-    down_part = dot(tables[2], hidden.astype(bf16)).astype(bf16)
+    down_part = dot_rows(hidden.astype(bf16), tables[2]).astype(bf16)
     input_part = (
-        dot(tables[0], gate_grad.astype(bf16)) + dot(tables[1], up_grad.astype(bf16))
+        dot_rows(gate_grad.astype(bf16), tables[0]) + dot_rows(up_grad.astype(bf16), tables[1])
     ).astype(bf16)
-    example = ids[...].astype(jnp.float32).T[:1, :]
+    example = rows_of(outs, 1, model, LANES).astype(jnp.float32)
+    example = jnp.concatenate([example] * (K2 // LANES), axis=1)
 
     def by_example(features):
+        rounded = features.astype(bf16).astype(jnp.float32)
         return jnp.concatenate(
-            [jnp.where(example == e, features, 0.0) for e in range(EX)], axis=0
+            [jnp.where(example == e, rounded, 0.0) for e in range(EX)], axis=1
         ).astype(bf16)
 
-    total[...] = (
-        before[...]
-        + dot_rows(down_part, by_example(out_acc[units:]))
-        + dot_rows(input_part, by_example(in_acc[2 * units :]))
+    total[...] = before[...] + lax.dot_general(
+        jnp.concatenate([down_part, input_part], axis=0),
+        jnp.concatenate([by_example(out_acc[...]), by_example(in_acc[...])], axis=0),
+        (((0,), (0,)), ((), ())),
+        preferred_element_type=jnp.float32,
     )
 
 
 def chunk(pieces, gate_rows, up_rows, down_rows, feature_table, tables, before):
-    own = pieces[0][0].shape[0]
     units, model = gate_rows.shape
-    short = -units % 16
-    if short:
-        gate_rows, up_rows, down_rows = (
-            jnp.pad(weight, ((0, short), (0, 0))) for weight in (gate_rows, up_rows, down_rows)
-        )
-        tables = jnp.pad(tables, ((0, 0), (0, 0), (0, short)))
-        units += short
-    rows = own * len(pieces)
-    depth = min(DEPTH, model)
+    count = len(pieces)
+    rows = pieces[0][0].shape[0] * count
     ins, in_at, outs, out_at = zip(*pieces)
-    f32, bf16 = jnp.float32, jnp.bfloat16
-    in_height, out_height = 2 * units + K2, units + K2
+    f32 = jnp.float32
 
     def kernel(*refs):
-        count = len(pieces)
         named = (refs[:count], refs[count : 2 * count], *refs[2 * count : 2 * count + 7])
-        chunk_kernel(own, (in_at, out_at), named, refs[2 * count + 7 :])
+        chunk_kernel((in_at, out_at), named, refs[2 * count + 7 :])
 
     return pl.pallas_call(
         kernel,
-        in_specs=[pl.BlockSpec(memory_space=pl.ANY)] * (2 * len(pieces) + 6),
+        in_specs=[pl.BlockSpec(memory_space=pltpu.VMEM)] * (2 * count + 6),
         out_specs=pl.BlockSpec(memory_space=pltpu.VMEM),
         out_shape=jax.ShapeDtypeStruct(before.shape, f32),
-        scratch_shapes=[
-            pltpu.VMEM((2, in_height, depth), bf16),
-            pltpu.VMEM((2, out_height, depth), bf16),
-            pltpu.VMEM((2, rows, depth), bf16),
-            pltpu.VMEM((2, rows, depth), bf16),
-            pltpu.VMEM((in_height, rows), f32),
-            pltpu.VMEM((out_height, rows), f32),
-            pltpu.VMEM(tables.shape, bf16),
-            pltpu.VMEM(before.shape, f32),
-            pltpu.VMEM((rows, LANES), bf16),
-            pltpu.SemaphoreType.DMA((2, 2, 3 + len(pieces))),
-            pltpu.SemaphoreType.DMA((2 + len(pieces),)),
-        ],
+        scratch_shapes=[pltpu.VMEM((rows, units), f32)] * 3 + [pltpu.VMEM((rows, K2), f32)] * 2,
         compiler_params=pltpu.CompilerParams(vmem_limit_bytes=VMEM_LIMIT),
         cost_estimate=pl.CostEstimate(
             flops=2 * rows * model * (3 * units + 2 * K2),

time: 167 us -> 169 us (1.012)
  Pallas kernels: 92.3 us -> 62.8 us
  local copies, waits for them, and re-layouts: 8.24 us -> 35.1 us
  waiting for transfers between devices: 40.6 us -> 47.5 us
  other arithmetic: 6.81 us -> 4.25 us
    pallas_call x5, Pallas kernels: 92.3 us -> 62.8 us  [chunk(): pl.pallas_call(kernel, in_specs=[pl.BlockSpec(memory_space=pltpu.VMEM)] *...]
    unnamed x44 -> x38, local copies, waits for them, and re-layouts: 5.48 us -> 34.2 us
    ppermute x22, waiting for transfers between devices: 40.6 us -> 47.5 us  [move(): return lax.ppermute(value, 'fsdp', pairs)]
    select_n x2, other arithmetic: 3.72 us -> 1.16 us  [sign_tables(): return jnp.where(matches, signed, jnp.zeros_like(signed))]
  transfers between devices with their start and end apart: 22 -> 22, of which waited for: 14 -> 16; matrix products, arithmetic and copies ran while one was open for 3% -> 1% of each run, Pallas kernels for 46% -> 29%
where the time goes in v3:
time: 169 us; the launch traced here: 168 us
  Pallas kernels  62.8 us (37%)
  waiting for transfers between devices  47.5 us (28%)
  local copies, waits for them, and re-layouts  35.1 us (21%)
  starting transfers between devices  18.4 us (11%)
  other arithmetic  4.25 us (3%)
    pallas_call x5, Pallas kernels, chunk(): pl.pallas_call(kernel, in_specs=[pl.BlockSpec(memory_space=pltpu.VMEM)] *...  62.8 us
    ppermute x22, waiting for transfers between devices, move(): return lax.ppermute(value, 'fsdp', pairs)  47.5 us
    unnamed x38, local copies, waits for them, and re-layouts  34.2 us
    ppermute x22, starting transfers between devices, move(): return lax.ppermute(value, 'fsdp', pairs)  18.4 us
  transfers between devices with their start and end apart: 22, of which 16 were waited for; matrix products, arithmetic and copies ran while one was open for 1% of the time, Pallas kernels for 29%

profile of v3, /device:TPU:0, one launch (start us, length us, event | category | flops | bytes accessed | tf_op | source)
XLA Modules:
  0.0 168.3 jit_solution(14539646178480305761)
XLA Ops:
  0.0 0.7 convert_element_type.10
  0.7 0.1 broadcast_in_dim.48
  0.8 1.4 pad_maximum_fusion.refs_0_.refs_2_
  2.2 0.5 collective-permute-start.2
  2.7 2.6 %collective-permute-start = (bf16[64,10368]{1,0:T(8,128)(2,1)S(1)}, bf16[64,10368]{1,0:T(8,128)(2,1)}, u32[]{:S(2)}, u32[]{:S(2)}) collective-permute-start(bf16[64,10368]{1,0:T(8,128)(2,1)S(1)} %pad_maximum_fusion.refs_0_.refs_2_), channel_id=1, source_target_pairs={{0,4},{1,13},{2,6},{3,15},{4,8},{5,1},{6,10},{7,3},{8,12},{9,5},{1... | collective-permute-start | bytes 3981320 | tf_op jit(solution)/shard_map/ppermute | solution.py:168
  5.3 1.5 collective-permute-start.1
  6.8 0.4 fusion.1.refs_8_.refs_12_
  7.3 0.7 fusion.refs_7_.refs_11_
  8.1 0.1 broadcast_in_dim.53.refs_9_
  8.1 0.3 copy-done.9
  8.4 3.5 %copy-done = bf16[5120,864]{0,1:T(8,128)(2,1)S(1)} copy-done((bf16[5120,864]{0,1:T(8,128)(2,1)S(1)}, bf16[5120,864]{0,1:T(8,128)(2,1)}, u32[]{:S(2)}) %copy-start) | copy-done | bytes 8847384
  11.9 3.5 %copy-done.3 = bf16[5120,864]{0,1:T(8,128)(2,1)S(1)} copy-done((bf16[5120,864]{0,1:T(8,128)(2,1)S(1)}, bf16[5120,864]{0,1:T(8,128)(2,1)}, u32[]{:S(2)}) %copy-start.3) | copy-done | bytes 8847384
  15.4 3.5 %copy-done.6 = bf16[864,5120]{1,0:T(8,128)(2,1)S(1)} copy-done((bf16[864,5120]{1,0:T(8,128)(2,1)S(1)}, bf16[864,5120]{1,0:T(8,128)(2,1)}, u32[]{:S(2)}) %copy-start.6) | copy-done | bytes 8847384
  19.0 11.8 %chunk.5.refs_13_ = f32[256,512]{1,0:T(8,128)S(1)} custom-call(bf16[64,10368]{1,0:T(8,128)(2,1)S(1)} %pad_maximum_fusion.refs_0_.refs_2_, bf16[64,10368]{1,0:T(8,128)(2,1)S(1)} %collective-permute-done.2.refs_1_.refs_3_, bf16[64,10368]{1,0:T(8,128)(2,1)S(1)} %pad_maximum_fusion.refs_0_.refs_2_, bf16[64,10368]{1,0:T(8,128)(2,1)S(1)} %collective-permute-done.2.refs_1_.refs_3_, ...), custom_call_target="tpu_custom_call" | custom-call | flops 4068474880 | bytes 31784960 | tf_op jit(solution)/shard_map/chunk/pallas_call | solution.py:138
  30.8 6.5 %collective-permute-done.refs_0_.refs_4_ = bf16[64,10368]{1,0:T(8,128)(2,1)} collective-permute-done((bf16[64,10368]{1,0:T(8,128)(2,1)S(1)}, bf16[64,10368]{1,0:T(8,128)(2,1)}, u32[]{:S(2)}, u32[]{:S(2)}) %collective-permute-start) | collective-permute-done | bytes 1327136 | tf_op jit(solution)/shard_map/ppermute | solution.py:168
  37.4 0.1 collective-permute-start.5
  37.5 0.4 collective-permute-start.6
  37.9 1.1 copy-done.12
  38.9 1.5 collective-permute-start.4
  40.4 1.0 collective-permute-done.5.refs_1_.refs_5_
  41.4 0.9 collective-permute-done.6.refs_3_.refs_7_
  42.3 3.5 %copy-done.4 = bf16[5120,864]{0,1:T(8,128)(2,1)S(1)} copy-done((bf16[5120,864]{0,1:T(8,128)(2,1)S(1)}, bf16[5120,864]{0,1:T(8,128)(2,1)}, u32[]{:S(2)}) %copy-start.4) | copy-done | bytes 8847384
  45.8 3.5 %copy-done.7 = bf16[864,5120]{1,0:T(8,128)(2,1)S(1)} copy-done((bf16[864,5120]{1,0:T(8,128)(2,1)S(1)}, bf16[864,5120]{1,0:T(8,128)(2,1)}, u32[]{:S(2)}) %copy-start.7) | copy-done | bytes 8847384
  49.3 1.3 copy-done.10
  50.7 1.3 copy-done.13
  52.0 13.6 %chunk.6.refs_13_ = f32[256,512]{1,0:T(8,128)S(1)} custom-call(bf16[64,10368]{1,0:T(8,128)(2,1)} %collective-permute-done.refs_0_.refs_4_, bf16[64,10368]{1,0:T(8,128)(2,1)S(1)} %collective-permute-done.5.refs_1_.refs_5_, bf16[64,10368]{1,0:T(8,128)(2,1)S(1)} %copy-done.13, bf16[64,10368]{1,0:T(8,128)(2,1)S(1)} %collective-permute-done.6.refs_3_.refs_7_, ...), custom_call_target="tpu_custom_call" | custom-call | flops 8136949760 | bytes 34406400 | tf_op jit(solution)/shard_map/chunk/pallas_call | solution.py:138
  65.6 5.1 %collective-permute-done.3.refs_0_.refs_4_ = bf16[64,10368]{1,0:T(8,128)(2,1)S(1)} collective-permute-done((bf16[64,10368]{1,0:T(8,128)(2,1)}, bf16[64,10368]{1,0:T(8,128)(2,1)S(1)}, u32[]{:S(2)}, u32[]{:S(2)}) %collective-permute-start.3) | collective-permute-done | bytes 1327136 | tf_op jit(solution)/shard_map/ppermute | solution.py:168
  70.7 0.3 collective-permute-start.10
  71.0 0.2 collective-permute-start.9
  71.2 1.3 collective-permute-start.7
  72.5 1.5 collective-permute-start.8
  74.0 1.6 collective-permute-done.9.refs_1_.refs_5_
  75.7 11.9 %chunk.7.refs_13_ = f32[256,512]{1,0:T(8,128)S(1)} custom-call(bf16[64,10368]{1,0:T(8,128)(2,1)S(1)} %collective-permute-done.3.refs_0_.refs_4_, bf16[64,10368]{1,0:T(8,128)(2,1)S(1)} %collective-permute-done.9.refs_1_.refs_5_, bf16[64,10368]{1,0:T(8,128)(2,1)S(1)} %collective-permute-done.4.refs_2_.refs_6_, ...), custom_call_target="tpu_custom_call" | custom-call | flops 8136949760 | bytes 34406400 | tf_op jit(solution)/shard_map/chunk/pallas_call | solution.py:138
  87.6 15.6 %collective-permute-done.7.refs_0_.refs_4_ = bf16[64,10368]{1,0:T(8,128)(2,1)S(1)} collective-permute-done((bf16[64,10368]{1,0:T(8,128)(2,1)S(1)}, bf16[64,10368]{1,0:T(8,128)(2,1)S(1)}, u32[]{:S(2)}, u32[]{:S(2)}) %collective-permute-start.7) | collective-permute-done | bytes 1327136 | tf_op jit(solution)/shard_map/ppermute | solution.py:168
  103.2 1.3 collective-permute-done.8.refs_2_.refs_6_
  104.5 0.1 collective-permute-start.13
  104.6 0.4 collective-permute-start.14
  105.1 0.2 collective-permute-start.12
  105.4 1.6 collective-permute-start.11
  106.9 0.6 collective-permute-done.13.refs_1_.refs_5_
  107.6 1.9 %collective-permute-done.14.refs_3_.refs_7_ = bf16[64,10368]{1,0:T(8,128)(2,1)S(1)} collective-permute-done((bf16[64,10368]{1,0:T(8,128)(2,1)S(1)}, bf16[64,10368]{1,0:T(8,128)(2,1)S(1)}, u32[]{:S(2)}, u32[]{:S(2)}) %collective-permute-start.14) | collective-permute-done | bytes 1327136 | tf_op jit(solution)/shard_map/ppermute | solution.py:168
  109.5 11.9 %chunk.8.refs_9_ = f32[256,512]{1,0:T(8,128)S(1)} custom-call(bf16[64,10368]{1,0:T(8,128)(2,1)S(1)} %collective-permute-done.7.refs_0_.refs_4_, bf16[64,10368]{1,0:T(8,128)(2,1)S(1)} %collective-permute-done.13.refs_1_.refs_5_, bf16[64,10368]{1,0:T(8,128)(2,1)S(1)} %collective-permute-done.8.refs_2_.refs_6_, ...), custom_call_target="tpu_custom_call" | custom-call | flops 8136949760 | bytes 34406400 | tf_op jit(solution)/shard_map/chunk/pallas_call | solution.py:138
  121.4 1.5 collective-permute-done.11.refs_0_
  122.8 0.1 collective-permute-start.16
  123.0 0.4 collective-permute-start.15
  123.3 2.9 %collective-permute-done.15.refs_1_ = bf16[64,5120]{1,0:T(8,128)(2,1)} collective-permute-done((bf16[64,5120]{1,0:T(8,128)(2,1)}, bf16[64,5120]{1,0:T(8,128)(2,1)}, u32[]{:S(2)}, u32[]{:S(2)}) %collective-permute-start.15) | collective-permute-done | bytes 655392 | tf_op jit(solution)/shard_map/ppermute | solution.py:168
  126.2 3.5 %copy-done.2 = bf16[5120,864]{0,1:T(8,128)(2,1)S(1)} copy-done((bf16[5120,864]{0,1:T(8,128)(2,1)S(1)}, bf16[5120,864]{0,1:T(8,128)(2,1)}, u32[]{:S(2)}) %copy-start.2) | copy-done | bytes 8847384
  129.8 3.5 %copy-done.5 = bf16[5120,864]{0,1:T(8,128)(2,1)S(1)} copy-done((bf16[5120,864]{0,1:T(8,128)(2,1)S(1)}, bf16[5120,864]{0,1:T(8,128)(2,1)}, u32[]{:S(2)}) %copy-start.5) | copy-done | bytes 8847384
  133.3 3.5 %copy-done.8 = bf16[864,5120]{1,0:T(8,128)(2,1)S(1)} copy-done((bf16[864,5120]{1,0:T(8,128)(2,1)S(1)}, bf16[864,5120]{1,0:T(8,128)(2,1)}, u32[]{:S(2)}) %copy-start.8) | copy-done | bytes 8847384
  136.8 1.3 copy-done.11
  138.1 13.5 %chunk.9 = f32[256,512]{1,0:T(8,128)S(1)} custom-call(bf16[64,5120]{1,0:T(8,128)(2,1)} %collective-permute-done.11.refs_0_, bf16[64,5120]{1,0:T(8,128)(2,1)} %collective-permute-done.15.refs_1_, bf16[64,5248]{1,0:T(8,128)(2,1)} %collective-permute-done.12.refs_2_, bf16[64,5248]{1,0:T(8,128)(2,1)} %collective-permute-done.16.refs_3_, ...), custom_call_target="tpu_custom_call" | custom-call | flops 4068474880 | bytes 31784960 | tf_op jit(solution)/shard_map/chunk/pallas_call | solution.py:138
  151.7 0.8 copy-done.14
  152.5 0.2 collective-permute-start.17
  152.7 1.4 collective-permute-done.17
  154.1 1.0 bitcast_add_fusion
  155.1 1.6 collective-permute-start.18
  156.6 4.1 %collective-permute-done.18 = f32[4,16,512]{2,1,0:T(8,128)S(1)} collective-permute-done((f32[4,16,512]{2,1,0:T(8,128)S(1)}, f32[4,16,512]{2,1,0:T(8,128)S(1)}, u32[]{:S(2)}, u32[]{:S(2)}) %collective-permute-start.18) | collective-permute-done | bytes 131104 | tf_op jit(solution)/shard_map/ppermute | solution.py:168
  160.7 1.0 collective-permute-start.19
  161.8 1.6 collective-permute-start.20
  163.4 1.2 collective-permute-start.21
  164.6 2.0 %collective-permute-done.19 = f32[16,512]{1,0:T(8,128)S(1)} collective-permute-done((f32[16,512]{1,0:T(8,128)S(1)}, f32[16,512]{1,0:T(8,128)S(1)}, u32[]{:S(2)}, u32[]{:S(2)}) %collective-permute-start.19) | collective-permute-done | bytes 32800 | tf_op jit(solution)/shard_map/ppermute | solution.py:168
  166.6 0.9 collective-permute-done.20
  167.5 0.2 collective-permute-done.21
  167.7 0.6 copy.11
  (41 shorter events, 0.3 us)
Async XLA Ops:
  0.0 6.8 %copy-start.18 = (s32[3,864]{1,0:T(4,128)S(1)}, s32[3,864]{1,0:T(4,128)}, u32[]{:S(2)}) copy-start(s32[3,864]{1,0:T(4,128)} %param.17) | copy-start | bytes 31108
  0.0 6.8 %copy-start.17 = (s32[3,864]{1,0:T(4,128)S(1)}, s32[3,864]{1,0:T(4,128)}, u32[]{:S(2)}) copy-start(s32[3,864]{1,0:T(4,128)} %param.16) | copy-start | bytes 31108
  0.8 6.5 %copy-start.16 = (s32[5120]{0:T(1024)S(1)}, s32[5120]{0:T(1024)}, u32[]{:S(2)}) copy-start(s32[5120]{0:T(1024)} %param.19) | copy-start | bytes 61444
  2.2 5.2 %copy-start.15 = (s32[5120]{0:T(1024)S(1)}, s32[5120]{0:T(1024)}, u32[]{:S(2)}) copy-start(s32[5120]{0:T(1024)} %param.18) | copy-start | bytes 61444
  2.2 5.9 %collective-permute-start.2 = (bf16[64,10368]{1,0:T(8,128)(2,1)S(1)}, bf16[64,10368]{1,0:T(8,128)(2,1)S(1)}, u32[]{:S(2)}, u32[]{:S(2)}) collective-permute-start(bf16[64,10368]{1,0:T(8,128)(2,1)S(1)} %pad_maximum_fusion.refs_0_.refs_2_), channel_id=1, source_target_pairs={{0,1},{1,0},{2,3},{3,2},{4,5},{5,4},{6,7},{7,6},{8,9},{9,8},{10,11... | collective-permute-start | bytes 3981320 | tf_op jit(solution)/shard_map/ppermute | solution.py:168
  2.7 34.7 %collective-permute-start = (bf16[64,10368]{1,0:T(8,128)(2,1)S(1)}, bf16[64,10368]{1,0:T(8,128)(2,1)}, u32[]{:S(2)}, u32[]{:S(2)}) collective-permute-start(bf16[64,10368]{1,0:T(8,128)(2,1)S(1)} %pad_maximum_fusion.refs_0_.refs_2_), channel_id=1, source_target_pairs={{0,4},{1,13},{2,6},{3,15},{4,8},{5,1},{6,10},{7,3},{8,12},{9,5},{1... | collective-permute-start | bytes 3981320 | tf_op jit(solution)/shard_map/ppermute | solution.py:168
  5.3 32.0 %collective-permute-start.1 = (bf16[64,10368]{1,0:T(8,128)(2,1)S(1)}, bf16[64,10368]{1,0:T(8,128)(2,1)S(1)}, u32[]{:S(2)}, u32[]{:S(2)}) collective-permute-start(bf16[64,10368]{1,0:T(8,128)(2,1)S(1)} %pad_maximum_fusion.refs_0_.refs_2_), channel_id=1, source_target_pairs={{0,2},{1,3},{2,0},{3,1},{4,6},{5,7},{6,4},{7,5},{8,10},{9,11},{10,... | collective-permute-start | bytes 3981320 | tf_op jit(solution)/shard_map/ppermute | solution.py:168
  7.3 1.1 copy-start.9
  8.4 3.5 %copy-start = (bf16[5120,864]{0,1:T(8,128)(2,1)S(1)}, bf16[5120,864]{0,1:T(8,128)(2,1)}, u32[]{:S(2)}) copy-start(bf16[5120,864]{0,1:T(8,128)(2,1)} %param.13) | copy-start | bytes 26542084
  11.9 3.5 %copy-start.3 = (bf16[5120,864]{0,1:T(8,128)(2,1)S(1)}, bf16[5120,864]{0,1:T(8,128)(2,1)}, u32[]{:S(2)}) copy-start(bf16[5120,864]{0,1:T(8,128)(2,1)} %param.14) | copy-start | bytes 26542084
  15.4 3.5 %copy-start.6 = (bf16[864,5120]{1,0:T(8,128)(2,1)S(1)}, bf16[864,5120]{1,0:T(8,128)(2,1)}, u32[]{:S(2)}) copy-start(bf16[864,5120]{1,0:T(8,128)(2,1)} %refs_6_.3) | copy-start | bytes 26542084
  18.9 23.4 %copy-start.1 = (bf16[5120,864]{0,1:T(8,128)(2,1)S(1)}, bf16[5120,864]{0,1:T(8,128)(2,1)}, u32[]{:S(2)}) copy-start(bf16[5120,864]{0,1:T(8,128)(2,1)} %param.13) | copy-start | bytes 26542084
  37.4 4.1 %collective-permute-start.5 = (bf16[64,10368]{1,0:T(8,128)(2,1)}, bf16[64,10368]{1,0:T(8,128)(2,1)S(1)}, u32[]{:S(2)}, u32[]{:S(2)}) collective-permute-start(bf16[64,10368]{1,0:T(8,128)(2,1)} %collective-permute-done.refs_0_.refs_4_), channel_id=1, source_target_pairs={{0,1},{1,0},{2,3},{3,2},{4,5},{5,4},{6,7},{7,6},{8,9},{9,8},{10,11... | collective-permute-start | bytes 3981320 | tf_op jit(solution)/shard_map/ppermute | solution.py:168
  37.5 4.8 %collective-permute-start.6 = (bf16[64,10368]{1,0:T(8,128)(2,1)S(1)}, bf16[64,10368]{1,0:T(8,128)(2,1)S(1)}, u32[]{:S(2)}, u32[]{:S(2)}) collective-permute-start(bf16[64,10368]{1,0:T(8,128)(2,1)S(1)} %collective-permute-done.1.refs_2_.refs_6_), channel_id=1, source_target_pairs={{0,1},{1,0},{2,3},{3,2},{4,5},{5,4},{6,7},{7,6},{8,9},{9,8},{10,11... | collective-permute-start | bytes 3981320 | tf_op jit(solution)/shard_map/ppermute | solution.py:168
  37.9 1.1 copy-start.12
  38.9 31.8 %collective-permute-start.3 = (bf16[64,10368]{1,0:T(8,128)(2,1)}, bf16[64,10368]{1,0:T(8,128)(2,1)S(1)}, u32[]{:S(2)}, u32[]{:S(2)}) collective-permute-start(bf16[64,10368]{1,0:T(8,128)(2,1)} %collective-permute-done.refs_0_.refs_4_), channel_id=1, source_target_pairs={{0,4},{1,13},{2,6},{3,15},{4,8},{5,1},{6,10},{7,3},{8,12},{9,5},{1... | collective-permute-start | bytes 3981320 | tf_op jit(solution)/shard_map/ppermute | solution.py:168
  38.9 31.8 %collective-permute-start.4 = (bf16[64,10368]{1,0:T(8,128)(2,1)}, bf16[64,10368]{1,0:T(8,128)(2,1)S(1)}, u32[]{:S(2)}, u32[]{:S(2)}) collective-permute-start(bf16[64,10368]{1,0:T(8,128)(2,1)} %collective-permute-done.refs_0_.refs_4_), channel_id=1, source_target_pairs={{0,2},{1,3},{2,0},{3,1},{4,6},{5,7},{6,4},{7,5},{8,10},{9,11},{10,... | collective-permute-start | bytes 3981320 | tf_op jit(solution)/shard_map/ppermute | solution.py:168
  42.3 3.5 %copy-start.4 = (bf16[5120,864]{0,1:T(8,128)(2,1)S(1)}, bf16[5120,864]{0,1:T(8,128)(2,1)}, u32[]{:S(2)}) copy-start(bf16[5120,864]{0,1:T(8,128)(2,1)} %param.14) | copy-start | bytes 26542084
  45.8 3.5 %copy-start.7 = (bf16[864,5120]{1,0:T(8,128)(2,1)S(1)}, bf16[864,5120]{1,0:T(8,128)(2,1)}, u32[]{:S(2)}) copy-start(bf16[864,5120]{1,0:T(8,128)(2,1)} %refs_6_.3) | copy-start | bytes 26542084
  49.3 1.3 copy-start.10
  50.7 1.3 copy-start.13
  70.7 3.3 %collective-permute-start.10 = (bf16[64,10368]{1,0:T(8,128)(2,1)S(1)}, bf16[64,10368]{1,0:T(8,128)(2,1)S(1)}, u32[]{:S(2)}, u32[]{:S(2)}) collective-permute-start(bf16[64,10368]{1,0:T(8,128)(2,1)S(1)} %collective-permute-done.4.refs_2_.refs_6_), channel_id=1, source_target_pairs={{0,1},{1,0},{2,3},{3,2},{4,5},{5,4},{6,7},{7,6},{8,9},{9,8},{10,11... | collective-permute-start | bytes 3981320 | tf_op jit(solution)/shard_map/ppermute | solution.py:168
  71.0 4.7 %collective-permute-start.9 = (bf16[64,10368]{1,0:T(8,128)(2,1)S(1)}, bf16[64,10368]{1,0:T(8,128)(2,1)S(1)}, u32[]{:S(2)}, u32[]{:S(2)}) collective-permute-start(bf16[64,10368]{1,0:T(8,128)(2,1)S(1)} %collective-permute-done.3.refs_0_.refs_4_), channel_id=1, source_target_pairs={{0,1},{1,0},{2,3},{3,2},{4,5},{5,4},{6,7},{7,6},{8,9},{9,8},{10,11... | collective-permute-start | bytes 3981320 | tf_op jit(solution)/shard_map/ppermute | solution.py:168
  71.2 32.0 %collective-permute-start.7 = (bf16[64,10368]{1,0:T(8,128)(2,1)S(1)}, bf16[64,10368]{1,0:T(8,128)(2,1)S(1)}, u32[]{:S(2)}, u32[]{:S(2)}) collective-permute-start(bf16[64,10368]{1,0:T(8,128)(2,1)S(1)} %collective-permute-done.3.refs_0_.refs_4_), channel_id=1, source_target_pairs={{0,4},{1,13},{2,6},{3,15},{4,8},{5,1},{6,10},{7,3},{8,12},{9,5},{1... | collective-permute-start | bytes 3981320 | tf_op jit(solution)/shard_map/ppermute | solution.py:168
  72.5 32.0 %collective-permute-start.8 = (bf16[64,10368]{1,0:T(8,128)(2,1)S(1)}, bf16[64,10368]{1,0:T(8,128)(2,1)S(1)}, u32[]{:S(2)}, u32[]{:S(2)}) collective-permute-start(bf16[64,10368]{1,0:T(8,128)(2,1)S(1)} %collective-permute-done.3.refs_0_.refs_4_), channel_id=1, source_target_pairs={{0,2},{1,3},{2,0},{3,1},{4,6},{5,7},{6,4},{7,5},{8,10},{9,11},{10,... | collective-permute-start | bytes 3981320 | tf_op jit(solution)/shard_map/ppermute | solution.py:168
  104.5 3.1 %collective-permute-start.13 = (bf16[64,10368]{1,0:T(8,128)(2,1)S(1)}, bf16[64,10368]{1,0:T(8,128)(2,1)S(1)}, u32[]{:S(2)}, u32[]{:S(2)}) collective-permute-start(bf16[64,10368]{1,0:T(8,128)(2,1)S(1)} %collective-permute-done.7.refs_0_.refs_4_), channel_id=1, source_target_pairs={{0,1},{1,0},{2,3},{3,2},{4,5},{5,4},{6,7},{7,6},{8,9},{9,8},{10,11... | collective-permute-start | bytes 3981320 | tf_op jit(solution)/shard_map/ppermute | solution.py:168
  104.6 4.9 %collective-permute-start.14 = (bf16[64,10368]{1,0:T(8,128)(2,1)S(1)}, bf16[64,10368]{1,0:T(8,128)(2,1)S(1)}, u32[]{:S(2)}, u32[]{:S(2)}) collective-permute-start(bf16[64,10368]{1,0:T(8,128)(2,1)S(1)} %collective-permute-done.8.refs_2_.refs_6_), channel_id=1, source_target_pairs={{0,1},{1,0},{2,3},{3,2},{4,5},{5,4},{6,7},{7,6},{8,9},{9,8},{10,11... | collective-permute-start | bytes 3981320 | tf_op jit(solution)/shard_map/ppermute | solution.py:168
  105.1 17.7 %collective-permute-start.12 = (bf16[64,5248]{1,0:T(8,128)(2,1)S(1)}, bf16[64,5248]{1,0:T(8,128)(2,1)}, u32[]{:S(2)}, u32[]{:S(2)}) collective-permute-start(bf16[64,5248]{1,0:T(8,128)(2,1)S(1)} %slice.7), channel_id=1, source_target_pairs={{0,4},{1,13},{2,6},{3,15},{4,8},{5,1},{6,10},{7,3},{8,12},{9,5},{1... | collective-permute-start | bytes 2015240 | tf_op jit(solution)/shard_map/ppermute | solution.py:168
  105.4 17.5 %collective-permute-start.11 = (bf16[64,5120]{1,0:T(8,128)(2,1)S(1)}, bf16[64,5120]{1,0:T(8,128)(2,1)}, u32[]{:S(2)}, u32[]{:S(2)}) collective-permute-start(bf16[64,5120]{1,0:T(8,128)(2,1)S(1)} %slice.6), channel_id=1, source_target_pairs={{0,2},{1,3},{2,0},{3,1},{4,6},{5,7},{6,4},{7,5},{8,10},{9,11},{10,... | collective-permute-start | bytes 1966088 | tf_op jit(solution)/shard_map/ppermute | solution.py:168
  122.8 3.4 %collective-permute-start.16 = (bf16[64,5248]{1,0:T(8,128)(2,1)}, bf16[64,5248]{1,0:T(8,128)(2,1)}, u32[]{:S(2)}, u32[]{:S(2)}) collective-permute-start(bf16[64,5248]{1,0:T(8,128)(2,1)} %collective-permute-done.12.refs_2_), channel_id=1, source_target_pairs={{0,1},{1,0},{2,3},{3,2},{4,5},{5,4},{6,7},{7,6},{8,9},{9,8},{10,11... | collective-permute-start | bytes 2015240 | tf_op jit(solution)/shard_map/ppermute | solution.py:168
  123.0 3.3 %collective-permute-start.15 = (bf16[64,5120]{1,0:T(8,128)(2,1)}, bf16[64,5120]{1,0:T(8,128)(2,1)}, u32[]{:S(2)}, u32[]{:S(2)}) collective-permute-start(bf16[64,5120]{1,0:T(8,128)(2,1)} %collective-permute-done.11.refs_0_), channel_id=1, source_target_pairs={{0,1},{1,0},{2,3},{3,2},{4,5},{5,4},{6,7},{7,6},{8,9},{9,8},{10,11... | collective-permute-start | bytes 1966088 | tf_op jit(solution)/shard_map/ppermute | solution.py:168
  126.2 3.5 %copy-start.2 = (bf16[5120,864]{0,1:T(8,128)(2,1)S(1)}, bf16[5120,864]{0,1:T(8,128)(2,1)}, u32[]{:S(2)}) copy-start(bf16[5120,864]{0,1:T(8,128)(2,1)} %param.13) | copy-start | bytes 26542084
  129.8 3.5 %copy-start.5 = (bf16[5120,864]{0,1:T(8,128)(2,1)S(1)}, bf16[5120,864]{0,1:T(8,128)(2,1)}, u32[]{:S(2)}) copy-start(bf16[5120,864]{0,1:T(8,128)(2,1)} %param.14) | copy-start | bytes 26542084
  133.3 3.5 %copy-start.8 = (bf16[864,5120]{1,0:T(8,128)(2,1)S(1)}, bf16[864,5120]{1,0:T(8,128)(2,1)}, u32[]{:S(2)}) copy-start(bf16[864,5120]{1,0:T(8,128)(2,1)} %refs_6_.3) | copy-start | bytes 26542084
  136.8 1.3 copy-start.11
  151.7 0.8 copy-start.14
  152.5 1.6 collective-permute-start.17
  155.1 5.6 %collective-permute-start.18 = (f32[4,16,512]{2,1,0:T(8,128)S(1)}, f32[4,16,512]{2,1,0:T(8,128)S(1)}, u32[]{:S(2)}, u32[]{:S(2)}) collective-permute-start(f32[4,16,512]{2,1,0:T(8,128)S(1)} %dynamic-slice_bitcast_fusion.1), channel_id=1, source_target_pairs={{0,2},{1,3},{2,0},{3,1},{4,6},{5,7},{6,4},{7,5},{8,10},{9,11},{10,... | collective-permute-start | bytes 393224 | tf_op jit(solution)/shard_map/ppermute | solution.py:168
  160.7 5.9 %collective-permute-start.19 = (f32[16,512]{1,0:T(8,128)S(1)}, f32[16,512]{1,0:T(8,128)S(1)}, u32[]{:S(2)}, u32[]{:S(2)}) collective-permute-start(f32[16,512]{1,0:T(8,128)S(1)} %get-tuple-element.31), channel_id=1, source_target_pairs={{0,4},{1,5},{2,6},{3,7},{4,8},{5,9},{6,10},{7,11},{8,12},{9,13},{1... | collective-permute-start | bytes 98312 | tf_op jit(solution)/shard_map/ppermute | solution.py:168
  161.8 5.7 %collective-permute-start.20 = (f32[16,512]{1,0:T(8,128)S(1)}, f32[16,512]{1,0:T(8,128)S(1)}, u32[]{:S(2)}, u32[]{:S(2)}) collective-permute-start(f32[16,512]{1,0:T(8,128)S(1)} %get-tuple-element.29), channel_id=1, source_target_pairs={{0,8},{1,9},{2,10},{3,11},{4,12},{5,13},{6,14},{7,15},{8,0},{9,1},... | collective-permute-start | bytes 98312 | tf_op jit(solution)/shard_map/ppermute | solution.py:168
  163.4 4.2 %collective-permute-start.21 = (f32[16,512]{1,0:T(8,128)S(1)}, f32[16,512]{1,0:T(8,128)S(1)}, u32[]{:S(2)}, u32[]{:S(2)}) collective-permute-start(f32[16,512]{1,0:T(8,128)S(1)} %get-tuple-element.30), channel_id=1, source_target_pairs={{0,12},{1,13},{2,14},{3,15},{4,0},{5,1},{6,2},{7,3},{8,4},{9,5},{1... | collective-permute-start | bytes 98312 | tf_op jit(solution)/shard_map/ppermute | solution.py:168

commit v4 on v3

--- a/solution.py
+++ b/solution.py
@@ -15,7 +15,7 @@
 OUTER = 4
 DEPTH = 1024
 LANES = 128
-VMEM_LIMIT = 16 << 20
+VMEM_LIMIT = 12 << 20
 
 
 def sign_tables(buckets, sign_bits, buckets_count):
@@ -47,12 +47,6 @@
 
     def inner_ring(self):
         return self.pairs(lambda o, i, c: (o, i + 1 - 2 * c, c))
-
-    def outer_shift(self, by):
-        return self.pairs(lambda o, i, c: (o + by, i, c))
-
-    def inner_shift(self, by):
-        return self.pairs(lambda o, i, c: (o, i + by, c))
 
     def core_swap(self):
         return self.pairs(lambda o, i, c: (o, i, 1 - c))
@@ -167,10 +161,6 @@
     def move(value, pairs):
         return lax.ppermute(value, "fsdp", pairs)
 
-    me = lax.axis_index("fsdp")
-    core = me % CORES
-    inner = (me // CORES) % layout.inner
-    outer = me // (CORES * layout.inner)
     rows = inputs.shape[0]
 
     unit_tables = sign_tables(unit_buckets, unit_signs, K1)
@@ -187,39 +177,30 @@
     both = lambda piece: (piece, 0, piece, width)
     swap = lambda piece: move(piece, layout.core_swap())
     if layout.inner == 2:
-        here, across = own, None
-        for step in range(layout.outer):
-            if step < layout.outer - 1:
-                coming = [
-                    move(here, layout.outer_ring()),
-                    move(here, layout.inner_ring()),
-                ]
-            else:
-                coming = [
-                    move(here[:, :width], layout.inner_ring()),
-                    move(across[:, width:], layout.outer_ring()),
-                ]
-            pieces = [both(here), both(swap(here))]
-            if across is not None:
-                pieces += [both(across), both(swap(across))]
-            total = add(pieces, total)
-            here, across, total = lax.optimization_barrier((*coming, total))
-        pieces = [(here, 0, across, 0), (swap(here), 0, swap(across), 0)]
+        last = layout.outer - 1
+        here, across, swapped = own, None, swap(own)
+        for step in range(last):
+            coming = [move(here, layout.outer_ring()), move(here, layout.inner_ring())]
+            if step:
+                total = add([both(piece) for piece in done], total)
+            ahead, across, total = lax.optimization_barrier((*coming, total))
+            done = [here, swapped, across, swap(across)]
+            here, swapped = ahead, swap(ahead)
+        coming = [
+            move(here[:, :width], layout.inner_ring()),
+            move(across[:, width:], layout.outer_ring()),
+        ]
+        total = add([both(piece) for piece in done], total)
+        *sides, total = lax.optimization_barrier((*coming, total))
+        split = lambda pair: (pair[0], 0, pair[1], 0)
+        pieces = [both(here), both(swapped), split(sides), split([swap(side) for side in sides])]
         total = add(pieces, total)
     else:
         total = add([both(lax.all_gather(own, "fsdp", axis=0, tiled=True))], total)
 
-    part = total.reshape(layout.outer, layout.inner, CORES, -1, EX * K2)
-    take = lambda v, at, axis: lax.dynamic_index_in_dim(v, at, axis, keepdims=False)
-    part = take(part, core, 2) + move(take(part, 1 - core, 2), layout.core_swap())
-    part = take(part, inner, 1) + sum(
-        move(take(part, (inner + by) % layout.inner, 1), layout.inner_shift(by))
-        for by in range(1, layout.inner)
-    )
-    part = take(part, outer, 0) + sum(
-        move(take(part, (outer + by) % layout.outer, 0), layout.outer_shift(by))
-        for by in range(1, layout.outer)
-    )
+    parts = total.astype(jnp.bfloat16).reshape(layout.count, -1, EX * K2)
+    parts = lax.all_to_all(parts, "fsdp", 0, 0)
+    part = jnp.sum(parts.astype(jnp.float32), axis=0)
     factor = (3.0 * SEQ * FF * D / (K1 * K2)) ** (-0.5)
     return (factor * part).reshape(-1, EX, K2).transpose(1, 0, 2)
 

time: 169 us -> 151 us (0.89)
  Pallas kernels: 62.8 us -> 47.6 us
  blocking collectives: 0 us -> 13.1 us
  local copies, waits for them, and re-layouts: 35.1 us -> 24.6 us
  starting transfers between devices: 18.4 us -> 14.3 us
    pallas_call x5 -> x4, Pallas kernels: 62.8 us -> 47.6 us  [chunk(): pl.pallas_call(kernel, in_specs=[pl.BlockSpec(memory_space=pltpu.VMEM)] *...]
    all_to_all x0 -> x1, blocking collectives: none -> 13.1 us  [on_device(): parts = lax.all_to_all(parts, 'fsdp', 0, 0)]
    unnamed x38 -> x34, local copies, waits for them, and re-layouts: 34.2 us -> 23.7 us
    ppermute x22 -> x17, starting transfers between devices: 18.4 us -> 14.3 us  [move(): return lax.ppermute(value, 'fsdp', pairs)]
    ppermute x22 -> x17, waiting for transfers between devices: 47.5 us -> 47.3 us  [move(): return lax.ppermute(value, 'fsdp', pairs)]
  transfers between devices with their start and end apart: 22 -> 17, of which waited for: 16 -> 8; matrix products, arithmetic and copies ran while one was open for 1% -> 1% of each run, Pallas kernels for 29% -> 24%
where the time goes in v4:
time: 151 us; the launch traced here: 150 us
  Pallas kernels  47.6 us (32%)
  waiting for transfers between devices  47.3 us (31%)
  local copies, waits for them, and re-layouts  24.6 us (16%)
  starting transfers between devices  14.3 us (9%)
  blocking collectives  13.1 us (9%)
  other arithmetic  3.3 us (2%)
    pallas_call x4, Pallas kernels, chunk(): pl.pallas_call(kernel, in_specs=[pl.BlockSpec(memory_space=pltpu.VMEM)] *...  47.6 us
    ppermute x17, waiting for transfers between devices, move(): return lax.ppermute(value, 'fsdp', pairs)  47.3 us
    unnamed x34, local copies, waits for them, and re-layouts  23.7 us
    ppermute x17, starting transfers between devices, move(): return lax.ppermute(value, 'fsdp', pairs)  14.3 us
    all_to_all x1, blocking collectives, on_device(): parts = lax.all_to_all(parts, 'fsdp', 0, 0)  13.1 us
  transfers between devices with their start and end apart: 17, of which 8 were waited for; matrix products, arithmetic and copies ran while one was open for 1% of the time, Pallas kernels for 24%

profile of v4, /device:TPU:0, one launch (start us, length us, event | category | flops | bytes accessed | tf_op | source)
XLA Modules:
  0.0 150.3 jit_solution(9830153228227433241)
XLA Ops:
  0.0 0.7 convert_element_type.16
  0.7 0.1 broadcast_in_dim.48
  0.8 1.4 pad_maximum_fusion.refs_0_.refs_4_
  2.1 0.0 copy-start.16
  2.1 0.0 copy-start.15
  2.2 3.1 %collective-permute-start = (bf16[64,10368]{1,0:T(8,128)(2,1)S(1)}, bf16[64,10368]{1,0:T(8,128)(2,1)S(1)}, u32[]{:S(2)}, u32[]{:S(2)}) collective-permute-start(bf16[64,10368]{1,0:T(8,128)(2,1)S(1)} %pad_maximum_fusion.refs_0_.refs_4_), channel_id=1, source_target_pairs={{0,4},{1,13},{2,6},{3,15},{4,8},{5,1},{6,10},{7,3},{8,12},{9,5},{1... | collective-permute-start | bytes 3981320 | tf_op jit(solution)/shard_map/ppermute | solution.py:162
  5.2 1.5 collective-permute-start.1
  6.7 1.3 collective-permute-start.4
  8.0 0.0 copy-done.14
  8.0 28.5 %collective-permute-done.refs_0_.refs_4_ = bf16[64,10368]{1,0:T(8,128)(2,1)S(1)} collective-permute-done((bf16[64,10368]{1,0:T(8,128)(2,1)S(1)}, bf16[64,10368]{1,0:T(8,128)(2,1)S(1)}, u32[]{:S(2)}, u32[]{:S(2)}) %collective-permute-start) | collective-permute-done | bytes 1327136 | tf_op jit(solution)/shard_map/ppermute | solution.py:162
  36.5 0.1 collective-permute-done.1.refs_2_.refs_6_
  36.7 0.0 collective-permute-start.2
  36.7 1.5 collective-permute-start.3
  38.2 1.7 %collective-permute-start.5 = (bf16[64,10368]{1,0:T(8,128)(2,1)S(1)}, bf16[64,10368]{1,0:T(8,128)(2,1)S(1)}, u32[]{:S(2)}, u32[]{:S(2)}) collective-permute-start(bf16[64,10368]{1,0:T(8,128)(2,1)S(1)} %collective-permute-done.1.refs_2_.refs_6_), channel_id=1, source_target_pairs={{0,1},{1,0},{2,3},{3,2},{4,5},{5,4},{6,7},{7,6},{8,9},{9,8},{10,11... | collective-permute-start | bytes 3981320 | tf_op jit(solution)/shard_map/ppermute | solution.py:162
  39.9 0.0 copy-done.13
  39.9 0.7 fusion.refs_11_
  40.6 0.0 copy-done.16
  40.7 0.0 copy-done.15
  40.7 0.4 fusion.1.refs_12_
  41.1 0.0 copy-done.7
  41.1 0.1 collective-permute-start.8
  41.2 0.0 collective-permute-done.4.refs_1_.refs_5_
  41.2 1.1 copy-done.9
  42.3 0.3 collective-permute-done.5.refs_3_.refs_7_
  42.6 1.1 copy-done.11
  43.7 0.0 copy-start
  43.7 3.5 %copy-done = bf16[5120,864]{0,1:T(8,128)(2,1)S(1)} copy-done((bf16[5120,864]{0,1:T(8,128)(2,1)S(1)}, bf16[5120,864]{0,1:T(8,128)(2,1)}, u32[]{:S(2)}) %copy-start) | copy-done | bytes 8847384
  47.2 3.5 %copy-done.2 = bf16[5120,864]{0,1:T(8,128)(2,1)S(1)} copy-done((bf16[5120,864]{0,1:T(8,128)(2,1)S(1)}, bf16[5120,864]{0,1:T(8,128)(2,1)}, u32[]{:S(2)}) %copy-start.2) | copy-done | bytes 8847384
  50.8 3.5 %copy-done.5 = bf16[864,5120]{1,0:T(8,128)(2,1)S(1)} copy-done((bf16[864,5120]{1,0:T(8,128)(2,1)S(1)}, bf16[864,5120]{1,0:T(8,128)(2,1)}, u32[]{:S(2)}) %copy-start.5) | copy-done | bytes 8847384
  54.3 1.3 copy-done.8
  55.6 1.3 copy-done.10
  56.9 1.3 copy-done.12
  58.2 11.9 %chunk.4.refs_13_ = f32[256,512]{1,0:T(8,128)S(1)} custom-call(bf16[64,10368]{1,0:T(8,128)(2,1)S(1)} %pad_maximum_fusion.refs_0_.refs_4_, bf16[64,10368]{1,0:T(8,128)(2,1)S(1)} %copy-done.10, bf16[64,10368]{1,0:T(8,128)(2,1)S(1)} %copy-done.8, bf16[64,10368]{1,0:T(8,128)(2,1)S(1)} %copy-done.12, bf16[64,10368]{1,0:T(8,128)(2,1)S(1)} %pad_maximum_fusion.refs_0_.refs_4_, ...), custom_call_target="tpu_custom_call" | custom-call | flops 8136949760 | bytes 34406400 | tf_op jit(solution)/shard_map/chunk/pallas_call | solution.py:132
  70.1 0.0 collective-permute-done.2.refs_0_.refs_4_
  70.1 0.0 collective-permute-done.3.refs_2_.refs_6_
  70.2 0.4 collective-permute-start.9
  70.6 0.5 collective-permute-start.6
  71.2 0.5 collective-permute-start.7
  71.7 1.5 collective-permute-start.13
  73.2 0.0 collective-permute-done.8.refs_1_.refs_5_
  73.2 0.1 collective-permute-done.9.refs_3_.refs_7_
  73.3 3.5 %copy-done.3 = bf16[5120,864]{0,1:T(8,128)(2,1)S(1)} copy-done((bf16[5120,864]{0,1:T(8,128)(2,1)S(1)}, bf16[5120,864]{0,1:T(8,128)(2,1)}, u32[]{:S(2)}) %copy-start.3) | copy-done | bytes 8847384
  76.8 3.5 %copy-done.6 = bf16[864,5120]{1,0:T(8,128)(2,1)S(1)} copy-done((bf16[864,5120]{1,0:T(8,128)(2,1)S(1)}, bf16[864,5120]{1,0:T(8,128)(2,1)}, u32[]{:S(2)}) %copy-start.6) | copy-done | bytes 8847384
  80.3 11.9 %chunk.5.refs_13_ = f32[256,512]{1,0:T(8,128)S(1)} custom-call(bf16[64,10368]{1,0:T(8,128)(2,1)S(1)} %collective-permute-done.refs_0_.refs_4_, bf16[64,10368]{1,0:T(8,128)(2,1)S(1)} %collective-permute-done.8.refs_1_.refs_5_, bf16[64,10368]{1,0:T(8,128)(2,1)S(1)} %collective-permute-done.3.refs_2_.refs_6_, ...), custom_call_target="tpu_custom_call" | custom-call | flops 8136949760 | bytes 34406400 | tf_op jit(solution)/shard_map/chunk/pallas_call | solution.py:132
  92.2 10.8 %collective-permute-done.6.refs_0_.refs_4_ = bf16[64,10368]{1,0:T(8,128)(2,1)S(1)} collective-permute-done((bf16[64,10368]{1,0:T(8,128)(2,1)S(1)}, bf16[64,10368]{1,0:T(8,128)(2,1)S(1)}, u32[]{:S(2)}, u32[]{:S(2)}) %collective-permute-start.6) | collective-permute-done | bytes 1327136 | tf_op jit(solution)/shard_map/ppermute | solution.py:162
  103.0 0.0 collective-permute-done.7.refs_2_.refs_6_
  103.0 0.1 collective-permute-start.14
  103.2 0.5 collective-permute-start.10
  103.7 0.5 collective-permute-start.12
  104.2 0.5 collective-permute-start.11
  104.7 0.0 collective-permute-done.13.refs_1_.refs_5_
  104.7 1.3 collective-permute-done.14.refs_3_.refs_7_
  106.1 0.0 copy-done.4
  106.1 11.9 %chunk.6.refs_13_ = f32[256,512]{1,0:T(8,128)S(1)} custom-call(bf16[64,10368]{1,0:T(8,128)(2,1)S(1)} %collective-permute-done.2.refs_0_.refs_4_, bf16[64,10368]{1,0:T(8,128)(2,1)S(1)} %collective-permute-done.13.refs_1_.refs_5_, bf16[64,10368]{1,0:T(8,128)(2,1)S(1)} %collective-permute-done.7.refs_2_.refs_6_, ...), custom_call_target="tpu_custom_call" | custom-call | flops 8136949760 | bytes 34406400 | tf_op jit(solution)/shard_map/chunk/pallas_call | solution.py:132
  118.0 3.6 %collective-permute-done.11.refs_2_ = bf16[64,5120]{1,0:T(8,128)(2,1)S(1)} collective-permute-done((bf16[64,5120]{1,0:T(8,128)(2,1)S(1)}, bf16[64,5120]{1,0:T(8,128)(2,1)S(1)}, u32[]{:S(2)}, u32[]{:S(2)}) %collective-permute-start.11) | collective-permute-done | bytes 655392 | tf_op jit(solution)/shard_map/ppermute | solution.py:162
  121.6 0.0 collective-permute-done.12.refs_6_
  121.6 0.1 collective-permute-start.16
  121.7 0.4 collective-permute-start.15
  122.1 0.0 collective-permute-done.10.refs_1_.refs_5_
  122.1 2.5 %collective-permute-done.15.refs_3_ = bf16[64,5120]{1,0:T(8,128)(2,1)S(1)} collective-permute-done((bf16[64,5120]{1,0:T(8,128)(2,1)S(1)}, bf16[64,5120]{1,0:T(8,128)(2,1)S(1)}, u32[]{:S(2)}, u32[]{:S(2)}) %collective-permute-start.15) | collective-permute-done | bytes 655392 | tf_op jit(solution)/shard_map/ppermute | solution.py:162
  124.6 0.0 collective-permute-done.16.refs_7_
  124.6 11.9 %chunk.7 = f32[256,512]{1,0:T(8,128)S(1)} custom-call(bf16[64,10368]{1,0:T(8,128)(2,1)S(1)} %collective-permute-done.6.refs_0_.refs_4_, bf16[64,10368]{1,0:T(8,128)(2,1)S(1)} %collective-permute-done.10.refs_1_.refs_5_, bf16[64,5120]{1,0:T(8,128)(2,1)S(1)} %collective-permute-done.11.refs_2_, bf16[64,5120]{1,0:T(8,128)(2,1)S(1)} %collective-permute-done.15.refs_3_, ...), custom_call_target="tpu_custom_call" | custom-call | flops 8136949760 | bytes 34406400 | tf_op jit(solution)/shard_map/chunk/pallas_call | solution.py:132
  136.6 13.1 %all_to_all.5 = bf16[16,16,512]{2,1,0:T(8,128)(2,1)S(1)} all-to-all(bf16[16,16,512]{2,1,0:T(8,128)(2,1)S(1)} %bitcast.12), channel_id=1, replica_groups=mesh['groups'=2,'fsdp'=16] {'fsdp'}, dimensions={0} | all-to-all | bytes 524288 | tf_op jit(solution)/shard_map/all_to_all | solution.py:202
  149.7 0.6 copy.11
  (24 shorter events, 0.3 us)
Async XLA Ops:
  0.0 8.0 %copy-start.14 = (s32[5120]{0:T(1024)S(1)}, s32[5120]{0:T(1024)}, u32[]{:S(2)}) copy-start(s32[5120]{0:T(1024)} %param.19) | copy-start | bytes 61444
  0.0 39.9 %copy-start.13 = (s32[5120]{0:T(1024)S(1)}, s32[5120]{0:T(1024)}, u32[]{:S(2)}) copy-start(s32[5120]{0:T(1024)} %param.18) | copy-start | bytes 61444
  2.1 38.5 %copy-start.16 = (s32[3,864]{1,0:T(4,128)S(1)}, s32[3,864]{1,0:T(4,128)}, u32[]{:S(2)}) copy-start(s32[3,864]{1,0:T(4,128)} %param.17) | copy-start | bytes 31108
  2.1 38.5 %copy-start.15 = (s32[3,864]{1,0:T(4,128)S(1)}, s32[3,864]{1,0:T(4,128)}, u32[]{:S(2)}) copy-start(s32[3,864]{1,0:T(4,128)} %param.16) | copy-start | bytes 31108
  2.2 34.4 %collective-permute-start = (bf16[64,10368]{1,0:T(8,128)(2,1)S(1)}, bf16[64,10368]{1,0:T(8,128)(2,1)S(1)}, u32[]{:S(2)}, u32[]{:S(2)}) collective-permute-start(bf16[64,10368]{1,0:T(8,128)(2,1)S(1)} %pad_maximum_fusion.refs_0_.refs_4_), channel_id=1, source_target_pairs={{0,4},{1,13},{2,6},{3,15},{4,8},{5,1},{6,10},{7,3},{8,12},{9,5},{1... | collective-permute-start | bytes 3981320 | tf_op jit(solution)/shard_map/ppermute | solution.py:162
  5.2 31.4 %collective-permute-start.1 = (bf16[64,10368]{1,0:T(8,128)(2,1)S(1)}, bf16[64,10368]{1,0:T(8,128)(2,1)S(1)}, u32[]{:S(2)}, u32[]{:S(2)}) collective-permute-start(bf16[64,10368]{1,0:T(8,128)(2,1)S(1)} %pad_maximum_fusion.refs_0_.refs_4_), channel_id=1, source_target_pairs={{0,2},{1,3},{2,0},{3,1},{4,6},{5,7},{6,4},{7,5},{8,10},{9,11},{10,... | collective-permute-start | bytes 3981320 | tf_op jit(solution)/shard_map/ppermute | solution.py:162
  6.7 34.5 %collective-permute-start.4 = (bf16[64,10368]{1,0:T(8,128)(2,1)S(1)}, bf16[64,10368]{1,0:T(8,128)(2,1)S(1)}, u32[]{:S(2)}, u32[]{:S(2)}) collective-permute-start(bf16[64,10368]{1,0:T(8,128)(2,1)S(1)} %pad_maximum_fusion.refs_0_.refs_4_), channel_id=1, source_target_pairs={{0,1},{1,0},{2,3},{3,2},{4,5},{5,4},{6,7},{7,6},{8,9},{9,8},{10,11... | collective-permute-start | bytes 3981320 | tf_op jit(solution)/shard_map/ppermute | solution.py:162
  36.7 4.4 %copy-start.7 = (bf16[64,10368]{1,0:T(8,128)(2,1)}, bf16[64,10368]{1,0:T(8,128)(2,1)S(1)}, u32[]{:S(2)}) copy-start(bf16[64,10368]{1,0:T(8,128)(2,1)S(1)} %collective-permute-done.1.refs_2_.refs_6_) | copy-start | bytes 3981316
  36.7 33.5 %collective-permute-start.2 = (bf16[64,10368]{1,0:T(8,128)(2,1)S(1)}, bf16[64,10368]{1,0:T(8,128)(2,1)S(1)}, u32[]{:S(2)}, u32[]{:S(2)}) collective-permute-start(bf16[64,10368]{1,0:T(8,128)(2,1)S(1)} %collective-permute-done.refs_0_.refs_4_), channel_id=1, source_target_pairs={{0,4},{1,13},{2,6},{3,15},{4,8},{5,1},{6,10},{7,3},{8,12},{9,5},{1... | collective-permute-start | bytes 3981320 | tf_op jit(solution)/shard_map/ppermute | solution.py:162
  36.7 33.5 %collective-permute-start.3 = (bf16[64,10368]{1,0:T(8,128)(2,1)S(1)}, bf16[64,10368]{1,0:T(8,128)(2,1)S(1)}, u32[]{:S(2)}, u32[]{:S(2)}) collective-permute-start(bf16[64,10368]{1,0:T(8,128)(2,1)S(1)} %collective-permute-done.refs_0_.refs_4_), channel_id=1, source_target_pairs={{0,2},{1,3},{2,0},{3,1},{4,6},{5,7},{6,4},{7,5},{8,10},{9,11},{10,... | collective-permute-start | bytes 3981320 | tf_op jit(solution)/shard_map/ppermute | solution.py:162
  38.2 4.4 %collective-permute-start.5 = (bf16[64,10368]{1,0:T(8,128)(2,1)S(1)}, bf16[64,10368]{1,0:T(8,128)(2,1)S(1)}, u32[]{:S(2)}, u32[]{:S(2)}) collective-permute-start(bf16[64,10368]{1,0:T(8,128)(2,1)S(1)} %collective-permute-done.1.refs_2_.refs_6_), channel_id=1, source_target_pairs={{0,1},{1,0},{2,3},{3,2},{4,5},{5,4},{6,7},{7,6},{8,9},{9,8},{10,11... | collective-permute-start | bytes 3981320 | tf_op jit(solution)/shard_map/ppermute | solution.py:162
  41.1 32.1 %collective-permute-start.8 = (bf16[64,10368]{1,0:T(8,128)(2,1)S(1)}, bf16[64,10368]{1,0:T(8,128)(2,1)S(1)}, u32[]{:S(2)}, u32[]{:S(2)}) collective-permute-start(bf16[64,10368]{1,0:T(8,128)(2,1)S(1)} %collective-permute-done.refs_0_.refs_4_), channel_id=1, source_target_pairs={{0,1},{1,0},{2,3},{3,2},{4,5},{5,4},{6,7},{7,6},{8,9},{9,8},{10,11... | collective-permute-start | bytes 3981320 | tf_op jit(solution)/shard_map/ppermute | solution.py:162
  41.2 1.1 copy-start.9
  42.6 1.1 copy-start.11
  43.7 3.5 %copy-start = (bf16[5120,864]{0,1:T(8,128)(2,1)S(1)}, bf16[5120,864]{0,1:T(8,128)(2,1)}, u32[]{:S(2)}) copy-start(bf16[5120,864]{0,1:T(8,128)(2,1)} %param.13) | copy-start | bytes 26542084
  47.2 3.5 %copy-start.2 = (bf16[5120,864]{0,1:T(8,128)(2,1)S(1)}, bf16[5120,864]{0,1:T(8,128)(2,1)}, u32[]{:S(2)}) copy-start(bf16[5120,864]{0,1:T(8,128)(2,1)} %param.14) | copy-start | bytes 26542084
  50.8 3.5 %copy-start.5 = (bf16[864,5120]{1,0:T(8,128)(2,1)S(1)}, bf16[864,5120]{1,0:T(8,128)(2,1)}, u32[]{:S(2)}) copy-start(bf16[864,5120]{1,0:T(8,128)(2,1)} %refs_10_.7) | copy-start | bytes 26542084
  54.3 1.3 copy-start.8
  55.6 1.3 copy-start.10
  56.9 1.3 copy-start.12
  58.2 15.1 %copy-start.1 = (bf16[5120,864]{0,1:T(8,128)(2,1)S(1)}, bf16[5120,864]{0,1:T(8,128)(2,1)}, u32[]{:S(2)}) copy-start(bf16[5120,864]{0,1:T(8,128)(2,1)} %param.13) | copy-start | bytes 26542084
  70.2 3.1 %collective-permute-start.9 = (bf16[64,10368]{1,0:T(8,128)(2,1)S(1)}, bf16[64,10368]{1,0:T(8,128)(2,1)S(1)}, u32[]{:S(2)}, u32[]{:S(2)}) collective-permute-start(bf16[64,10368]{1,0:T(8,128)(2,1)S(1)} %collective-permute-done.3.refs_2_.refs_6_), channel_id=1, source_target_pairs={{0,1},{1,0},{2,3},{3,2},{4,5},{5,4},{6,7},{7,6},{8,9},{9,8},{10,11... | collective-permute-start | bytes 3981320 | tf_op jit(solution)/shard_map/ppermute | solution.py:162
  70.6 32.4 %collective-permute-start.6 = (bf16[64,10368]{1,0:T(8,128)(2,1)S(1)}, bf16[64,10368]{1,0:T(8,128)(2,1)S(1)}, u32[]{:S(2)}, u32[]{:S(2)}) collective-permute-start(bf16[64,10368]{1,0:T(8,128)(2,1)S(1)} %collective-permute-done.2.refs_0_.refs_4_), channel_id=1, source_target_pairs={{0,4},{1,13},{2,6},{3,15},{4,8},{5,1},{6,10},{7,3},{8,12},{9,5},{1... | collective-permute-start | bytes 3981320 | tf_op jit(solution)/shard_map/ppermute | solution.py:162
  71.2 31.9 %collective-permute-start.7 = (bf16[64,10368]{1,0:T(8,128)(2,1)S(1)}, bf16[64,10368]{1,0:T(8,128)(2,1)S(1)}, u32[]{:S(2)}, u32[]{:S(2)}) collective-permute-start(bf16[64,10368]{1,0:T(8,128)(2,1)S(1)} %collective-permute-done.2.refs_0_.refs_4_), channel_id=1, source_target_pairs={{0,2},{1,3},{2,0},{3,1},{4,6},{5,7},{6,4},{7,5},{8,10},{9,11},{10,... | collective-permute-start | bytes 3981320 | tf_op jit(solution)/shard_map/ppermute | solution.py:162
  71.7 33.0 %collective-permute-start.13 = (bf16[64,10368]{1,0:T(8,128)(2,1)S(1)}, bf16[64,10368]{1,0:T(8,128)(2,1)S(1)}, u32[]{:S(2)}, u32[]{:S(2)}) collective-permute-start(bf16[64,10368]{1,0:T(8,128)(2,1)S(1)} %collective-permute-done.2.refs_0_.refs_4_), channel_id=1, source_target_pairs={{0,1},{1,0},{2,3},{3,2},{4,5},{5,4},{6,7},{7,6},{8,9},{9,8},{10,11... | collective-permute-start | bytes 3981320 | tf_op jit(solution)/shard_map/ppermute | solution.py:162
  73.3 3.5 %copy-start.3 = (bf16[5120,864]{0,1:T(8,128)(2,1)S(1)}, bf16[5120,864]{0,1:T(8,128)(2,1)}, u32[]{:S(2)}) copy-start(bf16[5120,864]{0,1:T(8,128)(2,1)} %param.14) | copy-start | bytes 26542084
  76.8 3.5 %copy-start.6 = (bf16[864,5120]{1,0:T(8,128)(2,1)S(1)}, bf16[864,5120]{1,0:T(8,128)(2,1)}, u32[]{:S(2)}) copy-start(bf16[864,5120]{1,0:T(8,128)(2,1)} %refs_10_.7) | copy-start | bytes 26542084
  80.3 25.7 %copy-start.4 = (bf16[5120,864]{0,1:T(8,128)(2,1)S(1)}, bf16[5120,864]{0,1:T(8,128)(2,1)}, u32[]{:S(2)}) copy-start(bf16[5120,864]{0,1:T(8,128)(2,1)} %param.14) | copy-start | bytes 26542084
  103.0 3.1 %collective-permute-start.14 = (bf16[64,10368]{1,0:T(8,128)(2,1)S(1)}, bf16[64,10368]{1,0:T(8,128)(2,1)S(1)}, u32[]{:S(2)}, u32[]{:S(2)}) collective-permute-start(bf16[64,10368]{1,0:T(8,128)(2,1)S(1)} %collective-permute-done.7.refs_2_.refs_6_), channel_id=1, source_target_pairs={{0,1},{1,0},{2,3},{3,2},{4,5},{5,4},{6,7},{7,6},{8,9},{9,8},{10,11... | collective-permute-start | bytes 3981320 | tf_op jit(solution)/shard_map/ppermute | solution.py:162
  103.2 18.9 %collective-permute-start.10 = (bf16[64,10368]{1,0:T(8,128)(2,1)S(1)}, bf16[64,10368]{1,0:T(8,128)(2,1)S(1)}, u32[]{:S(2)}, u32[]{:S(2)}) collective-permute-start(bf16[64,10368]{1,0:T(8,128)(2,1)S(1)} %collective-permute-done.6.refs_0_.refs_4_), channel_id=1, source_target_pairs={{0,1},{1,0},{2,3},{3,2},{4,5},{5,4},{6,7},{7,6},{8,9},{9,8},{10,11... | collective-permute-start | bytes 3981320 | tf_op jit(solution)/shard_map/ppermute | solution.py:162
  103.7 17.9 %collective-permute-start.12 = (bf16[64,5248]{1,0:T(8,128)(2,1)S(1)}, bf16[64,5248]{1,0:T(8,128)(2,1)S(1)}, u32[]{:S(2)}, u32[]{:S(2)}) collective-permute-start(bf16[64,5248]{1,0:T(8,128)(2,1)S(1)} %slice.7), channel_id=1, source_target_pairs={{0,4},{1,13},{2,6},{3,15},{4,8},{5,1},{6,10},{7,3},{8,12},{9,5},{1... | collective-permute-start | bytes 2015240 | tf_op jit(solution)/shard_map/ppermute | solution.py:162
  104.2 17.4 %collective-permute-start.11 = (bf16[64,5120]{1,0:T(8,128)(2,1)S(1)}, bf16[64,5120]{1,0:T(8,128)(2,1)S(1)}, u32[]{:S(2)}, u32[]{:S(2)}) collective-permute-start(bf16[64,5120]{1,0:T(8,128)(2,1)S(1)} %slice.6), channel_id=1, source_target_pairs={{0,2},{1,3},{2,0},{3,1},{4,6},{5,7},{6,4},{7,5},{8,10},{9,11},{10,... | collective-permute-start | bytes 1966088 | tf_op jit(solution)/shard_map/ppermute | solution.py:162
  121.6 3.1 %collective-permute-start.16 = (bf16[64,5248]{1,0:T(8,128)(2,1)S(1)}, bf16[64,5248]{1,0:T(8,128)(2,1)S(1)}, u32[]{:S(2)}, u32[]{:S(2)}) collective-permute-start(bf16[64,5248]{1,0:T(8,128)(2,1)S(1)} %collective-permute-done.12.refs_6_), channel_id=1, source_target_pairs={{0,1},{1,0},{2,3},{3,2},{4,5},{5,4},{6,7},{7,6},{8,9},{9,8},{10,11... | collective-permute-start | bytes 2015240 | tf_op jit(solution)/shard_map/ppermute | solution.py:162
  121.7 2.9 %collective-permute-start.15 = (bf16[64,5120]{1,0:T(8,128)(2,1)S(1)}, bf16[64,5120]{1,0:T(8,128)(2,1)S(1)}, u32[]{:S(2)}, u32[]{:S(2)}) collective-permute-start(bf16[64,5120]{1,0:T(8,128)(2,1)S(1)} %collective-permute-done.11.refs_2_), channel_id=1, source_target_pairs={{0,1},{1,0},{2,3},{3,2},{4,5},{5,4},{6,7},{7,6},{8,9},{9,8},{10,11... | collective-permute-start | bytes 1966088 | tf_op jit(solution)/shard_map/ppermute | solution.py:162

commit v5 on v4

--- a/solution.py
+++ b/solution.py
@@ -33,20 +33,17 @@
     def index(self, outer, inner, core):
         return ((outer % self.outer) * self.inner + inner % self.inner) * CORES + core
 
-    def pairs(self, step):
+    def pairs(self, step, cores=range(CORES)):
         places = [
-            (o, i, c)
-            for o in range(self.outer)
-            for i in range(self.inner)
-            for c in range(CORES)
+            (o, i, c) for o in range(self.outer) for i in range(self.inner) for c in cores
         ]
         return [(self.index(o, i, c), self.index(*step(o, i, c))) for o, i, c in places]
 
-    def outer_ring(self):
-        return self.pairs(lambda o, i, c: (o + 1 - 2 * c, i, c))
-
-    def inner_ring(self):
-        return self.pairs(lambda o, i, c: (o, i + 1 - 2 * c, c))
+    def outer_ring(self, *cores):
+        return self.pairs(lambda o, i, c: (o + 1 - 2 * c, i, c), *cores)
+
+    def inner_ring(self, *cores):
+        return self.pairs(lambda o, i, c: (o, i + 1 - 2 * c, c), *cores)
 
     def core_swap(self):
         return self.pairs(lambda o, i, c: (o, i, 1 - c))
@@ -179,9 +176,19 @@
     if layout.inner == 2:
         last = layout.outer - 1
         here, across, swapped = own, None, swap(own)
+        first = [move(own, ring([0])) for ring in (layout.outer_ring, layout.inner_ring)]
+        later, swapped, feature_table, unit_tables = lax.optimization_barrier(
+            (own, swapped, feature_table, unit_tables)
+        )
+        second = [move(later, ring([1])) for ring in (layout.outer_ring, layout.inner_ring)]
+        is_first = lax.axis_index("fsdp") % CORES == 0
         for step in range(last):
-            coming = [move(here, layout.outer_ring()), move(here, layout.inner_ring())]
-            if step:
+            if step == 0:
+                four = lax.optimization_barrier((*first, *second))
+                first, second = four[:2], four[2:]
+                coming = [jnp.where(is_first, *pair) for pair in zip(first, second)]
+            else:
+                coming = [move(here, layout.outer_ring()), move(here, layout.inner_ring())]
                 total = add([both(piece) for piece in done], total)
             ahead, across, total = lax.optimization_barrier((*coming, total))
             done = [here, swapped, across, swap(across)]

time: 151 us -> 160 us (1.060)
  starting transfers between devices: 14.3 us -> 30.3 us
  waiting for transfers between devices: 47.3 us -> 32.1 us
  other arithmetic: 3.3 us -> 7.68 us
  Pallas kernels: 47.6 us -> 51.3 us
    ppermute x17 -> x19, starting transfers between devices: 14.3 us -> 30.3 us  [move(): return lax.ppermute(value, 'fsdp', pairs)]
    ppermute x17 -> x19, waiting for transfers between devices: 47.3 us -> 32.1 us  [move(): return lax.ppermute(value, 'fsdp', pairs)]
    pallas_call x4, Pallas kernels: 47.6 us -> 51.3 us  [chunk(): pl.pallas_call(kernel, in_specs=[pl.BlockSpec(memory_space=pltpu.VMEM)] *...]
    select_n x0 -> x1, other arithmetic: none -> 2.18 us  [on_device(): coming = [jnp.where(is_first, *pair) for pair in zip(first, second)]]
    unnamed x34 -> x40, local copies, waits for them, and re-layouts: 23.7 us -> 23.5 us
  transfers between devices with their start and end apart: 17 -> 19, of which waited for: 8 -> 6; matrix products, arithmetic and copies ran while one was open for 1% -> 2% of each run, Pallas kernels for 24% -> 25%
where the time goes in v5:
time: 160 us
  Pallas kernels  51.3 us (32%)
  waiting for transfers between devices  32.1 us (20%)
  starting transfers between devices  30.3 us (19%)
  local copies, waits for them, and re-layouts  24.3 us (15%)
  blocking collectives  14.1 us (9%)
  other arithmetic  7.68 us (5%)
    pallas_call x4, Pallas kernels, chunk(): pl.pallas_call(kernel, in_specs=[pl.BlockSpec(memory_space=pltpu.VMEM)] *...  51.3 us
    ppermute x19, waiting for transfers between devices, move(): return lax.ppermute(value, 'fsdp', pairs)  32.1 us
    ppermute x19, starting transfers between devices, move(): return lax.ppermute(value, 'fsdp', pairs)  30.3 us
    unnamed x40, local copies, waits for them, and re-layouts  23.5 us
    all_to_all x1, blocking collectives, on_device(): parts = lax.all_to_all(parts, 'fsdp', 0, 0)  14.1 us
  transfers between devices with their start and end apart: 19, of which 6 were waited for; matrix products, arithmetic and copies ran while one was open for 2% of the time, Pallas kernels for 25%

profile of v5, /device:TPU:0, one launch (start us, length us, event | category | flops | bytes accessed | tf_op | source)
XLA Modules:
  0.0 159.9 jit_solution(6913145636073940280)
XLA Ops:
  0.0 0.7 convert_element_type.16
  0.7 0.1 broadcast_in_dim.48
  0.7 2.5 %pad_maximum_fusion.refs_0_.refs_4_ = bf16[64,10368]{1,0:T(8,128)(2,1)} fusion(bf16[64,128]{1,0:T(8,128)(2,1)S(1)} %broadcast_in_dim.48, bf16[64,5120]{1,0:T(8,128)(2,1)} %param.11, bf16[64,5120]{1,0:T(8,128)(2,1)} %param.10), kind=kLoop, calls=%fused_computation.4 | loop fusion | flops 3981312 | bytes 2654208 | tf_op jit(solution)/shard_map/concatenate | solution.py:167
  3.2 0.5 collective-permute-start.2
  3.7 4.6 %collective-permute-start = (bf16[64,10368]{1,0:T(8,128)(2,1)}, bf16[64,10368]{1,0:T(8,128)(2,1)}, u32[]{:S(2)}, u32[]{:S(2)}) collective-permute-start(bf16[64,10368]{1,0:T(8,128)(2,1)} %pad_maximum_fusion.refs_0_.refs_4_), channel_id=1, source_target_pairs={{0,4},{2,6},{4,8},{6,10},{8,12},{10,14},{12,0},{14,2},{16,20},{18,... | collective-permute-start | bytes 3981320 | tf_op jit(solution)/shard_map/ppermute | solution.py:159
  8.3 3.4 %collective-permute-start.1 = (bf16[64,10368]{1,0:T(8,128)(2,1)}, bf16[64,10368]{1,0:T(8,128)(2,1)}, u32[]{:S(2)}, u32[]{:S(2)}) collective-permute-start(bf16[64,10368]{1,0:T(8,128)(2,1)} %pad_maximum_fusion.refs_0_.refs_4_), channel_id=1, source_target_pairs={{0,2},{2,0},{4,6},{6,4},{8,10},{10,8},{12,14},{14,12},{16,18},{18,... | collective-permute-start | bytes 3981320 | tf_op jit(solution)/shard_map/ppermute | solution.py:159
  11.7 1.5 fusion.1.refs_12_
  13.3 0.7 fusion.refs_11_
  14.0 0.0 collective-permute-done.2.refs_1_.refs_5_
  14.1 0.0 copy-start.7
  14.1 1.1 copy-done.7
  15.1 1.8 %collective-permute-start.3 = (bf16[64,10368]{1,0:T(8,128)(2,1)}, bf16[64,10368]{1,0:T(8,128)(2,1)}, u32[]{:S(2)}, u32[]{:S(2)}) collective-permute-start(bf16[64,10368]{1,0:T(8,128)(2,1)} %pad_maximum_fusion.refs_0_.refs_4_), channel_id=1, source_target_pairs={{1,13},{3,15},{5,1},{7,3},{9,5},{11,7},{13,9},{15,11},{17,29},{19,... | collective-permute-start | bytes 3981320 | tf_op jit(solution)/shard_map/ppermute | solution.py:159
  16.9 1.8 %collective-permute-start.4 = (bf16[64,10368]{1,0:T(8,128)(2,1)}, bf16[64,10368]{1,0:T(8,128)(2,1)}, u32[]{:S(2)}, u32[]{:S(2)}) collective-permute-start(bf16[64,10368]{1,0:T(8,128)(2,1)} %pad_maximum_fusion.refs_0_.refs_4_), channel_id=1, source_target_pairs={{1,3},{3,1},{5,7},{7,5},{9,11},{11,9},{13,15},{15,13},{17,19},{19,... | collective-permute-start | bytes 3981320 | tf_op jit(solution)/shard_map/ppermute | solution.py:159
  18.7 15.0 %collective-permute-done = bf16[64,10368]{1,0:T(8,128)(2,1)} collective-permute-done((bf16[64,10368]{1,0:T(8,128)(2,1)}, bf16[64,10368]{1,0:T(8,128)(2,1)}, u32[]{:S(2)}, u32[]{:S(2)}) %collective-permute-start) | collective-permute-done | bytes 1327136 | tf_op jit(solution)/shard_map/ppermute | solution.py:159
  33.8 0.6 collective-permute-done.1
  34.4 0.0 collective-permute-done.3
  34.4 0.0 collective-permute-done.4
  34.4 0.0 slice-start
  34.4 2.2 %broadcast_select_fusion = (bf16[64,10368]{1,0:T(8,128)(2,1)S(1)}, bf16[64,10368]{1,0:T(8,128)(2,1)S(1)}) fusion(bf16[64,10368]{1,0:T(8,128)(2,1)} %collective-permute-done.1, bf16[64,10368]{1,0:T(8,128)(2,1)} %collective-permute-done.4, pred[]{:T(512)S(6)} %eq.16, bf16[64,10368]{1,0:T(8,128)(2,1)} %collective-permute-done, ...), kind=kLoop, calls=%fused_computation.5 | loop fusion | flops 1327104 | bytes 7962625 | tf_op jit(solution)/shard_map/jit(_where)/select_n | solution.py:189
  36.6 8.0 %collective-permute-start.7 = (bf16[64,10368]{1,0:T(8,128)(2,1)S(1)}, bf16[64,10368]{1,0:T(8,128)(2,1)S(1)}, u32[]{:S(2)}, u32[]{:S(2)}) collective-permute-start(bf16[64,10368]{1,0:T(8,128)(2,1)S(1)} %get-tuple-element.32.refs_2_.refs_6_), channel_id=1, source_target_pairs={{0,1},{1,0},{2,3},{3,2},{4,5},{5,4},{6,7},{7,6},{8,9},{9,8},{10,11... | collective-permute-start | bytes 3981320 | tf_op jit(solution)/shard_map/ppermute | solution.py:159
  44.6 1.6 collective-permute-start.5
  46.2 1.5 collective-permute-start.6
  47.7 0.2 collective-permute-start.10
  47.8 0.0 collective-permute-done.7.refs_3_.refs_7_
  47.9 0.0 copy-start
  47.9 3.5 %copy-done = bf16[5120,864]{0,1:T(8,128)(2,1)S(1)} copy-done((bf16[5120,864]{0,1:T(8,128)(2,1)S(1)}, bf16[5120,864]{0,1:T(8,128)(2,1)}, u32[]{:S(2)}) %copy-start) | copy-done | bytes 8847384
  51.4 3.5 %copy-done.1 = bf16[5120,864]{0,1:T(8,128)(2,1)S(1)} copy-done((bf16[5120,864]{0,1:T(8,128)(2,1)S(1)}, bf16[5120,864]{0,1:T(8,128)(2,1)}, u32[]{:S(2)}) %copy-start.1) | copy-done | bytes 8847384
  54.9 3.5 %copy-done.4 = bf16[864,5120]{1,0:T(8,128)(2,1)S(1)} copy-done((bf16[864,5120]{1,0:T(8,128)(2,1)S(1)}, bf16[864,5120]{1,0:T(8,128)(2,1)}, u32[]{:S(2)}) %copy-start.4) | copy-done | bytes 8847384
  58.5 13.8 %chunk.4.refs_13_ = f32[256,512]{1,0:T(8,128)S(1)} custom-call(bf16[64,10368]{1,0:T(8,128)(2,1)} %pad_maximum_fusion.refs_0_.refs_4_, bf16[64,10368]{1,0:T(8,128)(2,1)S(1)} %copy-done.8, bf16[64,10368]{1,0:T(8,128)(2,1)S(1)} %get-tuple-element.32.refs_2_.refs_6_, bf16[64,10368]{1,0:T(8,128)(2,1)S(1)} %collective-permute-done.7.refs_3_.refs_7_, ...), custom_call_target="tpu_custom_call" | custom-call | flops 8136949760 | bytes 34406400 | tf_op jit(solution)/shard_map/chunk/pallas_call | solution.py:129
  72.2 5.6 %collective-permute-done.5.refs_0_.refs_4_ = bf16[64,10368]{1,0:T(8,128)(2,1)} collective-permute-done((bf16[64,10368]{1,0:T(8,128)(2,1)S(1)}, bf16[64,10368]{1,0:T(8,128)(2,1)}, u32[]{:S(2)}, u32[]{:S(2)}) %collective-permute-start.5) | collective-permute-done | bytes 1327136 | tf_op jit(solution)/shard_map/ppermute | solution.py:159
  77.8 0.0 collective-permute-done.6.refs_2_.refs_6_
  77.8 0.0 collective-permute-start.11
  77.8 1.1 copy-done.9
  78.9 0.0 collective-permute-start.8
  78.9 1.7 %collective-permute-start.9 = (bf16[64,10368]{1,0:T(8,128)(2,1)}, bf16[64,10368]{1,0:T(8,128)(2,1)S(1)}, u32[]{:S(2)}, u32[]{:S(2)}) collective-permute-start(bf16[64,10368]{1,0:T(8,128)(2,1)} %collective-permute-done.5.refs_0_.refs_4_), channel_id=1, source_target_pairs={{0,2},{1,3},{2,0},{3,1},{4,6},{5,7},{6,4},{7,5},{8,10},{9,11},{10,... | collective-permute-start | bytes 3981320 | tf_op jit(solution)/shard_map/ppermute | solution.py:159
  80.6 1.4 collective-permute-start.15
  82.0 0.0 collective-permute-done.10.refs_1_.refs_5_
  82.0 1.1 copy-done.11
  83.1 0.0 collective-permute-done.11.refs_3_.refs_7_
  83.1 0.0 copy-start.2
  83.1 3.5 %copy-done.2 = bf16[5120,864]{0,1:T(8,128)(2,1)S(1)} copy-done((bf16[5120,864]{0,1:T(8,128)(2,1)S(1)}, bf16[5120,864]{0,1:T(8,128)(2,1)}, u32[]{:S(2)}) %copy-start.2) | copy-done | bytes 8847384
  86.6 3.5 %copy-done.5 = bf16[864,5120]{1,0:T(8,128)(2,1)S(1)} copy-done((bf16[864,5120]{1,0:T(8,128)(2,1)S(1)}, bf16[864,5120]{1,0:T(8,128)(2,1)}, u32[]{:S(2)}) %copy-start.5) | copy-done | bytes 8847384
  90.1 1.3 copy-done.10
  91.5 1.3 copy-done.12
  92.8 11.9 %chunk.5.refs_13_ = f32[256,512]{1,0:T(8,128)S(1)} custom-call(bf16[64,10368]{1,0:T(8,128)(2,1)S(1)} %get-tuple-element.30.refs_0_.refs_4_, bf16[64,10368]{1,0:T(8,128)(2,1)S(1)} %copy-done.12, bf16[64,10368]{1,0:T(8,128)(2,1)S(1)} %copy-done.10, bf16[64,10368]{1,0:T(8,128)(2,1)S(1)} %collective-permute-done.11.refs_3_.refs_7_, ...), custom_call_target="tpu_custom_call" | custom-call | flops 8136949760 | bytes 34406400 | tf_op jit(solution)/shard_map/chunk/pallas_call | solution.py:129
  104.7 6.4 %collective-permute-done.8.refs_0_.refs_4_ = bf16[64,10368]{1,0:T(8,128)(2,1)S(1)} collective-permute-done((bf16[64,10368]{1,0:T(8,128)(2,1)}, bf16[64,10368]{1,0:T(8,128)(2,1)S(1)}, u32[]{:S(2)}, u32[]{:S(2)}) %collective-permute-start.8) | collective-permute-done | bytes 1327136 | tf_op jit(solution)/shard_map/ppermute | solution.py:159
  111.1 0.0 collective-permute-done.9.refs_2_.refs_6_
  111.1 0.1 collective-permute-start.16
  111.3 0.5 collective-permute-start.12
  111.8 1.3 collective-permute-start.14
  113.1 1.5 collective-permute-start.13
  114.6 0.0 collective-permute-done.15.refs_1_.refs_5_
  114.6 0.0 collective-permute-done.16.refs_3_.refs_7_
  114.6 13.7 %chunk.6.refs_13_ = f32[256,512]{1,0:T(8,128)S(1)} custom-call(bf16[64,10368]{1,0:T(8,128)(2,1)} %collective-permute-done.5.refs_0_.refs_4_, bf16[64,10368]{1,0:T(8,128)(2,1)S(1)} %collective-permute-done.15.refs_1_.refs_5_, bf16[64,10368]{1,0:T(8,128)(2,1)S(1)} %collective-permute-done.9.refs_2_.refs_6_, ...), custom_call_target="tpu_custom_call" | custom-call | flops 8136949760 | bytes 34406400 | tf_op jit(solution)/shard_map/chunk/pallas_call | solution.py:129
  128.3 1.8 %collective-permute-done.13.refs_2_ = bf16[64,5120]{1,0:T(8,128)(2,1)S(1)} collective-permute-done((bf16[64,5120]{1,0:T(8,128)(2,1)S(1)}, bf16[64,5120]{1,0:T(8,128)(2,1)S(1)}, u32[]{:S(2)}, u32[]{:S(2)}) %collective-permute-start.13) | collective-permute-done | bytes 655392 | tf_op jit(solution)/shard_map/ppermute | solution.py:159
  130.2 0.0 collective-permute-done.14.refs_6_
  130.2 0.0 collective-permute-start.18
  130.2 0.5 collective-permute-start.17
  130.7 0.0 collective-permute-done.12.refs_1_.refs_5_
  130.7 2.5 %collective-permute-done.17.refs_3_ = bf16[64,5120]{1,0:T(8,128)(2,1)S(1)} collective-permute-done((bf16[64,5120]{1,0:T(8,128)(2,1)S(1)}, bf16[64,5120]{1,0:T(8,128)(2,1)S(1)}, u32[]{:S(2)}, u32[]{:S(2)}) %collective-permute-start.17) | collective-permute-done | bytes 655392 | tf_op jit(solution)/shard_map/ppermute | solution.py:159
  133.2 0.0 collective-permute-done.18.refs_7_
  133.2 11.9 %chunk.7 = f32[256,512]{1,0:T(8,128)S(1)} custom-call(bf16[64,10368]{1,0:T(8,128)(2,1)S(1)} %collective-permute-done.8.refs_0_.refs_4_, bf16[64,10368]{1,0:T(8,128)(2,1)S(1)} %collective-permute-done.12.refs_1_.refs_5_, bf16[64,5120]{1,0:T(8,128)(2,1)S(1)} %collective-permute-done.13.refs_2_, bf16[64,5120]{1,0:T(8,128)(2,1)S(1)} %collective-permute-done.17.refs_3_, ...), custom_call_target="tpu_custom_call" | custom-call | flops 8136949760 | bytes 34406400 | tf_op jit(solution)/shard_map/chunk/pallas_call | solution.py:129
  145.2 14.1 %all_to_all.5 = bf16[16,16,512]{2,1,0:T(8,128)(2,1)S(1)} all-to-all(bf16[16,16,512]{2,1,0:T(8,128)(2,1)S(1)} %bitcast.14), channel_id=1, replica_groups=mesh['groups'=2,'fsdp'=16] {'fsdp'}, dimensions={0} | all-to-all | bytes 524288 | tf_op jit(solution)/shard_map/all_to_all | solution.py:209
  159.3 0.6 copy.11
  (36 shorter events, 0.3 us)
Async XLA Ops:
  0.7 11.0 %copy-start.16 = (s32[3,864]{1,0:T(4,128)S(1)}, s32[3,864]{1,0:T(4,128)}, u32[]{:S(2)}) copy-start(s32[3,864]{1,0:T(4,128)} %param.17) | copy-start | bytes 31108
  0.7 11.0 %copy-start.15 = (s32[3,864]{1,0:T(4,128)S(1)}, s32[3,864]{1,0:T(4,128)}, u32[]{:S(2)}) copy-start(s32[3,864]{1,0:T(4,128)} %param.16) | copy-start | bytes 31108
  3.2 10.1 %copy-start.14 = (s32[5120]{0:T(1024)S(1)}, s32[5120]{0:T(1024)}, u32[]{:S(2)}) copy-start(s32[5120]{0:T(1024)} %param.19) | copy-start | bytes 61444
  3.2 10.1 %copy-start.13 = (s32[5120]{0:T(1024)S(1)}, s32[5120]{0:T(1024)}, u32[]{:S(2)}) copy-start(s32[5120]{0:T(1024)} %param.18) | copy-start | bytes 61444
  3.2 10.8 %collective-permute-start.2 = (bf16[64,10368]{1,0:T(8,128)(2,1)}, bf16[64,10368]{1,0:T(8,128)(2,1)S(1)}, u32[]{:S(2)}, u32[]{:S(2)}) collective-permute-start(bf16[64,10368]{1,0:T(8,128)(2,1)} %pad_maximum_fusion.refs_0_.refs_4_), channel_id=1, source_target_pairs={{0,1},{1,0},{2,3},{3,2},{4,5},{5,4},{6,7},{7,6},{8,9},{9,8},{10,11... | collective-permute-start | bytes 3981320 | tf_op jit(solution)/shard_map/ppermute | solution.py:159
  3.7 30.1 %collective-permute-start = (bf16[64,10368]{1,0:T(8,128)(2,1)}, bf16[64,10368]{1,0:T(8,128)(2,1)}, u32[]{:S(2)}, u32[]{:S(2)}) collective-permute-start(bf16[64,10368]{1,0:T(8,128)(2,1)} %pad_maximum_fusion.refs_0_.refs_4_), channel_id=1, source_target_pairs={{0,4},{2,6},{4,8},{6,10},{8,12},{10,14},{12,0},{14,2},{16,20},{18,... | collective-permute-start | bytes 3981320 | tf_op jit(solution)/shard_map/ppermute | solution.py:159
  8.3 26.1 %collective-permute-start.1 = (bf16[64,10368]{1,0:T(8,128)(2,1)}, bf16[64,10368]{1,0:T(8,128)(2,1)}, u32[]{:S(2)}, u32[]{:S(2)}) collective-permute-start(bf16[64,10368]{1,0:T(8,128)(2,1)} %pad_maximum_fusion.refs_0_.refs_4_), channel_id=1, source_target_pairs={{0,2},{2,0},{4,6},{6,4},{8,10},{10,8},{12,14},{14,12},{16,18},{18,... | collective-permute-start | bytes 3981320 | tf_op jit(solution)/shard_map/ppermute | solution.py:159
  14.1 1.1 copy-start.7
  15.1 19.2 %collective-permute-start.3 = (bf16[64,10368]{1,0:T(8,128)(2,1)}, bf16[64,10368]{1,0:T(8,128)(2,1)}, u32[]{:S(2)}, u32[]{:S(2)}) collective-permute-start(bf16[64,10368]{1,0:T(8,128)(2,1)} %pad_maximum_fusion.refs_0_.refs_4_), channel_id=1, source_target_pairs={{1,13},{3,15},{5,1},{7,3},{9,5},{11,7},{13,9},{15,11},{17,29},{19,... | collective-permute-start | bytes 3981320 | tf_op jit(solution)/shard_map/ppermute | solution.py:159
  16.9 17.4 %collective-permute-start.4 = (bf16[64,10368]{1,0:T(8,128)(2,1)}, bf16[64,10368]{1,0:T(8,128)(2,1)}, u32[]{:S(2)}, u32[]{:S(2)}) collective-permute-start(bf16[64,10368]{1,0:T(8,128)(2,1)} %pad_maximum_fusion.refs_0_.refs_4_), channel_id=1, source_target_pairs={{1,3},{3,1},{5,7},{7,5},{9,11},{11,9},{13,15},{15,13},{17,19},{19,... | collective-permute-start | bytes 3981320 | tf_op jit(solution)/shard_map/ppermute | solution.py:159
  34.4 13.5 %copy-start.6 = (bf16[3,256,864]{2,1,0:T(8,128)(2,1)S(1)}, bf16[3,256,864]{2,1,0:T(8,128)(2,1)}, u32[]{:S(2)}) copy-start(bf16[3,256,864]{2,1,0:T(8,128)(2,1)} %fusion.1.refs_12_) | copy-start | bytes 3981316
  34.4 13.5 %copy-start.8 = (bf16[64,10368]{1,0:T(8,128)(2,1)S(1)}, bf16[64,10368]{1,0:T(8,128)(2,1)}, u32[]{:S(2)}) copy-start(bf16[64,10368]{1,0:T(8,128)(2,1)} %copy-done.7) | copy-start | bytes 3981316
  34.4 48.7 %slice-start = ((s8[8847360]{0:T(1024)(128)(4,1)}), s8[4194304]{0:T(1024)(128)(4,1)S(1)}, s32[]{:S(2)}) async-start(s8[8847360]{0:T(1024)(128)(4,1)} %bitcast.5), calls=%async_computation.1 | async-start | bytes 8388608
  36.6 11.3 %collective-permute-start.7 = (bf16[64,10368]{1,0:T(8,128)(2,1)S(1)}, bf16[64,10368]{1,0:T(8,128)(2,1)S(1)}, u32[]{:S(2)}, u32[]{:S(2)}) collective-permute-start(bf16[64,10368]{1,0:T(8,128)(2,1)S(1)} %get-tuple-element.32.refs_2_.refs_6_), channel_id=1, source_target_pairs={{0,1},{1,0},{2,3},{3,2},{4,5},{5,4},{6,7},{7,6},{8,9},{9,8},{10,11... | collective-permute-start | bytes 3981320 | tf_op jit(solution)/shard_map/ppermute | solution.py:159
  44.6 33.2 %collective-permute-start.5 = (bf16[64,10368]{1,0:T(8,128)(2,1)S(1)}, bf16[64,10368]{1,0:T(8,128)(2,1)}, u32[]{:S(2)}, u32[]{:S(2)}) collective-permute-start(bf16[64,10368]{1,0:T(8,128)(2,1)S(1)} %get-tuple-element.30.refs_0_.refs_4_), channel_id=1, source_target_pairs={{0,4},{1,13},{2,6},{3,15},{4,8},{5,1},{6,10},{7,3},{8,12},{9,5},{1... | collective-permute-start | bytes 3981320 | tf_op jit(solution)/shard_map/ppermute | solution.py:159
  46.2 31.7 %collective-permute-start.6 = (bf16[64,10368]{1,0:T(8,128)(2,1)S(1)}, bf16[64,10368]{1,0:T(8,128)(2,1)S(1)}, u32[]{:S(2)}, u32[]{:S(2)}) collective-permute-start(bf16[64,10368]{1,0:T(8,128)(2,1)S(1)} %get-tuple-element.30.refs_0_.refs_4_), channel_id=1, source_target_pairs={{0,2},{1,3},{2,0},{3,1},{4,6},{5,7},{6,4},{7,5},{8,10},{9,11},{10,... | collective-permute-start | bytes 3981320 | tf_op jit(solution)/shard_map/ppermute | solution.py:159
  47.7 34.3 %collective-permute-start.10 = (bf16[64,10368]{1,0:T(8,128)(2,1)S(1)}, bf16[64,10368]{1,0:T(8,128)(2,1)S(1)}, u32[]{:S(2)}, u32[]{:S(2)}) collective-permute-start(bf16[64,10368]{1,0:T(8,128)(2,1)S(1)} %get-tuple-element.30.refs_0_.refs_4_), channel_id=1, source_target_pairs={{0,1},{1,0},{2,3},{3,2},{4,5},{5,4},{6,7},{7,6},{8,9},{9,8},{10,11... | collective-permute-start | bytes 3981320 | tf_op jit(solution)/shard_map/ppermute | solution.py:159
  47.9 3.5 %copy-start = (bf16[5120,864]{0,1:T(8,128)(2,1)S(1)}, bf16[5120,864]{0,1:T(8,128)(2,1)}, u32[]{:S(2)}) copy-start(bf16[5120,864]{0,1:T(8,128)(2,1)} %param.13) | copy-start | bytes 26542084
  51.4 3.5 %copy-start.1 = (bf16[5120,864]{0,1:T(8,128)(2,1)S(1)}, bf16[5120,864]{0,1:T(8,128)(2,1)}, u32[]{:S(2)}) copy-start(bf16[5120,864]{0,1:T(8,128)(2,1)} %param.14) | copy-start | bytes 26542084
  54.9 3.5 %copy-start.4 = (bf16[864,5120]{1,0:T(8,128)(2,1)S(1)}, bf16[864,5120]{1,0:T(8,128)(2,1)}, u32[]{:S(2)}) copy-start(bf16[864,5120]{1,0:T(8,128)(2,1)} %refs_10_.7) | copy-start | bytes 26542084
  58.5 24.6 %slice-start.1 = ((s8[8847360]{0:T(1024)(128)(4,1)}), s8[4194304]{0:T(1024)(128)(4,1)S(1)}, s32[]{:S(2)}) async-start(s8[8847360]{0:T(1024)(128)(4,1)} %bitcast.5), calls=%async_computation.2 | async-start | bytes 8388608
  58.5 24.6 %slice-start.2 = ((s8[8847360]{0:T(1024)(128)(4,1)}), s8[458752]{0:T(1024)(128)(4,1)S(1)}, s32[]{:S(2)}) async-start(s8[8847360]{0:T(1024)(128)(4,1)} %bitcast.5), calls=%async_computation.3 | async-start | bytes 917504
  77.8 5.3 %collective-permute-start.11 = (bf16[64,10368]{1,0:T(8,128)(2,1)S(1)}, bf16[64,10368]{1,0:T(8,128)(2,1)S(1)}, u32[]{:S(2)}, u32[]{:S(2)}) collective-permute-start(bf16[64,10368]{1,0:T(8,128)(2,1)S(1)} %collective-permute-done.6.refs_2_.refs_6_), channel_id=1, source_target_pairs={{0,1},{1,0},{2,3},{3,2},{4,5},{5,4},{6,7},{7,6},{8,9},{9,8},{10,11... | collective-permute-start | bytes 3981320 | tf_op jit(solution)/shard_map/ppermute | solution.py:159
  77.8 1.1 copy-start.9
  78.9 32.2 %collective-permute-start.8 = (bf16[64,10368]{1,0:T(8,128)(2,1)}, bf16[64,10368]{1,0:T(8,128)(2,1)S(1)}, u32[]{:S(2)}, u32[]{:S(2)}) collective-permute-start(bf16[64,10368]{1,0:T(8,128)(2,1)} %collective-permute-done.5.refs_0_.refs_4_), channel_id=1, source_target_pairs={{0,4},{1,13},{2,6},{3,15},{4,8},{5,1},{6,10},{7,3},{8,12},{9,5},{1... | collective-permute-start | bytes 3981320 | tf_op jit(solution)/shard_map/ppermute | solution.py:159
  78.9 32.2 %collective-permute-start.9 = (bf16[64,10368]{1,0:T(8,128)(2,1)}, bf16[64,10368]{1,0:T(8,128)(2,1)S(1)}, u32[]{:S(2)}, u32[]{:S(2)}) collective-permute-start(bf16[64,10368]{1,0:T(8,128)(2,1)} %collective-permute-done.5.refs_0_.refs_4_), channel_id=1, source_target_pairs={{0,2},{1,3},{2,0},{3,1},{4,6},{5,7},{6,4},{7,5},{8,10},{9,11},{10,... | collective-permute-start | bytes 3981320 | tf_op jit(solution)/shard_map/ppermute | solution.py:159
  80.6 34.0 %collective-permute-start.15 = (bf16[64,10368]{1,0:T(8,128)(2,1)}, bf16[64,10368]{1,0:T(8,128)(2,1)S(1)}, u32[]{:S(2)}, u32[]{:S(2)}) collective-permute-start(bf16[64,10368]{1,0:T(8,128)(2,1)} %collective-permute-done.5.refs_0_.refs_4_), channel_id=1, source_target_pairs={{0,1},{1,0},{2,3},{3,2},{4,5},{5,4},{6,7},{7,6},{8,9},{9,8},{10,11... | collective-permute-start | bytes 3981320 | tf_op jit(solution)/shard_map/ppermute | solution.py:159
  82.0 1.1 copy-start.11
  83.1 3.5 %copy-start.2 = (bf16[5120,864]{0,1:T(8,128)(2,1)S(1)}, bf16[5120,864]{0,1:T(8,128)(2,1)}, u32[]{:S(2)}) copy-start(bf16[5120,864]{0,1:T(8,128)(2,1)} %param.14) | copy-start | bytes 26542084
  86.6 3.5 %copy-start.5 = (bf16[864,5120]{1,0:T(8,128)(2,1)S(1)}, bf16[864,5120]{1,0:T(8,128)(2,1)}, u32[]{:S(2)}) copy-start(bf16[864,5120]{1,0:T(8,128)(2,1)} %refs_10_.7) | copy-start | bytes 26542084
  90.1 1.3 copy-start.10
  91.5 1.3 copy-start.12
  92.8 21.8 %copy-start.3 = (bf16[5120,864]{0,1:T(8,128)(2,1)S(1)}, bf16[5120,864]{0,1:T(8,128)(2,1)}, u32[]{:S(2)}) copy-start(bf16[5120,864]{0,1:T(8,128)(2,1)} %param.14) | copy-start | bytes 26542084
  111.1 3.5 %collective-permute-start.16 = (bf16[64,10368]{1,0:T(8,128)(2,1)S(1)}, bf16[64,10368]{1,0:T(8,128)(2,1)S(1)}, u32[]{:S(2)}, u32[]{:S(2)}) collective-permute-start(bf16[64,10368]{1,0:T(8,128)(2,1)S(1)} %collective-permute-done.9.refs_2_.refs_6_), channel_id=1, source_target_pairs={{0,1},{1,0},{2,3},{3,2},{4,5},{5,4},{6,7},{7,6},{8,9},{9,8},{10,11... | collective-permute-start | bytes 3981320 | tf_op jit(solution)/shard_map/ppermute | solution.py:159
  111.3 19.3 %collective-permute-start.12 = (bf16[64,10368]{1,0:T(8,128)(2,1)S(1)}, bf16[64,10368]{1,0:T(8,128)(2,1)S(1)}, u32[]{:S(2)}, u32[]{:S(2)}) collective-permute-start(bf16[64,10368]{1,0:T(8,128)(2,1)S(1)} %collective-permute-done.8.refs_0_.refs_4_), channel_id=1, source_target_pairs={{0,1},{1,0},{2,3},{3,2},{4,5},{5,4},{6,7},{7,6},{8,9},{9,8},{10,11... | collective-permute-start | bytes 3981320 | tf_op jit(solution)/shard_map/ppermute | solution.py:159
  111.8 18.4 %collective-permute-start.14 = (bf16[64,5248]{1,0:T(8,128)(2,1)S(1)}, bf16[64,5248]{1,0:T(8,128)(2,1)S(1)}, u32[]{:S(2)}, u32[]{:S(2)}) collective-permute-start(bf16[64,5248]{1,0:T(8,128)(2,1)S(1)} %slice.7), channel_id=1, source_target_pairs={{0,4},{1,13},{2,6},{3,15},{4,8},{5,1},{6,10},{7,3},{8,12},{9,5},{1... | collective-permute-start | bytes 2015240 | tf_op jit(solution)/shard_map/ppermute | solution.py:159
  113.1 17.1 %collective-permute-start.13 = (bf16[64,5120]{1,0:T(8,128)(2,1)S(1)}, bf16[64,5120]{1,0:T(8,128)(2,1)S(1)}, u32[]{:S(2)}, u32[]{:S(2)}) collective-permute-start(bf16[64,5120]{1,0:T(8,128)(2,1)S(1)} %slice.6), channel_id=1, source_target_pairs={{0,2},{1,3},{2,0},{3,1},{4,6},{5,7},{6,4},{7,5},{8,10},{9,11},{10,... | collective-permute-start | bytes 1966088 | tf_op jit(solution)/shard_map/ppermute | solution.py:159
  130.2 3.1 %collective-permute-start.18 = (bf16[64,5248]{1,0:T(8,128)(2,1)S(1)}, bf16[64,5248]{1,0:T(8,128)(2,1)S(1)}, u32[]{:S(2)}, u32[]{:S(2)}) collective-permute-start(bf16[64,5248]{1,0:T(8,128)(2,1)S(1)} %collective-permute-done.14.refs_6_), channel_id=1, source_target_pairs={{0,1},{1,0},{2,3},{3,2},{4,5},{5,4},{6,7},{7,6},{8,9},{9,8},{10,11... | collective-permute-start | bytes 2015240 | tf_op jit(solution)/shard_map/ppermute | solution.py:159
  130.2 3.1 %collective-permute-start.17 = (bf16[64,5120]{1,0:T(8,128)(2,1)S(1)}, bf16[64,5120]{1,0:T(8,128)(2,1)S(1)}, u32[]{:S(2)}, u32[]{:S(2)}) collective-permute-start(bf16[64,5120]{1,0:T(8,128)(2,1)S(1)} %collective-permute-done.13.refs_2_), channel_id=1, source_target_pairs={{0,1},{1,0},{2,3},{3,2},{4,5},{5,4},{6,7},{7,6},{8,9},{9,8},{10,11... | collective-permute-start | bytes 1966088 | tf_op jit(solution)/shard_map/ppermute | solution.py:159

commit v6 on v4

v6 whole, which is shorter than its diff:
```python
import jax
import jax.numpy as jnp
from jax import lax
from jax.experimental import pallas as pl
from jax.experimental.pallas import tpu as pltpu
from jax.sharding import PartitionSpec as P

D = 5120
FF = 13824
EX = 2
SEQ = 512
K1 = 256
K2 = 256
CORES = 2
OUTER = 4
DEPTH = 1024
LANES = 128
VMEM_LIMIT = 12 << 20


def sign_tables(buckets, sign_bits, buckets_count):
    matches = buckets[..., None, :] == jnp.arange(buckets_count, dtype=jnp.int32)[:, None]
    signed = (2 * sign_bits - 1).astype(jnp.bfloat16)[..., None, :]
    return jnp.where(matches, signed, jnp.zeros_like(signed))


class Layout:
    def __init__(self, count):
        self.outer = OUTER if count % (OUTER * CORES) == 0 else 1
        self.inner = count // (self.outer * CORES)
        self.count = count

    def index(self, outer, inner, core):
        return ((outer % self.outer) * self.inner + inner % self.inner) * CORES + core

    def pairs(self, step):
        places = [
            (o, i, c)
            for o in range(self.outer)
            for i in range(self.inner)
            for c in range(CORES)
        ]
        return [(self.index(o, i, c), self.index(*step(o, i, c))) for o, i, c in places]

    def outer_ring(self):
        return self.pairs(lambda o, i, c: (o + 1 - 2 * c, i, c))

    def inner_ring(self):
        return self.pairs(lambda o, i, c: (o, i + 1 - 2 * c, c))

    def core_swap(self):
        return self.pairs(lambda o, i, c: (o, i, 1 - c))


def dot(left, right):
    return jnp.dot(left, right, preferred_element_type=jnp.float32)


def dot_rows(left, right):
    return lax.dot_general(
        left, right, (((1,), (1,)), ((), ())), preferred_element_type=jnp.float32
    )


def joined(refs, lanes):
    parts = [ref[:, lanes] for ref in refs]
    return jnp.concatenate(parts, axis=0) if len(parts) > 1 else parts[0]


def add_products(refs, model, sums):
    depth = min(DEPTH, model)
    for acc, _ in sums:
        acc[...] = jnp.zeros_like(acc)

    def body(step, _):
        here = pl.ds(pl.multiple_of(step * depth, depth), depth)
        rows = joined(refs, here)
        for acc, weight in sums:
            acc[...] += dot_rows(rows, weight[:, here])
        return 0

    lax.fori_loop(0, model // depth, body, 0)


def forward_kernel(pieces, *refs):
    gate_w, up_w, feature_w, tables = refs[pieces : pieces + 4]
    to_gate, to_up, down_part, feature_in = refs[pieces + 4 : pieces + 8]
    gate_acc, up_acc, feature_acc = refs[pieces + 8 :]
    sums = ((gate_acc, gate_w), (up_acc, up_w), (feature_acc, feature_w))
    add_products(refs[:pieces], gate_w.shape[1], sums)
    gate, up = gate_acc[...], up_acc[...]
    sigmoid = jax.nn.sigmoid(gate)
    activated = gate * sigmoid
    to_gate[...] = up * sigmoid * (1.0 + gate * (1.0 - sigmoid))
    to_up[...] = activated
    hidden = (activated * up).astype(jnp.bfloat16)
    down_part[...] = dot_rows(hidden, tables[2]).astype(jnp.bfloat16)
    feature_in[...] = feature_acc[...].astype(jnp.bfloat16)


def backward_kernel(pieces, *refs):
    down_w, feature_w, tables, to_gate, to_up, down_part, feature_in, before = refs[
        pieces : pieces + 8
    ]
    total, hidden_acc, feature_acc = refs[pieces + 8 :]
    model = down_w.shape[1]
    add_products(refs[:pieces], model, ((hidden_acc, down_w), (feature_acc, feature_w)))
    bf16 = jnp.bfloat16
    hidden_grad = hidden_acc[...]
    gate_grad = (hidden_grad * to_gate[...]).astype(bf16)
    up_grad = (hidden_grad * to_up[...]).astype(bf16)
    input_part = (dot_rows(gate_grad, tables[0]) + dot_rows(up_grad, tables[1])).astype(bf16)
    example = joined(refs[:pieces], pl.ds(model, LANES)).astype(jnp.float32)
    example = jnp.concatenate([example] * (K2 // LANES), axis=1)

    def by_example(features):
        features = features.astype(jnp.float32)
        return jnp.concatenate(
            [jnp.where(example == e, features, 0.0) for e in range(EX)], axis=1
        ).astype(bf16)

    feature_out = feature_acc[...].astype(bf16)
    total[...] = before[...] + lax.dot_general(
        jnp.concatenate([down_part[...], input_part], axis=0),
        jnp.concatenate([by_example(feature_out), by_example(feature_in[...])], axis=0),
        (((0,), (0,)), ((), ())),
        preferred_element_type=jnp.float32,
    )


def on_chip(kernel, name, pieces, operands, outs, sums):
    rows = sum(piece.shape[0] for piece in pieces)
    vmem = pl.BlockSpec(memory_space=pltpu.VMEM)
    return pl.pallas_call(
        lambda *refs: kernel(len(pieces), *refs),
        in_specs=[vmem] * (len(pieces) + len(operands)),
        out_specs=[vmem] * len(outs),
        out_shape=outs,
        scratch_shapes=[pltpu.VMEM((rows, columns), jnp.float32) for columns in sums],
        compiler_params=pltpu.CompilerParams(vmem_limit_bytes=VMEM_LIMIT),
        cost_estimate=pl.CostEstimate(flops=0, bytes_accessed=0, transcendentals=0),
        name=name,
    )(*pieces, *operands)


def forward(pieces, gate_rows, up_rows, feature_table, tables):
    units, model = gate_rows.shape
    rows = sum(piece.shape[0] for piece in pieces)
    outs = [
        jax.ShapeDtypeStruct((rows, units), jnp.float32),
        jax.ShapeDtypeStruct((rows, units), jnp.float32),
        jax.ShapeDtypeStruct((rows, K1), jnp.bfloat16),
        jax.ShapeDtypeStruct((rows, K2), jnp.bfloat16),
    ]
    operands = (gate_rows, up_rows, feature_table, tables)
    return on_chip(forward_kernel, "forward", pieces, operands, outs, (units, units, K2))


def backward(pieces, down_rows, feature_table, tables, saved, before):
    units, model = down_rows.shape
    outs = [jax.ShapeDtypeStruct(before.shape, jnp.float32)]
    operands = (down_rows, feature_table, tables, *saved, before)
    return on_chip(backward_kernel, "backward", pieces, operands, outs, (units, K2))[0]


def on_device(
    layout,
    inputs,
    out_grad,
    example_ids,
    gate_weight,
    up_weight,
    down_weight,
    unit_buckets,
    unit_signs,
    feature_buckets,
    feature_signs,
):
    def move(value, pairs):
        return lax.ppermute(value, "fsdp", pairs)

    rows = inputs.shape[0]

    unit_tables = sign_tables(unit_buckets, unit_signs, K1)
    feature_table = sign_tables(feature_buckets, feature_signs, K2)

    example = jnp.broadcast_to(example_ids[:, None], (rows, LANES)).astype(jnp.bfloat16)
    tagged = jnp.concatenate([out_grad, example], axis=1)
    gate_rows, up_rows = gate_weight.T, up_weight.T
    total = jnp.zeros((K1, EX * K2), jnp.float32)

    if layout.inner == 2:
        ahead = lambda piece: move(piece, layout.outer_ring())
        aside = lambda piece: move(piece, layout.inner_ring())
        swap = lambda piece: [
            move(part, layout.core_swap()) for part in jnp.split(piece, 2, axis=0)
        ]
        after = lax.optimization_barrier
        last = layout.outer - 1
        here_in, here_out = inputs, tagged
        coming_in = ahead(here_in), aside(here_in)
        here_out, feature_table, unit_tables = after((here_out, feature_table, unit_tables))
        coming_out = ahead(here_out), aside(here_out)
        swapped_in = swap(here_in)
        for step in range(layout.outer + 1)[1:]:
            if step <= last:
                next_in, across_in, total = after((*coming_in, total))
                coming_in = (ahead(next_in) if step < last else None), aside(next_in)
            else:
                across_in, total = after((coming_in[1], total))
            swapped_across = swap(across_in)
            here_out, swapped_across = after((here_out, swapped_across))
            swapped_out = swap(here_out)
            pieces = [here_in, *swapped_in, across_in, *swapped_across]
            saved = forward(pieces, gate_rows, up_rows, feature_table, unit_tables)
            if step <= last:
                next_out, across_out, saved = after((*coming_out, saved))
            else:
                across_out, saved = after((coming_out[1], saved))
            if step < last:
                coming_out = ahead(next_out), aside(next_out)
            elif step == last:
                coming_out = None, ahead(across_out)
            pieces = [here_out, *swapped_out, across_out, *swap(across_out)]
            total = backward(pieces, down_weight, feature_table, unit_tables, saved, total)
            if step <= last:
                here_in, here_out = next_in, next_out
                here_in, total = after((here_in, total))
                swapped_in = swap(here_in)
    else:
        gather = lambda piece: lax.all_gather(piece, "fsdp", axis=0, tiled=True)
        saved = forward([gather(inputs)], gate_rows, up_rows, feature_table, unit_tables)
        total = backward([gather(tagged)], down_weight, feature_table, unit_tables, saved, total)

    parts = total.astype(jnp.bfloat16).reshape(layout.count, -1, EX * K2)
    parts = lax.all_to_all(parts, "fsdp", 0, 0)
    part = jnp.sum(parts.astype(jnp.float32), axis=0)
    factor = (3.0 * SEQ * FF * D / (K1 * K2)) ** (-0.5)
    return (factor * part).reshape(-1, EX, K2).transpose(1, 0, 2)


def solution(mesh):
    layout = Layout(mesh.shape["fsdp"])
    in_specs = (
        P(("groups", "fsdp"), None),
        P(("groups", "fsdp"), None),
        P(("groups", "fsdp")),
        P(None, "fsdp"),
        P(None, "fsdp"),
        P("fsdp", None),
        P(None, "fsdp"),
        P(None, "fsdp"),
        P(),
        P(),
    )
    out_specs = P("groups", "fsdp", None)
    return jax.shard_map(
        lambda *args: on_device(layout, *args),
        mesh=mesh,
        in_specs=in_specs,
        out_specs=out_specs,
        check_vma=False,
    )
```

time: 151 us -> 139 us (0.921)
  waiting for transfers between devices: 47.3 us -> 27 us
  starting transfers between devices: 14.3 us -> 28.8 us
  local copies, waits for them, and re-layouts: 24.6 us -> 12.2 us
  Pallas kernels: 47.6 us -> 52.9 us
    ppermute x17 -> x46, waiting for transfers between devices: 47.3 us -> 27 us  [move(): return lax.ppermute(value, 'fsdp', pairs)]
    ppermute x17 -> x46, starting transfers between devices: 14.3 us -> 28.8 us  [move(): return lax.ppermute(value, 'fsdp', pairs)]
    unnamed x34 -> x30, local copies, waits for them, and re-layouts: 23.7 us -> 10.7 us
    pallas_call x4 -> x8, Pallas kernels: 47.6 us -> 52.9 us  [on_chip(): pl.pallas_call(lambda *refs: kernel(len(pieces), *refs), in_specs=[vmem]...]
  transfers between devices with their start and end apart: 17 -> 46, of which waited for: 8 -> 22; matrix products, arithmetic and copies ran while one was open for 1% -> 4% of each run, Pallas kernels for 24% -> 34%
where the time goes in v6:
time: 139 us
  Pallas kernels  52.9 us (38%)
  starting transfers between devices  28.8 us (21%)
  waiting for transfers between devices  27 us (19%)
  blocking collectives  13.5 us (10%)
  local copies, waits for them, and re-layouts  12.2 us (9%)
  other arithmetic  4.12 us (3%)
    pallas_call x8, Pallas kernels, on_chip(): pl.pallas_call(lambda *refs: kernel(len(pieces), *refs), in_specs=[vmem]...  52.9 us
    ppermute x46, starting transfers between devices, move(): return lax.ppermute(value, 'fsdp', pairs)  28.8 us
    ppermute x46, waiting for transfers between devices, move(): return lax.ppermute(value, 'fsdp', pairs)  27 us
    all_to_all x1, blocking collectives, on_device(): parts = lax.all_to_all(parts, 'fsdp', 0, 0)  13.5 us
    unnamed x30, local copies, waits for them, and re-layouts  10.7 us
  transfers between devices with their start and end apart: 46, of which 22 were waited for; matrix products, arithmetic and copies ran while one was open for 4% of the time, Pallas kernels for 34%

profile of v6, /device:TPU:0, one launch (start us, length us, event | category | flops | bytes accessed | tf_op | source)
XLA Modules:
  0.0 138.8 jit_solution(5370972705163137703)
XLA Ops:
  0.0 3.0 %collective-permute-start.4 = (bf16[64,5120]{1,0:T(8,128)(2,1)}, bf16[64,5120]{1,0:T(8,128)(2,1)S(1)}, u32[]{:S(2)}, u32[]{:S(2)}) collective-permute-start(bf16[64,5120]{1,0:T(8,128)(2,1)} %refs_0_.1), channel_id=1, source_target_pairs={{0,4},{1,13},{2,6},{3,15},{4,8},{5,1},{6,10},{7,3},{8,12},{9,5},{1... | collective-permute-start | bytes 1966088 | tf_op jit(solution)/shard_map/ppermute | solution.py:180
  3.0 1.5 %collective-permute-start.5 = (bf16[64,5120]{1,0:T(8,128)(2,1)}, bf16[64,5120]{1,0:T(8,128)(2,1)S(1)}, u32[]{:S(2)}, u32[]{:S(2)}) collective-permute-start(bf16[64,5120]{1,0:T(8,128)(2,1)} %refs_0_.1), channel_id=1, source_target_pairs={{0,2},{1,3},{2,0},{3,1},{4,6},{5,7},{6,4},{7,5},{8,10},{9,11},{10,... | collective-permute-start | bytes 1966088 | tf_op jit(solution)/shard_map/ppermute | solution.py:180
  4.5 0.7 add_convert_fusion
  5.3 0.7 add_convert_fusion.1
  6.0 0.7 convert_element_type.16
  6.6 1.4 %fusion.refs_8_.refs_7_ = bf16[256,5120]{1,0:T(8,128)(2,1)S(1)} fusion(s32[5120]{0:T(1024)} %param.18, bf16[5120]{0:T(1024)(128)(2,1)S(1)} %add_convert_fusion), kind=kLoop, calls=%fused_computation.1 | loop fusion | flops 2621440 | bytes 2652160 | tf_op jit(solution)/shard_map/jit(_where)/select_n | solution.py:24
  8.1 0.4 fusion.1.refs_9_.refs_8_
  8.7 1.6 %collective-permute-start = (bf16[64,5248]{1,0:T(8,128)(2,1)S(1)}, bf16[64,5248]{1,0:T(8,128)(2,1)S(1)}, u32[]{:S(2)}, u32[]{:S(2)}) collective-permute-start(bf16[64,5248]{1,0:T(8,128)(2,1)S(1)} %pad_maximum_fusion.refs_0_), channel_id=1, source_target_pairs={{0,4},{1,13},{2,6},{3,15},{4,8},{5,1},{6,10},{7,3},{8,12},{9,5},{1... | collective-permute-start | bytes 2015240 | tf_op jit(solution)/shard_map/ppermute | solution.py:180
  10.3 0.5 collective-permute-start.1
  10.8 10.0 %collective-permute-done.4.refs_0_ = bf16[64,5120]{1,0:T(8,128)(2,1)S(1)} collective-permute-done((bf16[64,5120]{1,0:T(8,128)(2,1)}, bf16[64,5120]{1,0:T(8,128)(2,1)S(1)}, u32[]{:S(2)}, u32[]{:S(2)}) %collective-permute-start.4) | collective-permute-done | bytes 655392 | tf_op jit(solution)/shard_map/ppermute | solution.py:180
  20.9 0.8 collective-permute-start.6
  21.8 0.5 collective-permute-start.2
  22.3 0.6 collective-permute-done.6.refs_4_
  22.9 0.4 collective-permute-start.3
  23.4 1.3 collective-permute-start.16
  24.7 1.5 %collective-permute-start.17 = (bf16[64,5120]{1,0:T(8,128)(2,1)S(1)}, bf16[64,5120]{1,0:T(8,128)(2,1)S(1)}, u32[]{:S(2)}, u32[]{:S(2)}) collective-permute-start(bf16[64,5120]{1,0:T(8,128)(2,1)S(1)} %collective-permute-done.4.refs_0_), channel_id=1, source_target_pairs={{0,2},{1,3},{2,0},{3,1},{4,6},{5,7},{6,4},{7,5},{8,10},{9,11},{10,... | collective-permute-start | bytes 1966088 | tf_op jit(solution)/shard_map/ppermute | solution.py:180
  26.2 3.5 %copy-done = bf16[5120,864]{0,1:T(8,128)(2,1)S(1)} copy-done((bf16[5120,864]{0,1:T(8,128)(2,1)S(1)}, bf16[5120,864]{0,1:T(8,128)(2,1)}, u32[]{:S(2)}) %copy-start) | copy-done | bytes 8847384
  29.7 3.5 %copy-done.1 = bf16[5120,864]{0,1:T(8,128)(2,1)S(1)} copy-done((bf16[5120,864]{0,1:T(8,128)(2,1)S(1)}, bf16[5120,864]{0,1:T(8,128)(2,1)}, u32[]{:S(2)}) %copy-start.1) | copy-done | bytes 8847384
  33.2 7.8 %forward.4 = (f32[256,864]{1,0:T(8,128)S(1)}, f32[256,864]{1,0:T(8,128)S(1)}, bf16[256,256]{1,0:T(8,128)(2,1)S(1)}, bf16[256,256]{1,0:T(8,128)(2,1)S(1)}) custom-call(bf16[64,5120]{1,0:T(8,128)(2,1)S(1)} %copy-done.3, bf16[32,5120]{1,0:T(8,128)(2,1)S(1)} %collective-permute-done.2.refs_1_, bf16[32,5120]{1,0:T(8,128)(2,1)S(1)} %collective-permute-done.3.refs_2_, ...), custom_call_target="tpu_custom_call" | custom-call | tf_op jit(solution)/shard_map/forward/pallas_call | solution.py:134
  41.1 0.4 collective-permute-start.12
  41.7 0.4 collective-permute-start.10
  42.1 0.7 collective-permute-done.12.refs_4_
  43.3 1.6 %collective-permute-start.8 = (bf16[64,5248]{1,0:T(8,128)(2,1)S(1)}, bf16[64,5248]{1,0:T(8,128)(2,1)S(1)}, u32[]{:S(2)}, u32[]{:S(2)}) collective-permute-start(bf16[64,5248]{1,0:T(8,128)(2,1)S(1)} %collective-permute-done.refs_0_), channel_id=1, source_target_pairs={{0,4},{1,13},{2,6},{3,15},{4,8},{5,1},{6,10},{7,3},{8,12},{9,5},{1... | collective-permute-start | bytes 2015240 | tf_op jit(solution)/shard_map/ppermute | solution.py:180
  44.8 0.5 collective-permute-start.9
  45.5 3.7 %copy-done.2 = bf16[864,5120]{1,0:T(8,128)(2,1)S(1)} copy-done((bf16[864,5120]{1,0:T(8,128)(2,1)S(1)}, bf16[864,5120]{1,0:T(8,128)(2,1)}, u32[]{:S(2)}) %copy-start.2) | copy-done | bytes 8847384
  49.1 5.5 %backward.4.refs_13_ = f32[256,512]{1,0:T(8,128)S(1)} custom-call(bf16[64,5248]{1,0:T(8,128)(2,1)S(1)} %pad_maximum_fusion.refs_0_, bf16[32,5248]{1,0:T(8,128)(2,1)S(1)} %collective-permute-done.10.refs_1_, bf16[32,5248]{1,0:T(8,128)(2,1)S(1)} %collective-permute-done.11.refs_2_, bf16[64,5248]{1,0:T(8,128)(2,1)S(1)} %collective-permute-done.1.refs_3_, ...), custom_call_target="tpu_custom_call" | custom-call | tf_op jit(solution)/shard_map/backward/pallas_call | solution.py:134
  54.6 0.6 collective-permute-start.18
  55.3 0.5 collective-permute-start.14
  55.8 0.6 collective-permute-done.18.refs_4_
  56.5 0.4 collective-permute-start.15
  56.9 0.5 collective-permute-start.28
  57.5 1.4 %collective-permute-start.29 = (bf16[64,5120]{1,0:T(8,128)(2,1)S(1)}, bf16[64,5120]{1,0:T(8,128)(2,1)S(1)}, u32[]{:S(2)}, u32[]{:S(2)}) collective-permute-start(bf16[64,5120]{1,0:T(8,128)(2,1)S(1)} %collective-permute-done.16.refs_0_), channel_id=1, source_target_pairs={{0,2},{1,3},{2,0},{3,1},{4,6},{5,7},{6,4},{7,5},{8,10},{9,11},{10,... | collective-permute-start | bytes 1966088 | tf_op jit(solution)/shard_map/ppermute | solution.py:180
  58.9 1.4 %collective-permute-start.22 = (bf16[32,5248]{1,0:T(8,128)(2,1)S(1)}, bf16[32,5248]{1,0:T(8,128)(2,1)S(1)}, u32[]{:S(2)}, u32[]{:S(2)}) collective-permute-start(bf16[32,5248]{1,0:T(8,128)(2,1)S(1)} %get-tuple-element.158), channel_id=1, source_target_pairs={{0,1},{1,0},{2,3},{3,2},{4,5},{5,4},{6,7},{7,6},{8,9},{9,8},{10,11... | collective-permute-start | bytes 1007624 | tf_op jit(solution)/shard_map/ppermute | solution.py:180
  60.4 7.8 %forward.5 = (f32[256,864]{1,0:T(8,128)S(1)}, f32[256,864]{1,0:T(8,128)S(1)}, bf16[256,256]{1,0:T(8,128)(2,1)S(1)}, bf16[256,256]{1,0:T(8,128)(2,1)S(1)}) custom-call(bf16[64,5120]{1,0:T(8,128)(2,1)S(1)} %collective-permute-done.4.refs_0_, bf16[32,5120]{1,0:T(8,128)(2,1)S(1)} %collective-permute-done.14.refs_1_, ...), custom_call_target="tpu_custom_call" | custom-call | tf_op jit(solution)/shard_map/forward/pallas_call | solution.py:134
  68.3 0.5 collective-permute-start.24
  69.0 0.9 collective-permute-done.23.refs_2_
  70.4 0.5 collective-permute-start.21
  70.9 5.5 %backward.5.refs_13_ = f32[256,512]{1,0:T(8,128)S(1)} custom-call(bf16[64,5248]{1,0:T(8,128)(2,1)S(1)} %collective-permute-done.refs_0_, bf16[32,5248]{1,0:T(8,128)(2,1)S(1)} %collective-permute-done.22.refs_1_, bf16[32,5248]{1,0:T(8,128)(2,1)S(1)} %collective-permute-done.23.refs_2_, bf16[64,5248]{1,0:T(8,128)(2,1)S(1)} %collective-permute-done.9.refs_3_, ...), custom_call_target="tpu_custom_call" | custom-call | tf_op jit(solution)/shard_map/backward/pallas_call | solution.py:134
  76.4 1.3 collective-permute-done.28.refs_0_
  77.7 0.8 collective-permute-start.30
  78.6 0.5 collective-permute-start.26
  79.1 0.6 collective-permute-done.30.refs_4_
  79.8 0.4 collective-permute-start.27
  80.2 1.5 %collective-permute-start.32 = (bf16[64,5120]{1,0:T(8,128)(2,1)S(1)}, bf16[64,5120]{1,0:T(8,128)(2,1)S(1)}, u32[]{:S(2)}, u32[]{:S(2)}) collective-permute-start(bf16[64,5120]{1,0:T(8,128)(2,1)S(1)} %collective-permute-done.28.refs_0_), channel_id=1, source_target_pairs={{0,2},{1,3},{2,0},{3,1},{4,6},{5,7},{6,4},{7,5},{8,10},{9,11},{10,... | collective-permute-start | bytes 1966088 | tf_op jit(solution)/shard_map/ppermute | solution.py:180
  81.9 0.4 collective-permute-start.34
  82.4 7.8 %forward.6 = (f32[256,864]{1,0:T(8,128)S(1)}, f32[256,864]{1,0:T(8,128)S(1)}, bf16[256,256]{1,0:T(8,128)(2,1)S(1)}, bf16[256,256]{1,0:T(8,128)(2,1)S(1)}) custom-call(bf16[64,5120]{1,0:T(8,128)(2,1)S(1)} %collective-permute-done.16.refs_0_, bf16[32,5120]{1,0:T(8,128)(2,1)S(1)} %collective-permute-done.26.refs_1_, ...), custom_call_target="tpu_custom_call" | custom-call | tf_op jit(solution)/shard_map/forward/pallas_call | solution.py:134
  90.1 1.3 collective-permute-done.20.refs_0_
  91.6 1.3 collective-permute-start.35
  93.0 1.2 collective-permute-done.35.refs_4_
  94.2 0.5 collective-permute-done.36.refs_5_
  94.7 5.4 %backward.6.refs_13_ = f32[256,512]{1,0:T(8,128)S(1)} custom-call(bf16[64,5248]{1,0:T(8,128)(2,1)S(1)} %collective-permute-done.8.refs_0_, bf16[32,5248]{1,0:T(8,128)(2,1)S(1)} %collective-permute-done.33.refs_1_, bf16[32,5248]{1,0:T(8,128)(2,1)S(1)} %collective-permute-done.34.refs_2_, bf16[64,5248]{1,0:T(8,128)(2,1)S(1)} %collective-permute-done.21.refs_3_, ...), custom_call_target="tpu_custom_call" | custom-call | tf_op jit(solution)/shard_map/backward/pallas_call | solution.py:134
  100.1 5.5 %collective-permute-done.32.refs_3_ = bf16[64,5120]{1,0:T(8,128)(2,1)S(1)} collective-permute-done((bf16[64,5120]{1,0:T(8,128)(2,1)S(1)}, bf16[64,5120]{1,0:T(8,128)(2,1)S(1)}, u32[]{:S(2)}, u32[]{:S(2)}) %collective-permute-start.32) | collective-permute-done | bytes 655392 | tf_op jit(solution)/shard_map/ppermute | solution.py:180
  105.7 0.7 collective-permute-start.37
  106.5 0.5 collective-permute-start.42
  107.1 0.6 collective-permute-done.37.refs_4_
  107.7 0.5 collective-permute-done.38.refs_5_
  108.2 0.4 collective-permute-start.39
  109.1 7.8 %forward.7 = (f32[256,864]{1,0:T(8,128)S(1)}, f32[256,864]{1,0:T(8,128)S(1)}, bf16[256,256]{1,0:T(8,128)(2,1)S(1)}, bf16[256,256]{1,0:T(8,128)(2,1)S(1)}) custom-call(bf16[64,5120]{1,0:T(8,128)(2,1)S(1)} %collective-permute-done.28.refs_0_, bf16[32,5120]{1,0:T(8,128)(2,1)S(1)} %collective-permute-done.42.refs_1_, ...), custom_call_target="tpu_custom_call" | custom-call | tf_op jit(solution)/shard_map/forward/pallas_call | solution.py:134
  116.9 0.4 collective-permute-start.44
  117.5 1.1 collective-permute-done.44.refs_4_
  118.6 0.5 collective-permute-done.45.refs_5_
  119.1 5.4 %backward.7 = f32[256,512]{1,0:T(8,128)S(1)} custom-call(bf16[64,5248]{1,0:T(8,128)(2,1)S(1)} %collective-permute-done.20.refs_0_, bf16[32,5248]{1,0:T(8,128)(2,1)S(1)} %collective-permute-done.39.refs_1_, bf16[32,5248]{1,0:T(8,128)(2,1)S(1)} %collective-permute-done.40.refs_2_, bf16[64,5248]{1,0:T(8,128)(2,1)S(1)} %collective-permute-done.41.refs_3_, ...), custom_call_target="tpu_custom_call" | custom-call | tf_op jit(solution)/shard_map/backward/pallas_call | solution.py:134
  124.6 13.5 %all_to_all.5 = bf16[16,16,512]{2,1,0:T(8,128)(2,1)S(1)} all-to-all(bf16[16,16,512]{2,1,0:T(8,128)(2,1)S(1)} %bitcast.18), channel_id=1, replica_groups=mesh['groups'=2,'fsdp'=16] {'fsdp'}, dimensions={0} | all-to-all | bytes 524288 | tf_op jit(solution)/shard_map/all_to_all | solution.py:236
  138.1 0.6 copy.11
  (99 shorter events, 4.1 us)
Async XLA Ops:
  0.0 8.1 %copy-start.5 = (s32[3,864]{1,0:T(4,128)S(1)}, s32[3,864]{1,0:T(4,128)}, u32[]{:S(2)}) copy-start(s32[3,864]{1,0:T(4,128)} %param.16) | copy-start | bytes 31108
  0.0 8.6 %copy-start.4 = (bf16[64,5120]{1,0:T(8,128)(2,1)S(1)}, bf16[64,5120]{1,0:T(8,128)(2,1)}, u32[]{:S(2)}) copy-start(bf16[64,5120]{1,0:T(8,128)(2,1)} %param.11) | copy-start | bytes 1966084
  0.0 20.8 %collective-permute-start.4 = (bf16[64,5120]{1,0:T(8,128)(2,1)}, bf16[64,5120]{1,0:T(8,128)(2,1)S(1)}, u32[]{:S(2)}, u32[]{:S(2)}) collective-permute-start(bf16[64,5120]{1,0:T(8,128)(2,1)} %refs_0_.1), channel_id=1, source_target_pairs={{0,4},{1,13},{2,6},{3,15},{4,8},{5,1},{6,10},{7,3},{8,12},{9,5},{1... | collective-permute-start | bytes 1966088 | tf_op jit(solution)/shard_map/ppermute | solution.py:180
  3.0 17.8 %collective-permute-start.5 = (bf16[64,5120]{1,0:T(8,128)(2,1)}, bf16[64,5120]{1,0:T(8,128)(2,1)S(1)}, u32[]{:S(2)}, u32[]{:S(2)}) collective-permute-start(bf16[64,5120]{1,0:T(8,128)(2,1)} %refs_0_.1), channel_id=1, source_target_pairs={{0,2},{1,3},{2,0},{3,1},{4,6},{5,7},{6,4},{7,5},{8,10},{9,11},{10,... | collective-permute-start | bytes 1966088 | tf_op jit(solution)/shard_map/ppermute | solution.py:180
  8.1 13.6 %copy-start.3 = (bf16[64,5120]{1,0:T(8,128)(2,1)S(1)}, bf16[64,5120]{1,0:T(8,128)(2,1)}, u32[]{:S(2)}) copy-start(bf16[64,5120]{1,0:T(8,128)(2,1)} %refs_0_.1) | copy-start | bytes 1966084
  8.7 32.3 %collective-permute-start = (bf16[64,5248]{1,0:T(8,128)(2,1)S(1)}, bf16[64,5248]{1,0:T(8,128)(2,1)S(1)}, u32[]{:S(2)}, u32[]{:S(2)}) collective-permute-start(bf16[64,5248]{1,0:T(8,128)(2,1)S(1)} %pad_maximum_fusion.refs_0_), channel_id=1, source_target_pairs={{0,4},{1,13},{2,6},{3,15},{4,8},{5,1},{6,10},{7,3},{8,12},{9,5},{1... | collective-permute-start | bytes 2015240 | tf_op jit(solution)/shard_map/ppermute | solution.py:180
  10.3 30.7 %collective-permute-start.1 = (bf16[64,5248]{1,0:T(8,128)(2,1)S(1)}, bf16[64,5248]{1,0:T(8,128)(2,1)S(1)}, u32[]{:S(2)}, u32[]{:S(2)}) collective-permute-start(bf16[64,5248]{1,0:T(8,128)(2,1)S(1)} %pad_maximum_fusion.refs_0_), channel_id=1, source_target_pairs={{0,2},{1,3},{2,0},{3,1},{4,6},{5,7},{6,4},{7,5},{8,10},{9,11},{10,... | collective-permute-start | bytes 2015240 | tf_op jit(solution)/shard_map/ppermute | solution.py:180
  20.9 2.0 %collective-permute-start.6 = (bf16[32,5120]{1,0:T(8,128)(2,1)S(1)}, bf16[32,5120]{1,0:T(8,128)(2,1)S(1)}, u32[]{:S(2)}, u32[]{:S(2)}) collective-permute-start(bf16[32,5120]{1,0:T(8,128)(2,1)S(1)} %get-tuple-element.176), channel_id=1, source_target_pairs={{0,1},{1,0},{2,3},{3,2},{4,5},{5,4},{6,7},{7,6},{8,9},{9,8},{10,11... | collective-permute-start | bytes 983048 | tf_op jit(solution)/shard_map/ppermute | solution.py:180
  21.6 1.7 %collective-permute-start.7 = (bf16[32,5120]{1,0:T(8,128)(2,1)S(1)}, bf16[32,5120]{1,0:T(8,128)(2,1)S(1)}, u32[]{:S(2)}, u32[]{:S(2)}) collective-permute-start(bf16[32,5120]{1,0:T(8,128)(2,1)S(1)} %get-tuple-element.175), channel_id=1, source_target_pairs={{0,1},{1,0},{2,3},{3,2},{4,5},{5,4},{6,7},{7,6},{8,9},{9,8},{10,11... | collective-permute-start | bytes 983048 | tf_op jit(solution)/shard_map/ppermute | solution.py:180
  21.8 2.9 %collective-permute-start.2 = (bf16[32,5120]{1,0:T(8,128)(2,1)S(1)}, bf16[32,5120]{1,0:T(8,128)(2,1)S(1)}, u32[]{:S(2)}, u32[]{:S(2)}) collective-permute-start(bf16[32,5120]{1,0:T(8,128)(2,1)S(1)} %get-tuple-element.178), channel_id=1, source_target_pairs={{0,1},{1,0},{2,3},{3,2},{4,5},{5,4},{6,7},{7,6},{8,9},{9,8},{10,11... | collective-permute-start | bytes 983048 | tf_op jit(solution)/shard_map/ppermute | solution.py:180
  22.9 3.3 %collective-permute-start.3 = (bf16[32,5120]{1,0:T(8,128)(2,1)S(1)}, bf16[32,5120]{1,0:T(8,128)(2,1)S(1)}, u32[]{:S(2)}, u32[]{:S(2)}) collective-permute-start(bf16[32,5120]{1,0:T(8,128)(2,1)S(1)} %get-tuple-element.177), channel_id=1, source_target_pairs={{0,1},{1,0},{2,3},{3,2},{4,5},{5,4},{6,7},{7,6},{8,9},{9,8},{10,11... | collective-permute-start | bytes 983048 | tf_op jit(solution)/shard_map/ppermute | solution.py:180
  23.4 31.2 %collective-permute-start.16 = (bf16[64,5120]{1,0:T(8,128)(2,1)S(1)}, bf16[64,5120]{1,0:T(8,128)(2,1)S(1)}, u32[]{:S(2)}, u32[]{:S(2)}) collective-permute-start(bf16[64,5120]{1,0:T(8,128)(2,1)S(1)} %collective-permute-done.4.refs_0_), channel_id=1, source_target_pairs={{0,4},{1,13},{2,6},{3,15},{4,8},{5,1},{6,10},{7,3},{8,12},{9,5},{1... | collective-permute-start | bytes 1966088 | tf_op jit(solution)/shard_map/ppermute | solution.py:180
  24.7 29.9 %collective-permute-start.17 = (bf16[64,5120]{1,0:T(8,128)(2,1)S(1)}, bf16[64,5120]{1,0:T(8,128)(2,1)S(1)}, u32[]{:S(2)}, u32[]{:S(2)}) collective-permute-start(bf16[64,5120]{1,0:T(8,128)(2,1)S(1)} %collective-permute-done.4.refs_0_), channel_id=1, source_target_pairs={{0,2},{1,3},{2,0},{3,1},{4,6},{5,7},{6,4},{7,5},{8,10},{9,11},{10,... | collective-permute-start | bytes 1966088 | tf_op jit(solution)/shard_map/ppermute | solution.py:180
  26.2 3.5 %copy-start = (bf16[5120,864]{0,1:T(8,128)(2,1)S(1)}, bf16[5120,864]{0,1:T(8,128)(2,1)}, u32[]{:S(2)}) copy-start(bf16[5120,864]{0,1:T(8,128)(2,1)} %param.13) | copy-start | bytes 26542084
  29.7 3.5 %copy-start.1 = (bf16[5120,864]{0,1:T(8,128)(2,1)S(1)}, bf16[5120,864]{0,1:T(8,128)(2,1)}, u32[]{:S(2)}) copy-start(bf16[5120,864]{0,1:T(8,128)(2,1)} %param.14) | copy-start | bytes 26542084
  33.2 27.1 %slice-start.3 = ((s8[8847360]{0:T(1024)(128)(4,1)}), s8[4194304]{0:T(1024)(128)(4,1)S(1)}, s32[]{:S(2)}) async-start(s8[8847360]{0:T(1024)(128)(4,1)} %bitcast.11), calls=%async_computation.4 | async-start | bytes 8388608
  33.2 27.1 %slice-start.4 = ((s8[8847360]{0:T(1024)(128)(4,1)}), s8[4194304]{0:T(1024)(128)(4,1)S(1)}, s32[]{:S(2)}) async-start(s8[8847360]{0:T(1024)(128)(4,1)} %bitcast.11), calls=%async_computation.5 | async-start | bytes 8388608
  41.1 1.7 %collective-permute-start.12 = (bf16[32,5248]{1,0:T(8,128)(2,1)S(1)}, bf16[32,5248]{1,0:T(8,128)(2,1)S(1)}, u32[]{:S(2)}, u32[]{:S(2)}) collective-permute-start(bf16[32,5248]{1,0:T(8,128)(2,1)S(1)} %get-tuple-element.160), channel_id=1, source_target_pairs={{0,1},{1,0},{2,3},{3,2},{4,5},{5,4},{6,7},{7,6},{8,9},{9,8},{10,11... | collective-permute-start | bytes 1007624 | tf_op jit(solution)/shard_map/ppermute | solution.py:180
  41.4 1.8 %collective-permute-start.13 = (bf16[32,5248]{1,0:T(8,128)(2,1)S(1)}, bf16[32,5248]{1,0:T(8,128)(2,1)S(1)}, u32[]{:S(2)}, u32[]{:S(2)}) collective-permute-start(bf16[32,5248]{1,0:T(8,128)(2,1)S(1)} %get-tuple-element.159), channel_id=1, source_target_pairs={{0,1},{1,0},{2,3},{3,2},{4,5},{5,4},{6,7},{7,6},{8,9},{9,8},{10,11... | collective-permute-start | bytes 1007624 | tf_op jit(solution)/shard_map/ppermute | solution.py:180
  41.7 3.1 %collective-permute-start.10 = (bf16[32,5248]{1,0:T(8,128)(2,1)S(1)}, bf16[32,5248]{1,0:T(8,128)(2,1)S(1)}, u32[]{:S(2)}, u32[]{:S(2)}) collective-permute-start(bf16[32,5248]{1,0:T(8,128)(2,1)S(1)} %get-tuple-element.162), channel_id=1, source_target_pairs={{0,1},{1,0},{2,3},{3,2},{4,5},{5,4},{6,7},{7,6},{8,9},{9,8},{10,11... | collective-permute-start | bytes 1007624 | tf_op jit(solution)/shard_map/ppermute | solution.py:180
  42.8 2.6 %collective-permute-start.11 = (bf16[32,5248]{1,0:T(8,128)(2,1)S(1)}, bf16[32,5248]{1,0:T(8,128)(2,1)S(1)}, u32[]{:S(2)}, u32[]{:S(2)}) collective-permute-start(bf16[32,5248]{1,0:T(8,128)(2,1)S(1)} %get-tuple-element.161), channel_id=1, source_target_pairs={{0,1},{1,0},{2,3},{3,2},{4,5},{5,4},{6,7},{7,6},{8,9},{9,8},{10,11... | collective-permute-start | bytes 1007624 | tf_op jit(solution)/shard_map/ppermute | solution.py:180
  43.3 24.9 %collective-permute-start.8 = (bf16[64,5248]{1,0:T(8,128)(2,1)S(1)}, bf16[64,5248]{1,0:T(8,128)(2,1)S(1)}, u32[]{:S(2)}, u32[]{:S(2)}) collective-permute-start(bf16[64,5248]{1,0:T(8,128)(2,1)S(1)} %collective-permute-done.refs_0_), channel_id=1, source_target_pairs={{0,4},{1,13},{2,6},{3,15},{4,8},{5,1},{6,10},{7,3},{8,12},{9,5},{1... | collective-permute-start | bytes 2015240 | tf_op jit(solution)/shard_map/ppermute | solution.py:180
  44.8 23.4 %collective-permute-start.9 = (bf16[64,5248]{1,0:T(8,128)(2,1)S(1)}, bf16[64,5248]{1,0:T(8,128)(2,1)S(1)}, u32[]{:S(2)}, u32[]{:S(2)}) collective-permute-start(bf16[64,5248]{1,0:T(8,128)(2,1)S(1)} %collective-permute-done.refs_0_), channel_id=1, source_target_pairs={{0,2},{1,3},{2,0},{3,1},{4,6},{5,7},{6,4},{7,5},{8,10},{9,11},{10,... | collective-permute-start | bytes 2015240 | tf_op jit(solution)/shard_map/ppermute | solution.py:180
  45.4 15.0 %slice-start = ((s8[8847360]{0:T(1024)(128)(4,1)}), s8[4194304]{0:T(1024)(128)(4,1)S(1)}, s32[]{:S(2)}) async-start(s8[8847360]{0:T(1024)(128)(4,1)} %bitcast.5), calls=%async_computation.1 | async-start | bytes 8388608
  45.4 3.7 %copy-start.2 = (bf16[864,5120]{1,0:T(8,128)(2,1)S(1)}, bf16[864,5120]{1,0:T(8,128)(2,1)}, u32[]{:S(2)}) copy-start(bf16[864,5120]{1,0:T(8,128)(2,1)} %refs_6_.7) | copy-start | bytes 26542084
  49.1 11.2 %slice-start.1 = ((s8[8847360]{0:T(1024)(128)(4,1)}), s8[4194304]{0:T(1024)(128)(4,1)S(1)}, s32[]{:S(2)}) async-start(s8[8847360]{0:T(1024)(128)(4,1)} %bitcast.5), calls=%async_computation.2 | async-start | bytes 8388608
  49.1 11.2 %slice-start.2 = ((s8[8847360]{0:T(1024)(128)(4,1)}), s8[458752]{0:T(1024)(128)(4,1)S(1)}, s32[]{:S(2)}) async-start(s8[8847360]{0:T(1024)(128)(4,1)} %bitcast.5), calls=%async_computation.3 | async-start | bytes 917504
  49.1 11.3 %slice-start.5 = ((s8[8847360]{0:T(1024)(128)(4,1)}), s8[458752]{0:T(1024)(128)(4,1)S(1)}, s32[]{:S(2)}) async-start(s8[8847360]{0:T(1024)(128)(4,1)} %bitcast.11), calls=%async_computation.6 | async-start | bytes 917504
  54.6 1.8 %collective-permute-start.18 = (bf16[32,5120]{1,0:T(8,128)(2,1)S(1)}, bf16[32,5120]{1,0:T(8,128)(2,1)S(1)}, u32[]{:S(2)}, u32[]{:S(2)}) collective-permute-start(bf16[32,5120]{1,0:T(8,128)(2,1)S(1)} %get-tuple-element.172), channel_id=1, source_target_pairs={{0,1},{1,0},{2,3},{3,2},{4,5},{5,4},{6,7},{7,6},{8,9},{9,8},{10,11... | collective-permute-start | bytes 983048 | tf_op jit(solution)/shard_map/ppermute | solution.py:180
  55.2 1.7 %collective-permute-start.19 = (bf16[32,5120]{1,0:T(8,128)(2,1)S(1)}, bf16[32,5120]{1,0:T(8,128)(2,1)S(1)}, u32[]{:S(2)}, u32[]{:S(2)}) collective-permute-start(bf16[32,5120]{1,0:T(8,128)(2,1)S(1)} %get-tuple-element.171), channel_id=1, source_target_pairs={{0,1},{1,0},{2,3},{3,2},{4,5},{5,4},{6,7},{7,6},{8,9},{9,8},{10,11... | collective-permute-start | bytes 983048 | tf_op jit(solution)/shard_map/ppermute | solution.py:180
  55.3 2.2 %collective-permute-start.14 = (bf16[32,5120]{1,0:T(8,128)(2,1)S(1)}, bf16[32,5120]{1,0:T(8,128)(2,1)S(1)}, u32[]{:S(2)}, u32[]{:S(2)}) collective-permute-start(bf16[32,5120]{1,0:T(8,128)(2,1)S(1)} %get-tuple-element.174), channel_id=1, source_target_pairs={{0,1},{1,0},{2,3},{3,2},{4,5},{5,4},{6,7},{7,6},{8,9},{9,8},{10,11... | collective-permute-start | bytes 983048 | tf_op jit(solution)/shard_map/ppermute | solution.py:180
  56.5 2.5 %collective-permute-start.15 = (bf16[32,5120]{1,0:T(8,128)(2,1)S(1)}, bf16[32,5120]{1,0:T(8,128)(2,1)S(1)}, u32[]{:S(2)}, u32[]{:S(2)}) collective-permute-start(bf16[32,5120]{1,0:T(8,128)(2,1)S(1)} %get-tuple-element.173), channel_id=1, source_target_pairs={{0,1},{1,0},{2,3},{3,2},{4,5},{5,4},{6,7},{7,6},{8,9},{9,8},{10,11... | collective-permute-start | bytes 983048 | tf_op jit(solution)/shard_map/ppermute | solution.py:180
  56.9 20.8 %collective-permute-start.28 = (bf16[64,5120]{1,0:T(8,128)(2,1)S(1)}, bf16[64,5120]{1,0:T(8,128)(2,1)S(1)}, u32[]{:S(2)}, u32[]{:S(2)}) collective-permute-start(bf16[64,5120]{1,0:T(8,128)(2,1)S(1)} %collective-permute-done.16.refs_0_), channel_id=1, source_target_pairs={{0,4},{1,13},{2,6},{3,15},{4,8},{5,1},{6,10},{7,3},{8,12},{9,5},{1... | collective-permute-start | bytes 1966088 | tf_op jit(solution)/shard_map/ppermute | solution.py:180
  57.5 20.2 %collective-permute-start.29 = (bf16[64,5120]{1,0:T(8,128)(2,1)S(1)}, bf16[64,5120]{1,0:T(8,128)(2,1)S(1)}, u32[]{:S(2)}, u32[]{:S(2)}) collective-permute-start(bf16[64,5120]{1,0:T(8,128)(2,1)S(1)} %collective-permute-done.16.refs_0_), channel_id=1, source_target_pairs={{0,2},{1,3},{2,0},{3,1},{4,6},{5,7},{6,4},{7,5},{8,10},{9,11},{10,... | collective-permute-start | bytes 1966088 | tf_op jit(solution)/shard_map/ppermute | solution.py:180
  58.9 12.0 %slice-start.6 = ((s8[8847360]{0:T(1024)(128)(4,1)}), s8[4194304]{0:T(1024)(128)(4,1)S(1)}, s32[]{:S(2)}) async-start(s8[8847360]{0:T(1024)(128)(4,1)} %bitcast.16), calls=%async_computation.7 | async-start | bytes 8388608
  58.9 12.0 %slice-start.7 = ((s8[8847360]{0:T(1024)(128)(4,1)}), s8[4194304]{0:T(1024)(128)(4,1)S(1)}, s32[]{:S(2)}) async-start(s8[8847360]{0:T(1024)(128)(4,1)} %bitcast.16), calls=%async_computation.8 | async-start | bytes 8388608
  58.9 12.0 %slice-start.8 = ((s8[8847360]{0:T(1024)(128)(4,1)}), s8[458752]{0:T(1024)(128)(4,1)S(1)}, s32[]{:S(2)}) async-start(s8[8847360]{0:T(1024)(128)(4,1)} %bitcast.16), calls=%async_computation.9 | async-start | bytes 917504
  58.9 10.0 %collective-permute-start.22 = (bf16[32,5248]{1,0:T(8,128)(2,1)S(1)}, bf16[32,5248]{1,0:T(8,128)(2,1)S(1)}, u32[]{:S(2)}, u32[]{:S(2)}) collective-permute-start(bf16[32,5248]{1,0:T(8,128)(2,1)S(1)} %get-tuple-element.158), channel_id=1, source_target_pairs={{0,1},{1,0},{2,3},{3,2},{4,5},{5,4},{6,7},{7,6},{8,9},{9,8},{10,11... | collective-permute-start | bytes 1007624 | tf_op jit(solution)/shard_map/ppermute | solution.py:180
  68.2 1.7 %collective-permute-start.23 = (bf16[32,5248]{1,0:T(8,128)(2,1)S(1)}, bf16[32,5248]{1,0:T(8,128)(2,1)S(1)}, u32[]{:S(2)}, u32[]{:S(2)}) collective-permute-start(bf16[32,5248]{1,0:T(8,128)(2,1)S(1)} %get-tuple-element.157), channel_id=1, source_target_pairs={{0,1},{1,0},{2,3},{3,2},{4,5},{5,4},{6,7},{7,6},{8,9},{9,8},{10,11... | collective-permute-start | bytes 1007624 | tf_op jit(solution)/shard_map/ppermute | solution.py:180
  68.3 2.0 %collective-permute-start.24 = (bf16[32,5248]{1,0:T(8,128)(2,1)S(1)}, bf16[32,5248]{1,0:T(8,128)(2,1)S(1)}, u32[]{:S(2)}, u32[]{:S(2)}) collective-permute-start(bf16[32,5248]{1,0:T(8,128)(2,1)S(1)} %get-tuple-element.156), channel_id=1, source_target_pairs={{0,1},{1,0},{2,3},{3,2},{4,5},{5,4},{6,7},{7,6},{8,9},{9,8},{10,11... | collective-permute-start | bytes 1007624 | tf_op jit(solution)/shard_map/ppermute | solution.py:180
  68.9 2.0 %collective-permute-start.25 = (bf16[32,5248]{1,0:T(8,128)(2,1)S(1)}, bf16[32,5248]{1,0:T(8,128)(2,1)S(1)}, u32[]{:S(2)}, u32[]{:S(2)}) collective-permute-start(bf16[32,5248]{1,0:T(8,128)(2,1)S(1)} %get-tuple-element.155), channel_id=1, source_target_pairs={{0,1},{1,0},{2,3},{3,2},{4,5},{5,4},{6,7},{7,6},{8,9},{9,8},{10,11... | collective-permute-start | bytes 1007624 | tf_op jit(solution)/shard_map/ppermute | solution.py:180
  69.9 21.5 %collective-permute-start.20 = (bf16[64,5248]{1,0:T(8,128)(2,1)S(1)}, bf16[64,5248]{1,0:T(8,128)(2,1)S(1)}, u32[]{:S(2)}, u32[]{:S(2)}) collective-permute-start(bf16[64,5248]{1,0:T(8,128)(2,1)S(1)} %collective-permute-done.8.refs_0_), channel_id=1, source_target_pairs={{0,4},{1,13},{2,6},{3,15},{4,8},{5,1},{6,10},{7,3},{8,12},{9,5},{1... | collective-permute-start | bytes 2015240 | tf_op jit(solution)/shard_map/ppermute | solution.py:180
  70.4 21.2 %collective-permute-start.21 = (bf16[64,5248]{1,0:T(8,128)(2,1)S(1)}, bf16[64,5248]{1,0:T(8,128)(2,1)S(1)}, u32[]{:S(2)}, u32[]{:S(2)}) collective-permute-start(bf16[64,5248]{1,0:T(8,128)(2,1)S(1)} %collective-permute-done.8.refs_0_), channel_id=1, source_target_pairs={{0,2},{1,3},{2,0},{3,1},{4,6},{5,7},{6,4},{7,5},{8,10},{9,11},{10,... | collective-permute-start | bytes 2015240 | tf_op jit(solution)/shard_map/ppermute | solution.py:180
  77.7 2.0 %collective-permute-start.30 = (bf16[32,5120]{1,0:T(8,128)(2,1)S(1)}, bf16[32,5120]{1,0:T(8,128)(2,1)S(1)}, u32[]{:S(2)}, u32[]{:S(2)}) collective-permute-start(bf16[32,5120]{1,0:T(8,128)(2,1)S(1)} %get-tuple-element.168), channel_id=1, source_target_pairs={{0,1},{1,0},{2,3},{3,2},{4,5},{5,4},{6,7},{7,6},{8,9},{9,8},{10,11... | collective-permute-start | bytes 983048 | tf_op jit(solution)/shard_map/ppermute | solution.py:180
  78.5 1.7 %collective-permute-start.31 = (bf16[32,5120]{1,0:T(8,128)(2,1)S(1)}, bf16[32,5120]{1,0:T(8,128)(2,1)S(1)}, u32[]{:S(2)}, u32[]{:S(2)}) collective-permute-start(bf16[32,5120]{1,0:T(8,128)(2,1)S(1)} %get-tuple-element.167), channel_id=1, source_target_pairs={{0,1},{1,0},{2,3},{3,2},{4,5},{5,4},{6,7},{7,6},{8,9},{9,8},{10,11... | collective-permute-start | bytes 983048 | tf_op jit(solution)/shard_map/ppermute | solution.py:180
  78.6 3.2 %collective-permute-start.26 = (bf16[32,5120]{1,0:T(8,128)(2,1)S(1)}, bf16[32,5120]{1,0:T(8,128)(2,1)S(1)}, u32[]{:S(2)}, u32[]{:S(2)}) collective-permute-start(bf16[32,5120]{1,0:T(8,128)(2,1)S(1)} %get-tuple-element.170), channel_id=1, source_target_pairs={{0,1},{1,0},{2,3},{3,2},{4,5},{5,4},{6,7},{7,6},{8,9},{9,8},{10,11... | collective-permute-start | bytes 983048 | tf_op jit(solution)/shard_map/ppermute | solution.py:180
  79.8 2.2 %collective-permute-start.27 = (bf16[32,5120]{1,0:T(8,128)(2,1)S(1)}, bf16[32,5120]{1,0:T(8,128)(2,1)S(1)}, u32[]{:S(2)}, u32[]{:S(2)}) collective-permute-start(bf16[32,5120]{1,0:T(8,128)(2,1)S(1)} %get-tuple-element.169), channel_id=1, source_target_pairs={{0,1},{1,0},{2,3},{3,2},{4,5},{5,4},{6,7},{7,6},{8,9},{9,8},{10,11... | collective-permute-start | bytes 983048 | tf_op jit(solution)/shard_map/ppermute | solution.py:180
  80.2 25.4 %collective-permute-start.32 = (bf16[64,5120]{1,0:T(8,128)(2,1)S(1)}, bf16[64,5120]{1,0:T(8,128)(2,1)S(1)}, u32[]{:S(2)}, u32[]{:S(2)}) collective-permute-start(bf16[64,5120]{1,0:T(8,128)(2,1)S(1)} %collective-permute-done.28.refs_0_), channel_id=1, source_target_pairs={{0,2},{1,3},{2,0},{3,1},{4,6},{5,7},{6,4},{7,5},{8,10},{9,11},{10,... | collective-permute-start | bytes 1966088 | tf_op jit(solution)/shard_map/ppermute | solution.py:180
  81.8 11.2 %collective-permute-start.33 = (bf16[32,5248]{1,0:T(8,128)(2,1)S(1)}, bf16[32,5248]{1,0:T(8,128)(2,1)S(1)}, u32[]{:S(2)}, u32[]{:S(2)}) collective-permute-start(bf16[32,5248]{1,0:T(8,128)(2,1)S(1)} %get-tuple-element.154), channel_id=1, source_target_pairs={{0,1},{1,0},{2,3},{3,2},{4,5},{5,4},{6,7},{7,6},{8,9},{9,8},{10,11... | collective-permute-start | bytes 1007624 | tf_op jit(solution)/shard_map/ppermute | solution.py:180
  81.9 11.0 %collective-permute-start.34 = (bf16[32,5248]{1,0:T(8,128)(2,1)S(1)}, bf16[32,5248]{1,0:T(8,128)(2,1)S(1)}, u32[]{:S(2)}, u32[]{:S(2)}) collective-permute-start(bf16[32,5248]{1,0:T(8,128)(2,1)S(1)} %get-tuple-element.153), channel_id=1, source_target_pairs={{0,1},{1,0},{2,3},{3,2},{4,5},{5,4},{6,7},{7,6},{8,9},{9,8},{10,11... | collective-permute-start | bytes 1007624 | tf_op jit(solution)/shard_map/ppermute | solution.py:180
  91.6 2.6 %collective-permute-start.35 = (bf16[32,5248]{1,0:T(8,128)(2,1)S(1)}, bf16[32,5248]{1,0:T(8,128)(2,1)S(1)}, u32[]{:S(2)}, u32[]{:S(2)}) collective-permute-start(bf16[32,5248]{1,0:T(8,128)(2,1)S(1)} %get-tuple-element.152), channel_id=1, source_target_pairs={{0,1},{1,0},{2,3},{3,2},{4,5},{5,4},{6,7},{7,6},{8,9},{9,8},{10,11... | collective-permute-start | bytes 1007624 | tf_op jit(solution)/shard_map/ppermute | solution.py:180
  92.9 1.7 %collective-permute-start.36 = (bf16[32,5248]{1,0:T(8,128)(2,1)S(1)}, bf16[32,5248]{1,0:T(8,128)(2,1)S(1)}, u32[]{:S(2)}, u32[]{:S(2)}) collective-permute-start(bf16[32,5248]{1,0:T(8,128)(2,1)S(1)} %get-tuple-element.151), channel_id=1, source_target_pairs={{0,1},{1,0},{2,3},{3,2},{4,5},{5,4},{6,7},{7,6},{8,9},{9,8},{10,11... | collective-permute-start | bytes 1007624 | tf_op jit(solution)/shard_map/ppermute | solution.py:180
  93.0 23.8 %collective-permute-start.41 = (bf16[64,5248]{1,0:T(8,128)(2,1)S(1)}, bf16[64,5248]{1,0:T(8,128)(2,1)S(1)}, u32[]{:S(2)}, u32[]{:S(2)}) collective-permute-start(bf16[64,5248]{1,0:T(8,128)(2,1)S(1)} %collective-permute-done.21.refs_3_), channel_id=1, source_target_pairs={{0,4},{1,13},{2,6},{3,15},{4,8},{5,1},{6,10},{7,3},{8,12},{9,5},{1... | collective-permute-start | bytes 2015240 | tf_op jit(solution)/shard_map/ppermute | solution.py:180
  105.7 2.0 %collective-permute-start.37 = (bf16[32,5120]{1,0:T(8,128)(2,1)S(1)}, bf16[32,5120]{1,0:T(8,128)(2,1)S(1)}, u32[]{:S(2)}, u32[]{:S(2)}) collective-permute-start(bf16[32,5120]{1,0:T(8,128)(2,1)S(1)} %get-tuple-element.166), channel_id=1, source_target_pairs={{0,1},{1,0},{2,3},{3,2},{4,5},{5,4},{6,7},{7,6},{8,9},{9,8},{10,11... | collective-permute-start | bytes 983048 | tf_op jit(solution)/shard_map/ppermute | solution.py:180
  106.4 1.7 %collective-permute-start.38 = (bf16[32,5120]{1,0:T(8,128)(2,1)S(1)}, bf16[32,5120]{1,0:T(8,128)(2,1)S(1)}, u32[]{:S(2)}, u32[]{:S(2)}) collective-permute-start(bf16[32,5120]{1,0:T(8,128)(2,1)S(1)} %get-tuple-element.165), channel_id=1, source_target_pairs={{0,1},{1,0},{2,3},{3,2},{4,5},{5,4},{6,7},{7,6},{8,9},{9,8},{10,11... | collective-permute-start | bytes 983048 | tf_op jit(solution)/shard_map/ppermute | solution.py:180
  106.5 2.2 %collective-permute-start.42 = (bf16[32,5120]{1,0:T(8,128)(2,1)S(1)}, bf16[32,5120]{1,0:T(8,128)(2,1)S(1)}, u32[]{:S(2)}, u32[]{:S(2)}) collective-permute-start(bf16[32,5120]{1,0:T(8,128)(2,1)S(1)} %get-tuple-element.164), channel_id=1, source_target_pairs={{0,1},{1,0},{2,3},{3,2},{4,5},{5,4},{6,7},{7,6},{8,9},{9,8},{10,11... | collective-permute-start | bytes 983048 | tf_op jit(solution)/shard_map/ppermute | solution.py:180
  107.0 2.0 %collective-permute-start.43 = (bf16[32,5120]{1,0:T(8,128)(2,1)S(1)}, bf16[32,5120]{1,0:T(8,128)(2,1)S(1)}, u32[]{:S(2)}, u32[]{:S(2)}) collective-permute-start(bf16[32,5120]{1,0:T(8,128)(2,1)S(1)} %get-tuple-element.163), channel_id=1, source_target_pairs={{0,1},{1,0},{2,3},{3,2},{4,5},{5,4},{6,7},{7,6},{8,9},{9,8},{10,11... | collective-permute-start | bytes 983048 | tf_op jit(solution)/shard_map/ppermute | solution.py:180
  108.2 9.3 %collective-permute-start.39 = (bf16[32,5248]{1,0:T(8,128)(2,1)S(1)}, bf16[32,5248]{1,0:T(8,128)(2,1)S(1)}, u32[]{:S(2)}, u32[]{:S(2)}) collective-permute-start(bf16[32,5248]{1,0:T(8,128)(2,1)S(1)} %get-tuple-element.150), channel_id=1, source_target_pairs={{0,1},{1,0},{2,3},{3,2},{4,5},{5,4},{6,7},{7,6},{8,9},{9,8},{10,11... | collective-permute-start | bytes 1007624 | tf_op jit(solution)/shard_map/ppermute | solution.py:180
  108.6 8.9 %collective-permute-start.40 = (bf16[32,5248]{1,0:T(8,128)(2,1)S(1)}, bf16[32,5248]{1,0:T(8,128)(2,1)S(1)}, u32[]{:S(2)}, u32[]{:S(2)}) collective-permute-start(bf16[32,5248]{1,0:T(8,128)(2,1)S(1)} %get-tuple-element.149), channel_id=1, source_target_pairs={{0,1},{1,0},{2,3},{3,2},{4,5},{5,4},{6,7},{7,6},{8,9},{9,8},{10,11... | collective-permute-start | bytes 1007624 | tf_op jit(solution)/shard_map/ppermute | solution.py:180
  116.9 1.7 %collective-permute-start.44 = (bf16[32,5248]{1,0:T(8,128)(2,1)S(1)}, bf16[32,5248]{1,0:T(8,128)(2,1)S(1)}, u32[]{:S(2)}, u32[]{:S(2)}) collective-permute-start(bf16[32,5248]{1,0:T(8,128)(2,1)S(1)} %get-tuple-element.148), channel_id=1, source_target_pairs={{0,1},{1,0},{2,3},{3,2},{4,5},{5,4},{6,7},{7,6},{8,9},{9,8},{10,11... | collective-permute-start | bytes 1007624 | tf_op jit(solution)/shard_map/ppermute | solution.py:180
  117.3 1.8 %collective-permute-start.45 = (bf16[32,5248]{1,0:T(8,128)(2,1)S(1)}, bf16[32,5248]{1,0:T(8,128)(2,1)S(1)}, u32[]{:S(2)}, u32[]{:S(2)}) collective-permute-start(bf16[32,5248]{1,0:T(8,128)(2,1)S(1)} %get-tuple-element.147), channel_id=1, source_target_pairs={{0,1},{1,0},{2,3},{3,2},{4,5},{5,4},{6,7},{7,6},{8,9},{9,8},{10,11... | collective-permute-start | bytes 1007624 | tf_op jit(solution)/shard_map/ppermute | solution.py:180

commit v7 on v6

--- a/solution.py
+++ b/solution.py
@@ -13,7 +13,7 @@
 K2 = 256
 CORES = 2
 OUTER = 4
-DEPTH = 1024
+DEPTH = 2560
 LANES = 128
 VMEM_LIMIT = 12 << 20
 
@@ -196,37 +196,51 @@
             move(part, layout.core_swap()) for part in jnp.split(piece, 2, axis=0)
         ]
         after = lax.optimization_barrier
+        first_side = lambda rows_in: forward(
+            rows_in, gate_rows, up_rows, feature_table, unit_tables
+        )
+        other_side = lambda rows_out, saved, total: backward(
+            rows_out, down_weight, feature_table, unit_tables, saved, total
+        )
         last = layout.outer - 1
         here_in, here_out = inputs, tagged
         coming_in = ahead(here_in), aside(here_in)
         here_out, feature_table, unit_tables = after((here_out, feature_table, unit_tables))
         coming_out = ahead(here_out), aside(here_out)
         swapped_in = swap(here_in)
-        for step in range(layout.outer + 1)[1:]:
-            if step <= last:
-                next_in, across_in, total = after((*coming_in, total))
-                coming_in = (ahead(next_in) if step < last else None), aside(next_in)
-            else:
-                across_in, total = after((coming_in[1], total))
+        for step in range(1, last):
+            next_in, across_in, total = after((*coming_in, total))
+            coming_in = ahead(next_in), aside(next_in)
             swapped_across = swap(across_in)
             here_out, swapped_across = after((here_out, swapped_across))
             swapped_out = swap(here_out)
-            pieces = [here_in, *swapped_in, across_in, *swapped_across]
-            saved = forward(pieces, gate_rows, up_rows, feature_table, unit_tables)
-            if step <= last:
-                next_out, across_out, saved = after((*coming_out, saved))
-            else:
-                across_out, saved = after((coming_out[1], saved))
-            if step < last:
-                coming_out = ahead(next_out), aside(next_out)
-            elif step == last:
-                coming_out = None, ahead(across_out)
-            pieces = [here_out, *swapped_out, across_out, *swap(across_out)]
-            total = backward(pieces, down_weight, feature_table, unit_tables, saved, total)
-            if step <= last:
-                here_in, here_out = next_in, next_out
-                here_in, total = after((here_in, total))
-                swapped_in = swap(here_in)
+            saved = first_side([here_in, *swapped_in, across_in, *swapped_across])
+            next_out, across_out, saved = after((*coming_out, saved))
+            by_inner = aside(next_out) if step < last - 1 else ahead(across_out)
+            coming_out = ahead(next_out), by_inner
+            rows_out = [here_out, *swapped_out, across_out, *swap(across_out)]
+            total = other_side(rows_out, saved, total)
+            here_in, total = after((next_in, total))
+            here_out, swapped_in = next_out, swap(here_in)
+
+        last_in, across_in, total = after((*coming_in, total))
+        coming_in = aside(last_in)
+        swapped_last, swapped_across = after((swap(last_in), swap(across_in)))
+        saved = first_side([here_in, *swapped_in, last_in, *swapped_last])
+        last_out, saved = after((coming_out[0], saved))
+        coming_last = aside(last_out)
+        here_out, saved = after((here_out, saved))
+        rows_out = [here_out, *swap(here_out), last_out, *swap(last_out)]
+        corner_in, saved = after((coming_in, saved))
+        swapped_corner = swap(corner_in)
+        total = other_side(rows_out, saved, total)
+        corner_in, total = after((corner_in, total))
+        saved = first_side([across_in, *swapped_across, corner_in, *swapped_corner])
+        across_out, saved = after((coming_out[1], saved))
+        swapped_out = swap(across_out)
+        corner_out, saved = after((coming_last, saved))
+        rows_out = [across_out, *swapped_out, corner_out, *swap(corner_out)]
+        total = other_side(rows_out, saved, total)
     else:
         gather = lambda piece: lax.all_gather(piece, "fsdp", axis=0, tiled=True)
         saved = forward([gather(inputs)], gate_rows, up_rows, feature_table, unit_tables)

time: 139 us -> 139 us (level)
  Pallas kernels: 52.9 us -> 48.1 us
  waiting for transfers between devices: 27 us -> 30.6 us
    pallas_call x8, Pallas kernels: 52.9 us -> 48.1 us  [on_chip(): pl.pallas_call(lambda *refs: kernel(len(pieces), *refs), in_specs=[vmem]...]
    ppermute x46, waiting for transfers between devices: 27 us -> 30.6 us  [move(): return lax.ppermute(value, 'fsdp', pairs)]
  transfers between devices with their start and end apart: 46 -> 46, of which waited for: 22 -> 20; matrix products, arithmetic and copies ran while one was open for 4% -> 4% of each run, Pallas kernels for 34% -> 31%
where the time goes in v7:
time: 139 us; the launch traced here: 138 us
  Pallas kernels  48.1 us (35%)
  waiting for transfers between devices  30.6 us (22%)
  starting transfers between devices  28.7 us (21%)
  blocking collectives  14 us (10%)
  local copies, waits for them, and re-layouts  12.2 us (9%)
  other arithmetic  4.12 us (3%)
    pallas_call x8, Pallas kernels, on_chip(): pl.pallas_call(lambda *refs: kernel(len(pieces), *refs), in_specs=[vmem]...  48.1 us
    ppermute x46, waiting for transfers between devices, move(): return lax.ppermute(value, 'fsdp', pairs)  30.6 us
    ppermute x46, starting transfers between devices, move(): return lax.ppermute(value, 'fsdp', pairs)  28.7 us
    all_to_all x1, blocking collectives, on_device(): parts = lax.all_to_all(parts, 'fsdp', 0, 0)  14 us
    unnamed x30, local copies, waits for them, and re-layouts  10.7 us
  transfers between devices with their start and end apart: 46, of which 20 were waited for; matrix products, arithmetic and copies ran while one was open for 4% of the time, Pallas kernels for 31%

profile of v7, /device:TPU:0, one launch (start us, length us, event | category | flops | bytes accessed | tf_op | source)
XLA Modules:
  0.0 138.2 jit_solution(10190302466205490095)
XLA Ops:
  0.0 3.0 %collective-permute-start.4 = (bf16[64,5120]{1,0:T(8,128)(2,1)}, bf16[64,5120]{1,0:T(8,128)(2,1)S(1)}, u32[]{:S(2)}, u32[]{:S(2)}) collective-permute-start(bf16[64,5120]{1,0:T(8,128)(2,1)} %refs_0_.1), channel_id=1, source_target_pairs={{0,4},{1,13},{2,6},{3,15},{4,8},{5,1},{6,10},{7,3},{8,12},{9,5},{1... | collective-permute-start | bytes 1966088 | tf_op jit(solution)/shard_map/ppermute | solution.py:180
  3.0 1.5 %collective-permute-start.5 = (bf16[64,5120]{1,0:T(8,128)(2,1)}, bf16[64,5120]{1,0:T(8,128)(2,1)S(1)}, u32[]{:S(2)}, u32[]{:S(2)}) collective-permute-start(bf16[64,5120]{1,0:T(8,128)(2,1)} %refs_0_.1), channel_id=1, source_target_pairs={{0,2},{1,3},{2,0},{3,1},{4,6},{5,7},{6,4},{7,5},{8,10},{9,11},{10,... | collective-permute-start | bytes 1966088 | tf_op jit(solution)/shard_map/ppermute | solution.py:180
  4.5 0.7 add_convert_fusion
  5.3 0.7 add_convert_fusion.1
  6.0 0.7 convert_element_type.16
  6.6 1.4 %fusion.refs_8_.refs_7_ = bf16[256,5120]{1,0:T(8,128)(2,1)S(1)} fusion(s32[5120]{0:T(1024)} %param.18, bf16[5120]{0:T(1024)(128)(2,1)S(1)} %add_convert_fusion), kind=kLoop, calls=%fused_computation.1 | loop fusion | flops 2621440 | bytes 2652160 | tf_op jit(solution)/shard_map/jit(_where)/select_n | solution.py:24
  8.1 0.4 fusion.1.refs_9_.refs_8_
  8.7 1.6 %collective-permute-start = (bf16[64,5248]{1,0:T(8,128)(2,1)S(1)}, bf16[64,5248]{1,0:T(8,128)(2,1)S(1)}, u32[]{:S(2)}, u32[]{:S(2)}) collective-permute-start(bf16[64,5248]{1,0:T(8,128)(2,1)S(1)} %pad_maximum_fusion.refs_0_), channel_id=1, source_target_pairs={{0,4},{1,13},{2,6},{3,15},{4,8},{5,1},{6,10},{7,3},{8,12},{9,5},{1... | collective-permute-start | bytes 2015240 | tf_op jit(solution)/shard_map/ppermute | solution.py:180
  10.3 0.5 collective-permute-start.1
  10.8 10.0 %collective-permute-done.4.refs_0_ = bf16[64,5120]{1,0:T(8,128)(2,1)S(1)} collective-permute-done((bf16[64,5120]{1,0:T(8,128)(2,1)}, bf16[64,5120]{1,0:T(8,128)(2,1)S(1)}, u32[]{:S(2)}, u32[]{:S(2)}) %collective-permute-start.4) | collective-permute-done | bytes 655392 | tf_op jit(solution)/shard_map/ppermute | solution.py:180
  20.9 0.8 collective-permute-start.6
  21.8 0.5 collective-permute-start.2
  22.3 0.6 collective-permute-done.6.refs_4_
  22.9 0.4 collective-permute-start.3
  23.4 1.3 collective-permute-start.16
  24.7 1.5 %collective-permute-start.17 = (bf16[64,5120]{1,0:T(8,128)(2,1)S(1)}, bf16[64,5120]{1,0:T(8,128)(2,1)S(1)}, u32[]{:S(2)}, u32[]{:S(2)}) collective-permute-start(bf16[64,5120]{1,0:T(8,128)(2,1)S(1)} %collective-permute-done.4.refs_0_), channel_id=1, source_target_pairs={{0,2},{1,3},{2,0},{3,1},{4,6},{5,7},{6,4},{7,5},{8,10},{9,11},{10,... | collective-permute-start | bytes 1966088 | tf_op jit(solution)/shard_map/ppermute | solution.py:180
  26.2 3.5 %copy-done = bf16[5120,864]{0,1:T(8,128)(2,1)S(1)} copy-done((bf16[5120,864]{0,1:T(8,128)(2,1)S(1)}, bf16[5120,864]{0,1:T(8,128)(2,1)}, u32[]{:S(2)}) %copy-start) | copy-done | bytes 8847384
  29.7 3.5 %copy-done.1 = bf16[5120,864]{0,1:T(8,128)(2,1)S(1)} copy-done((bf16[5120,864]{0,1:T(8,128)(2,1)S(1)}, bf16[5120,864]{0,1:T(8,128)(2,1)}, u32[]{:S(2)}) %copy-start.1) | copy-done | bytes 8847384
  33.2 7.2 %forward.4 = (f32[256,864]{1,0:T(8,128)S(1)}, f32[256,864]{1,0:T(8,128)S(1)}, bf16[256,256]{1,0:T(8,128)(2,1)S(1)}, bf16[256,256]{1,0:T(8,128)(2,1)S(1)}) custom-call(bf16[64,5120]{1,0:T(8,128)(2,1)S(1)} %copy-done.3, bf16[32,5120]{1,0:T(8,128)(2,1)S(1)} %collective-permute-done.2.refs_1_, bf16[32,5120]{1,0:T(8,128)(2,1)S(1)} %collective-permute-done.3.refs_2_, ...), custom_call_target="tpu_custom_call" | custom-call | tf_op jit(solution)/shard_map/forward/pallas_call | solution.py:134
  40.5 0.4 collective-permute-start.12
  41.1 0.4 collective-permute-start.10
  41.5 0.7 collective-permute-done.12.refs_4_
  42.7 1.6 %collective-permute-start.8 = (bf16[64,5248]{1,0:T(8,128)(2,1)S(1)}, bf16[64,5248]{1,0:T(8,128)(2,1)S(1)}, u32[]{:S(2)}, u32[]{:S(2)}) collective-permute-start(bf16[64,5248]{1,0:T(8,128)(2,1)S(1)} %collective-permute-done.refs_0_), channel_id=1, source_target_pairs={{0,4},{1,13},{2,6},{3,15},{4,8},{5,1},{6,10},{7,3},{8,12},{9,5},{1... | collective-permute-start | bytes 2015240 | tf_op jit(solution)/shard_map/ppermute | solution.py:180
  44.3 0.5 collective-permute-start.9
  44.9 3.7 %copy-done.2 = bf16[864,5120]{1,0:T(8,128)(2,1)S(1)} copy-done((bf16[864,5120]{1,0:T(8,128)(2,1)S(1)}, bf16[864,5120]{1,0:T(8,128)(2,1)}, u32[]{:S(2)}) %copy-start.2) | copy-done | bytes 8847384
  48.5 4.8 %backward.4.refs_13_ = f32[256,512]{1,0:T(8,128)S(1)} custom-call(bf16[64,5248]{1,0:T(8,128)(2,1)S(1)} %pad_maximum_fusion.refs_0_, bf16[32,5248]{1,0:T(8,128)(2,1)S(1)} %collective-permute-done.10.refs_1_, bf16[32,5248]{1,0:T(8,128)(2,1)S(1)} %collective-permute-done.11.refs_2_, bf16[64,5248]{1,0:T(8,128)(2,1)S(1)} %collective-permute-done.1.refs_3_, ...), custom_call_target="tpu_custom_call" | custom-call | tf_op jit(solution)/shard_map/backward/pallas_call | solution.py:134
  53.4 0.6 collective-permute-start.18
  54.1 0.5 collective-permute-start.14
  54.6 0.6 collective-permute-done.18.refs_4_
  55.2 0.4 collective-permute-start.15
  55.7 0.5 collective-permute-start.21
  56.3 1.4 %collective-permute-start.22 = (bf16[64,5120]{1,0:T(8,128)(2,1)S(1)}, bf16[64,5120]{1,0:T(8,128)(2,1)S(1)}, u32[]{:S(2)}, u32[]{:S(2)}) collective-permute-start(bf16[64,5120]{1,0:T(8,128)(2,1)S(1)} %collective-permute-done.16.refs_0_), channel_id=1, source_target_pairs={{0,2},{1,3},{2,0},{3,1},{4,6},{5,7},{6,4},{7,5},{8,10},{9,11},{10,... | collective-permute-start | bytes 1966088 | tf_op jit(solution)/shard_map/ppermute | solution.py:180
  57.7 1.4 %collective-permute-start.23 = (bf16[32,5248]{1,0:T(8,128)(2,1)S(1)}, bf16[32,5248]{1,0:T(8,128)(2,1)S(1)}, u32[]{:S(2)}, u32[]{:S(2)}) collective-permute-start(bf16[32,5248]{1,0:T(8,128)(2,1)S(1)} %get-tuple-element.178), channel_id=1, source_target_pairs={{0,1},{1,0},{2,3},{3,2},{4,5},{5,4},{6,7},{7,6},{8,9},{9,8},{10,11... | collective-permute-start | bytes 1007624 | tf_op jit(solution)/shard_map/ppermute | solution.py:180
  59.2 7.2 %forward.5 = (f32[256,864]{1,0:T(8,128)S(1)}, f32[256,864]{1,0:T(8,128)S(1)}, bf16[256,256]{1,0:T(8,128)(2,1)S(1)}, bf16[256,256]{1,0:T(8,128)(2,1)S(1)}) custom-call(bf16[64,5120]{1,0:T(8,128)(2,1)S(1)} %collective-permute-done.4.refs_0_, bf16[32,5120]{1,0:T(8,128)(2,1)S(1)} %collective-permute-done.14.refs_1_, ...), custom_call_target="tpu_custom_call" | custom-call | tf_op jit(solution)/shard_map/forward/pallas_call | solution.py:134
  66.5 0.5 collective-permute-start.25
  67.2 0.9 collective-permute-done.24.refs_2_
  68.1 0.3 collective-permute-start.32
  68.6 0.5 collective-permute-done.26.refs_5_
  69.1 4.8 %backward.5.refs_13_ = f32[256,512]{1,0:T(8,128)S(1)} custom-call(bf16[64,5248]{1,0:T(8,128)(2,1)S(1)} %collective-permute-done.refs_0_, bf16[32,5248]{1,0:T(8,128)(2,1)S(1)} %collective-permute-done.23.refs_1_, bf16[32,5248]{1,0:T(8,128)(2,1)S(1)} %collective-permute-done.24.refs_2_, bf16[64,5248]{1,0:T(8,128)(2,1)S(1)} %collective-permute-done.9.refs_3_, ...), custom_call_target="tpu_custom_call" | custom-call | tf_op jit(solution)/shard_map/backward/pallas_call | solution.py:134
  73.9 3.8 %collective-permute-done.21.refs_3_ = bf16[64,5120]{1,0:T(8,128)(2,1)S(1)} collective-permute-done((bf16[64,5120]{1,0:T(8,128)(2,1)S(1)}, bf16[64,5120]{1,0:T(8,128)(2,1)S(1)}, u32[]{:S(2)}, u32[]{:S(2)}) %collective-permute-start.21) | collective-permute-done | bytes 655392 | tf_op jit(solution)/shard_map/ppermute | solution.py:180
  78.0 0.4 collective-permute-start.28
  78.6 0.4 collective-permute-start.30
  79.0 0.4 collective-permute-done.27.refs_4_
  79.6 0.3 collective-permute-done.28.refs_5_
  80.1 0.3 collective-permute-done.29.refs_1_
  80.4 0.5 collective-permute-done.30.refs_2_
  80.8 1.7 %collective-permute-start.31 = (bf16[64,5120]{1,0:T(8,128)(2,1)S(1)}, bf16[64,5120]{1,0:T(8,128)(2,1)S(1)}, u32[]{:S(2)}, u32[]{:S(2)}) collective-permute-start(bf16[64,5120]{1,0:T(8,128)(2,1)S(1)} %collective-permute-done.21.refs_3_), channel_id=1, source_target_pairs={{0,2},{1,3},{2,0},{3,1},{4,6},{5,7},{6,4},{7,5},{8,10},{9,11},{10,... | collective-permute-start | bytes 1966088 | tf_op jit(solution)/shard_map/ppermute | solution.py:180
  82.6 7.2 %forward.6 = (f32[256,864]{1,0:T(8,128)S(1)}, f32[256,864]{1,0:T(8,128)S(1)}, bf16[256,256]{1,0:T(8,128)(2,1)S(1)}, bf16[256,256]{1,0:T(8,128)(2,1)S(1)}) custom-call(bf16[64,5120]{1,0:T(8,128)(2,1)S(1)} %collective-permute-done.16.refs_0_, bf16[32,5120]{1,0:T(8,128)(2,1)S(1)} %collective-permute-done.33.refs_1_, ...), custom_call_target="tpu_custom_call" | custom-call | tf_op jit(solution)/shard_map/forward/pallas_call | solution.py:134
  89.8 2.3 %collective-permute-done.32.refs_3_ = bf16[64,5248]{1,0:T(8,128)(2,1)S(1)} collective-permute-done((bf16[64,5248]{1,0:T(8,128)(2,1)S(1)}, bf16[64,5248]{1,0:T(8,128)(2,1)S(1)}, u32[]{:S(2)}, u32[]{:S(2)}) %collective-permute-start.32) | collective-permute-done | bytes 671776 | tf_op jit(solution)/shard_map/ppermute | solution.py:180
  92.2 0.5 collective-permute-start.36
  92.9 4.8 %collective-permute-done.31.refs_3_ = bf16[64,5120]{1,0:T(8,128)(2,1)S(1)} collective-permute-done((bf16[64,5120]{1,0:T(8,128)(2,1)S(1)}, bf16[64,5120]{1,0:T(8,128)(2,1)S(1)}, u32[]{:S(2)}, u32[]{:S(2)}) %collective-permute-start.31) | collective-permute-done | bytes 655392 | tf_op jit(solution)/shard_map/ppermute | solution.py:180
  97.7 0.9 collective-permute-start.38
  98.7 0.5 collective-permute-start.40
  99.2 1.7 %collective-permute-start.43 = (bf16[64,5248]{1,0:T(8,128)(2,1)S(1)}, bf16[64,5248]{1,0:T(8,128)(2,1)S(1)}, u32[]{:S(2)}, u32[]{:S(2)}) collective-permute-start(bf16[64,5248]{1,0:T(8,128)(2,1)S(1)} %collective-permute-done.32.refs_3_), channel_id=1, source_target_pairs={{0,2},{1,3},{2,0},{3,1},{4,6},{5,7},{6,4},{7,5},{8,10},{9,11},{10,... | collective-permute-start | bytes 2015240 | tf_op jit(solution)/shard_map/ppermute | solution.py:180
  100.9 4.8 %backward.6.refs_13_ = f32[256,512]{1,0:T(8,128)S(1)} custom-call(bf16[64,5248]{1,0:T(8,128)(2,1)S(1)} %collective-permute-done.8.refs_0_, bf16[32,5248]{1,0:T(8,128)(2,1)S(1)} %collective-permute-done.35.refs_1_, bf16[32,5248]{1,0:T(8,128)(2,1)S(1)} %collective-permute-done.36.refs_2_, bf16[64,5248]{1,0:T(8,128)(2,1)S(1)} %collective-permute-done.32.refs_3_, ...), custom_call_target="tpu_custom_call" | custom-call | tf_op jit(solution)/shard_map/backward/pallas_call | solution.py:134
  105.8 7.2 %forward.7 = (f32[256,864]{1,0:T(8,128)S(1)}, f32[256,864]{1,0:T(8,128)S(1)}, bf16[256,256]{1,0:T(8,128)(2,1)S(1)}, bf16[256,256]{1,0:T(8,128)(2,1)S(1)}) custom-call(bf16[64,5120]{1,0:T(8,128)(2,1)S(1)} %collective-permute-done.22.refs_0_, bf16[32,5120]{1,0:T(8,128)(2,1)S(1)} %collective-permute-done.29.refs_1_, ...), custom_call_target="tpu_custom_call" | custom-call | tf_op jit(solution)/shard_map/forward/pallas_call | solution.py:134
  113.1 0.5 collective-permute-start.42
  113.6 2.6 %collective-permute-done.43.refs_3_ = bf16[64,5248]{1,0:T(8,128)(2,1)S(1)} collective-permute-done((bf16[64,5248]{1,0:T(8,128)(2,1)S(1)}, bf16[64,5248]{1,0:T(8,128)(2,1)S(1)}, u32[]{:S(2)}, u32[]{:S(2)}) %collective-permute-start.43) | collective-permute-done | bytes 671776 | tf_op jit(solution)/shard_map/ppermute | solution.py:180
  116.4 0.5 collective-permute-start.45
  116.9 1.1 collective-permute-done.44.refs_4_
  118.0 0.5 collective-permute-done.45.refs_5_
  118.5 4.9 %backward.7 = f32[256,512]{1,0:T(8,128)S(1)} custom-call(bf16[64,5248]{1,0:T(8,128)(2,1)S(1)} %collective-permute-done.20.refs_0_, bf16[32,5248]{1,0:T(8,128)(2,1)S(1)} %collective-permute-done.41.refs_1_, bf16[32,5248]{1,0:T(8,128)(2,1)S(1)} %collective-permute-done.42.refs_2_, bf16[64,5248]{1,0:T(8,128)(2,1)S(1)} %collective-permute-done.43.refs_3_, ...), custom_call_target="tpu_custom_call" | custom-call | tf_op jit(solution)/shard_map/backward/pallas_call | solution.py:134
  123.4 14.0 %all_to_all.5 = bf16[16,16,512]{2,1,0:T(8,128)(2,1)S(1)} all-to-all(bf16[16,16,512]{2,1,0:T(8,128)(2,1)S(1)} %bitcast.18), channel_id=1, replica_groups=mesh['groups'=2,'fsdp'=16] {'fsdp'}, dimensions={0} | all-to-all | bytes 524288 | tf_op jit(solution)/shard_map/all_to_all | solution.py:250
  137.5 0.6 copy.11
  (99 shorter events, 3.6 us)
Async XLA Ops:
  0.0 8.1 %copy-start.5 = (s32[3,864]{1,0:T(4,128)S(1)}, s32[3,864]{1,0:T(4,128)}, u32[]{:S(2)}) copy-start(s32[3,864]{1,0:T(4,128)} %param.16) | copy-start | bytes 31108
  0.0 8.6 %copy-start.4 = (bf16[64,5120]{1,0:T(8,128)(2,1)S(1)}, bf16[64,5120]{1,0:T(8,128)(2,1)}, u32[]{:S(2)}) copy-start(bf16[64,5120]{1,0:T(8,128)(2,1)} %param.11) | copy-start | bytes 1966084
  0.0 20.8 %collective-permute-start.4 = (bf16[64,5120]{1,0:T(8,128)(2,1)}, bf16[64,5120]{1,0:T(8,128)(2,1)S(1)}, u32[]{:S(2)}, u32[]{:S(2)}) collective-permute-start(bf16[64,5120]{1,0:T(8,128)(2,1)} %refs_0_.1), channel_id=1, source_target_pairs={{0,4},{1,13},{2,6},{3,15},{4,8},{5,1},{6,10},{7,3},{8,12},{9,5},{1... | collective-permute-start | bytes 1966088 | tf_op jit(solution)/shard_map/ppermute | solution.py:180
  3.0 17.8 %collective-permute-start.5 = (bf16[64,5120]{1,0:T(8,128)(2,1)}, bf16[64,5120]{1,0:T(8,128)(2,1)S(1)}, u32[]{:S(2)}, u32[]{:S(2)}) collective-permute-start(bf16[64,5120]{1,0:T(8,128)(2,1)} %refs_0_.1), channel_id=1, source_target_pairs={{0,2},{1,3},{2,0},{3,1},{4,6},{5,7},{6,4},{7,5},{8,10},{9,11},{10,... | collective-permute-start | bytes 1966088 | tf_op jit(solution)/shard_map/ppermute | solution.py:180
  8.1 13.6 %copy-start.3 = (bf16[64,5120]{1,0:T(8,128)(2,1)S(1)}, bf16[64,5120]{1,0:T(8,128)(2,1)}, u32[]{:S(2)}) copy-start(bf16[64,5120]{1,0:T(8,128)(2,1)} %refs_0_.1) | copy-start | bytes 1966084
  8.7 31.7 %collective-permute-start = (bf16[64,5248]{1,0:T(8,128)(2,1)S(1)}, bf16[64,5248]{1,0:T(8,128)(2,1)S(1)}, u32[]{:S(2)}, u32[]{:S(2)}) collective-permute-start(bf16[64,5248]{1,0:T(8,128)(2,1)S(1)} %pad_maximum_fusion.refs_0_), channel_id=1, source_target_pairs={{0,4},{1,13},{2,6},{3,15},{4,8},{5,1},{6,10},{7,3},{8,12},{9,5},{1... | collective-permute-start | bytes 2015240 | tf_op jit(solution)/shard_map/ppermute | solution.py:180
  10.3 30.1 %collective-permute-start.1 = (bf16[64,5248]{1,0:T(8,128)(2,1)S(1)}, bf16[64,5248]{1,0:T(8,128)(2,1)S(1)}, u32[]{:S(2)}, u32[]{:S(2)}) collective-permute-start(bf16[64,5248]{1,0:T(8,128)(2,1)S(1)} %pad_maximum_fusion.refs_0_), channel_id=1, source_target_pairs={{0,2},{1,3},{2,0},{3,1},{4,6},{5,7},{6,4},{7,5},{8,10},{9,11},{10,... | collective-permute-start | bytes 2015240 | tf_op jit(solution)/shard_map/ppermute | solution.py:180
  20.9 2.0 %collective-permute-start.6 = (bf16[32,5120]{1,0:T(8,128)(2,1)S(1)}, bf16[32,5120]{1,0:T(8,128)(2,1)S(1)}, u32[]{:S(2)}, u32[]{:S(2)}) collective-permute-start(bf16[32,5120]{1,0:T(8,128)(2,1)S(1)} %get-tuple-element.196), channel_id=1, source_target_pairs={{0,1},{1,0},{2,3},{3,2},{4,5},{5,4},{6,7},{7,6},{8,9},{9,8},{10,11... | collective-permute-start | bytes 983048 | tf_op jit(solution)/shard_map/ppermute | solution.py:180
  21.6 1.7 %collective-permute-start.7 = (bf16[32,5120]{1,0:T(8,128)(2,1)S(1)}, bf16[32,5120]{1,0:T(8,128)(2,1)S(1)}, u32[]{:S(2)}, u32[]{:S(2)}) collective-permute-start(bf16[32,5120]{1,0:T(8,128)(2,1)S(1)} %get-tuple-element.195), channel_id=1, source_target_pairs={{0,1},{1,0},{2,3},{3,2},{4,5},{5,4},{6,7},{7,6},{8,9},{9,8},{10,11... | collective-permute-start | bytes 983048 | tf_op jit(solution)/shard_map/ppermute | solution.py:180
  21.8 2.9 %collective-permute-start.2 = (bf16[32,5120]{1,0:T(8,128)(2,1)S(1)}, bf16[32,5120]{1,0:T(8,128)(2,1)S(1)}, u32[]{:S(2)}, u32[]{:S(2)}) collective-permute-start(bf16[32,5120]{1,0:T(8,128)(2,1)S(1)} %get-tuple-element.198), channel_id=1, source_target_pairs={{0,1},{1,0},{2,3},{3,2},{4,5},{5,4},{6,7},{7,6},{8,9},{9,8},{10,11... | collective-permute-start | bytes 983048 | tf_op jit(solution)/shard_map/ppermute | solution.py:180
  22.9 3.3 %collective-permute-start.3 = (bf16[32,5120]{1,0:T(8,128)(2,1)S(1)}, bf16[32,5120]{1,0:T(8,128)(2,1)S(1)}, u32[]{:S(2)}, u32[]{:S(2)}) collective-permute-start(bf16[32,5120]{1,0:T(8,128)(2,1)S(1)} %get-tuple-element.197), channel_id=1, source_target_pairs={{0,1},{1,0},{2,3},{3,2},{4,5},{5,4},{6,7},{7,6},{8,9},{9,8},{10,11... | collective-permute-start | bytes 983048 | tf_op jit(solution)/shard_map/ppermute | solution.py:180
  23.4 30.0 %collective-permute-start.16 = (bf16[64,5120]{1,0:T(8,128)(2,1)S(1)}, bf16[64,5120]{1,0:T(8,128)(2,1)S(1)}, u32[]{:S(2)}, u32[]{:S(2)}) collective-permute-start(bf16[64,5120]{1,0:T(8,128)(2,1)S(1)} %collective-permute-done.4.refs_0_), channel_id=1, source_target_pairs={{0,4},{1,13},{2,6},{3,15},{4,8},{5,1},{6,10},{7,3},{8,12},{9,5},{1... | collective-permute-start | bytes 1966088 | tf_op jit(solution)/shard_map/ppermute | solution.py:180
  24.7 28.7 %collective-permute-start.17 = (bf16[64,5120]{1,0:T(8,128)(2,1)S(1)}, bf16[64,5120]{1,0:T(8,128)(2,1)S(1)}, u32[]{:S(2)}, u32[]{:S(2)}) collective-permute-start(bf16[64,5120]{1,0:T(8,128)(2,1)S(1)} %collective-permute-done.4.refs_0_), channel_id=1, source_target_pairs={{0,2},{1,3},{2,0},{3,1},{4,6},{5,7},{6,4},{7,5},{8,10},{9,11},{10,... | collective-permute-start | bytes 1966088 | tf_op jit(solution)/shard_map/ppermute | solution.py:180
  26.2 3.5 %copy-start = (bf16[5120,864]{0,1:T(8,128)(2,1)S(1)}, bf16[5120,864]{0,1:T(8,128)(2,1)}, u32[]{:S(2)}) copy-start(bf16[5120,864]{0,1:T(8,128)(2,1)} %param.13) | copy-start | bytes 26542084
  29.7 3.5 %copy-start.1 = (bf16[5120,864]{0,1:T(8,128)(2,1)S(1)}, bf16[5120,864]{0,1:T(8,128)(2,1)}, u32[]{:S(2)}) copy-start(bf16[5120,864]{0,1:T(8,128)(2,1)} %param.14) | copy-start | bytes 26542084
  33.2 25.9 %slice-start.3 = ((s8[8847360]{0:T(1024)(128)(4,1)}), s8[4194304]{0:T(1024)(128)(4,1)S(1)}, s32[]{:S(2)}) async-start(s8[8847360]{0:T(1024)(128)(4,1)} %bitcast.11), calls=%async_computation.4 | async-start | bytes 8388608
  33.2 25.9 %slice-start.4 = ((s8[8847360]{0:T(1024)(128)(4,1)}), s8[4194304]{0:T(1024)(128)(4,1)S(1)}, s32[]{:S(2)}) async-start(s8[8847360]{0:T(1024)(128)(4,1)} %bitcast.11), calls=%async_computation.5 | async-start | bytes 8388608
  40.5 1.7 %collective-permute-start.12 = (bf16[32,5248]{1,0:T(8,128)(2,1)S(1)}, bf16[32,5248]{1,0:T(8,128)(2,1)S(1)}, u32[]{:S(2)}, u32[]{:S(2)}) collective-permute-start(bf16[32,5248]{1,0:T(8,128)(2,1)S(1)} %get-tuple-element.180), channel_id=1, source_target_pairs={{0,1},{1,0},{2,3},{3,2},{4,5},{5,4},{6,7},{7,6},{8,9},{9,8},{10,11... | collective-permute-start | bytes 1007624 | tf_op jit(solution)/shard_map/ppermute | solution.py:180
  40.9 1.8 %collective-permute-start.13 = (bf16[32,5248]{1,0:T(8,128)(2,1)S(1)}, bf16[32,5248]{1,0:T(8,128)(2,1)S(1)}, u32[]{:S(2)}, u32[]{:S(2)}) collective-permute-start(bf16[32,5248]{1,0:T(8,128)(2,1)S(1)} %get-tuple-element.179), channel_id=1, source_target_pairs={{0,1},{1,0},{2,3},{3,2},{4,5},{5,4},{6,7},{7,6},{8,9},{9,8},{10,11... | collective-permute-start | bytes 1007624 | tf_op jit(solution)/shard_map/ppermute | solution.py:180
  41.1 3.1 %collective-permute-start.10 = (bf16[32,5248]{1,0:T(8,128)(2,1)S(1)}, bf16[32,5248]{1,0:T(8,128)(2,1)S(1)}, u32[]{:S(2)}, u32[]{:S(2)}) collective-permute-start(bf16[32,5248]{1,0:T(8,128)(2,1)S(1)} %get-tuple-element.182), channel_id=1, source_target_pairs={{0,1},{1,0},{2,3},{3,2},{4,5},{5,4},{6,7},{7,6},{8,9},{9,8},{10,11... | collective-permute-start | bytes 1007624 | tf_op jit(solution)/shard_map/ppermute | solution.py:180
  42.2 2.6 %collective-permute-start.11 = (bf16[32,5248]{1,0:T(8,128)(2,1)S(1)}, bf16[32,5248]{1,0:T(8,128)(2,1)S(1)}, u32[]{:S(2)}, u32[]{:S(2)}) collective-permute-start(bf16[32,5248]{1,0:T(8,128)(2,1)S(1)} %get-tuple-element.181), channel_id=1, source_target_pairs={{0,1},{1,0},{2,3},{3,2},{4,5},{5,4},{6,7},{7,6},{8,9},{9,8},{10,11... | collective-permute-start | bytes 1007624 | tf_op jit(solution)/shard_map/ppermute | solution.py:180
  42.7 23.7 %collective-permute-start.8 = (bf16[64,5248]{1,0:T(8,128)(2,1)S(1)}, bf16[64,5248]{1,0:T(8,128)(2,1)S(1)}, u32[]{:S(2)}, u32[]{:S(2)}) collective-permute-start(bf16[64,5248]{1,0:T(8,128)(2,1)S(1)} %collective-permute-done.refs_0_), channel_id=1, source_target_pairs={{0,4},{1,13},{2,6},{3,15},{4,8},{5,1},{6,10},{7,3},{8,12},{9,5},{1... | collective-permute-start | bytes 2015240 | tf_op jit(solution)/shard_map/ppermute | solution.py:180
  44.3 22.2 %collective-permute-start.9 = (bf16[64,5248]{1,0:T(8,128)(2,1)S(1)}, bf16[64,5248]{1,0:T(8,128)(2,1)S(1)}, u32[]{:S(2)}, u32[]{:S(2)}) collective-permute-start(bf16[64,5248]{1,0:T(8,128)(2,1)S(1)} %collective-permute-done.refs_0_), channel_id=1, source_target_pairs={{0,2},{1,3},{2,0},{3,1},{4,6},{5,7},{6,4},{7,5},{8,10},{9,11},{10,... | collective-permute-start | bytes 2015240 | tf_op jit(solution)/shard_map/ppermute | solution.py:180
  44.8 14.3 %slice-start = ((s8[8847360]{0:T(1024)(128)(4,1)}), s8[4194304]{0:T(1024)(128)(4,1)S(1)}, s32[]{:S(2)}) async-start(s8[8847360]{0:T(1024)(128)(4,1)} %bitcast.5), calls=%async_computation.1 | async-start | bytes 8388608
  44.8 3.7 %copy-start.2 = (bf16[864,5120]{1,0:T(8,128)(2,1)S(1)}, bf16[864,5120]{1,0:T(8,128)(2,1)}, u32[]{:S(2)}) copy-start(bf16[864,5120]{1,0:T(8,128)(2,1)} %refs_6_.7) | copy-start | bytes 26542084
  48.5 10.6 %slice-start.1 = ((s8[8847360]{0:T(1024)(128)(4,1)}), s8[4194304]{0:T(1024)(128)(4,1)S(1)}, s32[]{:S(2)}) async-start(s8[8847360]{0:T(1024)(128)(4,1)} %bitcast.5), calls=%async_computation.2 | async-start | bytes 8388608
  48.5 10.6 %slice-start.2 = ((s8[8847360]{0:T(1024)(128)(4,1)}), s8[458752]{0:T(1024)(128)(4,1)S(1)}, s32[]{:S(2)}) async-start(s8[8847360]{0:T(1024)(128)(4,1)} %bitcast.5), calls=%async_computation.3 | async-start | bytes 917504
  48.5 10.6 %slice-start.5 = ((s8[8847360]{0:T(1024)(128)(4,1)}), s8[458752]{0:T(1024)(128)(4,1)S(1)}, s32[]{:S(2)}) async-start(s8[8847360]{0:T(1024)(128)(4,1)} %bitcast.11), calls=%async_computation.6 | async-start | bytes 917504
  53.4 1.8 %collective-permute-start.18 = (bf16[32,5120]{1,0:T(8,128)(2,1)S(1)}, bf16[32,5120]{1,0:T(8,128)(2,1)S(1)}, u32[]{:S(2)}, u32[]{:S(2)}) collective-permute-start(bf16[32,5120]{1,0:T(8,128)(2,1)S(1)} %get-tuple-element.192), channel_id=1, source_target_pairs={{0,1},{1,0},{2,3},{3,2},{4,5},{5,4},{6,7},{7,6},{8,9},{9,8},{10,11... | collective-permute-start | bytes 983048 | tf_op jit(solution)/shard_map/ppermute | solution.py:180
  54.0 1.7 %collective-permute-start.19 = (bf16[32,5120]{1,0:T(8,128)(2,1)S(1)}, bf16[32,5120]{1,0:T(8,128)(2,1)S(1)}, u32[]{:S(2)}, u32[]{:S(2)}) collective-permute-start(bf16[32,5120]{1,0:T(8,128)(2,1)S(1)} %get-tuple-element.191), channel_id=1, source_target_pairs={{0,1},{1,0},{2,3},{3,2},{4,5},{5,4},{6,7},{7,6},{8,9},{9,8},{10,11... | collective-permute-start | bytes 983048 | tf_op jit(solution)/shard_map/ppermute | solution.py:180
  54.1 2.2 %collective-permute-start.14 = (bf16[32,5120]{1,0:T(8,128)(2,1)S(1)}, bf16[32,5120]{1,0:T(8,128)(2,1)S(1)}, u32[]{:S(2)}, u32[]{:S(2)}) collective-permute-start(bf16[32,5120]{1,0:T(8,128)(2,1)S(1)} %get-tuple-element.194), channel_id=1, source_target_pairs={{0,1},{1,0},{2,3},{3,2},{4,5},{5,4},{6,7},{7,6},{8,9},{9,8},{10,11... | collective-permute-start | bytes 983048 | tf_op jit(solution)/shard_map/ppermute | solution.py:180
  55.2 2.5 %collective-permute-start.15 = (bf16[32,5120]{1,0:T(8,128)(2,1)S(1)}, bf16[32,5120]{1,0:T(8,128)(2,1)S(1)}, u32[]{:S(2)}, u32[]{:S(2)}) collective-permute-start(bf16[32,5120]{1,0:T(8,128)(2,1)S(1)} %get-tuple-element.193), channel_id=1, source_target_pairs={{0,1},{1,0},{2,3},{3,2},{4,5},{5,4},{6,7},{7,6},{8,9},{9,8},{10,11... | collective-permute-start | bytes 983048 | tf_op jit(solution)/shard_map/ppermute | solution.py:180
  55.7 22.0 %collective-permute-start.21 = (bf16[64,5120]{1,0:T(8,128)(2,1)S(1)}, bf16[64,5120]{1,0:T(8,128)(2,1)S(1)}, u32[]{:S(2)}, u32[]{:S(2)}) collective-permute-start(bf16[64,5120]{1,0:T(8,128)(2,1)S(1)} %collective-permute-done.16.refs_0_), channel_id=1, source_target_pairs={{0,4},{1,13},{2,6},{3,15},{4,8},{5,1},{6,10},{7,3},{8,12},{9,5},{1... | collective-permute-start | bytes 1966088 | tf_op jit(solution)/shard_map/ppermute | solution.py:180
  56.3 21.4 %collective-permute-start.22 = (bf16[64,5120]{1,0:T(8,128)(2,1)S(1)}, bf16[64,5120]{1,0:T(8,128)(2,1)S(1)}, u32[]{:S(2)}, u32[]{:S(2)}) collective-permute-start(bf16[64,5120]{1,0:T(8,128)(2,1)S(1)} %collective-permute-done.16.refs_0_), channel_id=1, source_target_pairs={{0,2},{1,3},{2,0},{3,1},{4,6},{5,7},{6,4},{7,5},{8,10},{9,11},{10,... | collective-permute-start | bytes 1966088 | tf_op jit(solution)/shard_map/ppermute | solution.py:180
  57.7 11.3 %slice-start.6 = ((s8[8847360]{0:T(1024)(128)(4,1)}), s8[4194304]{0:T(1024)(128)(4,1)S(1)}, s32[]{:S(2)}) async-start(s8[8847360]{0:T(1024)(128)(4,1)} %bitcast.16), calls=%async_computation.7 | async-start | bytes 8388608
  57.7 11.3 %slice-start.7 = ((s8[8847360]{0:T(1024)(128)(4,1)}), s8[4194304]{0:T(1024)(128)(4,1)S(1)}, s32[]{:S(2)}) async-start(s8[8847360]{0:T(1024)(128)(4,1)} %bitcast.16), calls=%async_computation.8 | async-start | bytes 8388608
  57.7 11.3 %slice-start.8 = ((s8[8847360]{0:T(1024)(128)(4,1)}), s8[458752]{0:T(1024)(128)(4,1)S(1)}, s32[]{:S(2)}) async-start(s8[8847360]{0:T(1024)(128)(4,1)} %bitcast.16), calls=%async_computation.9 | async-start | bytes 917504
  57.7 9.4 %collective-permute-start.23 = (bf16[32,5248]{1,0:T(8,128)(2,1)S(1)}, bf16[32,5248]{1,0:T(8,128)(2,1)S(1)}, u32[]{:S(2)}, u32[]{:S(2)}) collective-permute-start(bf16[32,5248]{1,0:T(8,128)(2,1)S(1)} %get-tuple-element.178), channel_id=1, source_target_pairs={{0,1},{1,0},{2,3},{3,2},{4,5},{5,4},{6,7},{7,6},{8,9},{9,8},{10,11... | collective-permute-start | bytes 1007624 | tf_op jit(solution)/shard_map/ppermute | solution.py:180
  66.4 1.7 %collective-permute-start.24 = (bf16[32,5248]{1,0:T(8,128)(2,1)S(1)}, bf16[32,5248]{1,0:T(8,128)(2,1)S(1)}, u32[]{:S(2)}, u32[]{:S(2)}) collective-permute-start(bf16[32,5248]{1,0:T(8,128)(2,1)S(1)} %get-tuple-element.177), channel_id=1, source_target_pairs={{0,1},{1,0},{2,3},{3,2},{4,5},{5,4},{6,7},{7,6},{8,9},{9,8},{10,11... | collective-permute-start | bytes 1007624 | tf_op jit(solution)/shard_map/ppermute | solution.py:180
  66.5 2.0 %collective-permute-start.25 = (bf16[32,5248]{1,0:T(8,128)(2,1)S(1)}, bf16[32,5248]{1,0:T(8,128)(2,1)S(1)}, u32[]{:S(2)}, u32[]{:S(2)}) collective-permute-start(bf16[32,5248]{1,0:T(8,128)(2,1)S(1)} %get-tuple-element.176), channel_id=1, source_target_pairs={{0,1},{1,0},{2,3},{3,2},{4,5},{5,4},{6,7},{7,6},{8,9},{9,8},{10,11... | collective-permute-start | bytes 1007624 | tf_op jit(solution)/shard_map/ppermute | solution.py:180
  67.1 2.0 %collective-permute-start.26 = (bf16[32,5248]{1,0:T(8,128)(2,1)S(1)}, bf16[32,5248]{1,0:T(8,128)(2,1)S(1)}, u32[]{:S(2)}, u32[]{:S(2)}) collective-permute-start(bf16[32,5248]{1,0:T(8,128)(2,1)S(1)} %get-tuple-element.175), channel_id=1, source_target_pairs={{0,1},{1,0},{2,3},{3,2},{4,5},{5,4},{6,7},{7,6},{8,9},{9,8},{10,11... | collective-permute-start | bytes 1007624 | tf_op jit(solution)/shard_map/ppermute | solution.py:180
  68.1 24.0 %collective-permute-start.32 = (bf16[64,5248]{1,0:T(8,128)(2,1)S(1)}, bf16[64,5248]{1,0:T(8,128)(2,1)S(1)}, u32[]{:S(2)}, u32[]{:S(2)}) collective-permute-start(bf16[64,5248]{1,0:T(8,128)(2,1)S(1)} %collective-permute-done.8.refs_0_), channel_id=1, source_target_pairs={{0,4},{1,13},{2,6},{3,15},{4,8},{5,1},{6,10},{7,3},{8,12},{9,5},{1... | collective-permute-start | bytes 2015240 | tf_op jit(solution)/shard_map/ppermute | solution.py:180
  77.7 1.7 %collective-permute-start.27 = (bf16[32,5120]{1,0:T(8,128)(2,1)S(1)}, bf16[32,5120]{1,0:T(8,128)(2,1)S(1)}, u32[]{:S(2)}, u32[]{:S(2)}) collective-permute-start(bf16[32,5120]{1,0:T(8,128)(2,1)S(1)} %get-tuple-element.190), channel_id=1, source_target_pairs={{0,1},{1,0},{2,3},{3,2},{4,5},{5,4},{6,7},{7,6},{8,9},{9,8},{10,11... | collective-permute-start | bytes 983048 | tf_op jit(solution)/shard_map/ppermute | solution.py:180
  78.0 1.9 %collective-permute-start.28 = (bf16[32,5120]{1,0:T(8,128)(2,1)S(1)}, bf16[32,5120]{1,0:T(8,128)(2,1)S(1)}, u32[]{:S(2)}, u32[]{:S(2)}) collective-permute-start(bf16[32,5120]{1,0:T(8,128)(2,1)S(1)} %get-tuple-element.189), channel_id=1, source_target_pairs={{0,1},{1,0},{2,3},{3,2},{4,5},{5,4},{6,7},{7,6},{8,9},{9,8},{10,11... | collective-permute-start | bytes 983048 | tf_op jit(solution)/shard_map/ppermute | solution.py:180
  78.4 2.0 %collective-permute-start.29 = (bf16[32,5120]{1,0:T(8,128)(2,1)S(1)}, bf16[32,5120]{1,0:T(8,128)(2,1)S(1)}, u32[]{:S(2)}, u32[]{:S(2)}) collective-permute-start(bf16[32,5120]{1,0:T(8,128)(2,1)S(1)} %get-tuple-element.188), channel_id=1, source_target_pairs={{0,1},{1,0},{2,3},{3,2},{4,5},{5,4},{6,7},{7,6},{8,9},{9,8},{10,11... | collective-permute-start | bytes 983048 | tf_op jit(solution)/shard_map/ppermute | solution.py:180
  78.6 2.3 %collective-permute-start.30 = (bf16[32,5120]{1,0:T(8,128)(2,1)S(1)}, bf16[32,5120]{1,0:T(8,128)(2,1)S(1)}, u32[]{:S(2)}, u32[]{:S(2)}) collective-permute-start(bf16[32,5120]{1,0:T(8,128)(2,1)S(1)} %get-tuple-element.187), channel_id=1, source_target_pairs={{0,1},{1,0},{2,3},{3,2},{4,5},{5,4},{6,7},{7,6},{8,9},{9,8},{10,11... | collective-permute-start | bytes 983048 | tf_op jit(solution)/shard_map/ppermute | solution.py:180
  79.4 3.1 %collective-permute-start.33 = (bf16[32,5120]{1,0:T(8,128)(2,1)S(1)}, bf16[32,5120]{1,0:T(8,128)(2,1)S(1)}, u32[]{:S(2)}, u32[]{:S(2)}) collective-permute-start(bf16[32,5120]{1,0:T(8,128)(2,1)S(1)} %get-tuple-element.186), channel_id=1, source_target_pairs={{0,1},{1,0},{2,3},{3,2},{4,5},{5,4},{6,7},{7,6},{8,9},{9,8},{10,11... | collective-permute-start | bytes 983048 | tf_op jit(solution)/shard_map/ppermute | solution.py:180
  79.9 2.7 %collective-permute-start.34 = (bf16[32,5120]{1,0:T(8,128)(2,1)S(1)}, bf16[32,5120]{1,0:T(8,128)(2,1)S(1)}, u32[]{:S(2)}, u32[]{:S(2)}) collective-permute-start(bf16[32,5120]{1,0:T(8,128)(2,1)S(1)} %get-tuple-element.185), channel_id=1, source_target_pairs={{0,1},{1,0},{2,3},{3,2},{4,5},{5,4},{6,7},{7,6},{8,9},{9,8},{10,11... | collective-permute-start | bytes 983048 | tf_op jit(solution)/shard_map/ppermute | solution.py:180
  80.4 32.6 %collective-permute-start.20 = (bf16[64,5248]{1,0:T(8,128)(2,1)S(1)}, bf16[64,5248]{1,0:T(8,128)(2,1)S(1)}, u32[]{:S(2)}, u32[]{:S(2)}) collective-permute-start(bf16[64,5248]{1,0:T(8,128)(2,1)S(1)} %collective-permute-done.9.refs_3_), channel_id=1, source_target_pairs={{0,4},{1,13},{2,6},{3,15},{4,8},{5,1},{6,10},{7,3},{8,12},{9,5},{1... | collective-permute-start | bytes 2015240 | tf_op jit(solution)/shard_map/ppermute | solution.py:180
  80.8 16.8 %collective-permute-start.31 = (bf16[64,5120]{1,0:T(8,128)(2,1)S(1)}, bf16[64,5120]{1,0:T(8,128)(2,1)S(1)}, u32[]{:S(2)}, u32[]{:S(2)}) collective-permute-start(bf16[64,5120]{1,0:T(8,128)(2,1)S(1)} %collective-permute-done.21.refs_3_), channel_id=1, source_target_pairs={{0,2},{1,3},{2,0},{3,1},{4,6},{5,7},{6,4},{7,5},{8,10},{9,11},{10,... | collective-permute-start | bytes 1966088 | tf_op jit(solution)/shard_map/ppermute | solution.py:180
  92.1 6.5 %collective-permute-start.35 = (bf16[32,5248]{1,0:T(8,128)(2,1)S(1)}, bf16[32,5248]{1,0:T(8,128)(2,1)S(1)}, u32[]{:S(2)}, u32[]{:S(2)}) collective-permute-start(bf16[32,5248]{1,0:T(8,128)(2,1)S(1)} %get-tuple-element.174), channel_id=1, source_target_pairs={{0,1},{1,0},{2,3},{3,2},{4,5},{5,4},{6,7},{7,6},{8,9},{9,8},{10,11... | collective-permute-start | bytes 1007624 | tf_op jit(solution)/shard_map/ppermute | solution.py:180
  92.2 6.5 %collective-permute-start.36 = (bf16[32,5248]{1,0:T(8,128)(2,1)S(1)}, bf16[32,5248]{1,0:T(8,128)(2,1)S(1)}, u32[]{:S(2)}, u32[]{:S(2)}) collective-permute-start(bf16[32,5248]{1,0:T(8,128)(2,1)S(1)} %get-tuple-element.173), channel_id=1, source_target_pairs={{0,1},{1,0},{2,3},{3,2},{4,5},{5,4},{6,7},{7,6},{8,9},{9,8},{10,11... | collective-permute-start | bytes 1007624 | tf_op jit(solution)/shard_map/ppermute | solution.py:180
  92.8 6.4 %collective-permute-start.37 = (bf16[32,5248]{1,0:T(8,128)(2,1)S(1)}, bf16[32,5248]{1,0:T(8,128)(2,1)S(1)}, u32[]{:S(2)}, u32[]{:S(2)}) collective-permute-start(bf16[32,5248]{1,0:T(8,128)(2,1)S(1)} %get-tuple-element.172), channel_id=1, source_target_pairs={{0,1},{1,0},{2,3},{3,2},{4,5},{5,4},{6,7},{7,6},{8,9},{9,8},{10,11... | collective-permute-start | bytes 1007624 | tf_op jit(solution)/shard_map/ppermute | solution.py:180
  97.7 3.3 %collective-permute-start.38 = (bf16[32,5248]{1,0:T(8,128)(2,1)S(1)}, bf16[32,5248]{1,0:T(8,128)(2,1)S(1)}, u32[]{:S(2)}, u32[]{:S(2)}) collective-permute-start(bf16[32,5248]{1,0:T(8,128)(2,1)S(1)} %get-tuple-element.171), channel_id=1, source_target_pairs={{0,1},{1,0},{2,3},{3,2},{4,5},{5,4},{6,7},{7,6},{8,9},{9,8},{10,11... | collective-permute-start | bytes 1007624 | tf_op jit(solution)/shard_map/ppermute | solution.py:180
  98.6 7.2 %collective-permute-start.39 = (bf16[32,5120]{1,0:T(8,128)(2,1)S(1)}, bf16[32,5120]{1,0:T(8,128)(2,1)S(1)}, u32[]{:S(2)}, u32[]{:S(2)}) collective-permute-start(bf16[32,5120]{1,0:T(8,128)(2,1)S(1)} %get-tuple-element.184), channel_id=1, source_target_pairs={{0,1},{1,0},{2,3},{3,2},{4,5},{5,4},{6,7},{7,6},{8,9},{9,8},{10,11... | collective-permute-start | bytes 983048 | tf_op jit(solution)/shard_map/ppermute | solution.py:180
  98.7 7.1 %collective-permute-start.40 = (bf16[32,5120]{1,0:T(8,128)(2,1)S(1)}, bf16[32,5120]{1,0:T(8,128)(2,1)S(1)}, u32[]{:S(2)}, u32[]{:S(2)}) collective-permute-start(bf16[32,5120]{1,0:T(8,128)(2,1)S(1)} %get-tuple-element.183), channel_id=1, source_target_pairs={{0,1},{1,0},{2,3},{3,2},{4,5},{5,4},{6,7},{7,6},{8,9},{9,8},{10,11... | collective-permute-start | bytes 983048 | tf_op jit(solution)/shard_map/ppermute | solution.py:180
  99.2 17.1 %collective-permute-start.43 = (bf16[64,5248]{1,0:T(8,128)(2,1)S(1)}, bf16[64,5248]{1,0:T(8,128)(2,1)S(1)}, u32[]{:S(2)}, u32[]{:S(2)}) collective-permute-start(bf16[64,5248]{1,0:T(8,128)(2,1)S(1)} %collective-permute-done.32.refs_3_), channel_id=1, source_target_pairs={{0,2},{1,3},{2,0},{3,1},{4,6},{5,7},{6,4},{7,5},{8,10},{9,11},{10,... | collective-permute-start | bytes 2015240 | tf_op jit(solution)/shard_map/ppermute | solution.py:180
  113.1 3.8 %collective-permute-start.41 = (bf16[32,5248]{1,0:T(8,128)(2,1)S(1)}, bf16[32,5248]{1,0:T(8,128)(2,1)S(1)}, u32[]{:S(2)}, u32[]{:S(2)}) collective-permute-start(bf16[32,5248]{1,0:T(8,128)(2,1)S(1)} %get-tuple-element.170), channel_id=1, source_target_pairs={{0,1},{1,0},{2,3},{3,2},{4,5},{5,4},{6,7},{7,6},{8,9},{9,8},{10,11... | collective-permute-start | bytes 1007624 | tf_op jit(solution)/shard_map/ppermute | solution.py:180
  113.1 3.8 %collective-permute-start.42 = (bf16[32,5248]{1,0:T(8,128)(2,1)S(1)}, bf16[32,5248]{1,0:T(8,128)(2,1)S(1)}, u32[]{:S(2)}, u32[]{:S(2)}) collective-permute-start(bf16[32,5248]{1,0:T(8,128)(2,1)S(1)} %get-tuple-element.169), channel_id=1, source_target_pairs={{0,1},{1,0},{2,3},{3,2},{4,5},{5,4},{6,7},{7,6},{8,9},{9,8},{10,11... | collective-permute-start | bytes 1007624 | tf_op jit(solution)/shard_map/ppermute | solution.py:180
  116.3 1.7 %collective-permute-start.44 = (bf16[32,5248]{1,0:T(8,128)(2,1)S(1)}, bf16[32,5248]{1,0:T(8,128)(2,1)S(1)}, u32[]{:S(2)}, u32[]{:S(2)}) collective-permute-start(bf16[32,5248]{1,0:T(8,128)(2,1)S(1)} %get-tuple-element.168), channel_id=1, source_target_pairs={{0,1},{1,0},{2,3},{3,2},{4,5},{5,4},{6,7},{7,6},{8,9},{9,8},{10,11... | collective-permute-start | bytes 1007624 | tf_op jit(solution)/shard_map/ppermute | solution.py:180
  116.4 2.1 %collective-permute-start.45 = (bf16[32,5248]{1,0:T(8,128)(2,1)S(1)}, bf16[32,5248]{1,0:T(8,128)(2,1)S(1)}, u32[]{:S(2)}, u32[]{:S(2)}) collective-permute-start(bf16[32,5248]{1,0:T(8,128)(2,1)S(1)} %get-tuple-element.167), channel_id=1, source_target_pairs={{0,1},{1,0},{2,3},{3,2},{4,5},{5,4},{6,7},{7,6},{8,9},{9,8},{10,11... | collective-permute-start | bytes 1007624 | tf_op jit(solution)/shard_map/ppermute | solution.py:180

commit v8 on v7

--- a/solution.py
+++ b/solution.py
@@ -189,11 +189,11 @@
     gate_rows, up_rows = gate_weight.T, up_weight.T
     total = jnp.zeros((K1, EX * K2), jnp.float32)
 
-    if layout.inner == 2:
+    if layout.inner == 2 and layout.outer > 2:
         ahead = lambda piece: move(piece, layout.outer_ring())
         aside = lambda piece: move(piece, layout.inner_ring())
-        swap = lambda piece: [
-            move(part, layout.core_swap()) for part in jnp.split(piece, 2, axis=0)
+        swap = lambda piece, parts=2: [
+            move(part, layout.core_swap()) for part in jnp.split(piece, parts, axis=0)
         ]
         after = lax.optimization_barrier
         first_side = lambda rows_in: forward(
@@ -219,6 +219,9 @@
             by_inner = aside(next_out) if step < last - 1 else ahead(across_out)
             coming_out = ahead(next_out), by_inner
             rows_out = [here_out, *swapped_out, across_out, *swap(across_out)]
+            if step == last - 1:
+                next_out, saved = after((next_out, saved))
+                swapped_here, saved = after((swap(next_out), saved))
             total = other_side(rows_out, saved, total)
             here_in, total = after((next_in, total))
             here_out, swapped_in = next_out, swap(here_in)
@@ -229,16 +232,13 @@
         saved = first_side([here_in, *swapped_in, last_in, *swapped_last])
         last_out, saved = after((coming_out[0], saved))
         coming_last = aside(last_out)
-        here_out, saved = after((here_out, saved))
-        rows_out = [here_out, *swap(here_out), last_out, *swap(last_out)]
-        corner_in, saved = after((coming_in, saved))
-        swapped_corner = swap(corner_in)
+        rows_out = [here_out, *swapped_here, last_out, *swap(last_out)]
         total = other_side(rows_out, saved, total)
-        corner_in, total = after((corner_in, total))
+        corner_in = coming_in
+        swapped_corner = swap(corner_in, 1)
         saved = first_side([across_in, *swapped_across, corner_in, *swapped_corner])
-        across_out, saved = after((coming_out[1], saved))
+        across_out, corner_out, total, saved = after((coming_out[1], coming_last, total, saved))
         swapped_out = swap(across_out)
-        corner_out, saved = after((coming_last, saved))
         rows_out = [across_out, *swapped_out, corner_out, *swap(corner_out)]
         total = other_side(rows_out, saved, total)
     else:

time: 139 us -> 133 us (0.957)
  waiting for transfers between devices: 30.6 us -> 26.4 us
  starting transfers between devices: 28.7 us -> 27.1 us
    ppermute x46 -> x45, waiting for transfers between devices: 30.6 us -> 26.4 us  [move(): return lax.ppermute(value, 'fsdp', pairs)]
    ppermute x46 -> x45, starting transfers between devices: 28.7 us -> 27.1 us  [move(): return lax.ppermute(value, 'fsdp', pairs)]
  transfers between devices with their start and end apart: 46 -> 45, of which waited for: 20 -> 27; matrix products, arithmetic and copies ran while one was open for 4% -> 4% of each run, Pallas kernels for 31% -> 33%
where the time goes in v8:
time: 133 us
  Pallas kernels  48.3 us (36%)
  starting transfers between devices  27.1 us (20%)
  waiting for transfers between devices  26.4 us (20%)
  blocking collectives  14.2 us (11%)
  local copies, waits for them, and re-layouts  12.2 us (9%)
  other arithmetic  4.12 us (3%)
    pallas_call x8, Pallas kernels, on_chip(): pl.pallas_call(lambda *refs: kernel(len(pieces), *refs), in_specs=[vmem]...  48.3 us
    ppermute x45, starting transfers between devices, move(): return lax.ppermute(value, 'fsdp', pairs)  27.1 us
    ppermute x45, waiting for transfers between devices, move(): return lax.ppermute(value, 'fsdp', pairs)  26.4 us
    all_to_all x1, blocking collectives, on_device(): parts = lax.all_to_all(parts, 'fsdp', 0, 0)  14.2 us
    unnamed x30, local copies, waits for them, and re-layouts  10.7 us
  transfers between devices with their start and end apart: 45, of which 27 were waited for; matrix products, arithmetic and copies ran while one was open for 4% of the time, Pallas kernels for 33%

profile of v8, /device:TPU:0, one launch (start us, length us, event | category | flops | bytes accessed | tf_op | source)
XLA Modules:
  0.0 132.7 jit_solution(6220727819595920709)
XLA Ops:
  0.0 3.0 %collective-permute-start.4 = (bf16[64,5120]{1,0:T(8,128)(2,1)}, bf16[64,5120]{1,0:T(8,128)(2,1)S(1)}, u32[]{:S(2)}, u32[]{:S(2)}) collective-permute-start(bf16[64,5120]{1,0:T(8,128)(2,1)} %refs_0_.1), channel_id=1, source_target_pairs={{0,4},{1,13},{2,6},{3,15},{4,8},{5,1},{6,10},{7,3},{8,12},{9,5},{1... | collective-permute-start | bytes 1966088 | tf_op jit(solution)/shard_map/ppermute | solution.py:180
  3.0 1.5 %collective-permute-start.5 = (bf16[64,5120]{1,0:T(8,128)(2,1)}, bf16[64,5120]{1,0:T(8,128)(2,1)S(1)}, u32[]{:S(2)}, u32[]{:S(2)}) collective-permute-start(bf16[64,5120]{1,0:T(8,128)(2,1)} %refs_0_.1), channel_id=1, source_target_pairs={{0,2},{1,3},{2,0},{3,1},{4,6},{5,7},{6,4},{7,5},{8,10},{9,11},{10,... | collective-permute-start | bytes 1966088 | tf_op jit(solution)/shard_map/ppermute | solution.py:180
  4.5 0.7 convert_element_type.16
  5.2 0.7 add_convert_fusion
  5.9 0.7 add_convert_fusion.1
  6.6 1.4 %fusion.refs_8_.refs_7_ = bf16[256,5120]{1,0:T(8,128)(2,1)S(1)} fusion(s32[5120]{0:T(1024)} %param.18, bf16[5120]{0:T(1024)(128)(2,1)S(1)} %add_convert_fusion), kind=kLoop, calls=%fused_computation.1 | loop fusion | flops 2621440 | bytes 2652160 | tf_op jit(solution)/shard_map/jit(_where)/select_n | solution.py:24
  8.1 0.4 fusion.1.refs_9_.refs_8_
  8.7 1.6 %collective-permute-start = (bf16[64,5248]{1,0:T(8,128)(2,1)S(1)}, bf16[64,5248]{1,0:T(8,128)(2,1)S(1)}, u32[]{:S(2)}, u32[]{:S(2)}) collective-permute-start(bf16[64,5248]{1,0:T(8,128)(2,1)S(1)} %pad_maximum_fusion.refs_0_), channel_id=1, source_target_pairs={{0,4},{1,13},{2,6},{3,15},{4,8},{5,1},{6,10},{7,3},{8,12},{9,5},{1... | collective-permute-start | bytes 2015240 | tf_op jit(solution)/shard_map/ppermute | solution.py:180
  10.3 0.5 collective-permute-start.1
  10.8 10.0 %collective-permute-done.4.refs_0_ = bf16[64,5120]{1,0:T(8,128)(2,1)S(1)} collective-permute-done((bf16[64,5120]{1,0:T(8,128)(2,1)}, bf16[64,5120]{1,0:T(8,128)(2,1)S(1)}, u32[]{:S(2)}, u32[]{:S(2)}) %collective-permute-start.4) | collective-permute-done | bytes 655392 | tf_op jit(solution)/shard_map/ppermute | solution.py:180
  20.9 0.8 collective-permute-start.6
  21.8 0.5 collective-permute-start.2
  22.3 0.6 collective-permute-done.6.refs_4_
  22.9 0.4 collective-permute-start.3
  23.4 1.3 %collective-permute-start.16 = (bf16[64,5120]{1,0:T(8,128)(2,1)S(1)}, bf16[64,5120]{1,0:T(8,128)(2,1)S(1)}, u32[]{:S(2)}, u32[]{:S(2)}) collective-permute-start(bf16[64,5120]{1,0:T(8,128)(2,1)S(1)} %collective-permute-done.4.refs_0_), channel_id=1, source_target_pairs={{0,4},{1,13},{2,6},{3,15},{4,8},{5,1},{6,10},{7,3},{8,12},{9,5},{1... | collective-permute-start | bytes 1966088 | tf_op jit(solution)/shard_map/ppermute | solution.py:180
  24.7 1.5 %collective-permute-start.17 = (bf16[64,5120]{1,0:T(8,128)(2,1)S(1)}, bf16[64,5120]{1,0:T(8,128)(2,1)S(1)}, u32[]{:S(2)}, u32[]{:S(2)}) collective-permute-start(bf16[64,5120]{1,0:T(8,128)(2,1)S(1)} %collective-permute-done.4.refs_0_), channel_id=1, source_target_pairs={{0,2},{1,3},{2,0},{3,1},{4,6},{5,7},{6,4},{7,5},{8,10},{9,11},{10,... | collective-permute-start | bytes 1966088 | tf_op jit(solution)/shard_map/ppermute | solution.py:180
  26.2 3.5 %copy-done = bf16[5120,864]{0,1:T(8,128)(2,1)S(1)} copy-done((bf16[5120,864]{0,1:T(8,128)(2,1)S(1)}, bf16[5120,864]{0,1:T(8,128)(2,1)}, u32[]{:S(2)}) %copy-start) | copy-done | bytes 8847384
  29.7 3.5 %copy-done.1 = bf16[5120,864]{0,1:T(8,128)(2,1)S(1)} copy-done((bf16[5120,864]{0,1:T(8,128)(2,1)S(1)}, bf16[5120,864]{0,1:T(8,128)(2,1)}, u32[]{:S(2)}) %copy-start.1) | copy-done | bytes 8847384
  33.2 7.2 %forward.4 = (f32[256,864]{1,0:T(8,128)S(1)}, f32[256,864]{1,0:T(8,128)S(1)}, bf16[256,256]{1,0:T(8,128)(2,1)S(1)}, bf16[256,256]{1,0:T(8,128)(2,1)S(1)}) custom-call(bf16[64,5120]{1,0:T(8,128)(2,1)S(1)} %copy-done.3, bf16[32,5120]{1,0:T(8,128)(2,1)S(1)} %collective-permute-done.2.refs_1_, bf16[32,5120]{1,0:T(8,128)(2,1)S(1)} %collective-permute-done.3.refs_2_, ...), custom_call_target="tpu_custom_call" | custom-call | tf_op jit(solution)/shard_map/forward/pallas_call | solution.py:134
  40.5 0.4 collective-permute-start.10
  41.1 0.4 collective-permute-start.12
  41.5 0.7 collective-permute-done.10.refs_1_
  42.7 1.6 %collective-permute-start.8 = (bf16[64,5248]{1,0:T(8,128)(2,1)S(1)}, bf16[64,5248]{1,0:T(8,128)(2,1)S(1)}, u32[]{:S(2)}, u32[]{:S(2)}) collective-permute-start(bf16[64,5248]{1,0:T(8,128)(2,1)S(1)} %collective-permute-done.refs_0_), channel_id=1, source_target_pairs={{0,4},{1,13},{2,6},{3,15},{4,8},{5,1},{6,10},{7,3},{8,12},{9,5},{1... | collective-permute-start | bytes 2015240 | tf_op jit(solution)/shard_map/ppermute | solution.py:180
  44.3 0.5 collective-permute-start.9
  44.9 3.7 %copy-done.2 = bf16[864,5120]{1,0:T(8,128)(2,1)S(1)} copy-done((bf16[864,5120]{1,0:T(8,128)(2,1)S(1)}, bf16[864,5120]{1,0:T(8,128)(2,1)}, u32[]{:S(2)}) %copy-start.2) | copy-done | bytes 8847384
  48.5 4.8 %backward.4.refs_13_ = f32[256,512]{1,0:T(8,128)S(1)} custom-call(bf16[64,5248]{1,0:T(8,128)(2,1)S(1)} %pad_maximum_fusion.refs_0_, bf16[32,5248]{1,0:T(8,128)(2,1)S(1)} %collective-permute-done.10.refs_1_, bf16[32,5248]{1,0:T(8,128)(2,1)S(1)} %collective-permute-done.11.refs_2_, bf16[64,5248]{1,0:T(8,128)(2,1)S(1)} %collective-permute-done.1.refs_3_, ...), custom_call_target="tpu_custom_call" | custom-call | tf_op jit(solution)/shard_map/backward/pallas_call | solution.py:134
  53.4 0.6 collective-permute-start.18
  54.1 0.5 collective-permute-start.14
  54.6 0.6 collective-permute-done.18.refs_4_
  55.2 0.4 collective-permute-start.15
  55.7 0.5 collective-permute-start.30
  56.3 1.4 %collective-permute-start.31 = (bf16[64,5120]{1,0:T(8,128)(2,1)S(1)}, bf16[64,5120]{1,0:T(8,128)(2,1)S(1)}, u32[]{:S(2)}, u32[]{:S(2)}) collective-permute-start(bf16[64,5120]{1,0:T(8,128)(2,1)S(1)} %collective-permute-done.16.refs_0_), channel_id=1, source_target_pairs={{0,2},{1,3},{2,0},{3,1},{4,6},{5,7},{6,4},{7,5},{8,10},{9,11},{10,... | collective-permute-start | bytes 1966088 | tf_op jit(solution)/shard_map/ppermute | solution.py:180
  57.7 1.4 %collective-permute-start.22 = (bf16[32,5248]{1,0:T(8,128)(2,1)S(1)}, bf16[32,5248]{1,0:T(8,128)(2,1)S(1)}, u32[]{:S(2)}, u32[]{:S(2)}) collective-permute-start(bf16[32,5248]{1,0:T(8,128)(2,1)S(1)} %get-tuple-element.170), channel_id=1, source_target_pairs={{0,1},{1,0},{2,3},{3,2},{4,5},{5,4},{6,7},{7,6},{8,9},{9,8},{10,11... | collective-permute-start | bytes 1007624 | tf_op jit(solution)/shard_map/ppermute | solution.py:180
  59.2 7.2 %forward.5 = (f32[256,864]{1,0:T(8,128)S(1)}, f32[256,864]{1,0:T(8,128)S(1)}, bf16[256,256]{1,0:T(8,128)(2,1)S(1)}, bf16[256,256]{1,0:T(8,128)(2,1)S(1)}) custom-call(bf16[64,5120]{1,0:T(8,128)(2,1)S(1)} %collective-permute-done.4.refs_0_, bf16[32,5120]{1,0:T(8,128)(2,1)S(1)} %collective-permute-done.14.refs_1_, ...), custom_call_target="tpu_custom_call" | custom-call | tf_op jit(solution)/shard_map/forward/pallas_call | solution.py:134
  66.5 0.5 collective-permute-start.27
  67.2 0.9 collective-permute-done.26.refs_1_
  69.4 0.3 collective-permute-done.24.refs_4_
  69.8 0.5 collective-permute-done.25.refs_5_
  70.3 4.9 %backward.5.refs_13_ = f32[256,512]{1,0:T(8,128)S(1)} custom-call(bf16[64,5248]{1,0:T(8,128)(2,1)S(1)} %collective-permute-done.refs_0_, bf16[32,5248]{1,0:T(8,128)(2,1)S(1)} %collective-permute-done.22.refs_1_, bf16[32,5248]{1,0:T(8,128)(2,1)S(1)} %collective-permute-done.23.refs_2_, bf16[64,5248]{1,0:T(8,128)(2,1)S(1)} %collective-permute-done.9.refs_3_, ...), custom_call_target="tpu_custom_call" | custom-call | tf_op jit(solution)/shard_map/backward/pallas_call | solution.py:134
  75.2 2.5 %collective-permute-done.30.refs_3_ = bf16[64,5120]{1,0:T(8,128)(2,1)S(1)} collective-permute-done((bf16[64,5120]{1,0:T(8,128)(2,1)S(1)}, bf16[64,5120]{1,0:T(8,128)(2,1)S(1)}, u32[]{:S(2)}, u32[]{:S(2)}) %collective-permute-start.30) | collective-permute-done | bytes 655392 | tf_op jit(solution)/shard_map/ppermute | solution.py:180
  77.7 1.8 %collective-permute-start.39 = (bf16[64,5120]{1,0:T(8,128)(2,1)S(1)}, bf16[64,5120]{1,0:T(8,128)(2,1)S(1)}, u32[]{:S(2)}, u32[]{:S(2)}) collective-permute-start(bf16[64,5120]{1,0:T(8,128)(2,1)S(1)} %collective-permute-done.30.refs_3_), channel_id=1, source_target_pairs={{0,2},{1,3},{2,0},{3,1},{4,6},{5,7},{6,4},{7,5},{8,10},{9,11},{10,... | collective-permute-start | bytes 1966088 | tf_op jit(solution)/shard_map/ppermute | solution.py:180
  79.5 0.5 collective-permute-start.33
  80.2 0.9 collective-permute-done.32.refs_4_
  82.2 0.6 collective-permute-done.35.refs_2_
  82.8 0.5 collective-permute-done.28.refs_1_
  83.3 0.5 collective-permute-done.29.refs_2_
  83.7 7.4 %forward.6 = (f32[256,864]{1,0:T(8,128)S(1)}, f32[256,864]{1,0:T(8,128)S(1)}, bf16[256,256]{1,0:T(8,128)(2,1)S(1)}, bf16[256,256]{1,0:T(8,128)(2,1)S(1)}) custom-call(bf16[64,5120]{1,0:T(8,128)(2,1)S(1)} %collective-permute-done.16.refs_0_, bf16[32,5120]{1,0:T(8,128)(2,1)S(1)} %collective-permute-done.28.refs_1_, ...), custom_call_target="tpu_custom_call" | custom-call | tf_op jit(solution)/shard_map/forward/pallas_call | solution.py:134
  91.1 0.9 collective-permute-done.21.refs_3_
  92.1 1.7 %collective-permute-start.36 = (bf16[64,5248]{1,0:T(8,128)(2,1)S(1)}, bf16[64,5248]{1,0:T(8,128)(2,1)S(1)}, u32[]{:S(2)}, u32[]{:S(2)}) collective-permute-start(bf16[64,5248]{1,0:T(8,128)(2,1)S(1)} %collective-permute-done.21.refs_3_), channel_id=1, source_target_pairs={{0,2},{1,3},{2,0},{3,1},{4,6},{5,7},{6,4},{7,5},{8,10},{9,11},{10,... | collective-permute-start | bytes 2015240 | tf_op jit(solution)/shard_map/ppermute | solution.py:180
  93.8 0.8 collective-permute-done.39.refs_3_
  94.6 0.6 collective-permute-start.37
  95.3 1.9 %collective-permute-done.37.refs_4_ = bf16[32,5248]{1,0:T(8,128)(2,1)S(1)} collective-permute-done((bf16[32,5248]{1,0:T(8,128)(2,1)S(1)}, bf16[32,5248]{1,0:T(8,128)(2,1)S(1)}, u32[]{:S(2)}, u32[]{:S(2)}) %collective-permute-start.37) | collective-permute-done | bytes 335904 | tf_op jit(solution)/shard_map/ppermute | solution.py:180
  97.2 0.5 collective-permute-done.38.refs_5_
  97.7 4.8 %backward.6.refs_13_ = f32[256,512]{1,0:T(8,128)S(1)} custom-call(bf16[64,5248]{1,0:T(8,128)(2,1)S(1)} %collective-permute-done.8.refs_0_, bf16[32,5248]{1,0:T(8,128)(2,1)S(1)} %collective-permute-done.26.refs_1_, bf16[32,5248]{1,0:T(8,128)(2,1)S(1)} %collective-permute-done.27.refs_2_, bf16[64,5248]{1,0:T(8,128)(2,1)S(1)} %collective-permute-done.21.refs_3_, ...), custom_call_target="tpu_custom_call" | custom-call | tf_op jit(solution)/shard_map/backward/pallas_call | solution.py:134
  102.5 7.2 %forward.7 = (f32[256,864]{1,0:T(8,128)S(1)}, f32[256,864]{1,0:T(8,128)S(1)}, bf16[256,256]{1,0:T(8,128)(2,1)S(1)}, bf16[256,256]{1,0:T(8,128)(2,1)S(1)}) custom-call(bf16[64,5120]{1,0:T(8,128)(2,1)S(1)} %collective-permute-done.31.refs_0_, bf16[32,5120]{1,0:T(8,128)(2,1)S(1)} %collective-permute-done.34.refs_1_, ...), custom_call_target="tpu_custom_call" | custom-call | tf_op jit(solution)/shard_map/forward/pallas_call | solution.py:134
  110.0 0.4 collective-permute-start.42
  110.6 0.4 collective-permute-start.44
  111.0 0.5 collective-permute-done.41.refs_1_
  111.5 0.5 collective-permute-done.42.refs_2_
  111.9 0.5 collective-permute-done.43.refs_4_
  112.4 0.5 collective-permute-done.44.refs_5_
  112.9 4.8 %backward.7 = f32[256,512]{1,0:T(8,128)S(1)} custom-call(bf16[64,5248]{1,0:T(8,128)(2,1)S(1)} %collective-permute-done.20.refs_0_, bf16[32,5248]{1,0:T(8,128)(2,1)S(1)} %collective-permute-done.41.refs_1_, bf16[32,5248]{1,0:T(8,128)(2,1)S(1)} %collective-permute-done.42.refs_2_, bf16[64,5248]{1,0:T(8,128)(2,1)S(1)} %collective-permute-done.36.refs_3_, ...), custom_call_target="tpu_custom_call" | custom-call | tf_op jit(solution)/shard_map/backward/pallas_call | solution.py:134
  117.8 14.2 %all_to_all.5 = bf16[16,16,512]{2,1,0:T(8,128)(2,1)S(1)} all-to-all(bf16[16,16,512]{2,1,0:T(8,128)(2,1)S(1)} %bitcast.18), channel_id=1, replica_groups=mesh['groups'=2,'fsdp'=16] {'fsdp'}, dimensions={0} | all-to-all | bytes 524288 | tf_op jit(solution)/shard_map/all_to_all | solution.py:250
  132.1 0.6 copy.11
  (96 shorter events, 5.3 us)
Async XLA Ops:
  0.0 8.1 %copy-start.5 = (s32[3,864]{1,0:T(4,128)S(1)}, s32[3,864]{1,0:T(4,128)}, u32[]{:S(2)}) copy-start(s32[3,864]{1,0:T(4,128)} %param.16) | copy-start | bytes 31108
  0.0 8.6 %copy-start.4 = (bf16[64,5120]{1,0:T(8,128)(2,1)S(1)}, bf16[64,5120]{1,0:T(8,128)(2,1)}, u32[]{:S(2)}) copy-start(bf16[64,5120]{1,0:T(8,128)(2,1)} %param.11) | copy-start | bytes 1966084
  0.0 20.8 %collective-permute-start.4 = (bf16[64,5120]{1,0:T(8,128)(2,1)}, bf16[64,5120]{1,0:T(8,128)(2,1)S(1)}, u32[]{:S(2)}, u32[]{:S(2)}) collective-permute-start(bf16[64,5120]{1,0:T(8,128)(2,1)} %refs_0_.1), channel_id=1, source_target_pairs={{0,4},{1,13},{2,6},{3,15},{4,8},{5,1},{6,10},{7,3},{8,12},{9,5},{1... | collective-permute-start | bytes 1966088 | tf_op jit(solution)/shard_map/ppermute | solution.py:180
  3.0 17.8 %collective-permute-start.5 = (bf16[64,5120]{1,0:T(8,128)(2,1)}, bf16[64,5120]{1,0:T(8,128)(2,1)S(1)}, u32[]{:S(2)}, u32[]{:S(2)}) collective-permute-start(bf16[64,5120]{1,0:T(8,128)(2,1)} %refs_0_.1), channel_id=1, source_target_pairs={{0,2},{1,3},{2,0},{3,1},{4,6},{5,7},{6,4},{7,5},{8,10},{9,11},{10,... | collective-permute-start | bytes 1966088 | tf_op jit(solution)/shard_map/ppermute | solution.py:180
  8.1 13.6 %copy-start.3 = (bf16[64,5120]{1,0:T(8,128)(2,1)S(1)}, bf16[64,5120]{1,0:T(8,128)(2,1)}, u32[]{:S(2)}) copy-start(bf16[64,5120]{1,0:T(8,128)(2,1)} %refs_0_.1) | copy-start | bytes 1966084
  8.7 31.7 %collective-permute-start = (bf16[64,5248]{1,0:T(8,128)(2,1)S(1)}, bf16[64,5248]{1,0:T(8,128)(2,1)S(1)}, u32[]{:S(2)}, u32[]{:S(2)}) collective-permute-start(bf16[64,5248]{1,0:T(8,128)(2,1)S(1)} %pad_maximum_fusion.refs_0_), channel_id=1, source_target_pairs={{0,4},{1,13},{2,6},{3,15},{4,8},{5,1},{6,10},{7,3},{8,12},{9,5},{1... | collective-permute-start | bytes 2015240 | tf_op jit(solution)/shard_map/ppermute | solution.py:180
  10.3 30.1 %collective-permute-start.1 = (bf16[64,5248]{1,0:T(8,128)(2,1)S(1)}, bf16[64,5248]{1,0:T(8,128)(2,1)S(1)}, u32[]{:S(2)}, u32[]{:S(2)}) collective-permute-start(bf16[64,5248]{1,0:T(8,128)(2,1)S(1)} %pad_maximum_fusion.refs_0_), channel_id=1, source_target_pairs={{0,2},{1,3},{2,0},{3,1},{4,6},{5,7},{6,4},{7,5},{8,10},{9,11},{10,... | collective-permute-start | bytes 2015240 | tf_op jit(solution)/shard_map/ppermute | solution.py:180
  20.9 2.0 %collective-permute-start.6 = (bf16[32,5120]{1,0:T(8,128)(2,1)S(1)}, bf16[32,5120]{1,0:T(8,128)(2,1)S(1)}, u32[]{:S(2)}, u32[]{:S(2)}) collective-permute-start(bf16[32,5120]{1,0:T(8,128)(2,1)S(1)} %get-tuple-element.186), channel_id=1, source_target_pairs={{0,1},{1,0},{2,3},{3,2},{4,5},{5,4},{6,7},{7,6},{8,9},{9,8},{10,11... | collective-permute-start | bytes 983048 | tf_op jit(solution)/shard_map/ppermute | solution.py:180
  21.6 1.7 %collective-permute-start.7 = (bf16[32,5120]{1,0:T(8,128)(2,1)S(1)}, bf16[32,5120]{1,0:T(8,128)(2,1)S(1)}, u32[]{:S(2)}, u32[]{:S(2)}) collective-permute-start(bf16[32,5120]{1,0:T(8,128)(2,1)S(1)} %get-tuple-element.185), channel_id=1, source_target_pairs={{0,1},{1,0},{2,3},{3,2},{4,5},{5,4},{6,7},{7,6},{8,9},{9,8},{10,11... | collective-permute-start | bytes 983048 | tf_op jit(solution)/shard_map/ppermute | solution.py:180
  21.8 2.9 %collective-permute-start.2 = (bf16[32,5120]{1,0:T(8,128)(2,1)S(1)}, bf16[32,5120]{1,0:T(8,128)(2,1)S(1)}, u32[]{:S(2)}, u32[]{:S(2)}) collective-permute-start(bf16[32,5120]{1,0:T(8,128)(2,1)S(1)} %get-tuple-element.188), channel_id=1, source_target_pairs={{0,1},{1,0},{2,3},{3,2},{4,5},{5,4},{6,7},{7,6},{8,9},{9,8},{10,11... | collective-permute-start | bytes 983048 | tf_op jit(solution)/shard_map/ppermute | solution.py:180
  22.9 3.3 %collective-permute-start.3 = (bf16[32,5120]{1,0:T(8,128)(2,1)S(1)}, bf16[32,5120]{1,0:T(8,128)(2,1)S(1)}, u32[]{:S(2)}, u32[]{:S(2)}) collective-permute-start(bf16[32,5120]{1,0:T(8,128)(2,1)S(1)} %get-tuple-element.187), channel_id=1, source_target_pairs={{0,1},{1,0},{2,3},{3,2},{4,5},{5,4},{6,7},{7,6},{8,9},{9,8},{10,11... | collective-permute-start | bytes 983048 | tf_op jit(solution)/shard_map/ppermute | solution.py:180
  23.4 30.0 %collective-permute-start.16 = (bf16[64,5120]{1,0:T(8,128)(2,1)S(1)}, bf16[64,5120]{1,0:T(8,128)(2,1)S(1)}, u32[]{:S(2)}, u32[]{:S(2)}) collective-permute-start(bf16[64,5120]{1,0:T(8,128)(2,1)S(1)} %collective-permute-done.4.refs_0_), channel_id=1, source_target_pairs={{0,4},{1,13},{2,6},{3,15},{4,8},{5,1},{6,10},{7,3},{8,12},{9,5},{1... | collective-permute-start | bytes 1966088 | tf_op jit(solution)/shard_map/ppermute | solution.py:180
  24.7 28.7 %collective-permute-start.17 = (bf16[64,5120]{1,0:T(8,128)(2,1)S(1)}, bf16[64,5120]{1,0:T(8,128)(2,1)S(1)}, u32[]{:S(2)}, u32[]{:S(2)}) collective-permute-start(bf16[64,5120]{1,0:T(8,128)(2,1)S(1)} %collective-permute-done.4.refs_0_), channel_id=1, source_target_pairs={{0,2},{1,3},{2,0},{3,1},{4,6},{5,7},{6,4},{7,5},{8,10},{9,11},{10,... | collective-permute-start | bytes 1966088 | tf_op jit(solution)/shard_map/ppermute | solution.py:180
  26.2 3.5 %copy-start = (bf16[5120,864]{0,1:T(8,128)(2,1)S(1)}, bf16[5120,864]{0,1:T(8,128)(2,1)}, u32[]{:S(2)}) copy-start(bf16[5120,864]{0,1:T(8,128)(2,1)} %param.13) | copy-start | bytes 26542084
  29.7 3.5 %copy-start.1 = (bf16[5120,864]{0,1:T(8,128)(2,1)S(1)}, bf16[5120,864]{0,1:T(8,128)(2,1)}, u32[]{:S(2)}) copy-start(bf16[5120,864]{0,1:T(8,128)(2,1)} %param.14) | copy-start | bytes 26542084
  33.2 25.9 %slice-start.3 = ((s8[8847360]{0:T(1024)(128)(4,1)}), s8[4194304]{0:T(1024)(128)(4,1)S(1)}, s32[]{:S(2)}) async-start(s8[8847360]{0:T(1024)(128)(4,1)} %bitcast.11), calls=%async_computation.4 | async-start | bytes 8388608
  33.2 25.9 %slice-start.4 = ((s8[8847360]{0:T(1024)(128)(4,1)}), s8[4194304]{0:T(1024)(128)(4,1)S(1)}, s32[]{:S(2)}) async-start(s8[8847360]{0:T(1024)(128)(4,1)} %bitcast.11), calls=%async_computation.5 | async-start | bytes 8388608
  40.5 1.7 %collective-permute-start.10 = (bf16[32,5248]{1,0:T(8,128)(2,1)S(1)}, bf16[32,5248]{1,0:T(8,128)(2,1)S(1)}, u32[]{:S(2)}, u32[]{:S(2)}) collective-permute-start(bf16[32,5248]{1,0:T(8,128)(2,1)S(1)} %get-tuple-element.174), channel_id=1, source_target_pairs={{0,1},{1,0},{2,3},{3,2},{4,5},{5,4},{6,7},{7,6},{8,9},{9,8},{10,11... | collective-permute-start | bytes 1007624 | tf_op jit(solution)/shard_map/ppermute | solution.py:180
  40.9 1.8 %collective-permute-start.11 = (bf16[32,5248]{1,0:T(8,128)(2,1)S(1)}, bf16[32,5248]{1,0:T(8,128)(2,1)S(1)}, u32[]{:S(2)}, u32[]{:S(2)}) collective-permute-start(bf16[32,5248]{1,0:T(8,128)(2,1)S(1)} %get-tuple-element.173), channel_id=1, source_target_pairs={{0,1},{1,0},{2,3},{3,2},{4,5},{5,4},{6,7},{7,6},{8,9},{9,8},{10,11... | collective-permute-start | bytes 1007624 | tf_op jit(solution)/shard_map/ppermute | solution.py:180
  41.1 3.1 %collective-permute-start.12 = (bf16[32,5248]{1,0:T(8,128)(2,1)S(1)}, bf16[32,5248]{1,0:T(8,128)(2,1)S(1)}, u32[]{:S(2)}, u32[]{:S(2)}) collective-permute-start(bf16[32,5248]{1,0:T(8,128)(2,1)S(1)} %get-tuple-element.172), channel_id=1, source_target_pairs={{0,1},{1,0},{2,3},{3,2},{4,5},{5,4},{6,7},{7,6},{8,9},{9,8},{10,11... | collective-permute-start | bytes 1007624 | tf_op jit(solution)/shard_map/ppermute | solution.py:180
  42.2 2.6 %collective-permute-start.13 = (bf16[32,5248]{1,0:T(8,128)(2,1)S(1)}, bf16[32,5248]{1,0:T(8,128)(2,1)S(1)}, u32[]{:S(2)}, u32[]{:S(2)}) collective-permute-start(bf16[32,5248]{1,0:T(8,128)(2,1)S(1)} %get-tuple-element.171), channel_id=1, source_target_pairs={{0,1},{1,0},{2,3},{3,2},{4,5},{5,4},{6,7},{7,6},{8,9},{9,8},{10,11... | collective-permute-start | bytes 1007624 | tf_op jit(solution)/shard_map/ppermute | solution.py:180
  42.7 23.7 %collective-permute-start.8 = (bf16[64,5248]{1,0:T(8,128)(2,1)S(1)}, bf16[64,5248]{1,0:T(8,128)(2,1)S(1)}, u32[]{:S(2)}, u32[]{:S(2)}) collective-permute-start(bf16[64,5248]{1,0:T(8,128)(2,1)S(1)} %collective-permute-done.refs_0_), channel_id=1, source_target_pairs={{0,4},{1,13},{2,6},{3,15},{4,8},{5,1},{6,10},{7,3},{8,12},{9,5},{1... | collective-permute-start | bytes 2015240 | tf_op jit(solution)/shard_map/ppermute | solution.py:180
  44.3 22.1 %collective-permute-start.9 = (bf16[64,5248]{1,0:T(8,128)(2,1)S(1)}, bf16[64,5248]{1,0:T(8,128)(2,1)S(1)}, u32[]{:S(2)}, u32[]{:S(2)}) collective-permute-start(bf16[64,5248]{1,0:T(8,128)(2,1)S(1)} %collective-permute-done.refs_0_), channel_id=1, source_target_pairs={{0,2},{1,3},{2,0},{3,1},{4,6},{5,7},{6,4},{7,5},{8,10},{9,11},{10,... | collective-permute-start | bytes 2015240 | tf_op jit(solution)/shard_map/ppermute | solution.py:180
  44.8 14.4 %slice-start = ((s8[8847360]{0:T(1024)(128)(4,1)}), s8[4194304]{0:T(1024)(128)(4,1)S(1)}, s32[]{:S(2)}) async-start(s8[8847360]{0:T(1024)(128)(4,1)} %bitcast.5), calls=%async_computation.1 | async-start | bytes 8388608
  44.8 3.7 %copy-start.2 = (bf16[864,5120]{1,0:T(8,128)(2,1)S(1)}, bf16[864,5120]{1,0:T(8,128)(2,1)}, u32[]{:S(2)}) copy-start(bf16[864,5120]{1,0:T(8,128)(2,1)} %refs_6_.7) | copy-start | bytes 26542084
  48.5 10.6 %slice-start.1 = ((s8[8847360]{0:T(1024)(128)(4,1)}), s8[4194304]{0:T(1024)(128)(4,1)S(1)}, s32[]{:S(2)}) async-start(s8[8847360]{0:T(1024)(128)(4,1)} %bitcast.5), calls=%async_computation.2 | async-start | bytes 8388608
  48.5 10.6 %slice-start.2 = ((s8[8847360]{0:T(1024)(128)(4,1)}), s8[458752]{0:T(1024)(128)(4,1)S(1)}, s32[]{:S(2)}) async-start(s8[8847360]{0:T(1024)(128)(4,1)} %bitcast.5), calls=%async_computation.3 | async-start | bytes 917504
  48.5 10.6 %slice-start.5 = ((s8[8847360]{0:T(1024)(128)(4,1)}), s8[458752]{0:T(1024)(128)(4,1)S(1)}, s32[]{:S(2)}) async-start(s8[8847360]{0:T(1024)(128)(4,1)} %bitcast.11), calls=%async_computation.6 | async-start | bytes 917504
  53.4 1.8 %collective-permute-start.18 = (bf16[32,5120]{1,0:T(8,128)(2,1)S(1)}, bf16[32,5120]{1,0:T(8,128)(2,1)S(1)}, u32[]{:S(2)}, u32[]{:S(2)}) collective-permute-start(bf16[32,5120]{1,0:T(8,128)(2,1)S(1)} %get-tuple-element.182), channel_id=1, source_target_pairs={{0,1},{1,0},{2,3},{3,2},{4,5},{5,4},{6,7},{7,6},{8,9},{9,8},{10,11... | collective-permute-start | bytes 983048 | tf_op jit(solution)/shard_map/ppermute | solution.py:180
  54.0 1.7 %collective-permute-start.19 = (bf16[32,5120]{1,0:T(8,128)(2,1)S(1)}, bf16[32,5120]{1,0:T(8,128)(2,1)S(1)}, u32[]{:S(2)}, u32[]{:S(2)}) collective-permute-start(bf16[32,5120]{1,0:T(8,128)(2,1)S(1)} %get-tuple-element.181), channel_id=1, source_target_pairs={{0,1},{1,0},{2,3},{3,2},{4,5},{5,4},{6,7},{7,6},{8,9},{9,8},{10,11... | collective-permute-start | bytes 983048 | tf_op jit(solution)/shard_map/ppermute | solution.py:180
  54.1 2.2 %collective-permute-start.14 = (bf16[32,5120]{1,0:T(8,128)(2,1)S(1)}, bf16[32,5120]{1,0:T(8,128)(2,1)S(1)}, u32[]{:S(2)}, u32[]{:S(2)}) collective-permute-start(bf16[32,5120]{1,0:T(8,128)(2,1)S(1)} %get-tuple-element.184), channel_id=1, source_target_pairs={{0,1},{1,0},{2,3},{3,2},{4,5},{5,4},{6,7},{7,6},{8,9},{9,8},{10,11... | collective-permute-start | bytes 983048 | tf_op jit(solution)/shard_map/ppermute | solution.py:180
  55.2 2.5 %collective-permute-start.15 = (bf16[32,5120]{1,0:T(8,128)(2,1)S(1)}, bf16[32,5120]{1,0:T(8,128)(2,1)S(1)}, u32[]{:S(2)}, u32[]{:S(2)}) collective-permute-start(bf16[32,5120]{1,0:T(8,128)(2,1)S(1)} %get-tuple-element.183), channel_id=1, source_target_pairs={{0,1},{1,0},{2,3},{3,2},{4,5},{5,4},{6,7},{7,6},{8,9},{9,8},{10,11... | collective-permute-start | bytes 983048 | tf_op jit(solution)/shard_map/ppermute | solution.py:180
  55.7 22.0 %collective-permute-start.30 = (bf16[64,5120]{1,0:T(8,128)(2,1)S(1)}, bf16[64,5120]{1,0:T(8,128)(2,1)S(1)}, u32[]{:S(2)}, u32[]{:S(2)}) collective-permute-start(bf16[64,5120]{1,0:T(8,128)(2,1)S(1)} %collective-permute-done.16.refs_0_), channel_id=1, source_target_pairs={{0,4},{1,13},{2,6},{3,15},{4,8},{5,1},{6,10},{7,3},{8,12},{9,5},{1... | collective-permute-start | bytes 1966088 | tf_op jit(solution)/shard_map/ppermute | solution.py:180
  56.3 21.4 %collective-permute-start.31 = (bf16[64,5120]{1,0:T(8,128)(2,1)S(1)}, bf16[64,5120]{1,0:T(8,128)(2,1)S(1)}, u32[]{:S(2)}, u32[]{:S(2)}) collective-permute-start(bf16[64,5120]{1,0:T(8,128)(2,1)S(1)} %collective-permute-done.16.refs_0_), channel_id=1, source_target_pairs={{0,2},{1,3},{2,0},{3,1},{4,6},{5,7},{6,4},{7,5},{8,10},{9,11},{10,... | collective-permute-start | bytes 1966088 | tf_op jit(solution)/shard_map/ppermute | solution.py:180
  57.7 12.6 %slice-start.6 = ((s8[8847360]{0:T(1024)(128)(4,1)}), s8[4194304]{0:T(1024)(128)(4,1)S(1)}, s32[]{:S(2)}) async-start(s8[8847360]{0:T(1024)(128)(4,1)} %bitcast.16), calls=%async_computation.7 | async-start | bytes 8388608
  57.7 12.6 %slice-start.7 = ((s8[8847360]{0:T(1024)(128)(4,1)}), s8[4194304]{0:T(1024)(128)(4,1)S(1)}, s32[]{:S(2)}) async-start(s8[8847360]{0:T(1024)(128)(4,1)} %bitcast.16), calls=%async_computation.8 | async-start | bytes 8388608
  57.7 12.6 %slice-start.8 = ((s8[8847360]{0:T(1024)(128)(4,1)}), s8[458752]{0:T(1024)(128)(4,1)S(1)}, s32[]{:S(2)}) async-start(s8[8847360]{0:T(1024)(128)(4,1)} %bitcast.16), calls=%async_computation.9 | async-start | bytes 917504
  57.7 9.4 %collective-permute-start.22 = (bf16[32,5248]{1,0:T(8,128)(2,1)S(1)}, bf16[32,5248]{1,0:T(8,128)(2,1)S(1)}, u32[]{:S(2)}, u32[]{:S(2)}) collective-permute-start(bf16[32,5248]{1,0:T(8,128)(2,1)S(1)} %get-tuple-element.170), channel_id=1, source_target_pairs={{0,1},{1,0},{2,3},{3,2},{4,5},{5,4},{6,7},{7,6},{8,9},{9,8},{10,11... | collective-permute-start | bytes 1007624 | tf_op jit(solution)/shard_map/ppermute | solution.py:180
  66.4 1.7 %collective-permute-start.26 = (bf16[32,5248]{1,0:T(8,128)(2,1)S(1)}, bf16[32,5248]{1,0:T(8,128)(2,1)S(1)}, u32[]{:S(2)}, u32[]{:S(2)}) collective-permute-start(bf16[32,5248]{1,0:T(8,128)(2,1)S(1)} %get-tuple-element.166), channel_id=1, source_target_pairs={{0,1},{1,0},{2,3},{3,2},{4,5},{5,4},{6,7},{7,6},{8,9},{9,8},{10,11... | collective-permute-start | bytes 1007624 | tf_op jit(solution)/shard_map/ppermute | solution.py:180
  66.5 2.1 %collective-permute-start.27 = (bf16[32,5248]{1,0:T(8,128)(2,1)S(1)}, bf16[32,5248]{1,0:T(8,128)(2,1)S(1)}, u32[]{:S(2)}, u32[]{:S(2)}) collective-permute-start(bf16[32,5248]{1,0:T(8,128)(2,1)S(1)} %get-tuple-element.165), channel_id=1, source_target_pairs={{0,1},{1,0},{2,3},{3,2},{4,5},{5,4},{6,7},{7,6},{8,9},{9,8},{10,11... | collective-permute-start | bytes 1007624 | tf_op jit(solution)/shard_map/ppermute | solution.py:180
  67.1 2.0 %collective-permute-start.23 = (bf16[32,5248]{1,0:T(8,128)(2,1)S(1)}, bf16[32,5248]{1,0:T(8,128)(2,1)S(1)}, u32[]{:S(2)}, u32[]{:S(2)}) collective-permute-start(bf16[32,5248]{1,0:T(8,128)(2,1)S(1)} %get-tuple-element.169), channel_id=1, source_target_pairs={{0,1},{1,0},{2,3},{3,2},{4,5},{5,4},{6,7},{7,6},{8,9},{9,8},{10,11... | collective-permute-start | bytes 1007624 | tf_op jit(solution)/shard_map/ppermute | solution.py:180
  68.2 1.6 %collective-permute-start.24 = (bf16[32,5248]{1,0:T(8,128)(2,1)S(1)}, bf16[32,5248]{1,0:T(8,128)(2,1)S(1)}, u32[]{:S(2)}, u32[]{:S(2)}) collective-permute-start(bf16[32,5248]{1,0:T(8,128)(2,1)S(1)} %get-tuple-element.168), channel_id=1, source_target_pairs={{0,1},{1,0},{2,3},{3,2},{4,5},{5,4},{6,7},{7,6},{8,9},{9,8},{10,11... | collective-permute-start | bytes 1007624 | tf_op jit(solution)/shard_map/ppermute | solution.py:180
  68.6 1.6 %collective-permute-start.25 = (bf16[32,5248]{1,0:T(8,128)(2,1)S(1)}, bf16[32,5248]{1,0:T(8,128)(2,1)S(1)}, u32[]{:S(2)}, u32[]{:S(2)}) collective-permute-start(bf16[32,5248]{1,0:T(8,128)(2,1)S(1)} %get-tuple-element.167), channel_id=1, source_target_pairs={{0,1},{1,0},{2,3},{3,2},{4,5},{5,4},{6,7},{7,6},{8,9},{9,8},{10,11... | collective-permute-start | bytes 1007624 | tf_op jit(solution)/shard_map/ppermute | solution.py:180
  69.1 23.0 %collective-permute-start.21 = (bf16[64,5248]{1,0:T(8,128)(2,1)S(1)}, bf16[64,5248]{1,0:T(8,128)(2,1)S(1)}, u32[]{:S(2)}, u32[]{:S(2)}) collective-permute-start(bf16[64,5248]{1,0:T(8,128)(2,1)S(1)} %collective-permute-done.8.refs_0_), channel_id=1, source_target_pairs={{0,4},{1,13},{2,6},{3,15},{4,8},{5,1},{6,10},{7,3},{8,12},{9,5},{1... | collective-permute-start | bytes 2015240 | tf_op jit(solution)/shard_map/ppermute | solution.py:180
  77.7 16.9 %collective-permute-start.39 = (bf16[64,5120]{1,0:T(8,128)(2,1)S(1)}, bf16[64,5120]{1,0:T(8,128)(2,1)S(1)}, u32[]{:S(2)}, u32[]{:S(2)}) collective-permute-start(bf16[64,5120]{1,0:T(8,128)(2,1)S(1)} %collective-permute-done.30.refs_3_), channel_id=1, source_target_pairs={{0,2},{1,3},{2,0},{3,1},{4,6},{5,7},{6,4},{7,5},{8,10},{9,11},{10,... | collective-permute-start | bytes 1966088 | tf_op jit(solution)/shard_map/ppermute | solution.py:180
  79.5 1.6 %collective-permute-start.32 = (bf16[32,5120]{1,0:T(8,128)(2,1)S(1)}, bf16[32,5120]{1,0:T(8,128)(2,1)S(1)}, u32[]{:S(2)}, u32[]{:S(2)}) collective-permute-start(bf16[32,5120]{1,0:T(8,128)(2,1)S(1)} %get-tuple-element.178), channel_id=1, source_target_pairs={{0,1},{1,0},{2,3},{3,2},{4,5},{5,4},{6,7},{7,6},{8,9},{9,8},{10,11... | collective-permute-start | bytes 983048 | tf_op jit(solution)/shard_map/ppermute | solution.py:180
  79.5 2.1 %collective-permute-start.33 = (bf16[32,5120]{1,0:T(8,128)(2,1)S(1)}, bf16[32,5120]{1,0:T(8,128)(2,1)S(1)}, u32[]{:S(2)}, u32[]{:S(2)}) collective-permute-start(bf16[32,5120]{1,0:T(8,128)(2,1)S(1)} %get-tuple-element.177), channel_id=1, source_target_pairs={{0,1},{1,0},{2,3},{3,2},{4,5},{5,4},{6,7},{7,6},{8,9},{9,8},{10,11... | collective-permute-start | bytes 983048 | tf_op jit(solution)/shard_map/ppermute | solution.py:180
  80.1 2.0 %collective-permute-start.34 = (bf16[32,5120]{1,0:T(8,128)(2,1)S(1)}, bf16[32,5120]{1,0:T(8,128)(2,1)S(1)}, u32[]{:S(2)}, u32[]{:S(2)}) collective-permute-start(bf16[32,5120]{1,0:T(8,128)(2,1)S(1)} %get-tuple-element.176), channel_id=1, source_target_pairs={{0,1},{1,0},{2,3},{3,2},{4,5},{5,4},{6,7},{7,6},{8,9},{9,8},{10,11... | collective-permute-start | bytes 983048 | tf_op jit(solution)/shard_map/ppermute | solution.py:180
  81.2 1.6 %collective-permute-start.35 = (bf16[32,5120]{1,0:T(8,128)(2,1)S(1)}, bf16[32,5120]{1,0:T(8,128)(2,1)S(1)}, u32[]{:S(2)}, u32[]{:S(2)}) collective-permute-start(bf16[32,5120]{1,0:T(8,128)(2,1)S(1)} %get-tuple-element.175), channel_id=1, source_target_pairs={{0,1},{1,0},{2,3},{3,2},{4,5},{5,4},{6,7},{7,6},{8,9},{9,8},{10,11... | collective-permute-start | bytes 983048 | tf_op jit(solution)/shard_map/ppermute | solution.py:180
  81.6 1.6 %collective-permute-start.28 = (bf16[32,5120]{1,0:T(8,128)(2,1)S(1)}, bf16[32,5120]{1,0:T(8,128)(2,1)S(1)}, u32[]{:S(2)}, u32[]{:S(2)}) collective-permute-start(bf16[32,5120]{1,0:T(8,128)(2,1)S(1)} %get-tuple-element.180), channel_id=1, source_target_pairs={{0,1},{1,0},{2,3},{3,2},{4,5},{5,4},{6,7},{7,6},{8,9},{9,8},{10,11... | collective-permute-start | bytes 983048 | tf_op jit(solution)/shard_map/ppermute | solution.py:180
  82.1 1.6 %collective-permute-start.29 = (bf16[32,5120]{1,0:T(8,128)(2,1)S(1)}, bf16[32,5120]{1,0:T(8,128)(2,1)S(1)}, u32[]{:S(2)}, u32[]{:S(2)}) collective-permute-start(bf16[32,5120]{1,0:T(8,128)(2,1)S(1)} %get-tuple-element.179), channel_id=1, source_target_pairs={{0,1},{1,0},{2,3},{3,2},{4,5},{5,4},{6,7},{7,6},{8,9},{9,8},{10,11... | collective-permute-start | bytes 983048 | tf_op jit(solution)/shard_map/ppermute | solution.py:180
  82.8 26.9 %collective-permute-start.20 = (bf16[64,5248]{1,0:T(8,128)(2,1)S(1)}, bf16[64,5248]{1,0:T(8,128)(2,1)S(1)}, u32[]{:S(2)}, u32[]{:S(2)}) collective-permute-start(bf16[64,5248]{1,0:T(8,128)(2,1)S(1)} %collective-permute-done.9.refs_3_), channel_id=1, source_target_pairs={{0,4},{1,13},{2,6},{3,15},{4,8},{5,1},{6,10},{7,3},{8,12},{9,5},{1... | collective-permute-start | bytes 2015240 | tf_op jit(solution)/shard_map/ppermute | solution.py:180
  92.1 17.6 %collective-permute-start.36 = (bf16[64,5248]{1,0:T(8,128)(2,1)S(1)}, bf16[64,5248]{1,0:T(8,128)(2,1)S(1)}, u32[]{:S(2)}, u32[]{:S(2)}) collective-permute-start(bf16[64,5248]{1,0:T(8,128)(2,1)S(1)} %collective-permute-done.21.refs_3_), channel_id=1, source_target_pairs={{0,2},{1,3},{2,0},{3,1},{4,6},{5,7},{6,4},{7,5},{8,10},{9,11},{10,... | collective-permute-start | bytes 2015240 | tf_op jit(solution)/shard_map/ppermute | solution.py:180
  94.6 7.9 %collective-permute-start.40 = (bf16[64,5120]{1,0:T(8,128)(2,1)S(1)}, bf16[64,5120]{1,0:T(8,128)(2,1)S(1)}, u32[]{:S(2)}, u32[]{:S(2)}) collective-permute-start(bf16[64,5120]{1,0:T(8,128)(2,1)S(1)} %collective-permute-done.39.refs_3_), channel_id=1, source_target_pairs={{0,1},{1,0},{2,3},{3,2},{4,5},{5,4},{6,7},{7,6},{8,9},{9,8},{10,11... | collective-permute-start | bytes 1966088 | tf_op jit(solution)/shard_map/ppermute | solution.py:180
  94.6 2.5 %collective-permute-start.37 = (bf16[32,5248]{1,0:T(8,128)(2,1)S(1)}, bf16[32,5248]{1,0:T(8,128)(2,1)S(1)}, u32[]{:S(2)}, u32[]{:S(2)}) collective-permute-start(bf16[32,5248]{1,0:T(8,128)(2,1)S(1)} %get-tuple-element.164), channel_id=1, source_target_pairs={{0,1},{1,0},{2,3},{3,2},{4,5},{5,4},{6,7},{7,6},{8,9},{9,8},{10,11... | collective-permute-start | bytes 1007624 | tf_op jit(solution)/shard_map/ppermute | solution.py:180
  95.2 2.4 %collective-permute-start.38 = (bf16[32,5248]{1,0:T(8,128)(2,1)S(1)}, bf16[32,5248]{1,0:T(8,128)(2,1)S(1)}, u32[]{:S(2)}, u32[]{:S(2)}) collective-permute-start(bf16[32,5248]{1,0:T(8,128)(2,1)S(1)} %get-tuple-element.163), channel_id=1, source_target_pairs={{0,1},{1,0},{2,3},{3,2},{4,5},{5,4},{6,7},{7,6},{8,9},{9,8},{10,11... | collective-permute-start | bytes 1007624 | tf_op jit(solution)/shard_map/ppermute | solution.py:180
  109.8 1.7 %collective-permute-start.41 = (bf16[32,5248]{1,0:T(8,128)(2,1)S(1)}, bf16[32,5248]{1,0:T(8,128)(2,1)S(1)}, u32[]{:S(2)}, u32[]{:S(2)}) collective-permute-start(bf16[32,5248]{1,0:T(8,128)(2,1)S(1)} %get-tuple-element.162), channel_id=1, source_target_pairs={{0,1},{1,0},{2,3},{3,2},{4,5},{5,4},{6,7},{7,6},{8,9},{9,8},{10,11... | collective-permute-start | bytes 1007624 | tf_op jit(solution)/shard_map/ppermute | solution.py:180
  110.0 2.0 %collective-permute-start.42 = (bf16[32,5248]{1,0:T(8,128)(2,1)S(1)}, bf16[32,5248]{1,0:T(8,128)(2,1)S(1)}, u32[]{:S(2)}, u32[]{:S(2)}) collective-permute-start(bf16[32,5248]{1,0:T(8,128)(2,1)S(1)} %get-tuple-element.161), channel_id=1, source_target_pairs={{0,1},{1,0},{2,3},{3,2},{4,5},{5,4},{6,7},{7,6},{8,9},{9,8},{10,11... | collective-permute-start | bytes 1007624 | tf_op jit(solution)/shard_map/ppermute | solution.py:180
  110.4 2.0 %collective-permute-start.43 = (bf16[32,5248]{1,0:T(8,128)(2,1)S(1)}, bf16[32,5248]{1,0:T(8,128)(2,1)S(1)}, u32[]{:S(2)}, u32[]{:S(2)}) collective-permute-start(bf16[32,5248]{1,0:T(8,128)(2,1)S(1)} %get-tuple-element.160), channel_id=1, source_target_pairs={{0,1},{1,0},{2,3},{3,2},{4,5},{5,4},{6,7},{7,6},{8,9},{9,8},{10,11... | collective-permute-start | bytes 1007624 | tf_op jit(solution)/shard_map/ppermute | solution.py:180
  110.6 2.3 %collective-permute-start.44 = (bf16[32,5248]{1,0:T(8,128)(2,1)S(1)}, bf16[32,5248]{1,0:T(8,128)(2,1)S(1)}, u32[]{:S(2)}, u32[]{:S(2)}) collective-permute-start(bf16[32,5248]{1,0:T(8,128)(2,1)S(1)} %get-tuple-element.159), channel_id=1, source_target_pairs={{0,1},{1,0},{2,3},{3,2},{4,5},{5,4},{6,7},{7,6},{8,9},{9,8},{10,11... | collective-permute-start | bytes 1007624 | tf_op jit(solution)/shard_map/ppermute | solution.py:180

commit v9 on v8

--- a/solution.py
+++ b/solution.py
@@ -13,7 +13,7 @@
 K2 = 256
 CORES = 2
 OUTER = 4
-DEPTH = 2560
+TILE = 256
 LANES = 128
 VMEM_LIMIT = 12 << 20
 
@@ -62,32 +62,35 @@
     )
 
 
-def joined(refs, lanes):
-    parts = [ref[:, lanes] for ref in refs]
-    return jnp.concatenate(parts, axis=0) if len(parts) > 1 else parts[0]
-
-
-def add_products(refs, model, sums):
-    depth = min(DEPTH, model)
-    for acc, _ in sums:
-        acc[...] = jnp.zeros_like(acc)
-
-    def body(step, _):
-        here = pl.ds(pl.multiple_of(step * depth, depth), depth)
-        rows = joined(refs, here)
-        for acc, weight in sums:
-            acc[...] += dot_rows(rows, weight[:, here])
-        return 0
-
-    lax.fori_loop(0, model // depth, body, 0)
+def products(refs, rows, model, outs):
+    if rows is None:
+        rows = refs[0]
+    else:
+        own = 0
+        for ref in refs:
+            rows[pl.ds(own, ref.shape[0]), :] = ref[:, :model]
+            own += ref.shape[0]
+    for out, weight in outs:
+        units = weight.shape[0]
+        tiles = units // TILE
+
+        def body(tile, _, out=out, weight=weight):
+            here = pl.ds(pl.multiple_of(tile * TILE, TILE), TILE)
+            out[:, here] = dot_rows(rows[:, :model], weight[here, :])
+            return 0
+
+        lax.fori_loop(0, tiles, body, 0)
+        if units % TILE:
+            here = slice(tiles * TILE, units)
+            out[:, here] = dot_rows(rows[:, :model], weight[here, :])
 
 
 def forward_kernel(pieces, *refs):
     gate_w, up_w, feature_w, tables = refs[pieces : pieces + 4]
     to_gate, to_up, down_part, feature_in = refs[pieces + 4 : pieces + 8]
-    gate_acc, up_acc, feature_acc = refs[pieces + 8 :]
-    sums = ((gate_acc, gate_w), (up_acc, up_w), (feature_acc, feature_w))
-    add_products(refs[:pieces], gate_w.shape[1], sums)
+    gate_acc, up_acc, feature_acc, *rows = refs[pieces + 8 :]
+    outs = ((gate_acc, gate_w), (up_acc, up_w), (feature_acc, feature_w))
+    products(refs[:pieces], *(rows or [None]), gate_w.shape[1], outs)
     gate, up = gate_acc[...], up_acc[...]
     sigmoid = jax.nn.sigmoid(gate)
     activated = gate * sigmoid
@@ -102,15 +105,17 @@
     down_w, feature_w, tables, to_gate, to_up, down_part, feature_in, before = refs[
         pieces : pieces + 8
     ]
-    total, hidden_acc, feature_acc = refs[pieces + 8 :]
+    total, hidden_acc, feature_acc, *rows = refs[pieces + 8 :]
     model = down_w.shape[1]
-    add_products(refs[:pieces], model, ((hidden_acc, down_w), (feature_acc, feature_w)))
+    outs = ((hidden_acc, down_w), (feature_acc, feature_w))
+    products(refs[:pieces], *(rows or [None]), model, outs)
     bf16 = jnp.bfloat16
     hidden_grad = hidden_acc[...]
     gate_grad = (hidden_grad * to_gate[...]).astype(bf16)
     up_grad = (hidden_grad * to_up[...]).astype(bf16)
     input_part = (dot_rows(gate_grad, tables[0]) + dot_rows(up_grad, tables[1])).astype(bf16)
-    example = joined(refs[:pieces], pl.ds(model, LANES)).astype(jnp.float32)
+    example = [ref[:, model:].astype(jnp.float32) for ref in refs[:pieces]]
+    example = jnp.concatenate(example, axis=0) if pieces > 1 else example[0]
     example = jnp.concatenate([example] * (K2 // LANES), axis=1)
 
     def by_example(features):
@@ -128,7 +133,7 @@
     )
 
 
-def on_chip(kernel, name, pieces, operands, outs, sums):
+def on_chip(kernel, name, pieces, operands, outs, sums, model):
     rows = sum(piece.shape[0] for piece in pieces)
     vmem = pl.BlockSpec(memory_space=pltpu.VMEM)
     return pl.pallas_call(
@@ -136,7 +141,8 @@
         in_specs=[vmem] * (len(pieces) + len(operands)),
         out_specs=[vmem] * len(outs),
         out_shape=outs,
-        scratch_shapes=[pltpu.VMEM((rows, columns), jnp.float32) for columns in sums],
+        scratch_shapes=[pltpu.VMEM((rows, columns), jnp.float32) for columns in sums]
+        + [pltpu.VMEM((rows, model), jnp.bfloat16)] * (len(pieces) > 1),
         compiler_params=pltpu.CompilerParams(vmem_limit_bytes=VMEM_LIMIT),
         cost_estimate=pl.CostEstimate(flops=0, bytes_accessed=0, transcendentals=0),
         name=name,
@@ -153,14 +159,14 @@
         jax.ShapeDtypeStruct((rows, K2), jnp.bfloat16),
     ]
     operands = (gate_rows, up_rows, feature_table, tables)
-    return on_chip(forward_kernel, "forward", pieces, operands, outs, (units, units, K2))
+    return on_chip(forward_kernel, "forward", pieces, operands, outs, (units, units, K2), model)
 
 
 def backward(pieces, down_rows, feature_table, tables, saved, before):
     units, model = down_rows.shape
     outs = [jax.ShapeDtypeStruct(before.shape, jnp.float32)]
     operands = (down_rows, feature_table, tables, *saved, before)
-    return on_chip(backward_kernel, "backward", pieces, operands, outs, (units, K2))[0]
+    return on_chip(backward_kernel, "backward", pieces, operands, outs, (units, K2), model)[0]
 
 
 def on_device(

time: 133 us -> 134 us (level)
  Pallas kernels: 48.3 us -> 52 us
  waiting for transfers between devices: 26.4 us -> 24.5 us
    pallas_call x8, Pallas kernels: 48.3 us -> 52 us  [on_chip(): pl.pallas_call(lambda *refs: kernel(len(pieces), *refs), in_specs=[vmem]...]
    ppermute x45, waiting for transfers between devices: 26.4 us -> 24.5 us  [move(): return lax.ppermute(value, 'fsdp', pairs)]
  transfers between devices with their start and end apart: 45 -> 45, of which waited for: 27 -> 27; matrix products, arithmetic and copies ran while one was open for 4% -> 4% of each run, Pallas kernels for 33% -> 35%
where the time goes in v9:
time: 134 us
  Pallas kernels  52 us (39%)
  starting transfers between devices  27.1 us (20%)
  waiting for transfers between devices  24.5 us (18%)
  blocking collectives  13.8 us (10%)
  local copies, waits for them, and re-layouts  12.2 us (9%)
  other arithmetic  4.12 us (3%)
    pallas_call x8, Pallas kernels, on_chip(): pl.pallas_call(lambda *refs: kernel(len(pieces), *refs), in_specs=[vmem]...  52 us
    ppermute x45, starting transfers between devices, move(): return lax.ppermute(value, 'fsdp', pairs)  27.1 us
    ppermute x45, waiting for transfers between devices, move(): return lax.ppermute(value, 'fsdp', pairs)  24.5 us
    all_to_all x1, blocking collectives, on_device(): parts = lax.all_to_all(parts, 'fsdp', 0, 0)  13.8 us
    unnamed x30, local copies, waits for them, and re-layouts  10.7 us
  transfers between devices with their start and end apart: 45, of which 27 were waited for; matrix products, arithmetic and copies ran while one was open for 4% of the time, Pallas kernels for 35%

profile of v9, /device:TPU:0, one launch (start us, length us, event | category | flops | bytes accessed | tf_op | source)
XLA Modules:
  0.0 133.9 jit_solution(1859892157603652421)
XLA Ops:
  0.0 3.0 %collective-permute-start.4 = (bf16[64,5120]{1,0:T(8,128)(2,1)}, bf16[64,5120]{1,0:T(8,128)(2,1)S(1)}, u32[]{:S(2)}, u32[]{:S(2)}) collective-permute-start(bf16[64,5120]{1,0:T(8,128)(2,1)} %refs_0_.1), channel_id=1, source_target_pairs={{0,4},{1,13},{2,6},{3,15},{4,8},{5,1},{6,10},{7,3},{8,12},{9,5},{1... | collective-permute-start | bytes 1966088 | tf_op jit(solution)/shard_map/ppermute | solution.py:186
  3.0 1.5 %collective-permute-start.5 = (bf16[64,5120]{1,0:T(8,128)(2,1)}, bf16[64,5120]{1,0:T(8,128)(2,1)S(1)}, u32[]{:S(2)}, u32[]{:S(2)}) collective-permute-start(bf16[64,5120]{1,0:T(8,128)(2,1)} %refs_0_.1), channel_id=1, source_target_pairs={{0,2},{1,3},{2,0},{3,1},{4,6},{5,7},{6,4},{7,5},{8,10},{9,11},{10,... | collective-permute-start | bytes 1966088 | tf_op jit(solution)/shard_map/ppermute | solution.py:186
  4.5 0.7 convert_element_type.16
  5.2 0.7 add_convert_fusion
  5.9 0.7 add_convert_fusion.1
  6.6 1.4 %fusion.refs_8_.refs_7_ = bf16[256,5120]{1,0:T(8,128)(2,1)S(1)} fusion(s32[5120]{0:T(1024)} %param.18, bf16[5120]{0:T(1024)(128)(2,1)S(1)} %add_convert_fusion), kind=kLoop, calls=%fused_computation.1 | loop fusion | flops 2621440 | bytes 2652160 | tf_op jit(solution)/shard_map/jit(_where)/select_n | solution.py:24
  8.1 0.4 fusion.1.refs_9_.refs_8_
  8.7 1.6 %collective-permute-start = (bf16[64,5248]{1,0:T(8,128)(2,1)S(1)}, bf16[64,5248]{1,0:T(8,128)(2,1)S(1)}, u32[]{:S(2)}, u32[]{:S(2)}) collective-permute-start(bf16[64,5248]{1,0:T(8,128)(2,1)S(1)} %pad_maximum_fusion.refs_0_), channel_id=1, source_target_pairs={{0,4},{1,13},{2,6},{3,15},{4,8},{5,1},{6,10},{7,3},{8,12},{9,5},{1... | collective-permute-start | bytes 2015240 | tf_op jit(solution)/shard_map/ppermute | solution.py:186
  10.3 0.5 collective-permute-start.1
  10.8 10.0 %collective-permute-done.4.refs_0_ = bf16[64,5120]{1,0:T(8,128)(2,1)S(1)} collective-permute-done((bf16[64,5120]{1,0:T(8,128)(2,1)}, bf16[64,5120]{1,0:T(8,128)(2,1)S(1)}, u32[]{:S(2)}, u32[]{:S(2)}) %collective-permute-start.4) | collective-permute-done | bytes 655392 | tf_op jit(solution)/shard_map/ppermute | solution.py:186
  20.9 0.8 collective-permute-start.6
  21.8 0.5 collective-permute-start.2
  22.3 0.6 collective-permute-done.6.refs_4_
  22.9 0.4 collective-permute-start.3
  23.4 1.3 %collective-permute-start.16 = (bf16[64,5120]{1,0:T(8,128)(2,1)S(1)}, bf16[64,5120]{1,0:T(8,128)(2,1)S(1)}, u32[]{:S(2)}, u32[]{:S(2)}) collective-permute-start(bf16[64,5120]{1,0:T(8,128)(2,1)S(1)} %collective-permute-done.4.refs_0_), channel_id=1, source_target_pairs={{0,4},{1,13},{2,6},{3,15},{4,8},{5,1},{6,10},{7,3},{8,12},{9,5},{1... | collective-permute-start | bytes 1966088 | tf_op jit(solution)/shard_map/ppermute | solution.py:186
  24.7 1.5 %collective-permute-start.17 = (bf16[64,5120]{1,0:T(8,128)(2,1)S(1)}, bf16[64,5120]{1,0:T(8,128)(2,1)S(1)}, u32[]{:S(2)}, u32[]{:S(2)}) collective-permute-start(bf16[64,5120]{1,0:T(8,128)(2,1)S(1)} %collective-permute-done.4.refs_0_), channel_id=1, source_target_pairs={{0,2},{1,3},{2,0},{3,1},{4,6},{5,7},{6,4},{7,5},{8,10},{9,11},{10,... | collective-permute-start | bytes 1966088 | tf_op jit(solution)/shard_map/ppermute | solution.py:186
  26.2 3.5 %copy-done = bf16[5120,864]{0,1:T(8,128)(2,1)S(1)} copy-done((bf16[5120,864]{0,1:T(8,128)(2,1)S(1)}, bf16[5120,864]{0,1:T(8,128)(2,1)}, u32[]{:S(2)}) %copy-start) | copy-done | bytes 8847384
  29.7 3.5 %copy-done.1 = bf16[5120,864]{0,1:T(8,128)(2,1)S(1)} copy-done((bf16[5120,864]{0,1:T(8,128)(2,1)S(1)}, bf16[5120,864]{0,1:T(8,128)(2,1)}, u32[]{:S(2)}) %copy-start.1) | copy-done | bytes 8847384
  33.2 7.9 %forward.4 = (f32[256,864]{1,0:T(8,128)S(1)}, f32[256,864]{1,0:T(8,128)S(1)}, bf16[256,256]{1,0:T(8,128)(2,1)S(1)}, bf16[256,256]{1,0:T(8,128)(2,1)S(1)}) custom-call(bf16[64,5120]{1,0:T(8,128)(2,1)S(1)} %copy-done.3, bf16[32,5120]{1,0:T(8,128)(2,1)S(1)} %collective-permute-done.2.refs_1_, bf16[32,5120]{1,0:T(8,128)(2,1)S(1)} %collective-permute-done.3.refs_2_, ...), custom_call_target="tpu_custom_call" | custom-call | tf_op jit(solution)/shard_map/forward/pallas_call | solution.py:139
  41.2 0.4 collective-permute-start.10
  41.8 0.4 collective-permute-start.12
  42.2 0.7 collective-permute-done.10.refs_1_
  43.4 1.6 %collective-permute-start.8 = (bf16[64,5248]{1,0:T(8,128)(2,1)S(1)}, bf16[64,5248]{1,0:T(8,128)(2,1)S(1)}, u32[]{:S(2)}, u32[]{:S(2)}) collective-permute-start(bf16[64,5248]{1,0:T(8,128)(2,1)S(1)} %collective-permute-done.refs_0_), channel_id=1, source_target_pairs={{0,4},{1,13},{2,6},{3,15},{4,8},{5,1},{6,10},{7,3},{8,12},{9,5},{1... | collective-permute-start | bytes 2015240 | tf_op jit(solution)/shard_map/ppermute | solution.py:186
  45.0 0.5 collective-permute-start.9
  45.6 3.7 %copy-done.2 = bf16[864,5120]{1,0:T(8,128)(2,1)S(1)} copy-done((bf16[864,5120]{1,0:T(8,128)(2,1)S(1)}, bf16[864,5120]{1,0:T(8,128)(2,1)}, u32[]{:S(2)}) %copy-start.2) | copy-done | bytes 8847384
  49.3 5.1 %backward.4.refs_13_ = f32[256,512]{1,0:T(8,128)S(1)} custom-call(bf16[64,5248]{1,0:T(8,128)(2,1)S(1)} %pad_maximum_fusion.refs_0_, bf16[32,5248]{1,0:T(8,128)(2,1)S(1)} %collective-permute-done.10.refs_1_, bf16[32,5248]{1,0:T(8,128)(2,1)S(1)} %collective-permute-done.11.refs_2_, bf16[64,5248]{1,0:T(8,128)(2,1)S(1)} %collective-permute-done.1.refs_3_, ...), custom_call_target="tpu_custom_call" | custom-call | tf_op jit(solution)/shard_map/backward/pallas_call | solution.py:139
  54.4 0.5 collective-permute-start.18
  55.1 0.5 collective-permute-start.14
  55.6 0.6 collective-permute-done.18.refs_4_
  56.2 0.4 collective-permute-start.15
  56.7 0.5 collective-permute-start.30
  57.3 1.4 %collective-permute-start.31 = (bf16[64,5120]{1,0:T(8,128)(2,1)S(1)}, bf16[64,5120]{1,0:T(8,128)(2,1)S(1)}, u32[]{:S(2)}, u32[]{:S(2)}) collective-permute-start(bf16[64,5120]{1,0:T(8,128)(2,1)S(1)} %collective-permute-done.16.refs_0_), channel_id=1, source_target_pairs={{0,2},{1,3},{2,0},{3,1},{4,6},{5,7},{6,4},{7,5},{8,10},{9,11},{10,... | collective-permute-start | bytes 1966088 | tf_op jit(solution)/shard_map/ppermute | solution.py:186
  58.7 1.4 %collective-permute-start.22 = (bf16[32,5248]{1,0:T(8,128)(2,1)S(1)}, bf16[32,5248]{1,0:T(8,128)(2,1)S(1)}, u32[]{:S(2)}, u32[]{:S(2)}) collective-permute-start(bf16[32,5248]{1,0:T(8,128)(2,1)S(1)} %get-tuple-element.170), channel_id=1, source_target_pairs={{0,1},{1,0},{2,3},{3,2},{4,5},{5,4},{6,7},{7,6},{8,9},{9,8},{10,11... | collective-permute-start | bytes 1007624 | tf_op jit(solution)/shard_map/ppermute | solution.py:186
  60.1 7.9 %forward.5 = (f32[256,864]{1,0:T(8,128)S(1)}, f32[256,864]{1,0:T(8,128)S(1)}, bf16[256,256]{1,0:T(8,128)(2,1)S(1)}, bf16[256,256]{1,0:T(8,128)(2,1)S(1)}) custom-call(bf16[64,5120]{1,0:T(8,128)(2,1)S(1)} %collective-permute-done.4.refs_0_, bf16[32,5120]{1,0:T(8,128)(2,1)S(1)} %collective-permute-done.14.refs_1_, ...), custom_call_target="tpu_custom_call" | custom-call | tf_op jit(solution)/shard_map/forward/pallas_call | solution.py:139
  68.2 0.5 collective-permute-start.27
  68.9 0.9 collective-permute-done.26.refs_1_
  70.0 0.3 collective-permute-done.27.refs_2_
  71.5 0.5 collective-permute-done.25.refs_5_
  72.0 5.1 %backward.5.refs_13_ = f32[256,512]{1,0:T(8,128)S(1)} custom-call(bf16[64,5248]{1,0:T(8,128)(2,1)S(1)} %collective-permute-done.refs_0_, bf16[32,5248]{1,0:T(8,128)(2,1)S(1)} %collective-permute-done.22.refs_1_, bf16[32,5248]{1,0:T(8,128)(2,1)S(1)} %collective-permute-done.23.refs_2_, bf16[64,5248]{1,0:T(8,128)(2,1)S(1)} %collective-permute-done.9.refs_3_, ...), custom_call_target="tpu_custom_call" | custom-call | tf_op jit(solution)/shard_map/backward/pallas_call | solution.py:139
  77.1 0.6 collective-permute-done.30.refs_3_
  77.7 1.8 %collective-permute-start.39 = (bf16[64,5120]{1,0:T(8,128)(2,1)S(1)}, bf16[64,5120]{1,0:T(8,128)(2,1)S(1)}, u32[]{:S(2)}, u32[]{:S(2)}) collective-permute-start(bf16[64,5120]{1,0:T(8,128)(2,1)S(1)} %collective-permute-done.30.refs_3_), channel_id=1, source_target_pairs={{0,2},{1,3},{2,0},{3,1},{4,6},{5,7},{6,4},{7,5},{8,10},{9,11},{10,... | collective-permute-start | bytes 1966088 | tf_op jit(solution)/shard_map/ppermute | solution.py:186
  79.5 0.5 collective-permute-start.33
  80.2 0.9 collective-permute-done.32.refs_4_
  82.2 0.6 collective-permute-done.35.refs_2_
  82.8 0.5 collective-permute-done.28.refs_1_
  83.3 0.5 collective-permute-done.29.refs_2_
  83.7 7.9 %forward.6 = (f32[256,864]{1,0:T(8,128)S(1)}, f32[256,864]{1,0:T(8,128)S(1)}, bf16[256,256]{1,0:T(8,128)(2,1)S(1)}, bf16[256,256]{1,0:T(8,128)(2,1)S(1)}) custom-call(bf16[64,5120]{1,0:T(8,128)(2,1)S(1)} %collective-permute-done.16.refs_0_, bf16[32,5120]{1,0:T(8,128)(2,1)S(1)} %collective-permute-done.28.refs_1_, ...), custom_call_target="tpu_custom_call" | custom-call | tf_op jit(solution)/shard_map/forward/pallas_call | solution.py:139
  91.7 0.4 collective-permute-done.21.refs_3_
  92.1 1.7 %collective-permute-start.36 = (bf16[64,5248]{1,0:T(8,128)(2,1)S(1)}, bf16[64,5248]{1,0:T(8,128)(2,1)S(1)}, u32[]{:S(2)}, u32[]{:S(2)}) collective-permute-start(bf16[64,5248]{1,0:T(8,128)(2,1)S(1)} %collective-permute-done.21.refs_3_), channel_id=1, source_target_pairs={{0,2},{1,3},{2,0},{3,1},{4,6},{5,7},{6,4},{7,5},{8,10},{9,11},{10,... | collective-permute-start | bytes 2015240 | tf_op jit(solution)/shard_map/ppermute | solution.py:186
  93.8 1.2 collective-permute-done.39.refs_3_
  95.1 0.6 collective-permute-start.37
  95.8 1.9 %collective-permute-done.37.refs_4_ = bf16[32,5248]{1,0:T(8,128)(2,1)S(1)} collective-permute-done((bf16[32,5248]{1,0:T(8,128)(2,1)S(1)}, bf16[32,5248]{1,0:T(8,128)(2,1)S(1)}, u32[]{:S(2)}, u32[]{:S(2)}) %collective-permute-start.37) | collective-permute-done | bytes 335904 | tf_op jit(solution)/shard_map/ppermute | solution.py:186
  97.6 0.5 collective-permute-done.38.refs_5_
  98.1 5.1 %backward.6.refs_13_ = f32[256,512]{1,0:T(8,128)S(1)} custom-call(bf16[64,5248]{1,0:T(8,128)(2,1)S(1)} %collective-permute-done.8.refs_0_, bf16[32,5248]{1,0:T(8,128)(2,1)S(1)} %collective-permute-done.26.refs_1_, bf16[32,5248]{1,0:T(8,128)(2,1)S(1)} %collective-permute-done.27.refs_2_, bf16[64,5248]{1,0:T(8,128)(2,1)S(1)} %collective-permute-done.21.refs_3_, ...), custom_call_target="tpu_custom_call" | custom-call | tf_op jit(solution)/shard_map/backward/pallas_call | solution.py:139
  103.2 7.9 %forward.7 = (f32[256,864]{1,0:T(8,128)S(1)}, f32[256,864]{1,0:T(8,128)S(1)}, bf16[256,256]{1,0:T(8,128)(2,1)S(1)}, bf16[256,256]{1,0:T(8,128)(2,1)S(1)}) custom-call(bf16[64,5120]{1,0:T(8,128)(2,1)S(1)} %collective-permute-done.31.refs_0_, bf16[32,5120]{1,0:T(8,128)(2,1)S(1)} %collective-permute-done.34.refs_1_, ...), custom_call_target="tpu_custom_call" | custom-call | tf_op jit(solution)/shard_map/forward/pallas_call | solution.py:139
  111.4 0.4 collective-permute-start.42
  112.0 0.4 collective-permute-start.44
  112.4 0.5 collective-permute-done.41.refs_1_
  112.9 0.5 collective-permute-done.42.refs_2_
  113.4 0.5 collective-permute-done.43.refs_4_
  113.9 0.5 collective-permute-done.44.refs_5_
  114.3 5.1 %backward.7 = f32[256,512]{1,0:T(8,128)S(1)} custom-call(bf16[64,5248]{1,0:T(8,128)(2,1)S(1)} %collective-permute-done.20.refs_0_, bf16[32,5248]{1,0:T(8,128)(2,1)S(1)} %collective-permute-done.41.refs_1_, bf16[32,5248]{1,0:T(8,128)(2,1)S(1)} %collective-permute-done.42.refs_2_, bf16[64,5248]{1,0:T(8,128)(2,1)S(1)} %collective-permute-done.36.refs_3_, ...), custom_call_target="tpu_custom_call" | custom-call | tf_op jit(solution)/shard_map/backward/pallas_call | solution.py:139
  119.5 13.8 %all_to_all.5 = bf16[16,16,512]{2,1,0:T(8,128)(2,1)S(1)} all-to-all(bf16[16,16,512]{2,1,0:T(8,128)(2,1)S(1)} %bitcast.18), channel_id=1, replica_groups=mesh['groups'=2,'fsdp'=16] {'fsdp'}, dimensions={0} | all-to-all | bytes 524288 | tf_op jit(solution)/shard_map/all_to_all | solution.py:256
  133.3 0.6 copy.11
  (96 shorter events, 5.3 us)
Async XLA Ops:
  0.0 8.1 %copy-start.5 = (s32[3,864]{1,0:T(4,128)S(1)}, s32[3,864]{1,0:T(4,128)}, u32[]{:S(2)}) copy-start(s32[3,864]{1,0:T(4,128)} %param.16) | copy-start | bytes 31108
  0.0 8.6 %copy-start.4 = (bf16[64,5120]{1,0:T(8,128)(2,1)S(1)}, bf16[64,5120]{1,0:T(8,128)(2,1)}, u32[]{:S(2)}) copy-start(bf16[64,5120]{1,0:T(8,128)(2,1)} %param.11) | copy-start | bytes 1966084
  0.0 20.8 %collective-permute-start.4 = (bf16[64,5120]{1,0:T(8,128)(2,1)}, bf16[64,5120]{1,0:T(8,128)(2,1)S(1)}, u32[]{:S(2)}, u32[]{:S(2)}) collective-permute-start(bf16[64,5120]{1,0:T(8,128)(2,1)} %refs_0_.1), channel_id=1, source_target_pairs={{0,4},{1,13},{2,6},{3,15},{4,8},{5,1},{6,10},{7,3},{8,12},{9,5},{1... | collective-permute-start | bytes 1966088 | tf_op jit(solution)/shard_map/ppermute | solution.py:186
  3.0 17.8 %collective-permute-start.5 = (bf16[64,5120]{1,0:T(8,128)(2,1)}, bf16[64,5120]{1,0:T(8,128)(2,1)S(1)}, u32[]{:S(2)}, u32[]{:S(2)}) collective-permute-start(bf16[64,5120]{1,0:T(8,128)(2,1)} %refs_0_.1), channel_id=1, source_target_pairs={{0,2},{1,3},{2,0},{3,1},{4,6},{5,7},{6,4},{7,5},{8,10},{9,11},{10,... | collective-permute-start | bytes 1966088 | tf_op jit(solution)/shard_map/ppermute | solution.py:186
  8.1 13.6 %copy-start.3 = (bf16[64,5120]{1,0:T(8,128)(2,1)S(1)}, bf16[64,5120]{1,0:T(8,128)(2,1)}, u32[]{:S(2)}) copy-start(bf16[64,5120]{1,0:T(8,128)(2,1)} %refs_0_.1) | copy-start | bytes 1966084
  8.7 32.5 %collective-permute-start = (bf16[64,5248]{1,0:T(8,128)(2,1)S(1)}, bf16[64,5248]{1,0:T(8,128)(2,1)S(1)}, u32[]{:S(2)}, u32[]{:S(2)}) collective-permute-start(bf16[64,5248]{1,0:T(8,128)(2,1)S(1)} %pad_maximum_fusion.refs_0_), channel_id=1, source_target_pairs={{0,4},{1,13},{2,6},{3,15},{4,8},{5,1},{6,10},{7,3},{8,12},{9,5},{1... | collective-permute-start | bytes 2015240 | tf_op jit(solution)/shard_map/ppermute | solution.py:186
  10.3 30.8 %collective-permute-start.1 = (bf16[64,5248]{1,0:T(8,128)(2,1)S(1)}, bf16[64,5248]{1,0:T(8,128)(2,1)S(1)}, u32[]{:S(2)}, u32[]{:S(2)}) collective-permute-start(bf16[64,5248]{1,0:T(8,128)(2,1)S(1)} %pad_maximum_fusion.refs_0_), channel_id=1, source_target_pairs={{0,2},{1,3},{2,0},{3,1},{4,6},{5,7},{6,4},{7,5},{8,10},{9,11},{10,... | collective-permute-start | bytes 2015240 | tf_op jit(solution)/shard_map/ppermute | solution.py:186
  20.9 2.0 %collective-permute-start.6 = (bf16[32,5120]{1,0:T(8,128)(2,1)S(1)}, bf16[32,5120]{1,0:T(8,128)(2,1)S(1)}, u32[]{:S(2)}, u32[]{:S(2)}) collective-permute-start(bf16[32,5120]{1,0:T(8,128)(2,1)S(1)} %get-tuple-element.186), channel_id=1, source_target_pairs={{0,1},{1,0},{2,3},{3,2},{4,5},{5,4},{6,7},{7,6},{8,9},{9,8},{10,11... | collective-permute-start | bytes 983048 | tf_op jit(solution)/shard_map/ppermute | solution.py:186
  21.6 1.7 %collective-permute-start.7 = (bf16[32,5120]{1,0:T(8,128)(2,1)S(1)}, bf16[32,5120]{1,0:T(8,128)(2,1)S(1)}, u32[]{:S(2)}, u32[]{:S(2)}) collective-permute-start(bf16[32,5120]{1,0:T(8,128)(2,1)S(1)} %get-tuple-element.185), channel_id=1, source_target_pairs={{0,1},{1,0},{2,3},{3,2},{4,5},{5,4},{6,7},{7,6},{8,9},{9,8},{10,11... | collective-permute-start | bytes 983048 | tf_op jit(solution)/shard_map/ppermute | solution.py:186
  21.8 2.9 %collective-permute-start.2 = (bf16[32,5120]{1,0:T(8,128)(2,1)S(1)}, bf16[32,5120]{1,0:T(8,128)(2,1)S(1)}, u32[]{:S(2)}, u32[]{:S(2)}) collective-permute-start(bf16[32,5120]{1,0:T(8,128)(2,1)S(1)} %get-tuple-element.188), channel_id=1, source_target_pairs={{0,1},{1,0},{2,3},{3,2},{4,5},{5,4},{6,7},{7,6},{8,9},{9,8},{10,11... | collective-permute-start | bytes 983048 | tf_op jit(solution)/shard_map/ppermute | solution.py:186
  22.9 3.3 %collective-permute-start.3 = (bf16[32,5120]{1,0:T(8,128)(2,1)S(1)}, bf16[32,5120]{1,0:T(8,128)(2,1)S(1)}, u32[]{:S(2)}, u32[]{:S(2)}) collective-permute-start(bf16[32,5120]{1,0:T(8,128)(2,1)S(1)} %get-tuple-element.187), channel_id=1, source_target_pairs={{0,1},{1,0},{2,3},{3,2},{4,5},{5,4},{6,7},{7,6},{8,9},{9,8},{10,11... | collective-permute-start | bytes 983048 | tf_op jit(solution)/shard_map/ppermute | solution.py:186
  23.4 31.0 %collective-permute-start.16 = (bf16[64,5120]{1,0:T(8,128)(2,1)S(1)}, bf16[64,5120]{1,0:T(8,128)(2,1)S(1)}, u32[]{:S(2)}, u32[]{:S(2)}) collective-permute-start(bf16[64,5120]{1,0:T(8,128)(2,1)S(1)} %collective-permute-done.4.refs_0_), channel_id=1, source_target_pairs={{0,4},{1,13},{2,6},{3,15},{4,8},{5,1},{6,10},{7,3},{8,12},{9,5},{1... | collective-permute-start | bytes 1966088 | tf_op jit(solution)/shard_map/ppermute | solution.py:186
  24.7 29.6 %collective-permute-start.17 = (bf16[64,5120]{1,0:T(8,128)(2,1)S(1)}, bf16[64,5120]{1,0:T(8,128)(2,1)S(1)}, u32[]{:S(2)}, u32[]{:S(2)}) collective-permute-start(bf16[64,5120]{1,0:T(8,128)(2,1)S(1)} %collective-permute-done.4.refs_0_), channel_id=1, source_target_pairs={{0,2},{1,3},{2,0},{3,1},{4,6},{5,7},{6,4},{7,5},{8,10},{9,11},{10,... | collective-permute-start | bytes 1966088 | tf_op jit(solution)/shard_map/ppermute | solution.py:186
  26.2 3.5 %copy-start = (bf16[5120,864]{0,1:T(8,128)(2,1)S(1)}, bf16[5120,864]{0,1:T(8,128)(2,1)}, u32[]{:S(2)}) copy-start(bf16[5120,864]{0,1:T(8,128)(2,1)} %param.13) | copy-start | bytes 26542084
  29.7 3.5 %copy-start.1 = (bf16[5120,864]{0,1:T(8,128)(2,1)S(1)}, bf16[5120,864]{0,1:T(8,128)(2,1)}, u32[]{:S(2)}) copy-start(bf16[5120,864]{0,1:T(8,128)(2,1)} %param.14) | copy-start | bytes 26542084
  33.2 26.9 %slice-start.3 = ((s8[8847360]{0:T(1024)(128)(4,1)}), s8[4194304]{0:T(1024)(128)(4,1)S(1)}, s32[]{:S(2)}) async-start(s8[8847360]{0:T(1024)(128)(4,1)} %bitcast.11), calls=%async_computation.4 | async-start | bytes 8388608
  33.2 26.9 %slice-start.4 = ((s8[8847360]{0:T(1024)(128)(4,1)}), s8[4194304]{0:T(1024)(128)(4,1)S(1)}, s32[]{:S(2)}) async-start(s8[8847360]{0:T(1024)(128)(4,1)} %bitcast.11), calls=%async_computation.5 | async-start | bytes 8388608
  41.2 1.7 %collective-permute-start.10 = (bf16[32,5248]{1,0:T(8,128)(2,1)S(1)}, bf16[32,5248]{1,0:T(8,128)(2,1)S(1)}, u32[]{:S(2)}, u32[]{:S(2)}) collective-permute-start(bf16[32,5248]{1,0:T(8,128)(2,1)S(1)} %get-tuple-element.174), channel_id=1, source_target_pairs={{0,1},{1,0},{2,3},{3,2},{4,5},{5,4},{6,7},{7,6},{8,9},{9,8},{10,11... | collective-permute-start | bytes 1007624 | tf_op jit(solution)/shard_map/ppermute | solution.py:186
  41.6 1.8 %collective-permute-start.11 = (bf16[32,5248]{1,0:T(8,128)(2,1)S(1)}, bf16[32,5248]{1,0:T(8,128)(2,1)S(1)}, u32[]{:S(2)}, u32[]{:S(2)}) collective-permute-start(bf16[32,5248]{1,0:T(8,128)(2,1)S(1)} %get-tuple-element.173), channel_id=1, source_target_pairs={{0,1},{1,0},{2,3},{3,2},{4,5},{5,4},{6,7},{7,6},{8,9},{9,8},{10,11... | collective-permute-start | bytes 1007624 | tf_op jit(solution)/shard_map/ppermute | solution.py:186
  41.8 3.1 %collective-permute-start.12 = (bf16[32,5248]{1,0:T(8,128)(2,1)S(1)}, bf16[32,5248]{1,0:T(8,128)(2,1)S(1)}, u32[]{:S(2)}, u32[]{:S(2)}) collective-permute-start(bf16[32,5248]{1,0:T(8,128)(2,1)S(1)} %get-tuple-element.172), channel_id=1, source_target_pairs={{0,1},{1,0},{2,3},{3,2},{4,5},{5,4},{6,7},{7,6},{8,9},{9,8},{10,11... | collective-permute-start | bytes 1007624 | tf_op jit(solution)/shard_map/ppermute | solution.py:186
  42.9 2.6 %collective-permute-start.13 = (bf16[32,5248]{1,0:T(8,128)(2,1)S(1)}, bf16[32,5248]{1,0:T(8,128)(2,1)S(1)}, u32[]{:S(2)}, u32[]{:S(2)}) collective-permute-start(bf16[32,5248]{1,0:T(8,128)(2,1)S(1)} %get-tuple-element.171), channel_id=1, source_target_pairs={{0,1},{1,0},{2,3},{3,2},{4,5},{5,4},{6,7},{7,6},{8,9},{9,8},{10,11... | collective-permute-start | bytes 1007624 | tf_op jit(solution)/shard_map/ppermute | solution.py:186
  43.4 24.7 %collective-permute-start.8 = (bf16[64,5248]{1,0:T(8,128)(2,1)S(1)}, bf16[64,5248]{1,0:T(8,128)(2,1)S(1)}, u32[]{:S(2)}, u32[]{:S(2)}) collective-permute-start(bf16[64,5248]{1,0:T(8,128)(2,1)S(1)} %collective-permute-done.refs_0_), channel_id=1, source_target_pairs={{0,4},{1,13},{2,6},{3,15},{4,8},{5,1},{6,10},{7,3},{8,12},{9,5},{1... | collective-permute-start | bytes 2015240 | tf_op jit(solution)/shard_map/ppermute | solution.py:186
  45.0 23.1 %collective-permute-start.9 = (bf16[64,5248]{1,0:T(8,128)(2,1)S(1)}, bf16[64,5248]{1,0:T(8,128)(2,1)S(1)}, u32[]{:S(2)}, u32[]{:S(2)}) collective-permute-start(bf16[64,5248]{1,0:T(8,128)(2,1)S(1)} %collective-permute-done.refs_0_), channel_id=1, source_target_pairs={{0,2},{1,3},{2,0},{3,1},{4,6},{5,7},{6,4},{7,5},{8,10},{9,11},{10,... | collective-permute-start | bytes 2015240 | tf_op jit(solution)/shard_map/ppermute | solution.py:186
  45.5 14.6 %slice-start = ((s8[8847360]{0:T(1024)(128)(4,1)}), s8[4194304]{0:T(1024)(128)(4,1)S(1)}, s32[]{:S(2)}) async-start(s8[8847360]{0:T(1024)(128)(4,1)} %bitcast.5), calls=%async_computation.1 | async-start | bytes 8388608
  45.6 3.7 %copy-start.2 = (bf16[864,5120]{1,0:T(8,128)(2,1)S(1)}, bf16[864,5120]{1,0:T(8,128)(2,1)}, u32[]{:S(2)}) copy-start(bf16[864,5120]{1,0:T(8,128)(2,1)} %refs_6_.7) | copy-start | bytes 26542084
  49.3 10.9 %slice-start.1 = ((s8[8847360]{0:T(1024)(128)(4,1)}), s8[4194304]{0:T(1024)(128)(4,1)S(1)}, s32[]{:S(2)}) async-start(s8[8847360]{0:T(1024)(128)(4,1)} %bitcast.5), calls=%async_computation.2 | async-start | bytes 8388608
  49.3 10.9 %slice-start.2 = ((s8[8847360]{0:T(1024)(128)(4,1)}), s8[458752]{0:T(1024)(128)(4,1)S(1)}, s32[]{:S(2)}) async-start(s8[8847360]{0:T(1024)(128)(4,1)} %bitcast.5), calls=%async_computation.3 | async-start | bytes 917504
  49.3 10.9 %slice-start.5 = ((s8[8847360]{0:T(1024)(128)(4,1)}), s8[458752]{0:T(1024)(128)(4,1)S(1)}, s32[]{:S(2)}) async-start(s8[8847360]{0:T(1024)(128)(4,1)} %bitcast.11), calls=%async_computation.6 | async-start | bytes 917504
  54.4 1.8 %collective-permute-start.18 = (bf16[32,5120]{1,0:T(8,128)(2,1)S(1)}, bf16[32,5120]{1,0:T(8,128)(2,1)S(1)}, u32[]{:S(2)}, u32[]{:S(2)}) collective-permute-start(bf16[32,5120]{1,0:T(8,128)(2,1)S(1)} %get-tuple-element.182), channel_id=1, source_target_pairs={{0,1},{1,0},{2,3},{3,2},{4,5},{5,4},{6,7},{7,6},{8,9},{9,8},{10,11... | collective-permute-start | bytes 983048 | tf_op jit(solution)/shard_map/ppermute | solution.py:186
  55.0 1.7 %collective-permute-start.19 = (bf16[32,5120]{1,0:T(8,128)(2,1)S(1)}, bf16[32,5120]{1,0:T(8,128)(2,1)S(1)}, u32[]{:S(2)}, u32[]{:S(2)}) collective-permute-start(bf16[32,5120]{1,0:T(8,128)(2,1)S(1)} %get-tuple-element.181), channel_id=1, source_target_pairs={{0,1},{1,0},{2,3},{3,2},{4,5},{5,4},{6,7},{7,6},{8,9},{9,8},{10,11... | collective-permute-start | bytes 983048 | tf_op jit(solution)/shard_map/ppermute | solution.py:186
  55.1 2.2 %collective-permute-start.14 = (bf16[32,5120]{1,0:T(8,128)(2,1)S(1)}, bf16[32,5120]{1,0:T(8,128)(2,1)S(1)}, u32[]{:S(2)}, u32[]{:S(2)}) collective-permute-start(bf16[32,5120]{1,0:T(8,128)(2,1)S(1)} %get-tuple-element.184), channel_id=1, source_target_pairs={{0,1},{1,0},{2,3},{3,2},{4,5},{5,4},{6,7},{7,6},{8,9},{9,8},{10,11... | collective-permute-start | bytes 983048 | tf_op jit(solution)/shard_map/ppermute | solution.py:186
  56.2 2.5 %collective-permute-start.15 = (bf16[32,5120]{1,0:T(8,128)(2,1)S(1)}, bf16[32,5120]{1,0:T(8,128)(2,1)S(1)}, u32[]{:S(2)}, u32[]{:S(2)}) collective-permute-start(bf16[32,5120]{1,0:T(8,128)(2,1)S(1)} %get-tuple-element.183), channel_id=1, source_target_pairs={{0,1},{1,0},{2,3},{3,2},{4,5},{5,4},{6,7},{7,6},{8,9},{9,8},{10,11... | collective-permute-start | bytes 983048 | tf_op jit(solution)/shard_map/ppermute | solution.py:186
  56.7 21.0 %collective-permute-start.30 = (bf16[64,5120]{1,0:T(8,128)(2,1)S(1)}, bf16[64,5120]{1,0:T(8,128)(2,1)S(1)}, u32[]{:S(2)}, u32[]{:S(2)}) collective-permute-start(bf16[64,5120]{1,0:T(8,128)(2,1)S(1)} %collective-permute-done.16.refs_0_), channel_id=1, source_target_pairs={{0,4},{1,13},{2,6},{3,15},{4,8},{5,1},{6,10},{7,3},{8,12},{9,5},{1... | collective-permute-start | bytes 1966088 | tf_op jit(solution)/shard_map/ppermute | solution.py:186
  57.3 20.4 %collective-permute-start.31 = (bf16[64,5120]{1,0:T(8,128)(2,1)S(1)}, bf16[64,5120]{1,0:T(8,128)(2,1)S(1)}, u32[]{:S(2)}, u32[]{:S(2)}) collective-permute-start(bf16[64,5120]{1,0:T(8,128)(2,1)S(1)} %collective-permute-done.16.refs_0_), channel_id=1, source_target_pairs={{0,2},{1,3},{2,0},{3,1},{4,6},{5,7},{6,4},{7,5},{8,10},{9,11},{10,... | collective-permute-start | bytes 1966088 | tf_op jit(solution)/shard_map/ppermute | solution.py:186
  58.7 13.3 %slice-start.6 = ((s8[8847360]{0:T(1024)(128)(4,1)}), s8[4194304]{0:T(1024)(128)(4,1)S(1)}, s32[]{:S(2)}) async-start(s8[8847360]{0:T(1024)(128)(4,1)} %bitcast.16), calls=%async_computation.7 | async-start | bytes 8388608
  58.7 13.3 %slice-start.7 = ((s8[8847360]{0:T(1024)(128)(4,1)}), s8[4194304]{0:T(1024)(128)(4,1)S(1)}, s32[]{:S(2)}) async-start(s8[8847360]{0:T(1024)(128)(4,1)} %bitcast.16), calls=%async_computation.8 | async-start | bytes 8388608
  58.7 13.3 %slice-start.8 = ((s8[8847360]{0:T(1024)(128)(4,1)}), s8[458752]{0:T(1024)(128)(4,1)S(1)}, s32[]{:S(2)}) async-start(s8[8847360]{0:T(1024)(128)(4,1)} %bitcast.16), calls=%async_computation.9 | async-start | bytes 917504
  58.7 10.1 %collective-permute-start.22 = (bf16[32,5248]{1,0:T(8,128)(2,1)S(1)}, bf16[32,5248]{1,0:T(8,128)(2,1)S(1)}, u32[]{:S(2)}, u32[]{:S(2)}) collective-permute-start(bf16[32,5248]{1,0:T(8,128)(2,1)S(1)} %get-tuple-element.170), channel_id=1, source_target_pairs={{0,1},{1,0},{2,3},{3,2},{4,5},{5,4},{6,7},{7,6},{8,9},{9,8},{10,11... | collective-permute-start | bytes 1007624 | tf_op jit(solution)/shard_map/ppermute | solution.py:186
  68.1 1.7 %collective-permute-start.26 = (bf16[32,5248]{1,0:T(8,128)(2,1)S(1)}, bf16[32,5248]{1,0:T(8,128)(2,1)S(1)}, u32[]{:S(2)}, u32[]{:S(2)}) collective-permute-start(bf16[32,5248]{1,0:T(8,128)(2,1)S(1)} %get-tuple-element.166), channel_id=1, source_target_pairs={{0,1},{1,0},{2,3},{3,2},{4,5},{5,4},{6,7},{7,6},{8,9},{9,8},{10,11... | collective-permute-start | bytes 1007624 | tf_op jit(solution)/shard_map/ppermute | solution.py:186
  68.2 2.1 %collective-permute-start.27 = (bf16[32,5248]{1,0:T(8,128)(2,1)S(1)}, bf16[32,5248]{1,0:T(8,128)(2,1)S(1)}, u32[]{:S(2)}, u32[]{:S(2)}) collective-permute-start(bf16[32,5248]{1,0:T(8,128)(2,1)S(1)} %get-tuple-element.165), channel_id=1, source_target_pairs={{0,1},{1,0},{2,3},{3,2},{4,5},{5,4},{6,7},{7,6},{8,9},{9,8},{10,11... | collective-permute-start | bytes 1007624 | tf_op jit(solution)/shard_map/ppermute | solution.py:186
  68.8 2.0 %collective-permute-start.23 = (bf16[32,5248]{1,0:T(8,128)(2,1)S(1)}, bf16[32,5248]{1,0:T(8,128)(2,1)S(1)}, u32[]{:S(2)}, u32[]{:S(2)}) collective-permute-start(bf16[32,5248]{1,0:T(8,128)(2,1)S(1)} %get-tuple-element.169), channel_id=1, source_target_pairs={{0,1},{1,0},{2,3},{3,2},{4,5},{5,4},{6,7},{7,6},{8,9},{9,8},{10,11... | collective-permute-start | bytes 1007624 | tf_op jit(solution)/shard_map/ppermute | solution.py:186
  69.8 1.6 %collective-permute-start.24 = (bf16[32,5248]{1,0:T(8,128)(2,1)S(1)}, bf16[32,5248]{1,0:T(8,128)(2,1)S(1)}, u32[]{:S(2)}, u32[]{:S(2)}) collective-permute-start(bf16[32,5248]{1,0:T(8,128)(2,1)S(1)} %get-tuple-element.168), channel_id=1, source_target_pairs={{0,1},{1,0},{2,3},{3,2},{4,5},{5,4},{6,7},{7,6},{8,9},{9,8},{10,11... | collective-permute-start | bytes 1007624 | tf_op jit(solution)/shard_map/ppermute | solution.py:186
  70.3 1.6 %collective-permute-start.25 = (bf16[32,5248]{1,0:T(8,128)(2,1)S(1)}, bf16[32,5248]{1,0:T(8,128)(2,1)S(1)}, u32[]{:S(2)}, u32[]{:S(2)}) collective-permute-start(bf16[32,5248]{1,0:T(8,128)(2,1)S(1)} %get-tuple-element.167), channel_id=1, source_target_pairs={{0,1},{1,0},{2,3},{3,2},{4,5},{5,4},{6,7},{7,6},{8,9},{9,8},{10,11... | collective-permute-start | bytes 1007624 | tf_op jit(solution)/shard_map/ppermute | solution.py:186
  70.8 21.3 %collective-permute-start.21 = (bf16[64,5248]{1,0:T(8,128)(2,1)S(1)}, bf16[64,5248]{1,0:T(8,128)(2,1)S(1)}, u32[]{:S(2)}, u32[]{:S(2)}) collective-permute-start(bf16[64,5248]{1,0:T(8,128)(2,1)S(1)} %collective-permute-done.8.refs_0_), channel_id=1, source_target_pairs={{0,4},{1,13},{2,6},{3,15},{4,8},{5,1},{6,10},{7,3},{8,12},{9,5},{1... | collective-permute-start | bytes 2015240 | tf_op jit(solution)/shard_map/ppermute | solution.py:186
  77.7 17.3 %collective-permute-start.39 = (bf16[64,5120]{1,0:T(8,128)(2,1)S(1)}, bf16[64,5120]{1,0:T(8,128)(2,1)S(1)}, u32[]{:S(2)}, u32[]{:S(2)}) collective-permute-start(bf16[64,5120]{1,0:T(8,128)(2,1)S(1)} %collective-permute-done.30.refs_3_), channel_id=1, source_target_pairs={{0,2},{1,3},{2,0},{3,1},{4,6},{5,7},{6,4},{7,5},{8,10},{9,11},{10,... | collective-permute-start | bytes 1966088 | tf_op jit(solution)/shard_map/ppermute | solution.py:186
  79.5 1.6 %collective-permute-start.32 = (bf16[32,5120]{1,0:T(8,128)(2,1)S(1)}, bf16[32,5120]{1,0:T(8,128)(2,1)S(1)}, u32[]{:S(2)}, u32[]{:S(2)}) collective-permute-start(bf16[32,5120]{1,0:T(8,128)(2,1)S(1)} %get-tuple-element.178), channel_id=1, source_target_pairs={{0,1},{1,0},{2,3},{3,2},{4,5},{5,4},{6,7},{7,6},{8,9},{9,8},{10,11... | collective-permute-start | bytes 983048 | tf_op jit(solution)/shard_map/ppermute | solution.py:186
  79.5 2.1 %collective-permute-start.33 = (bf16[32,5120]{1,0:T(8,128)(2,1)S(1)}, bf16[32,5120]{1,0:T(8,128)(2,1)S(1)}, u32[]{:S(2)}, u32[]{:S(2)}) collective-permute-start(bf16[32,5120]{1,0:T(8,128)(2,1)S(1)} %get-tuple-element.177), channel_id=1, source_target_pairs={{0,1},{1,0},{2,3},{3,2},{4,5},{5,4},{6,7},{7,6},{8,9},{9,8},{10,11... | collective-permute-start | bytes 983048 | tf_op jit(solution)/shard_map/ppermute | solution.py:186
  80.1 2.0 %collective-permute-start.34 = (bf16[32,5120]{1,0:T(8,128)(2,1)S(1)}, bf16[32,5120]{1,0:T(8,128)(2,1)S(1)}, u32[]{:S(2)}, u32[]{:S(2)}) collective-permute-start(bf16[32,5120]{1,0:T(8,128)(2,1)S(1)} %get-tuple-element.176), channel_id=1, source_target_pairs={{0,1},{1,0},{2,3},{3,2},{4,5},{5,4},{6,7},{7,6},{8,9},{9,8},{10,11... | collective-permute-start | bytes 983048 | tf_op jit(solution)/shard_map/ppermute | solution.py:186
  81.2 1.6 %collective-permute-start.35 = (bf16[32,5120]{1,0:T(8,128)(2,1)S(1)}, bf16[32,5120]{1,0:T(8,128)(2,1)S(1)}, u32[]{:S(2)}, u32[]{:S(2)}) collective-permute-start(bf16[32,5120]{1,0:T(8,128)(2,1)S(1)} %get-tuple-element.175), channel_id=1, source_target_pairs={{0,1},{1,0},{2,3},{3,2},{4,5},{5,4},{6,7},{7,6},{8,9},{9,8},{10,11... | collective-permute-start | bytes 983048 | tf_op jit(solution)/shard_map/ppermute | solution.py:186
  81.6 1.6 %collective-permute-start.28 = (bf16[32,5120]{1,0:T(8,128)(2,1)S(1)}, bf16[32,5120]{1,0:T(8,128)(2,1)S(1)}, u32[]{:S(2)}, u32[]{:S(2)}) collective-permute-start(bf16[32,5120]{1,0:T(8,128)(2,1)S(1)} %get-tuple-element.180), channel_id=1, source_target_pairs={{0,1},{1,0},{2,3},{3,2},{4,5},{5,4},{6,7},{7,6},{8,9},{9,8},{10,11... | collective-permute-start | bytes 983048 | tf_op jit(solution)/shard_map/ppermute | solution.py:186
  82.1 1.6 %collective-permute-start.29 = (bf16[32,5120]{1,0:T(8,128)(2,1)S(1)}, bf16[32,5120]{1,0:T(8,128)(2,1)S(1)}, u32[]{:S(2)}, u32[]{:S(2)}) collective-permute-start(bf16[32,5120]{1,0:T(8,128)(2,1)S(1)} %get-tuple-element.179), channel_id=1, source_target_pairs={{0,1},{1,0},{2,3},{3,2},{4,5},{5,4},{6,7},{7,6},{8,9},{9,8},{10,11... | collective-permute-start | bytes 983048 | tf_op jit(solution)/shard_map/ppermute | solution.py:186
  82.8 28.3 %collective-permute-start.20 = (bf16[64,5248]{1,0:T(8,128)(2,1)S(1)}, bf16[64,5248]{1,0:T(8,128)(2,1)S(1)}, u32[]{:S(2)}, u32[]{:S(2)}) collective-permute-start(bf16[64,5248]{1,0:T(8,128)(2,1)S(1)} %collective-permute-done.9.refs_3_), channel_id=1, source_target_pairs={{0,4},{1,13},{2,6},{3,15},{4,8},{5,1},{6,10},{7,3},{8,12},{9,5},{1... | collective-permute-start | bytes 2015240 | tf_op jit(solution)/shard_map/ppermute | solution.py:186
  92.1 19.1 %collective-permute-start.36 = (bf16[64,5248]{1,0:T(8,128)(2,1)S(1)}, bf16[64,5248]{1,0:T(8,128)(2,1)S(1)}, u32[]{:S(2)}, u32[]{:S(2)}) collective-permute-start(bf16[64,5248]{1,0:T(8,128)(2,1)S(1)} %collective-permute-done.21.refs_3_), channel_id=1, source_target_pairs={{0,2},{1,3},{2,0},{3,1},{4,6},{5,7},{6,4},{7,5},{8,10},{9,11},{10,... | collective-permute-start | bytes 2015240 | tf_op jit(solution)/shard_map/ppermute | solution.py:186
  95.1 8.1 %collective-permute-start.40 = (bf16[64,5120]{1,0:T(8,128)(2,1)S(1)}, bf16[64,5120]{1,0:T(8,128)(2,1)S(1)}, u32[]{:S(2)}, u32[]{:S(2)}) collective-permute-start(bf16[64,5120]{1,0:T(8,128)(2,1)S(1)} %collective-permute-done.39.refs_3_), channel_id=1, source_target_pairs={{0,1},{1,0},{2,3},{3,2},{4,5},{5,4},{6,7},{7,6},{8,9},{9,8},{10,11... | collective-permute-start | bytes 1966088 | tf_op jit(solution)/shard_map/ppermute | solution.py:186
  95.1 2.5 %collective-permute-start.37 = (bf16[32,5248]{1,0:T(8,128)(2,1)S(1)}, bf16[32,5248]{1,0:T(8,128)(2,1)S(1)}, u32[]{:S(2)}, u32[]{:S(2)}) collective-permute-start(bf16[32,5248]{1,0:T(8,128)(2,1)S(1)} %get-tuple-element.164), channel_id=1, source_target_pairs={{0,1},{1,0},{2,3},{3,2},{4,5},{5,4},{6,7},{7,6},{8,9},{9,8},{10,11... | collective-permute-start | bytes 1007624 | tf_op jit(solution)/shard_map/ppermute | solution.py:186
  95.7 2.4 %collective-permute-start.38 = (bf16[32,5248]{1,0:T(8,128)(2,1)S(1)}, bf16[32,5248]{1,0:T(8,128)(2,1)S(1)}, u32[]{:S(2)}, u32[]{:S(2)}) collective-permute-start(bf16[32,5248]{1,0:T(8,128)(2,1)S(1)} %get-tuple-element.163), channel_id=1, source_target_pairs={{0,1},{1,0},{2,3},{3,2},{4,5},{5,4},{6,7},{7,6},{8,9},{9,8},{10,11... | collective-permute-start | bytes 1007624 | tf_op jit(solution)/shard_map/ppermute | solution.py:186
  111.2 1.7 %collective-permute-start.41 = (bf16[32,5248]{1,0:T(8,128)(2,1)S(1)}, bf16[32,5248]{1,0:T(8,128)(2,1)S(1)}, u32[]{:S(2)}, u32[]{:S(2)}) collective-permute-start(bf16[32,5248]{1,0:T(8,128)(2,1)S(1)} %get-tuple-element.162), channel_id=1, source_target_pairs={{0,1},{1,0},{2,3},{3,2},{4,5},{5,4},{6,7},{7,6},{8,9},{9,8},{10,11... | collective-permute-start | bytes 1007624 | tf_op jit(solution)/shard_map/ppermute | solution.py:186
  111.4 2.0 %collective-permute-start.42 = (bf16[32,5248]{1,0:T(8,128)(2,1)S(1)}, bf16[32,5248]{1,0:T(8,128)(2,1)S(1)}, u32[]{:S(2)}, u32[]{:S(2)}) collective-permute-start(bf16[32,5248]{1,0:T(8,128)(2,1)S(1)} %get-tuple-element.161), channel_id=1, source_target_pairs={{0,1},{1,0},{2,3},{3,2},{4,5},{5,4},{6,7},{7,6},{8,9},{9,8},{10,11... | collective-permute-start | bytes 1007624 | tf_op jit(solution)/shard_map/ppermute | solution.py:186
  111.8 2.0 %collective-permute-start.43 = (bf16[32,5248]{1,0:T(8,128)(2,1)S(1)}, bf16[32,5248]{1,0:T(8,128)(2,1)S(1)}, u32[]{:S(2)}, u32[]{:S(2)}) collective-permute-start(bf16[32,5248]{1,0:T(8,128)(2,1)S(1)} %get-tuple-element.160), channel_id=1, source_target_pairs={{0,1},{1,0},{2,3},{3,2},{4,5},{5,4},{6,7},{7,6},{8,9},{9,8},{10,11... | collective-permute-start | bytes 1007624 | tf_op jit(solution)/shard_map/ppermute | solution.py:186
  112.0 2.3 %collective-permute-start.44 = (bf16[32,5248]{1,0:T(8,128)(2,1)S(1)}, bf16[32,5248]{1,0:T(8,128)(2,1)S(1)}, u32[]{:S(2)}, u32[]{:S(2)}) collective-permute-start(bf16[32,5248]{1,0:T(8,128)(2,1)S(1)} %get-tuple-element.159), channel_id=1, source_target_pairs={{0,1},{1,0},{2,3},{3,2},{4,5},{5,4},{6,7},{7,6},{8,9},{9,8},{10,11... | collective-permute-start | bytes 1007624 | tf_op jit(solution)/shard_map/ppermute | solution.py:186

commit v10 on v8

--- a/solution.py
+++ b/solution.py
@@ -14,12 +14,13 @@
 CORES = 2
 OUTER = 4
 DEPTH = 2560
+WIDE_ELEMENTS = 256 * 5120
 LANES = 128
 VMEM_LIMIT = 12 << 20
 
 
-def sign_tables(buckets, sign_bits, buckets_count):
-    matches = buckets[..., None, :] == jnp.arange(buckets_count, dtype=jnp.int32)[:, None]
+def sign_tables(buckets, sign_bits, order):
+    matches = buckets[..., None, :] == order[:, None]
     signed = (2 * sign_bits - 1).astype(jnp.bfloat16)[..., None, :]
     return jnp.where(matches, signed, jnp.zeros_like(signed))
 
@@ -67,8 +68,7 @@
     return jnp.concatenate(parts, axis=0) if len(parts) > 1 else parts[0]
 
 
-def add_products(refs, model, sums):
-    depth = min(DEPTH, model)
+def add_products(refs, model, sums, depth):
     for acc, _ in sums:
         acc[...] = jnp.zeros_like(acc)
 
@@ -87,7 +87,7 @@
     to_gate, to_up, down_part, feature_in = refs[pieces + 4 : pieces + 8]
     gate_acc, up_acc, feature_acc = refs[pieces + 8 :]
     sums = ((gate_acc, gate_w), (up_acc, up_w), (feature_acc, feature_w))
-    add_products(refs[:pieces], gate_w.shape[1], sums)
+    add_products(refs[:pieces], gate_w.shape[1], sums, min(DEPTH, gate_w.shape[1]))
     gate, up = gate_acc[...], up_acc[...]
     sigmoid = jax.nn.sigmoid(gate)
     activated = gate * sigmoid
@@ -104,7 +104,9 @@
     ]
     total, hidden_acc, feature_acc = refs[pieces + 8 :]
     model = down_w.shape[1]
-    add_products(refs[:pieces], model, ((hidden_acc, down_w), (feature_acc, feature_w)))
+    wide = hidden_acc.shape[0] * model <= WIDE_ELEMENTS
+    sums = ((hidden_acc, down_w), (feature_acc, feature_w))
+    add_products(refs[:pieces], model, sums, model if wide else min(DEPTH, model))
     bf16 = jnp.bfloat16
     hidden_grad = hidden_acc[...]
     gate_grad = (hidden_grad * to_gate[...]).astype(bf16)
@@ -181,8 +183,11 @@
 
     rows = inputs.shape[0]
 
-    unit_tables = sign_tables(unit_buckets, unit_signs, K1)
-    feature_table = sign_tables(feature_buckets, feature_signs, K2)
+    own_rows = K1 // layout.count
+    order = jnp.arange(K1, dtype=jnp.int32).reshape(-1, CORES, own_rows).swapaxes(0, 1)
+    order = jnp.where(lax.axis_index("fsdp") % CORES == 0, order, order[::-1]).reshape(-1)
+    unit_tables = sign_tables(unit_buckets, unit_signs, order)
+    feature_table = sign_tables(feature_buckets, feature_signs, jnp.arange(K2, dtype=jnp.int32))
 
     example = jnp.broadcast_to(example_ids[:, None], (rows, LANES)).astype(jnp.bfloat16)
     tagged = jnp.concatenate([out_grad, example], axis=1)
@@ -246,8 +251,11 @@
         saved = forward([gather(inputs)], gate_rows, up_rows, feature_table, unit_tables)
         total = backward([gather(tagged)], down_weight, feature_table, unit_tables, saved, total)
 
-    parts = total.astype(jnp.bfloat16).reshape(layout.count, -1, EX * K2)
-    parts = lax.all_to_all(parts, "fsdp", 0, 0)
+    half = K1 // CORES
+    part = total[:half] + move(total[half:].astype(jnp.bfloat16), layout.core_swap())
+    parts = part.astype(jnp.bfloat16).reshape(-1, own_rows, EX * K2)
+    chips = [list(range(core, layout.count, CORES)) for core in range(CORES)]
+    parts = lax.all_to_all(parts, "fsdp", 0, 0, axis_index_groups=chips)
     part = jnp.sum(parts.astype(jnp.float32), axis=0)
     factor = (3.0 * SEQ * FF * D / (K1 * K2)) ** (-0.5)
     return (factor * part).reshape(-1, EX, K2).transpose(1, 0, 2)

time: 133 us -> 131 us (0.985)
  blocking collectives: 14.2 us -> 11.4 us
  waiting for transfers between devices: 26.4 us -> 28.5 us
    all_to_all x1, blocking collectives: 14.2 us -> 11.4 us  [on_device(): parts = lax.all_to_all(parts, 'fsdp', 0, 0, axis_index_groups=chips)]
    ppermute x45 -> x46, waiting for transfers between devices: 26.4 us -> 28.5 us  [move(): return lax.ppermute(value, 'fsdp', pairs)]
    ppermute x45 -> x46, starting transfers between devices: 27.1 us -> 27.3 us  [move(): return lax.ppermute(value, 'fsdp', pairs)]
  transfers between devices with their start and end apart: 45 -> 46, of which waited for: 27 -> 28; matrix products, arithmetic and copies ran while one was open for 4% -> 4% of each run, Pallas kernels for 33% -> 32%
where the time goes in v10:
time: 131 us
  Pallas kernels  47 us (36%)
  waiting for transfers between devices  28.5 us (22%)
  starting transfers between devices  27.3 us (21%)
  local copies, waits for them, and re-layouts  12.3 us (9%)
  blocking collectives  11.4 us (9%)
  other arithmetic  4.13 us (3%)
    pallas_call x8, Pallas kernels, on_chip(): pl.pallas_call(lambda *refs: kernel(len(pieces), *refs), in_specs=[vmem]...  47 us
    ppermute x46, waiting for transfers between devices, move(): return lax.ppermute(value, 'fsdp', pairs)  28.5 us
    ppermute x46, starting transfers between devices, move(): return lax.ppermute(value, 'fsdp', pairs)  27.3 us
    all_to_all x1, blocking collectives, on_device(): parts = lax.all_to_all(parts, 'fsdp', 0, 0, axis_index_groups=chips)  11.4 us
    unnamed x30, local copies, waits for them, and re-layouts  10.7 us
  transfers between devices with their start and end apart: 46, of which 28 were waited for; matrix products, arithmetic and copies ran while one was open for 4% of the time, Pallas kernels for 32%

profile of v10, /device:TPU:0, one launch (start us, length us, event | category | flops | bytes accessed | tf_op | source)
XLA Modules:
  0.0 131.0 jit_solution(9638256721520574233)
XLA Ops:
  0.0 3.0 %collective-permute-start.4 = (bf16[64,5120]{1,0:T(8,128)(2,1)}, bf16[64,5120]{1,0:T(8,128)(2,1)S(1)}, u32[]{:S(2)}, u32[]{:S(2)}) collective-permute-start(bf16[64,5120]{1,0:T(8,128)(2,1)} %refs_0_.1), channel_id=1, source_target_pairs={{0,4},{1,13},{2,6},{3,15},{4,8},{5,1},{6,10},{7,3},{8,12},{9,5},{1... | collective-permute-start | bytes 1966088 | tf_op jit(solution)/shard_map/ppermute | solution.py:182
  3.0 1.5 %collective-permute-start.5 = (bf16[64,5120]{1,0:T(8,128)(2,1)}, bf16[64,5120]{1,0:T(8,128)(2,1)S(1)}, u32[]{:S(2)}, u32[]{:S(2)}) collective-permute-start(bf16[64,5120]{1,0:T(8,128)(2,1)} %refs_0_.1), channel_id=1, source_target_pairs={{0,2},{1,3},{2,0},{3,1},{4,6},{5,7},{6,4},{7,5},{8,10},{9,11},{10,... | collective-permute-start | bytes 1966088 | tf_op jit(solution)/shard_map/ppermute | solution.py:182
  4.5 0.7 convert_element_type.20
  5.2 0.7 add_convert_fusion
  6.0 0.7 add_convert_fusion.1
  6.7 1.4 %fusion.refs_8_.refs_7_ = bf16[256,5120]{1,0:T(8,128)(2,1)S(1)} fusion(s32[5120]{0:T(1024)} %param.18, bf16[5120]{0:T(1024)(128)(2,1)S(1)} %add_convert_fusion), kind=kLoop, calls=%fused_computation.1 | loop fusion | flops 2621440 | bytes 2652160 | tf_op jit(solution)/shard_map/jit(_where)/select_n | solution.py:25
  8.2 0.4 compare_select_fusion.refs_9_.refs_8_
  8.8 1.6 %collective-permute-start = (bf16[64,5248]{1,0:T(8,128)(2,1)S(1)}, bf16[64,5248]{1,0:T(8,128)(2,1)S(1)}, u32[]{:S(2)}, u32[]{:S(2)}) collective-permute-start(bf16[64,5248]{1,0:T(8,128)(2,1)S(1)} %pad_maximum_fusion.refs_0_), channel_id=1, source_target_pairs={{0,4},{1,13},{2,6},{3,15},{4,8},{5,1},{6,10},{7,3},{8,12},{9,5},{1... | collective-permute-start | bytes 2015240 | tf_op jit(solution)/shard_map/ppermute | solution.py:182
  10.4 0.5 collective-permute-start.1
  11.0 9.8 %collective-permute-done.4.refs_0_ = bf16[64,5120]{1,0:T(8,128)(2,1)S(1)} collective-permute-done((bf16[64,5120]{1,0:T(8,128)(2,1)}, bf16[64,5120]{1,0:T(8,128)(2,1)S(1)}, u32[]{:S(2)}, u32[]{:S(2)}) %collective-permute-start.4) | collective-permute-done | bytes 655392 | tf_op jit(solution)/shard_map/ppermute | solution.py:182
  20.9 0.8 collective-permute-start.6
  21.8 0.5 collective-permute-start.2
  22.3 0.6 collective-permute-done.6.refs_4_
  22.9 0.4 collective-permute-start.3
  23.4 1.3 %collective-permute-start.16 = (bf16[64,5120]{1,0:T(8,128)(2,1)S(1)}, bf16[64,5120]{1,0:T(8,128)(2,1)S(1)}, u32[]{:S(2)}, u32[]{:S(2)}) collective-permute-start(bf16[64,5120]{1,0:T(8,128)(2,1)S(1)} %collective-permute-done.4.refs_0_), channel_id=1, source_target_pairs={{0,4},{1,13},{2,6},{3,15},{4,8},{5,1},{6,10},{7,3},{8,12},{9,5},{1... | collective-permute-start | bytes 1966088 | tf_op jit(solution)/shard_map/ppermute | solution.py:182
  24.7 1.5 %collective-permute-start.17 = (bf16[64,5120]{1,0:T(8,128)(2,1)S(1)}, bf16[64,5120]{1,0:T(8,128)(2,1)S(1)}, u32[]{:S(2)}, u32[]{:S(2)}) collective-permute-start(bf16[64,5120]{1,0:T(8,128)(2,1)S(1)} %collective-permute-done.4.refs_0_), channel_id=1, source_target_pairs={{0,2},{1,3},{2,0},{3,1},{4,6},{5,7},{6,4},{7,5},{8,10},{9,11},{10,... | collective-permute-start | bytes 1966088 | tf_op jit(solution)/shard_map/ppermute | solution.py:182
  26.2 3.5 %copy-done = bf16[5120,864]{0,1:T(8,128)(2,1)S(1)} copy-done((bf16[5120,864]{0,1:T(8,128)(2,1)S(1)}, bf16[5120,864]{0,1:T(8,128)(2,1)}, u32[]{:S(2)}) %copy-start) | copy-done | bytes 8847384
  29.7 3.5 %copy-done.1 = bf16[5120,864]{0,1:T(8,128)(2,1)S(1)} copy-done((bf16[5120,864]{0,1:T(8,128)(2,1)S(1)}, bf16[5120,864]{0,1:T(8,128)(2,1)}, u32[]{:S(2)}) %copy-start.1) | copy-done | bytes 8847384
  33.2 7.2 %forward.4 = (f32[256,864]{1,0:T(8,128)S(1)}, f32[256,864]{1,0:T(8,128)S(1)}, bf16[256,256]{1,0:T(8,128)(2,1)S(1)}, bf16[256,256]{1,0:T(8,128)(2,1)S(1)}) custom-call(bf16[64,5120]{1,0:T(8,128)(2,1)S(1)} %copy-done.3, bf16[32,5120]{1,0:T(8,128)(2,1)S(1)} %collective-permute-done.2.refs_1_, bf16[32,5120]{1,0:T(8,128)(2,1)S(1)} %collective-permute-done.3.refs_2_, ...), custom_call_target="tpu_custom_call" | custom-call | tf_op jit(solution)/shard_map/forward/pallas_call | solution.py:136
  40.5 0.4 collective-permute-start.10
  41.1 0.4 collective-permute-start.12
  41.5 0.7 collective-permute-done.10.refs_1_
  42.7 1.6 %collective-permute-start.8 = (bf16[64,5248]{1,0:T(8,128)(2,1)S(1)}, bf16[64,5248]{1,0:T(8,128)(2,1)S(1)}, u32[]{:S(2)}, u32[]{:S(2)}) collective-permute-start(bf16[64,5248]{1,0:T(8,128)(2,1)S(1)} %collective-permute-done.refs_0_), channel_id=1, source_target_pairs={{0,4},{1,13},{2,6},{3,15},{4,8},{5,1},{6,10},{7,3},{8,12},{9,5},{1... | collective-permute-start | bytes 2015240 | tf_op jit(solution)/shard_map/ppermute | solution.py:182
  44.3 0.5 collective-permute-start.9
  44.9 3.7 %copy-done.2 = bf16[864,5120]{1,0:T(8,128)(2,1)S(1)} copy-done((bf16[864,5120]{1,0:T(8,128)(2,1)S(1)}, bf16[864,5120]{1,0:T(8,128)(2,1)}, u32[]{:S(2)}) %copy-start.2) | copy-done | bytes 8847384
  48.5 4.5 %backward.4.refs_13_ = f32[256,512]{1,0:T(8,128)S(1)} custom-call(bf16[64,5248]{1,0:T(8,128)(2,1)S(1)} %pad_maximum_fusion.refs_0_, bf16[32,5248]{1,0:T(8,128)(2,1)S(1)} %collective-permute-done.10.refs_1_, bf16[32,5248]{1,0:T(8,128)(2,1)S(1)} %collective-permute-done.11.refs_2_, bf16[64,5248]{1,0:T(8,128)(2,1)S(1)} %collective-permute-done.1.refs_3_, ...), custom_call_target="tpu_custom_call" | custom-call | tf_op jit(solution)/shard_map/backward/pallas_call | solution.py:136
  53.1 0.6 collective-permute-start.18
  53.8 0.5 collective-permute-start.14
  54.3 0.6 collective-permute-done.18.refs_4_
  54.9 0.4 collective-permute-start.15
  55.4 0.5 collective-permute-start.30
  56.0 1.4 %collective-permute-start.31 = (bf16[64,5120]{1,0:T(8,128)(2,1)S(1)}, bf16[64,5120]{1,0:T(8,128)(2,1)S(1)}, u32[]{:S(2)}, u32[]{:S(2)}) collective-permute-start(bf16[64,5120]{1,0:T(8,128)(2,1)S(1)} %collective-permute-done.16.refs_0_), channel_id=1, source_target_pairs={{0,2},{1,3},{2,0},{3,1},{4,6},{5,7},{6,4},{7,5},{8,10},{9,11},{10,... | collective-permute-start | bytes 1966088 | tf_op jit(solution)/shard_map/ppermute | solution.py:182
  57.4 1.4 %collective-permute-start.22 = (bf16[32,5248]{1,0:T(8,128)(2,1)S(1)}, bf16[32,5248]{1,0:T(8,128)(2,1)S(1)}, u32[]{:S(2)}, u32[]{:S(2)}) collective-permute-start(bf16[32,5248]{1,0:T(8,128)(2,1)S(1)} %get-tuple-element.170), channel_id=1, source_target_pairs={{0,1},{1,0},{2,3},{3,2},{4,5},{5,4},{6,7},{7,6},{8,9},{9,8},{10,11... | collective-permute-start | bytes 1007624 | tf_op jit(solution)/shard_map/ppermute | solution.py:182
  58.8 7.2 %forward.5 = (f32[256,864]{1,0:T(8,128)S(1)}, f32[256,864]{1,0:T(8,128)S(1)}, bf16[256,256]{1,0:T(8,128)(2,1)S(1)}, bf16[256,256]{1,0:T(8,128)(2,1)S(1)}) custom-call(bf16[64,5120]{1,0:T(8,128)(2,1)S(1)} %collective-permute-done.4.refs_0_, bf16[32,5120]{1,0:T(8,128)(2,1)S(1)} %collective-permute-done.14.refs_1_, ...), custom_call_target="tpu_custom_call" | custom-call | tf_op jit(solution)/shard_map/forward/pallas_call | solution.py:136
  66.2 0.5 collective-permute-start.27
  66.9 0.9 collective-permute-done.26.refs_1_
  69.5 0.5 collective-permute-done.25.refs_5_
  70.0 4.5 %backward.5.refs_13_ = f32[256,512]{1,0:T(8,128)S(1)} custom-call(bf16[64,5248]{1,0:T(8,128)(2,1)S(1)} %collective-permute-done.refs_0_, bf16[32,5248]{1,0:T(8,128)(2,1)S(1)} %collective-permute-done.22.refs_1_, bf16[32,5248]{1,0:T(8,128)(2,1)S(1)} %collective-permute-done.23.refs_2_, bf16[64,5248]{1,0:T(8,128)(2,1)S(1)} %collective-permute-done.9.refs_3_, ...), custom_call_target="tpu_custom_call" | custom-call | tf_op jit(solution)/shard_map/backward/pallas_call | solution.py:136
  74.5 3.2 %collective-permute-done.30.refs_3_ = bf16[64,5120]{1,0:T(8,128)(2,1)S(1)} collective-permute-done((bf16[64,5120]{1,0:T(8,128)(2,1)S(1)}, bf16[64,5120]{1,0:T(8,128)(2,1)S(1)}, u32[]{:S(2)}, u32[]{:S(2)}) %collective-permute-start.30) | collective-permute-done | bytes 655392 | tf_op jit(solution)/shard_map/ppermute | solution.py:182
  77.7 1.8 %collective-permute-start.39 = (bf16[64,5120]{1,0:T(8,128)(2,1)S(1)}, bf16[64,5120]{1,0:T(8,128)(2,1)S(1)}, u32[]{:S(2)}, u32[]{:S(2)}) collective-permute-start(bf16[64,5120]{1,0:T(8,128)(2,1)S(1)} %collective-permute-done.30.refs_3_), channel_id=1, source_target_pairs={{0,2},{1,3},{2,0},{3,1},{4,6},{5,7},{6,4},{7,5},{8,10},{9,11},{10,... | collective-permute-start | bytes 1966088 | tf_op jit(solution)/shard_map/ppermute | solution.py:182
  79.5 0.5 collective-permute-start.33
  80.2 0.9 collective-permute-done.32.refs_4_
  82.2 0.6 collective-permute-done.35.refs_2_
  82.8 0.5 collective-permute-done.28.refs_1_
  83.3 0.5 collective-permute-done.29.refs_2_
  83.7 7.2 %forward.6 = (f32[256,864]{1,0:T(8,128)S(1)}, f32[256,864]{1,0:T(8,128)S(1)}, bf16[256,256]{1,0:T(8,128)(2,1)S(1)}, bf16[256,256]{1,0:T(8,128)(2,1)S(1)}) custom-call(bf16[64,5120]{1,0:T(8,128)(2,1)S(1)} %collective-permute-done.16.refs_0_, bf16[32,5120]{1,0:T(8,128)(2,1)S(1)} %collective-permute-done.28.refs_1_, ...), custom_call_target="tpu_custom_call" | custom-call | tf_op jit(solution)/shard_map/forward/pallas_call | solution.py:136
  90.9 1.2 collective-permute-done.21.refs_3_
  92.1 1.7 %collective-permute-start.36 = (bf16[64,5248]{1,0:T(8,128)(2,1)S(1)}, bf16[64,5248]{1,0:T(8,128)(2,1)S(1)}, u32[]{:S(2)}, u32[]{:S(2)}) collective-permute-start(bf16[64,5248]{1,0:T(8,128)(2,1)S(1)} %collective-permute-done.21.refs_3_), channel_id=1, source_target_pairs={{0,2},{1,3},{2,0},{3,1},{4,6},{5,7},{6,4},{7,5},{8,10},{9,11},{10,... | collective-permute-start | bytes 2015240 | tf_op jit(solution)/shard_map/ppermute | solution.py:182
  93.8 0.9 collective-permute-done.39.refs_3_
  94.8 0.6 collective-permute-start.37
  95.4 1.9 %collective-permute-done.37.refs_4_ = bf16[32,5248]{1,0:T(8,128)(2,1)S(1)} collective-permute-done((bf16[32,5248]{1,0:T(8,128)(2,1)S(1)}, bf16[32,5248]{1,0:T(8,128)(2,1)S(1)}, u32[]{:S(2)}, u32[]{:S(2)}) %collective-permute-start.37) | collective-permute-done | bytes 335904 | tf_op jit(solution)/shard_map/ppermute | solution.py:182
  97.3 0.5 collective-permute-done.38.refs_5_
  97.8 4.5 %backward.6.refs_13_ = f32[256,512]{1,0:T(8,128)S(1)} custom-call(bf16[64,5248]{1,0:T(8,128)(2,1)S(1)} %collective-permute-done.8.refs_0_, bf16[32,5248]{1,0:T(8,128)(2,1)S(1)} %collective-permute-done.26.refs_1_, bf16[32,5248]{1,0:T(8,128)(2,1)S(1)} %collective-permute-done.27.refs_2_, bf16[64,5248]{1,0:T(8,128)(2,1)S(1)} %collective-permute-done.21.refs_3_, ...), custom_call_target="tpu_custom_call" | custom-call | tf_op jit(solution)/shard_map/backward/pallas_call | solution.py:136
  102.3 7.4 %forward.7 = (f32[256,864]{1,0:T(8,128)S(1)}, f32[256,864]{1,0:T(8,128)S(1)}, bf16[256,256]{1,0:T(8,128)(2,1)S(1)}, bf16[256,256]{1,0:T(8,128)(2,1)S(1)}) custom-call(bf16[64,5120]{1,0:T(8,128)(2,1)S(1)} %collective-permute-done.31.refs_0_, bf16[32,5120]{1,0:T(8,128)(2,1)S(1)} %collective-permute-done.34.refs_1_, ...), custom_call_target="tpu_custom_call" | custom-call | tf_op jit(solution)/shard_map/forward/pallas_call | solution.py:136
  110.0 0.4 collective-permute-start.42
  110.7 0.4 collective-permute-start.44
  111.0 0.5 collective-permute-done.41.refs_1_
  111.5 0.5 collective-permute-done.42.refs_2_
  112.0 0.5 collective-permute-done.43.refs_4_
  112.5 0.5 collective-permute-done.44.refs_5_
  113.0 4.5 %backward.7 = f32[256,512]{1,0:T(8,128)S(1)} custom-call(bf16[64,5248]{1,0:T(8,128)(2,1)S(1)} %collective-permute-done.20.refs_0_, bf16[32,5248]{1,0:T(8,128)(2,1)S(1)} %collective-permute-done.41.refs_1_, bf16[32,5248]{1,0:T(8,128)(2,1)S(1)} %collective-permute-done.42.refs_2_, bf16[64,5248]{1,0:T(8,128)(2,1)S(1)} %collective-permute-done.36.refs_3_, ...), custom_call_target="tpu_custom_call" | custom-call | tf_op jit(solution)/shard_map/backward/pallas_call | solution.py:136
  117.7 1.2 collective-permute-done.45
  119.0 11.4 %all_to_all.5 = bf16[8,16,512]{2,1,0:T(8,128)(2,1)S(1)} all-to-all(bf16[8,16,512]{2,1,0:T(8,128)(2,1)S(1)} %bitcast.18), channel_id=1, replica_groups={{0,2,4,6,8,10,12,14},{1,3,5,7,9,11,13,15},{16,18,20,22,24,26,28,30},{17..., dimensions={0} | all-to-all | bytes 262144 | tf_op jit(solution)/shard_map/all_to_all | solution.py:258
  130.4 0.6 copy.11
  (102 shorter events, 5.9 us)
Async XLA Ops:
  0.0 8.2 %copy-start.5 = (s32[3,864]{1,0:T(4,128)S(1)}, s32[3,864]{1,0:T(4,128)}, u32[]{:S(2)}) copy-start(s32[3,864]{1,0:T(4,128)} %param.16) | copy-start | bytes 31108
  0.0 8.7 %copy-start.4 = (bf16[64,5120]{1,0:T(8,128)(2,1)S(1)}, bf16[64,5120]{1,0:T(8,128)(2,1)}, u32[]{:S(2)}) copy-start(bf16[64,5120]{1,0:T(8,128)(2,1)} %param.11) | copy-start | bytes 1966084
  0.0 20.8 %collective-permute-start.4 = (bf16[64,5120]{1,0:T(8,128)(2,1)}, bf16[64,5120]{1,0:T(8,128)(2,1)S(1)}, u32[]{:S(2)}, u32[]{:S(2)}) collective-permute-start(bf16[64,5120]{1,0:T(8,128)(2,1)} %refs_0_.1), channel_id=1, source_target_pairs={{0,4},{1,13},{2,6},{3,15},{4,8},{5,1},{6,10},{7,3},{8,12},{9,5},{1... | collective-permute-start | bytes 1966088 | tf_op jit(solution)/shard_map/ppermute | solution.py:182
  3.0 17.8 %collective-permute-start.5 = (bf16[64,5120]{1,0:T(8,128)(2,1)}, bf16[64,5120]{1,0:T(8,128)(2,1)S(1)}, u32[]{:S(2)}, u32[]{:S(2)}) collective-permute-start(bf16[64,5120]{1,0:T(8,128)(2,1)} %refs_0_.1), channel_id=1, source_target_pairs={{0,2},{1,3},{2,0},{3,1},{4,6},{5,7},{6,4},{7,5},{8,10},{9,11},{10,... | collective-permute-start | bytes 1966088 | tf_op jit(solution)/shard_map/ppermute | solution.py:182
  8.2 13.5 %copy-start.3 = (bf16[64,5120]{1,0:T(8,128)(2,1)S(1)}, bf16[64,5120]{1,0:T(8,128)(2,1)}, u32[]{:S(2)}) copy-start(bf16[64,5120]{1,0:T(8,128)(2,1)} %refs_0_.1) | copy-start | bytes 1966084
  8.8 31.6 %collective-permute-start = (bf16[64,5248]{1,0:T(8,128)(2,1)S(1)}, bf16[64,5248]{1,0:T(8,128)(2,1)S(1)}, u32[]{:S(2)}, u32[]{:S(2)}) collective-permute-start(bf16[64,5248]{1,0:T(8,128)(2,1)S(1)} %pad_maximum_fusion.refs_0_), channel_id=1, source_target_pairs={{0,4},{1,13},{2,6},{3,15},{4,8},{5,1},{6,10},{7,3},{8,12},{9,5},{1... | collective-permute-start | bytes 2015240 | tf_op jit(solution)/shard_map/ppermute | solution.py:182
  10.4 30.0 %collective-permute-start.1 = (bf16[64,5248]{1,0:T(8,128)(2,1)S(1)}, bf16[64,5248]{1,0:T(8,128)(2,1)S(1)}, u32[]{:S(2)}, u32[]{:S(2)}) collective-permute-start(bf16[64,5248]{1,0:T(8,128)(2,1)S(1)} %pad_maximum_fusion.refs_0_), channel_id=1, source_target_pairs={{0,2},{1,3},{2,0},{3,1},{4,6},{5,7},{6,4},{7,5},{8,10},{9,11},{10,... | collective-permute-start | bytes 2015240 | tf_op jit(solution)/shard_map/ppermute | solution.py:182
  20.9 2.0 %collective-permute-start.6 = (bf16[32,5120]{1,0:T(8,128)(2,1)S(1)}, bf16[32,5120]{1,0:T(8,128)(2,1)S(1)}, u32[]{:S(2)}, u32[]{:S(2)}) collective-permute-start(bf16[32,5120]{1,0:T(8,128)(2,1)S(1)} %get-tuple-element.186), channel_id=1, source_target_pairs={{0,1},{1,0},{2,3},{3,2},{4,5},{5,4},{6,7},{7,6},{8,9},{9,8},{10,11... | collective-permute-start | bytes 983048 | tf_op jit(solution)/shard_map/ppermute | solution.py:182
  21.6 1.7 %collective-permute-start.7 = (bf16[32,5120]{1,0:T(8,128)(2,1)S(1)}, bf16[32,5120]{1,0:T(8,128)(2,1)S(1)}, u32[]{:S(2)}, u32[]{:S(2)}) collective-permute-start(bf16[32,5120]{1,0:T(8,128)(2,1)S(1)} %get-tuple-element.185), channel_id=1, source_target_pairs={{0,1},{1,0},{2,3},{3,2},{4,5},{5,4},{6,7},{7,6},{8,9},{9,8},{10,11... | collective-permute-start | bytes 983048 | tf_op jit(solution)/shard_map/ppermute | solution.py:182
  21.8 2.9 %collective-permute-start.2 = (bf16[32,5120]{1,0:T(8,128)(2,1)S(1)}, bf16[32,5120]{1,0:T(8,128)(2,1)S(1)}, u32[]{:S(2)}, u32[]{:S(2)}) collective-permute-start(bf16[32,5120]{1,0:T(8,128)(2,1)S(1)} %get-tuple-element.188), channel_id=1, source_target_pairs={{0,1},{1,0},{2,3},{3,2},{4,5},{5,4},{6,7},{7,6},{8,9},{9,8},{10,11... | collective-permute-start | bytes 983048 | tf_op jit(solution)/shard_map/ppermute | solution.py:182
  22.9 3.3 %collective-permute-start.3 = (bf16[32,5120]{1,0:T(8,128)(2,1)S(1)}, bf16[32,5120]{1,0:T(8,128)(2,1)S(1)}, u32[]{:S(2)}, u32[]{:S(2)}) collective-permute-start(bf16[32,5120]{1,0:T(8,128)(2,1)S(1)} %get-tuple-element.187), channel_id=1, source_target_pairs={{0,1},{1,0},{2,3},{3,2},{4,5},{5,4},{6,7},{7,6},{8,9},{9,8},{10,11... | collective-permute-start | bytes 983048 | tf_op jit(solution)/shard_map/ppermute | solution.py:182
  23.4 29.7 %collective-permute-start.16 = (bf16[64,5120]{1,0:T(8,128)(2,1)S(1)}, bf16[64,5120]{1,0:T(8,128)(2,1)S(1)}, u32[]{:S(2)}, u32[]{:S(2)}) collective-permute-start(bf16[64,5120]{1,0:T(8,128)(2,1)S(1)} %collective-permute-done.4.refs_0_), channel_id=1, source_target_pairs={{0,4},{1,13},{2,6},{3,15},{4,8},{5,1},{6,10},{7,3},{8,12},{9,5},{1... | collective-permute-start | bytes 1966088 | tf_op jit(solution)/shard_map/ppermute | solution.py:182
  24.7 28.3 %collective-permute-start.17 = (bf16[64,5120]{1,0:T(8,128)(2,1)S(1)}, bf16[64,5120]{1,0:T(8,128)(2,1)S(1)}, u32[]{:S(2)}, u32[]{:S(2)}) collective-permute-start(bf16[64,5120]{1,0:T(8,128)(2,1)S(1)} %collective-permute-done.4.refs_0_), channel_id=1, source_target_pairs={{0,2},{1,3},{2,0},{3,1},{4,6},{5,7},{6,4},{7,5},{8,10},{9,11},{10,... | collective-permute-start | bytes 1966088 | tf_op jit(solution)/shard_map/ppermute | solution.py:182
  26.2 3.5 %copy-start = (bf16[5120,864]{0,1:T(8,128)(2,1)S(1)}, bf16[5120,864]{0,1:T(8,128)(2,1)}, u32[]{:S(2)}) copy-start(bf16[5120,864]{0,1:T(8,128)(2,1)} %param.13) | copy-start | bytes 26542084
  29.7 3.5 %copy-start.1 = (bf16[5120,864]{0,1:T(8,128)(2,1)S(1)}, bf16[5120,864]{0,1:T(8,128)(2,1)}, u32[]{:S(2)}) copy-start(bf16[5120,864]{0,1:T(8,128)(2,1)} %param.14) | copy-start | bytes 26542084
  33.2 25.6 %slice-start.3 = ((s8[8847360]{0:T(1024)(128)(4,1)}), s8[4194304]{0:T(1024)(128)(4,1)S(1)}, s32[]{:S(2)}) async-start(s8[8847360]{0:T(1024)(128)(4,1)} %bitcast.11), calls=%async_computation.4 | async-start | bytes 8388608
  33.2 25.6 %slice-start.4 = ((s8[8847360]{0:T(1024)(128)(4,1)}), s8[4194304]{0:T(1024)(128)(4,1)S(1)}, s32[]{:S(2)}) async-start(s8[8847360]{0:T(1024)(128)(4,1)} %bitcast.11), calls=%async_computation.5 | async-start | bytes 8388608
  40.5 1.7 %collective-permute-start.10 = (bf16[32,5248]{1,0:T(8,128)(2,1)S(1)}, bf16[32,5248]{1,0:T(8,128)(2,1)S(1)}, u32[]{:S(2)}, u32[]{:S(2)}) collective-permute-start(bf16[32,5248]{1,0:T(8,128)(2,1)S(1)} %get-tuple-element.174), channel_id=1, source_target_pairs={{0,1},{1,0},{2,3},{3,2},{4,5},{5,4},{6,7},{7,6},{8,9},{9,8},{10,11... | collective-permute-start | bytes 1007624 | tf_op jit(solution)/shard_map/ppermute | solution.py:182
  40.9 1.8 %collective-permute-start.11 = (bf16[32,5248]{1,0:T(8,128)(2,1)S(1)}, bf16[32,5248]{1,0:T(8,128)(2,1)S(1)}, u32[]{:S(2)}, u32[]{:S(2)}) collective-permute-start(bf16[32,5248]{1,0:T(8,128)(2,1)S(1)} %get-tuple-element.173), channel_id=1, source_target_pairs={{0,1},{1,0},{2,3},{3,2},{4,5},{5,4},{6,7},{7,6},{8,9},{9,8},{10,11... | collective-permute-start | bytes 1007624 | tf_op jit(solution)/shard_map/ppermute | solution.py:182
  41.1 3.1 %collective-permute-start.12 = (bf16[32,5248]{1,0:T(8,128)(2,1)S(1)}, bf16[32,5248]{1,0:T(8,128)(2,1)S(1)}, u32[]{:S(2)}, u32[]{:S(2)}) collective-permute-start(bf16[32,5248]{1,0:T(8,128)(2,1)S(1)} %get-tuple-element.172), channel_id=1, source_target_pairs={{0,1},{1,0},{2,3},{3,2},{4,5},{5,4},{6,7},{7,6},{8,9},{9,8},{10,11... | collective-permute-start | bytes 1007624 | tf_op jit(solution)/shard_map/ppermute | solution.py:182
  42.2 2.6 %collective-permute-start.13 = (bf16[32,5248]{1,0:T(8,128)(2,1)S(1)}, bf16[32,5248]{1,0:T(8,128)(2,1)S(1)}, u32[]{:S(2)}, u32[]{:S(2)}) collective-permute-start(bf16[32,5248]{1,0:T(8,128)(2,1)S(1)} %get-tuple-element.171), channel_id=1, source_target_pairs={{0,1},{1,0},{2,3},{3,2},{4,5},{5,4},{6,7},{7,6},{8,9},{9,8},{10,11... | collective-permute-start | bytes 1007624 | tf_op jit(solution)/shard_map/ppermute | solution.py:182
  42.7 23.4 %collective-permute-start.8 = (bf16[64,5248]{1,0:T(8,128)(2,1)S(1)}, bf16[64,5248]{1,0:T(8,128)(2,1)S(1)}, u32[]{:S(2)}, u32[]{:S(2)}) collective-permute-start(bf16[64,5248]{1,0:T(8,128)(2,1)S(1)} %collective-permute-done.refs_0_), channel_id=1, source_target_pairs={{0,4},{1,13},{2,6},{3,15},{4,8},{5,1},{6,10},{7,3},{8,12},{9,5},{1... | collective-permute-start | bytes 2015240 | tf_op jit(solution)/shard_map/ppermute | solution.py:182
  44.3 21.8 %collective-permute-start.9 = (bf16[64,5248]{1,0:T(8,128)(2,1)S(1)}, bf16[64,5248]{1,0:T(8,128)(2,1)S(1)}, u32[]{:S(2)}, u32[]{:S(2)}) collective-permute-start(bf16[64,5248]{1,0:T(8,128)(2,1)S(1)} %collective-permute-done.refs_0_), channel_id=1, source_target_pairs={{0,2},{1,3},{2,0},{3,1},{4,6},{5,7},{6,4},{7,5},{8,10},{9,11},{10,... | collective-permute-start | bytes 2015240 | tf_op jit(solution)/shard_map/ppermute | solution.py:182
  44.8 14.0 %slice-start = ((s8[8847360]{0:T(1024)(128)(4,1)}), s8[4194304]{0:T(1024)(128)(4,1)S(1)}, s32[]{:S(2)}) async-start(s8[8847360]{0:T(1024)(128)(4,1)} %bitcast.5), calls=%async_computation.1 | async-start | bytes 8388608
  44.8 3.7 %copy-start.2 = (bf16[864,5120]{1,0:T(8,128)(2,1)S(1)}, bf16[864,5120]{1,0:T(8,128)(2,1)}, u32[]{:S(2)}) copy-start(bf16[864,5120]{1,0:T(8,128)(2,1)} %refs_6_.7) | copy-start | bytes 26542084
  48.5 10.3 %slice-start.1 = ((s8[8847360]{0:T(1024)(128)(4,1)}), s8[4194304]{0:T(1024)(128)(4,1)S(1)}, s32[]{:S(2)}) async-start(s8[8847360]{0:T(1024)(128)(4,1)} %bitcast.5), calls=%async_computation.2 | async-start | bytes 8388608
  48.5 10.3 %slice-start.2 = ((s8[8847360]{0:T(1024)(128)(4,1)}), s8[458752]{0:T(1024)(128)(4,1)S(1)}, s32[]{:S(2)}) async-start(s8[8847360]{0:T(1024)(128)(4,1)} %bitcast.5), calls=%async_computation.3 | async-start | bytes 917504
  48.5 10.3 %slice-start.5 = ((s8[8847360]{0:T(1024)(128)(4,1)}), s8[458752]{0:T(1024)(128)(4,1)S(1)}, s32[]{:S(2)}) async-start(s8[8847360]{0:T(1024)(128)(4,1)} %bitcast.11), calls=%async_computation.6 | async-start | bytes 917504
  53.1 1.8 %collective-permute-start.18 = (bf16[32,5120]{1,0:T(8,128)(2,1)S(1)}, bf16[32,5120]{1,0:T(8,128)(2,1)S(1)}, u32[]{:S(2)}, u32[]{:S(2)}) collective-permute-start(bf16[32,5120]{1,0:T(8,128)(2,1)S(1)} %get-tuple-element.182), channel_id=1, source_target_pairs={{0,1},{1,0},{2,3},{3,2},{4,5},{5,4},{6,7},{7,6},{8,9},{9,8},{10,11... | collective-permute-start | bytes 983048 | tf_op jit(solution)/shard_map/ppermute | solution.py:182
  53.7 1.7 %collective-permute-start.19 = (bf16[32,5120]{1,0:T(8,128)(2,1)S(1)}, bf16[32,5120]{1,0:T(8,128)(2,1)S(1)}, u32[]{:S(2)}, u32[]{:S(2)}) collective-permute-start(bf16[32,5120]{1,0:T(8,128)(2,1)S(1)} %get-tuple-element.181), channel_id=1, source_target_pairs={{0,1},{1,0},{2,3},{3,2},{4,5},{5,4},{6,7},{7,6},{8,9},{9,8},{10,11... | collective-permute-start | bytes 983048 | tf_op jit(solution)/shard_map/ppermute | solution.py:182
  53.8 2.2 %collective-permute-start.14 = (bf16[32,5120]{1,0:T(8,128)(2,1)S(1)}, bf16[32,5120]{1,0:T(8,128)(2,1)S(1)}, u32[]{:S(2)}, u32[]{:S(2)}) collective-permute-start(bf16[32,5120]{1,0:T(8,128)(2,1)S(1)} %get-tuple-element.184), channel_id=1, source_target_pairs={{0,1},{1,0},{2,3},{3,2},{4,5},{5,4},{6,7},{7,6},{8,9},{9,8},{10,11... | collective-permute-start | bytes 983048 | tf_op jit(solution)/shard_map/ppermute | solution.py:182
  54.9 2.5 %collective-permute-start.15 = (bf16[32,5120]{1,0:T(8,128)(2,1)S(1)}, bf16[32,5120]{1,0:T(8,128)(2,1)S(1)}, u32[]{:S(2)}, u32[]{:S(2)}) collective-permute-start(bf16[32,5120]{1,0:T(8,128)(2,1)S(1)} %get-tuple-element.183), channel_id=1, source_target_pairs={{0,1},{1,0},{2,3},{3,2},{4,5},{5,4},{6,7},{7,6},{8,9},{9,8},{10,11... | collective-permute-start | bytes 983048 | tf_op jit(solution)/shard_map/ppermute | solution.py:182
  55.4 22.3 %collective-permute-start.30 = (bf16[64,5120]{1,0:T(8,128)(2,1)S(1)}, bf16[64,5120]{1,0:T(8,128)(2,1)S(1)}, u32[]{:S(2)}, u32[]{:S(2)}) collective-permute-start(bf16[64,5120]{1,0:T(8,128)(2,1)S(1)} %collective-permute-done.16.refs_0_), channel_id=1, source_target_pairs={{0,4},{1,13},{2,6},{3,15},{4,8},{5,1},{6,10},{7,3},{8,12},{9,5},{1... | collective-permute-start | bytes 1966088 | tf_op jit(solution)/shard_map/ppermute | solution.py:182
  56.0 21.7 %collective-permute-start.31 = (bf16[64,5120]{1,0:T(8,128)(2,1)S(1)}, bf16[64,5120]{1,0:T(8,128)(2,1)S(1)}, u32[]{:S(2)}, u32[]{:S(2)}) collective-permute-start(bf16[64,5120]{1,0:T(8,128)(2,1)S(1)} %collective-permute-done.16.refs_0_), channel_id=1, source_target_pairs={{0,2},{1,3},{2,0},{3,1},{4,6},{5,7},{6,4},{7,5},{8,10},{9,11},{10,... | collective-permute-start | bytes 1966088 | tf_op jit(solution)/shard_map/ppermute | solution.py:182
  57.4 12.6 %slice-start.6 = ((s8[8847360]{0:T(1024)(128)(4,1)}), s8[4194304]{0:T(1024)(128)(4,1)S(1)}, s32[]{:S(2)}) async-start(s8[8847360]{0:T(1024)(128)(4,1)} %bitcast.16), calls=%async_computation.7 | async-start | bytes 8388608
  57.4 12.6 %slice-start.7 = ((s8[8847360]{0:T(1024)(128)(4,1)}), s8[4194304]{0:T(1024)(128)(4,1)S(1)}, s32[]{:S(2)}) async-start(s8[8847360]{0:T(1024)(128)(4,1)} %bitcast.16), calls=%async_computation.8 | async-start | bytes 8388608
  57.4 12.6 %slice-start.8 = ((s8[8847360]{0:T(1024)(128)(4,1)}), s8[458752]{0:T(1024)(128)(4,1)S(1)}, s32[]{:S(2)}) async-start(s8[8847360]{0:T(1024)(128)(4,1)} %bitcast.16), calls=%async_computation.9 | async-start | bytes 917504
  57.4 9.4 %collective-permute-start.22 = (bf16[32,5248]{1,0:T(8,128)(2,1)S(1)}, bf16[32,5248]{1,0:T(8,128)(2,1)S(1)}, u32[]{:S(2)}, u32[]{:S(2)}) collective-permute-start(bf16[32,5248]{1,0:T(8,128)(2,1)S(1)} %get-tuple-element.170), channel_id=1, source_target_pairs={{0,1},{1,0},{2,3},{3,2},{4,5},{5,4},{6,7},{7,6},{8,9},{9,8},{10,11... | collective-permute-start | bytes 1007624 | tf_op jit(solution)/shard_map/ppermute | solution.py:182
  66.1 1.7 %collective-permute-start.26 = (bf16[32,5248]{1,0:T(8,128)(2,1)S(1)}, bf16[32,5248]{1,0:T(8,128)(2,1)S(1)}, u32[]{:S(2)}, u32[]{:S(2)}) collective-permute-start(bf16[32,5248]{1,0:T(8,128)(2,1)S(1)} %get-tuple-element.166), channel_id=1, source_target_pairs={{0,1},{1,0},{2,3},{3,2},{4,5},{5,4},{6,7},{7,6},{8,9},{9,8},{10,11... | collective-permute-start | bytes 1007624 | tf_op jit(solution)/shard_map/ppermute | solution.py:182
  66.2 2.1 %collective-permute-start.27 = (bf16[32,5248]{1,0:T(8,128)(2,1)S(1)}, bf16[32,5248]{1,0:T(8,128)(2,1)S(1)}, u32[]{:S(2)}, u32[]{:S(2)}) collective-permute-start(bf16[32,5248]{1,0:T(8,128)(2,1)S(1)} %get-tuple-element.165), channel_id=1, source_target_pairs={{0,1},{1,0},{2,3},{3,2},{4,5},{5,4},{6,7},{7,6},{8,9},{9,8},{10,11... | collective-permute-start | bytes 1007624 | tf_op jit(solution)/shard_map/ppermute | solution.py:182
  66.7 2.0 %collective-permute-start.23 = (bf16[32,5248]{1,0:T(8,128)(2,1)S(1)}, bf16[32,5248]{1,0:T(8,128)(2,1)S(1)}, u32[]{:S(2)}, u32[]{:S(2)}) collective-permute-start(bf16[32,5248]{1,0:T(8,128)(2,1)S(1)} %get-tuple-element.169), channel_id=1, source_target_pairs={{0,1},{1,0},{2,3},{3,2},{4,5},{5,4},{6,7},{7,6},{8,9},{9,8},{10,11... | collective-permute-start | bytes 1007624 | tf_op jit(solution)/shard_map/ppermute | solution.py:182
  67.8 1.6 %collective-permute-start.24 = (bf16[32,5248]{1,0:T(8,128)(2,1)S(1)}, bf16[32,5248]{1,0:T(8,128)(2,1)S(1)}, u32[]{:S(2)}, u32[]{:S(2)}) collective-permute-start(bf16[32,5248]{1,0:T(8,128)(2,1)S(1)} %get-tuple-element.168), channel_id=1, source_target_pairs={{0,1},{1,0},{2,3},{3,2},{4,5},{5,4},{6,7},{7,6},{8,9},{9,8},{10,11... | collective-permute-start | bytes 1007624 | tf_op jit(solution)/shard_map/ppermute | solution.py:182
  68.3 1.6 %collective-permute-start.25 = (bf16[32,5248]{1,0:T(8,128)(2,1)S(1)}, bf16[32,5248]{1,0:T(8,128)(2,1)S(1)}, u32[]{:S(2)}, u32[]{:S(2)}) collective-permute-start(bf16[32,5248]{1,0:T(8,128)(2,1)S(1)} %get-tuple-element.167), channel_id=1, source_target_pairs={{0,1},{1,0},{2,3},{3,2},{4,5},{5,4},{6,7},{7,6},{8,9},{9,8},{10,11... | collective-permute-start | bytes 1007624 | tf_op jit(solution)/shard_map/ppermute | solution.py:182
  68.8 23.3 %collective-permute-start.21 = (bf16[64,5248]{1,0:T(8,128)(2,1)S(1)}, bf16[64,5248]{1,0:T(8,128)(2,1)S(1)}, u32[]{:S(2)}, u32[]{:S(2)}) collective-permute-start(bf16[64,5248]{1,0:T(8,128)(2,1)S(1)} %collective-permute-done.8.refs_0_), channel_id=1, source_target_pairs={{0,4},{1,13},{2,6},{3,15},{4,8},{5,1},{6,10},{7,3},{8,12},{9,5},{1... | collective-permute-start | bytes 2015240 | tf_op jit(solution)/shard_map/ppermute | solution.py:182
  77.7 17.0 %collective-permute-start.39 = (bf16[64,5120]{1,0:T(8,128)(2,1)S(1)}, bf16[64,5120]{1,0:T(8,128)(2,1)S(1)}, u32[]{:S(2)}, u32[]{:S(2)}) collective-permute-start(bf16[64,5120]{1,0:T(8,128)(2,1)S(1)} %collective-permute-done.30.refs_3_), channel_id=1, source_target_pairs={{0,2},{1,3},{2,0},{3,1},{4,6},{5,7},{6,4},{7,5},{8,10},{9,11},{10,... | collective-permute-start | bytes 1966088 | tf_op jit(solution)/shard_map/ppermute | solution.py:182
  79.5 1.6 %collective-permute-start.32 = (bf16[32,5120]{1,0:T(8,128)(2,1)S(1)}, bf16[32,5120]{1,0:T(8,128)(2,1)S(1)}, u32[]{:S(2)}, u32[]{:S(2)}) collective-permute-start(bf16[32,5120]{1,0:T(8,128)(2,1)S(1)} %get-tuple-element.178), channel_id=1, source_target_pairs={{0,1},{1,0},{2,3},{3,2},{4,5},{5,4},{6,7},{7,6},{8,9},{9,8},{10,11... | collective-permute-start | bytes 983048 | tf_op jit(solution)/shard_map/ppermute | solution.py:182
  79.5 2.1 %collective-permute-start.33 = (bf16[32,5120]{1,0:T(8,128)(2,1)S(1)}, bf16[32,5120]{1,0:T(8,128)(2,1)S(1)}, u32[]{:S(2)}, u32[]{:S(2)}) collective-permute-start(bf16[32,5120]{1,0:T(8,128)(2,1)S(1)} %get-tuple-element.177), channel_id=1, source_target_pairs={{0,1},{1,0},{2,3},{3,2},{4,5},{5,4},{6,7},{7,6},{8,9},{9,8},{10,11... | collective-permute-start | bytes 983048 | tf_op jit(solution)/shard_map/ppermute | solution.py:182
  80.1 2.0 %collective-permute-start.34 = (bf16[32,5120]{1,0:T(8,128)(2,1)S(1)}, bf16[32,5120]{1,0:T(8,128)(2,1)S(1)}, u32[]{:S(2)}, u32[]{:S(2)}) collective-permute-start(bf16[32,5120]{1,0:T(8,128)(2,1)S(1)} %get-tuple-element.176), channel_id=1, source_target_pairs={{0,1},{1,0},{2,3},{3,2},{4,5},{5,4},{6,7},{7,6},{8,9},{9,8},{10,11... | collective-permute-start | bytes 983048 | tf_op jit(solution)/shard_map/ppermute | solution.py:182
  81.2 1.6 %collective-permute-start.35 = (bf16[32,5120]{1,0:T(8,128)(2,1)S(1)}, bf16[32,5120]{1,0:T(8,128)(2,1)S(1)}, u32[]{:S(2)}, u32[]{:S(2)}) collective-permute-start(bf16[32,5120]{1,0:T(8,128)(2,1)S(1)} %get-tuple-element.175), channel_id=1, source_target_pairs={{0,1},{1,0},{2,3},{3,2},{4,5},{5,4},{6,7},{7,6},{8,9},{9,8},{10,11... | collective-permute-start | bytes 983048 | tf_op jit(solution)/shard_map/ppermute | solution.py:182
  81.6 1.6 %collective-permute-start.28 = (bf16[32,5120]{1,0:T(8,128)(2,1)S(1)}, bf16[32,5120]{1,0:T(8,128)(2,1)S(1)}, u32[]{:S(2)}, u32[]{:S(2)}) collective-permute-start(bf16[32,5120]{1,0:T(8,128)(2,1)S(1)} %get-tuple-element.180), channel_id=1, source_target_pairs={{0,1},{1,0},{2,3},{3,2},{4,5},{5,4},{6,7},{7,6},{8,9},{9,8},{10,11... | collective-permute-start | bytes 983048 | tf_op jit(solution)/shard_map/ppermute | solution.py:182
  82.1 1.6 %collective-permute-start.29 = (bf16[32,5120]{1,0:T(8,128)(2,1)S(1)}, bf16[32,5120]{1,0:T(8,128)(2,1)S(1)}, u32[]{:S(2)}, u32[]{:S(2)}) collective-permute-start(bf16[32,5120]{1,0:T(8,128)(2,1)S(1)} %get-tuple-element.179), channel_id=1, source_target_pairs={{0,1},{1,0},{2,3},{3,2},{4,5},{5,4},{6,7},{7,6},{8,9},{9,8},{10,11... | collective-permute-start | bytes 983048 | tf_op jit(solution)/shard_map/ppermute | solution.py:182
  82.8 26.9 %collective-permute-start.20 = (bf16[64,5248]{1,0:T(8,128)(2,1)S(1)}, bf16[64,5248]{1,0:T(8,128)(2,1)S(1)}, u32[]{:S(2)}, u32[]{:S(2)}) collective-permute-start(bf16[64,5248]{1,0:T(8,128)(2,1)S(1)} %collective-permute-done.9.refs_3_), channel_id=1, source_target_pairs={{0,4},{1,13},{2,6},{3,15},{4,8},{5,1},{6,10},{7,3},{8,12},{9,5},{1... | collective-permute-start | bytes 2015240 | tf_op jit(solution)/shard_map/ppermute | solution.py:182
  92.1 17.7 %collective-permute-start.36 = (bf16[64,5248]{1,0:T(8,128)(2,1)S(1)}, bf16[64,5248]{1,0:T(8,128)(2,1)S(1)}, u32[]{:S(2)}, u32[]{:S(2)}) collective-permute-start(bf16[64,5248]{1,0:T(8,128)(2,1)S(1)} %collective-permute-done.21.refs_3_), channel_id=1, source_target_pairs={{0,2},{1,3},{2,0},{3,1},{4,6},{5,7},{6,4},{7,5},{8,10},{9,11},{10,... | collective-permute-start | bytes 2015240 | tf_op jit(solution)/shard_map/ppermute | solution.py:182
  94.7 7.6 %collective-permute-start.40 = (bf16[64,5120]{1,0:T(8,128)(2,1)S(1)}, bf16[64,5120]{1,0:T(8,128)(2,1)S(1)}, u32[]{:S(2)}, u32[]{:S(2)}) collective-permute-start(bf16[64,5120]{1,0:T(8,128)(2,1)S(1)} %collective-permute-done.39.refs_3_), channel_id=1, source_target_pairs={{0,1},{1,0},{2,3},{3,2},{4,5},{5,4},{6,7},{7,6},{8,9},{9,8},{10,11... | collective-permute-start | bytes 1966088 | tf_op jit(solution)/shard_map/ppermute | solution.py:182
  94.8 2.5 %collective-permute-start.37 = (bf16[32,5248]{1,0:T(8,128)(2,1)S(1)}, bf16[32,5248]{1,0:T(8,128)(2,1)S(1)}, u32[]{:S(2)}, u32[]{:S(2)}) collective-permute-start(bf16[32,5248]{1,0:T(8,128)(2,1)S(1)} %get-tuple-element.164), channel_id=1, source_target_pairs={{0,1},{1,0},{2,3},{3,2},{4,5},{5,4},{6,7},{7,6},{8,9},{9,8},{10,11... | collective-permute-start | bytes 1007624 | tf_op jit(solution)/shard_map/ppermute | solution.py:182
  95.3 2.4 %collective-permute-start.38 = (bf16[32,5248]{1,0:T(8,128)(2,1)S(1)}, bf16[32,5248]{1,0:T(8,128)(2,1)S(1)}, u32[]{:S(2)}, u32[]{:S(2)}) collective-permute-start(bf16[32,5248]{1,0:T(8,128)(2,1)S(1)} %get-tuple-element.163), channel_id=1, source_target_pairs={{0,1},{1,0},{2,3},{3,2},{4,5},{5,4},{6,7},{7,6},{8,9},{9,8},{10,11... | collective-permute-start | bytes 1007624 | tf_op jit(solution)/shard_map/ppermute | solution.py:182
  109.8 1.7 %collective-permute-start.41 = (bf16[32,5248]{1,0:T(8,128)(2,1)S(1)}, bf16[32,5248]{1,0:T(8,128)(2,1)S(1)}, u32[]{:S(2)}, u32[]{:S(2)}) collective-permute-start(bf16[32,5248]{1,0:T(8,128)(2,1)S(1)} %get-tuple-element.162), channel_id=1, source_target_pairs={{0,1},{1,0},{2,3},{3,2},{4,5},{5,4},{6,7},{7,6},{8,9},{9,8},{10,11... | collective-permute-start | bytes 1007624 | tf_op jit(solution)/shard_map/ppermute | solution.py:182
  110.0 2.0 %collective-permute-start.42 = (bf16[32,5248]{1,0:T(8,128)(2,1)S(1)}, bf16[32,5248]{1,0:T(8,128)(2,1)S(1)}, u32[]{:S(2)}, u32[]{:S(2)}) collective-permute-start(bf16[32,5248]{1,0:T(8,128)(2,1)S(1)} %get-tuple-element.161), channel_id=1, source_target_pairs={{0,1},{1,0},{2,3},{3,2},{4,5},{5,4},{6,7},{7,6},{8,9},{9,8},{10,11... | collective-permute-start | bytes 1007624 | tf_op jit(solution)/shard_map/ppermute | solution.py:182
  110.5 2.0 %collective-permute-start.43 = (bf16[32,5248]{1,0:T(8,128)(2,1)S(1)}, bf16[32,5248]{1,0:T(8,128)(2,1)S(1)}, u32[]{:S(2)}, u32[]{:S(2)}) collective-permute-start(bf16[32,5248]{1,0:T(8,128)(2,1)S(1)} %get-tuple-element.160), channel_id=1, source_target_pairs={{0,1},{1,0},{2,3},{3,2},{4,5},{5,4},{6,7},{7,6},{8,9},{9,8},{10,11... | collective-permute-start | bytes 1007624 | tf_op jit(solution)/shard_map/ppermute | solution.py:182
  110.7 2.3 %collective-permute-start.44 = (bf16[32,5248]{1,0:T(8,128)(2,1)S(1)}, bf16[32,5248]{1,0:T(8,128)(2,1)S(1)}, u32[]{:S(2)}, u32[]{:S(2)}) collective-permute-start(bf16[32,5248]{1,0:T(8,128)(2,1)S(1)} %get-tuple-element.159), channel_id=1, source_target_pairs={{0,1},{1,0},{2,3},{3,2},{4,5},{5,4},{6,7},{7,6},{8,9},{9,8},{10,11... | collective-permute-start | bytes 1007624 | tf_op jit(solution)/shard_map/ppermute | solution.py:182
  117.5 1.4 %collective-permute-start.45 = (bf16[128,512]{1,0:T(8,128)(2,1)S(1)}, bf16[128,512]{1,0:T(8,128)(2,1)S(1)}, u32[]{:S(2)}, u32[]{:S(2)}) collective-permute-start(bf16[128,512]{1,0:T(8,128)(2,1)S(1)} %slice.15), channel_id=1, source_target_pairs={{0,1},{1,0},{2,3},{3,2},{4,5},{5,4},{6,7},{7,6},{8,9},{9,8},{10,11... | collective-permute-start | bytes 393224 | tf_op jit(solution)/shard_map/ppermute | solution.py:182
